TPU v7x, 32 devices: a whole 2x2x4 slice. The times are simulated.
32 devices in a mesh: dp: 8 (over y, x, core), expert: 4 (over z).
Axes of the slice: x: 2, y: 2, z: 4, core: 2. Of those that a mesh axis runs over, the one named last changes fastest.
Arguments:
- grad_out: bfloat16 [4096, 2048], P(('dp', 'expert')), may hold values from -6 to 6
- expert_ids: int32 [4096, 8], P(('dp', 'expert')), may hold values from 0 to 15, all different within a row; in each aligned block of 128 rows (0 to 127, 128 to 255, ...) at most 72 rows name the same one
- route_weights: bfloat16 [4096, 8], P(('dp', 'expert')), may hold values from 0.049804688 to 0.5
- hidden_cache: bfloat16 [8, 16, 4, 72, 768], P('dp', 'expert'), may hold values from -0.29882812 to 0.29882812
- w_down: bfloat16 [16, 768, 2048], P('expert', 'dp'), may hold values from -0.21875 to 0.21875
Outputs:
- grad_hidden: bfloat16 [8, 16, 4, 72, 768], P('dp', 'expert')
- grad_down: bfloat16 [16, 768, 2048], P('expert', 'dp')
- grad_probs: float32 [4096, 8], P(('dp', 'expert'))
Inputs may be any that keep to these rules, and one draw needn't show every extreme that they name: `expert_ids`: in each aligned block of 128 rows (the rows of one device) every row names 8 different experts and no expert is named by more than 72 rows; some expert is named by exactly 72 rows in some blocks.
All inputs are finite; a program needn't handle non-finite values.
Results may differ from a plain program's by a relative error of at most 0.012.
Values may be sent and summed in bfloat16 or wider, within the bound.
No kernel may reach another device: no remote copies, remote signals or barrier semaphores. Data moves between devices by JAX's collectives and lax.ppermute only.
A program may use at most 128 MiB of HBM per device.

v0:
```python
import jax
import jax.numpy as jnp
from jax import lax
from jax.sharding import PartitionSpec as P

EXPERTS = 16
TOP = 8
CAP = 72


def route_table(expert_ids):
    routed = expert_ids.reshape(-1)
    total_routes = routed.shape[0]
    onehot = (routed[:, None] == jnp.arange(EXPERTS, dtype=jnp.int32)[None, :]).astype(jnp.int32)
    before = jnp.cumsum(onehot, axis=0) - onehot
    slot_rank = jnp.sum(before * onehot, axis=1)
    target = routed * CAP + slot_rank
    route_of = (
        jnp.zeros((EXPERTS * CAP,), jnp.int32)
        .at[target]
        .set(jnp.arange(total_routes, dtype=jnp.int32))
    )
    filled = jnp.zeros((EXPERTS * CAP,), jnp.int32).at[target].set(1)
    return (target, route_of, filled)


def per_device(grad_out, expert_ids, route_weights, hidden_cache, w_down):
    hidden = hidden_cache[0]
    target, route_of, filled = route_table(expert_ids)
    picked = grad_out[route_of // TOP]
    outgoing = jnp.where(filled[:, None] > 0, picked, jnp.zeros_like(picked)).reshape(
        EXPERTS, 1, CAP, -1
    )
    picked_weights = route_weights.reshape(-1)[route_of]
    outgoing_weights = jnp.where(
        filled > 0, picked_weights, jnp.zeros_like(picked_weights)
    ).reshape(EXPERTS, 1, CAP)
    received, weights_in = (
        lax.all_to_all(outgoing, "expert", split_axis=0, concat_axis=1, tiled=True),
        lax.all_to_all(outgoing_weights, "expert", split_axis=0, concat_axis=1, tiled=True),
    )
    back = jnp.einsum(
        "escd,efd->escf",
        received,
        lax.all_gather(w_down, "dp", axis=1, tiled=True),
        preferred_element_type=jnp.float32,
    )
    weight_f = weights_in.astype(jnp.float32)[..., None]
    grad_hidden = (weight_f * back).astype(jnp.bfloat16)
    slot_grads = jnp.sum(back * hidden.astype(jnp.float32), axis=-1)
    scaled = (weight_f * received.astype(jnp.float32)).astype(jnp.bfloat16)
    summed = lax.psum_scatter(
        jnp.einsum("escf,escd->fed", hidden, scaled, preferred_element_type=jnp.float32).astype(
            jnp.bfloat16
        ),
        "dp",
        scatter_dimension=0,
        tiled=True,
    ).astype(jnp.float32)
    grad_down = summed.transpose(1, 0, 2).astype(jnp.bfloat16)
    returned = lax.all_to_all(slot_grads, "expert", split_axis=1, concat_axis=0, tiled=True)
    grad_probs = returned.reshape(-1)[target].reshape(expert_ids.shape)
    return (grad_hidden[None], grad_down, grad_probs)


def solution(mesh):
    placed = (
        P(("dp", "expert"), None),
        P(("dp", "expert"), None),
        P(("dp", "expert"), None),
        P("dp", "expert", None, None, None),
        P("expert", "dp", None),
    )
    return jax.shard_map(
        per_device,
        mesh=mesh,
        in_specs=placed,
        out_specs=(
            P("dp", "expert", None, None, None),
            P("expert", "dp", None),
            P(("dp", "expert"), None),
        ),
        check_vma=False,
    )
```

profile of v0, /device:TPU:0, one launch (start us, length us, event | category | flops | bytes accessed | tf_op | source)
XLA Modules:
  0.0 386.4 jit_solution(9249815294104867439)
XLA Ops:
  7.2 0.0 copy-start
  7.2 0.0 all-gather.2.cloned.1.call-start
  7.2 0.7 all-gather.2.cloned.1.call-update
  7.9 0.8 copy.39
  8.7 0.1 eq.29
  8.8 0.1 eq.25
  8.9 4.5 %reduce-window.6 = s32[16,8,128]{2,1,0:T(8,128)S(1)} reduce-window(s32[16,8,128]{2,1,0:T(8,128)S(1)} %fusion.13, s32[]{:T(128)} %constant.11.clone.1), window={size=1x1x128 pad=0_0x0_0x127_0}, to_apply=%region_0.0 | reduce-window | flops 2080768 | bytes 131076 | tf_op jit(solution)/shard_map/reduce-window
  13.4 0.1 slice.14
  13.5 0.1 copy.41
  13.7 0.1 copy.42
  13.7 0.7 broadcast_multiply_fusion
  14.4 0.1 copy.38
  14.5 0.1 mul.40
  14.6 0.8 copy.43
  15.4 0.1 reshape.95
  15.5 0.1 broadcast_add_fusion
  15.7 4.3 %scatter_custom_fusion.1 = s32[1152]{0:T(1024)S(1)} fusion(s32[1024]{0:T(1024)S(1)} %bitcast.75, s32[1024]{0:T(1024)S(1)} %iota.11, s32[]{:T(128)} %constant.11.clone.1), kind=kCustom, calls=%fused_computation.42 | custom fusion | bytes 4612 | tf_op jit(solution)/shard_map/scatter | solution.py:21
  20.0 4.3 %scatter_custom_fusion = s32[1152]{0:T(1024)S(1)} fusion(s32[1024]{0:T(1024)S(1)} %bitcast.76, s32[1024]{0:T(1024)S(1)} %broadcast.76, s32[]{:T(128)} %constant.11.clone.1), kind=kCustom, calls=%fused_computation.45 | custom fusion | bytes 4612 | tf_op jit(solution)/shard_map/scatter | solution.py:23
  24.4 7.3 %gather_fusion = bf16[1152]{0:T(1024)(128)(2,1)S(1)} fusion(bf16[1024]{0:T(1024)(128)(2,1)S(1)} %reshape.95, s32[2048]{0:T(1024)S(1)} %get-tuple-element.22), kind=kCustom, calls=%fused_computation | custom fusion | bytes 9216 | tf_op jit(solution)/shard_map/gather | solution.py:34
  31.7 0.1 reshape.145
  31.8 0.5 broadcast.102
  32.3 0.7 reduce
  33.0 0.7 reshape.151
  33.7 6.3 %all-to-all-start = ((bf16[4,2,144]{2,1,0:T(2,128)(2,1)}), bf16[4,2,144]{2,1,0:T(2,128)(2,1)S(1)}, u32[]{:S(2)}, u32[]{:S(2)}) async-start(bf16[4,2,144]{2,1,0:T(2,128)(2,1)} %reshape.151), calls=%async_computation | async-start | bytes 8192 | tf_op jit(solution)/shard_map/all_to_all | solution.py:40
  40.0 0.1 broadcast_in_dim.37
  40.1 6.0 %gather_fusion.1 = bf16[1152,2048]{1,0:T(8,128)(2,1)} fusion(bf16[128,2048]{1,0:T(8,128)(2,1)S(1)} %copy-done, s32[2048]{0:T(1024)S(1)} %get-tuple-element.21), kind=kCustom, calls=%fused_computation.1 | custom fusion | bytes 9441792 | tf_op jit(solution)/shard_map/gather | solution.py:30
  46.1 6.3 %broadcast_select_fusion = bf16[16,1,72,2048]{3,2,1,0:T(8,128)(2,1)} fusion(bf16[16,1,72,2048]{3,2,1,0:T(8,128)(2,1)} %bitcast.69, pred[16,72]{1,0:T(8,128)(4,1)S(1)} %broadcast_in_dim.37), kind=kLoop, calls=%fused_computation.13 | loop fusion | flops 2359296 | bytes 9438336 | tf_op jit(solution)/shard_map/jit(_where)/select_n | solution.py:31
  52.3 5.2 %all-to-all-start.1 = ((bf16[16,1,72,2048]{3,2,1,0:T(8,128)(2,1)}), bf16[16,1,72,2048]{3,2,1,0:T(8,128)(2,1)}, u32[]{:S(2)}, u32[]{:S(2)}) async-start(bf16[16,1,72,2048]{3,2,1,0:T(8,128)(2,1)} %broadcast_select_fusion), calls=%async_computation.1 | async-start | bytes 9437184 | tf_op jit(solution)/shard_map/all_to_all | solution.py:39
  57.5 0.1 all-reduce.3.cloned.1.call-start
  57.6 0.1 reshape.152
  57.7 103.5 %all-to-all-done.1 = bf16[16,1,72,2048]{3,2,1,0:T(8,128)(2,1)} async-done(((bf16[16,1,72,2048]{3,2,1,0:T(8,128)(2,1)}), bf16[16,1,72,2048]{3,2,1,0:T(8,128)(2,1)}, u32[]{:S(2)}, u32[]{:S(2)}) %all-to-all-start.1) | async-done | bytes 4718624 | tf_op jit(solution)/shard_map/all_to_all | solution.py:39
  161.2 13.8 %fusion = bf16[768,4,2048]{0,2,1:T(8,128)(2,1)} fusion(f32[4,4,72]{2,1,0:T(4,128)S(1)} %copy.46, bf16[4,4,1,72,2048]{4,3,1,0,2:T(8,128)(2,1)} %bitcast.9, bf16[1,4,4,72,768]{4,3,2,1,0:T(8,128)(2,1)S(1)} %copy-done.2), kind=kOutput, calls=%fused_computation.6 | convolution fusion | flops 3637248000 | bytes 19075584 | tf_op jit(solution)/shard_map/escf,escd->fed/dot_general | solution.py:53
  175.0 21.7 %copy.50 = bf16[768,4,2048]{2,1,0:T(4,128)(2,1)} copy(bf16[768,4,2048]{0,2,1:T(8,128)(2,1)} %fusion) | data formatting | bytes 25165824 | tf_op jit(solution)/shard_map/convert_element_type | solution.py:53
  196.8 0.0 all-reduce.3.cloned.1.call-update
  196.8 0.6 copy-done.3
  197.4 0.6 dynamic-slice
  198.7 0.0 all-gather.2.cloned.1.call-done
  198.7 12.5 %multiply_reduce_fusion = (f32[4,4,72]{2,1,0:T(4,128)S(1)}, bf16[1,4,4,72,768]{4,3,2,1,0:T(8,128)(2,1)}) fusion(bf16[1,4,4,72,768]{4,3,2,1,0:T(8,128)(2,1)S(1)} %copy-done.2, f32[4,4,72]{2,1,0:T(4,128)S(1)} %copy.46, bf16[4,768,2048]{2,1,0:T(8,128)(2,1)} %all-gather.2.cloned.1.call-done, bf16[4,4,1,72,2048]{4,3,1,0,2:T(8,128)(2,1)} %bitcast.9), kind=kOutput, calls=%fused_computation.16 | convolution fusion | flops 3628301312 | bytes 20849664 | tf_op jit(solution)/shard_map/escd,efd->escf/dot_general | solution.py:42
  211.2 0.6 copy.51
  211.8 3.2 all-to-all-start.2
  215.1 0.0 copy-start.1
  215.1 153.3 %all-reduce.3.cloned.1.call-done = bf16[768,4,2048]{2,1,0:T(4,128)(2,1)} async-done(((bf16[768,4,2048]{2,1,0:T(4,128)(2,1)}), bf16[768,4,2048]{2,1,0:T(4,128)(2,1)}) %all-reduce.3.cloned.1.call-update) | async-done | bytes 12582928
  368.4 2.1 dynamic-slice_bitcast_fusion
  370.5 2.0 copy.52
  372.5 0.1 reshape.97
  372.6 6.2 %gather_fusion.2 = f32[1024]{0:T(1024)S(1)} fusion(f32[1152]{0:T(1024)S(1)} %reshape.97, s32[1024]{0:T(1024)S(1)} %broadcast_clamp_fusion), kind=kCustom, calls=%fused_computation.2 | custom fusion | bytes 12288 | tf_op jit(solution)/shard_map/gather | solution.py:62
  378.8 0.1 reshape.98
  378.9 0.7 copy.53
  (21 shorter events, 0.1 us)
Async XLA Ops:
  7.2 32.9 %copy-start = (bf16[128,2048]{1,0:T(8,128)(2,1)S(1)}, bf16[128,2048]{1,0:T(8,128)(2,1)}, u32[]{:S(2)}) copy-start(bf16[128,2048]{1,0:T(8,128)(2,1)} %param.5) | copy-start | bytes 1572868
  7.2 191.5 %all-gather.2.cloned.1.call-start = ((), (), s32[]{:S(2)}) async-start(), calls=%async_computation.3 | async-start | bytes 14155776 | tf_op jit(solution)/shard_map/all_gather | solution.py:45
  33.7 18.7 %all-to-all-start = ((bf16[4,2,144]{2,1,0:T(2,128)(2,1)}), bf16[4,2,144]{2,1,0:T(2,128)(2,1)S(1)}, u32[]{:S(2)}, u32[]{:S(2)}) async-start(bf16[4,2,144]{2,1,0:T(2,128)(2,1)} %reshape.151), calls=%async_computation | async-start | bytes 8192 | tf_op jit(solution)/shard_map/all_to_all | solution.py:40
  52.3 108.9 %copy-start.2 = (bf16[1,4,4,72,768]{4,3,2,1,0:T(8,128)(2,1)S(1)}, bf16[1,4,4,72,768]{4,3,2,1,0:T(8,128)(2,1)}, u32[]{:S(2)}) copy-start(bf16[1,4,4,72,768]{4,3,2,1,0:T(8,128)(2,1)} %param.8) | copy-start | bytes 5308420
  52.3 108.9 %all-to-all-start.1 = ((bf16[16,1,72,2048]{3,2,1,0:T(8,128)(2,1)}), bf16[16,1,72,2048]{3,2,1,0:T(8,128)(2,1)}, u32[]{:S(2)}, u32[]{:S(2)}) async-start(bf16[16,1,72,2048]{3,2,1,0:T(8,128)(2,1)} %broadcast_select_fusion), calls=%async_computation.1 | async-start | bytes 9437184 | tf_op jit(solution)/shard_map/all_to_all | solution.py:39
  57.5 310.8 %all-reduce.3.cloned.1.call-start = ((), (), s32[]{:S(2)}) async-start(), calls=%async_computation.4 | async-start | bytes 25165824
  196.8 0.7 copy-start.3
  211.8 160.7 %all-to-all-start.2 = ((f32[4,4,72]{2,0,1:T(4,128)}), f32[4,4,72]{2,0,1:T(4,128)S(1)}, u32[]{:S(2)}, u32[]{:S(2)}) async-start(f32[4,4,72]{2,0,1:T(4,128)} %copy.51), calls=%async_computation.2 | async-start | bytes 16384 | tf_op jit(solution)/shard_map/all_to_all | solution.py:61
  215.1 164.5 %copy-start.1 = (bf16[128,2048]{1,0:T(8,128)(2,1)S(1)}, bf16[128,2048]{1,0:T(8,128)(2,1)}, u32[]{:S(2)}) copy-start(bf16[128,2048]{1,0:T(8,128)(2,1)} %param.5) | copy-start | bytes 1572868
Sparse Core Ops, SparseCore 0:
  9.9 74.8 all-gather.1
  196.9 171.3 all-reduce.2
where the time goes:
time: 387 us; the launch traced here: 386 us
  waiting for transfers between devices  258 us (67%)
  local copies, waits for them, and re-layouts  60.4 us (16%)
  matrix products  26.3 us (7%)
  starting transfers between devices  14.9 us (4%)
  between operations  14.9 us (4%)
  other arithmetic  12.3 us (3%)
    unnamed x3, waiting for transfers between devices  154 us
    all_to_all x1, waiting for transfers between devices, per_device(): lax.all_to_all(outgoing, 'expert', split_axis=0, concat_axis=1, tiled=True)  104 us
    convert_element_type x1, local copies, waits for them, and re-layouts, per_device(): jnp.einsum('escf,escd->fed', hidden, scaled, preferred_element_type=jnp.f...  21.7 us
    dot_general x1, matrix products, per_device(): jnp.einsum('escf,escd->fed', hidden, scaled, preferred_element_type=jnp.f...  13.8 us
    dot_general x1, matrix products, per_device(): jnp.einsum('escd,efd->escf', received, lax.all_gather(w_down, 'dp', axis=...  12.5 us
  transfers between devices with their start and end apart: 5, of which 2 were waited for; matrix products, arithmetic and copies ran while one was open for 24% of the time, Pallas kernels for 0%

commit v1 on v0

v1 whole, which is shorter than its diff:
```python
import functools

import jax
import jax.numpy as jnp
from jax import lax
from jax.experimental import pallas as pl
from jax.experimental.pallas import tpu as pltpu
from jax.sharding import PartitionSpec as P

EXPERTS = 16
CAP = 72
BF = jnp.bfloat16
F32 = jnp.float32


def iota(shape, dim):
    return lax.broadcasted_iota(jnp.int32, shape, dim)


def hidden_kernel(n, sc_ref, tab_ref, hid_ref, hst_ref, wt_ref, rank_ref):
    experts, toks = tab_ref.shape[2], tab_ref.shape[3]
    wt = tab_ref[0, 0].astype(F32)
    named = wt > 0
    earlier = (iota((toks, toks), 0) < iota((toks, toks), 1)).astype(BF)
    rank = jnp.dot(named.astype(F32).astype(BF), earlier, preferred_element_type=F32)
    slots = iota((CAP, toks), 0).astype(F32)
    for e in range(experts):
        w_row, r_row = wt[e : e + 1], rank[e : e + 1]
        place = jnp.where(slots == r_row, w_row, 0.0).astype(BF)
        moved = lax.dot_general(
            hid_ref[0, e, 0], place, (((0,), (0,)), ((), ())), preferred_element_type=F32
        )
        hst_ref[e] = moved.astype(BF)
        wt_ref[0, e] = w_row
        rank_ref[0, e] = r_row


def hidden_to_tokens(n, scalars, table, hid, f):
    experts, toks = table.shape[2], table.shape[3]
    src = lambda k, sc: lax.rem(sc[0] + n - k, n)
    row = jax.ShapeDtypeStruct((n, experts, 1, toks), F32)
    row_spec = pl.BlockSpec((1, experts, 1, toks), lambda k, sc: (k, 0, 0, 0))
    return pl.pallas_call(
        functools.partial(hidden_kernel, n),
        out_shape=(jax.ShapeDtypeStruct((experts, f, n * toks), BF), row, row),
        grid_spec=pltpu.PrefetchScalarGridSpec(
            num_scalar_prefetch=1,
            grid=(n,),
            in_specs=[
                pl.BlockSpec((1, 1, experts, toks), lambda k, sc: (sc[2] * n + src(k, sc), sc[0], 0, 0)),
                pl.BlockSpec((1, experts, 1, CAP, f), lambda k, sc: (0, 0, src(k, sc), 0, sc[1])),
            ],
            out_specs=(
                pl.BlockSpec((experts, f, toks), lambda k, sc: (0, 0, k)),
                row_spec,
                row_spec,
            ),
        ),
        cost_estimate=pl.CostEstimate(
            flops=2 * n * experts * CAP * f * toks, bytes_accessed=4 * n * experts * f * toks, transcendentals=0
        ),
    )(scalars, table, hid)


def back_kernel(n, sc_ref, tok0_ref, tok1_ref, w_ref, hid_ref, wt_ref, rank_ref, gh_ref, sg_ref):
    toks = wt_ref.shape[3]
    half = tok0_ref.shape[1]
    over_d = (((1,), (1,)), ((), ()))
    z = lax.dot_general(tok0_ref[...], w_ref[0, :, :half], over_d, preferred_element_type=F32)
    z = z + lax.dot_general(tok1_ref[...], w_ref[0, :, half:], over_d, preferred_element_type=F32)
    eye = iota((toks, toks), 0) == iota((toks, toks), 1)
    slots = iota((CAP, toks), 0).astype(F32)
    for k in range(n):
        s = lax.rem(sc_ref[0] + n - k, n)
        w_row, r_row = wt_ref[k, 0], rank_ref[k, 0]
        pick = jnp.where((slots == r_row) & (w_row > 0), 1.0, 0.0).astype(BF)
        w_col = jnp.sum(jnp.where(eye, w_row, 0.0), axis=1, keepdims=True)
        zk = z[k * toks : (k + 1) * toks]
        weighted = (zk * w_col).astype(BF)
        gh_ref[0, s] = jnp.dot(pick, weighted, preferred_element_type=F32).astype(BF)
        hid = lax.dot_general(
            pick, hid_ref[0, 0, s], (((0,), (0,)), ((), ())), preferred_element_type=F32
        )
        sg_col = jnp.sum(zk * hid, axis=1, keepdims=True)
        sg_ref[s, 0] = jnp.sum(jnp.where(eye, sg_col, 0.0), axis=0, keepdims=True)


def backward(n, scalars, tok0, tok1, w, hid, wt, rank):
    experts, f, d = w.shape
    rows, half = tok0.shape
    toks = wt.shape[3]
    row_spec = pl.BlockSpec((n, 1, 1, toks), lambda e, sc: (0, e, 0, 0))
    whole = pl.BlockSpec((rows, half), lambda e, sc: (0, 0))
    return pl.pallas_call(
        functools.partial(back_kernel, n),
        out_shape=(
            jax.ShapeDtypeStruct((experts, n, CAP, f), BF),
            jax.ShapeDtypeStruct((n, experts, 1, toks), F32),
        ),
        grid_spec=pltpu.PrefetchScalarGridSpec(
            num_scalar_prefetch=1,
            grid=(experts,),
            in_specs=[
                whole,
                whole,
                pl.BlockSpec((1, f, d), lambda e, sc: (e, 0, 0)),
                pl.BlockSpec((1, 1, n, CAP, f), lambda e, sc: (0, e, 0, 0, sc[1])),
                row_spec,
                row_spec,
            ],
            out_specs=(pl.BlockSpec((1, n, CAP, f), lambda e, sc: (e, 0, 0, 0)), row_spec),
        ),
        compiler_params=pltpu.CompilerParams(vmem_limit_bytes=48 << 20),
        cost_estimate=pl.CostEstimate(
            flops=2 * rows * d * experts * f,
            bytes_accessed=2 * (rows * d + experts * f * d + experts * n * CAP * f * 2),
            transcendentals=0,
        ),
    )(scalars, tok0, tok1, w, hid, wt, rank)


def part_kernel(bands, sc_ref, own_ref, nb_ref, tok_own_ref, tok_nb_ref, send_ref, keep_ref):
    total = jnp.dot(own_ref[...], tok_own_ref[...], preferred_element_type=F32)
    total = total + jnp.dot(nb_ref[...], tok_nb_ref[...], preferred_element_type=F32)
    _, experts, band, cols = send_ref.shape
    total = total.reshape(experts, bands, band, cols).astype(BF)
    for a in range(bands):
        rel = sc_ref[0] ^ a
        for ref, bit in ((send_ref, 1), (keep_ref, 0)):

            @pl.when(rel % 2 == bit)
            def _():
                ref[rel // 2] = total[:, a]


def partial_grad(bands, band, scalars, own, nb, tok_own, tok_nb):
    rows, k = own.shape
    cols = tok_own.shape[1]
    block = min(256, cols)
    experts = rows // (bands * band)
    out = jax.ShapeDtypeStruct((bands // 2, experts, band, cols), BF)
    out_spec = pl.BlockSpec((bands // 2, experts, band, block), lambda c, sc: (0, 0, 0, c))
    hs_spec = pl.BlockSpec((rows, k), lambda c, sc: (0, 0))
    tok_spec = pl.BlockSpec((k, block), lambda c, sc: (0, c))
    return pl.pallas_call(
        functools.partial(part_kernel, bands),
        out_shape=(out, out),
        grid_spec=pltpu.PrefetchScalarGridSpec(
            num_scalar_prefetch=1,
            grid=(cols // block,),
            in_specs=[hs_spec, hs_spec, tok_spec, tok_spec],
            out_specs=(out_spec, out_spec),
        ),
        compiler_params=pltpu.CompilerParams(vmem_limit_bytes=48 << 20),
        cost_estimate=pl.CostEstimate(
            flops=4 * rows * k * cols, bytes_accessed=2 * (rows * cols + 2 * k * cols + 2 * rows * k), transcendentals=0
        ),
    )(scalars, own, nb, tok_own, tok_nb)


def per_device(n_dp, n, grad_out, expert_ids, route_weights, hidden_cache, w_down):
    dp, z = lax.axis_index("dp"), lax.axis_index("expert")
    bands = n_dp // 2
    upper, j = dp // bands, dp % bands
    experts, band, d = w_down.shape
    toks = grad_out.shape[0]
    f = bands * band

    def swap(x, bit):
        return lax.ppermute(x, "dp", [(i, i ^ bit) for i in range(n_dp)])

    ids = expert_ids[None] == jnp.arange(EXPERTS, dtype=jnp.int32)[:, None, None]
    table = jnp.sum(jnp.where(ids, route_weights.astype(F32)[None], 0.0), axis=2).astype(BF)
    tables = lax.all_gather(table, ("dp", "expert"), axis=0, tiled=False)
    tables = tables.reshape(n_dp * n, n, experts, toks)

    half = d // 2
    tok_own, tok_nb = [], []
    for h in range(2):
        mine = grad_out[:, h * half : (h + 1) * half]
        blocks = [mine] + [
            lax.ppermute(mine, "expert", [(i, (i + k) % n) for i in range(n)]) for k in range(1, n)
        ]
        tok_own.append(jnp.concatenate(blocks, axis=0))
        tok_nb.append(swap(tok_own[h], bands))

    outgoing = lax.dynamic_slice_in_dim(hidden_cache, (1 - upper) * f, f, axis=4)
    hid_nb = swap(outgoing, bands)

    pieces = {0: w_down}
    bit = bands // 2
    while bit:
        for r in list(pieces):
            pieces[r ^ bit] = swap(pieces[r], bit)
        bit //= 2
    w = jnp.zeros((experts, f, d), BF)
    for r, piece in pieces.items():
        w = lax.dynamic_update_slice(w, piece, (0, (j ^ r) * band, 0))

    sc_own = jnp.stack([z, upper, dp]).astype(jnp.int32)
    sc_nb = jnp.stack([z, 0 * z, dp ^ bands]).astype(jnp.int32)
    hs_own, wt_own, rank_own = hidden_to_tokens(n, sc_own, tables, hidden_cache, f)
    hs_nb, wt_nb, rank_nb = hidden_to_tokens(n, sc_nb, tables, hid_nb, f)
    hs_own, hs_nb = hs_own.reshape(experts * f, -1), hs_nb.reshape(experts * f, -1)

    sc_j = jnp.stack([j]).astype(jnp.int32)
    halves = []
    for h in range(2):
        send, keep = partial_grad(bands, band, sc_j, hs_own, hs_nb, tok_own[h], tok_nb[h])
        terms = [keep, swap(send, 1)]
        bit = bands // 2
        while bit > 1:
            mid = bit // 2
            going = sum(t[mid:].astype(F32) for t in terms).astype(BF)
            terms = [t[:mid] for t in terms] + [swap(going, bit)]
            bit //= 2
        halves.append(sum(t[0].astype(F32) for t in terms).astype(BF))
    grad_down = jnp.concatenate(halves, axis=2)

    gh_own, sg_own = backward(n, sc_own, tok_own[0], tok_own[1], w, hidden_cache, wt_own, rank_own)
    gh_nb, sg_nb = backward(n, sc_nb, tok_nb[0], tok_nb[1], w, hid_nb, wt_nb, rank_nb)
    gh_in = swap(gh_nb, bands)
    grad_hidden = jnp.where(
        upper == 0,
        jnp.concatenate([gh_own, gh_in], axis=3),
        jnp.concatenate([gh_in, gh_own], axis=3),
    )
    sg = sg_own.reshape(n, experts, toks) + swap(sg_nb.reshape(n, experts, toks), bands)
    by_expert = lax.all_to_all(sg, "expert", split_axis=0, concat_axis=0, tiled=True)
    by_expert = by_expert.reshape(EXPERTS, 1, toks)
    chosen = expert_ids.T[None] == jnp.arange(EXPERTS, dtype=jnp.int32)[:, None, None]
    grad_probs = jnp.sum(jnp.where(chosen, by_expert, 0.0), axis=0).T
    return grad_hidden[None], grad_down, grad_probs


def solution(mesh):
    tokens = P(("dp", "expert"), None)
    cache = P("dp", "expert", None, None, None)
    weights = P("expert", "dp", None)
    return jax.shard_map(
        functools.partial(per_device, mesh.shape["dp"], mesh.shape["expert"]),
        mesh=mesh,
        in_specs=(tokens, tokens, tokens, cache, weights),
        out_specs=(cache, weights, tokens),
        check_vma=False,
    )
```

time: 387 us -> 224 us (0.58)
  waiting for transfers between devices: 258 us -> 46.9 us
  blocking collectives: 0 us -> 76.9 us
  local copies, waits for them, and re-layouts: 60.4 us -> 14 us
  Pallas kernels: 0 us -> 43 us
  matrix products: 26.3 us -> 0 us
  between operations: 14.9 us -> 0.92 us
  starting transfers between devices: 14.9 us -> 24 us
  other arithmetic: 12.3 us -> 17.1 us
    unnamed x3 -> x0, waiting for transfers between devices: 154 us -> none
    all_to_all x3 -> x1, waiting for transfers between devices: 104 us -> 4.67 us  [per_device(): lax.all_to_all(sg, 'expert', split_axis=0, concat_axis=0, tiled=True)]
    all_gather x0 -> x1, blocking collectives: none -> 76.9 us  [per_device(): tables = lax.all_gather(table, ('dp', 'expert'), axis=0, tiled=False)]
    pallas_call x0 -> x6, Pallas kernels: none -> 43 us  [the longest x2 18 us: backward(): pl.pallas_call(functools.partial(back_kernel, n), out_shape=(jax.ShapeDty...]
    ppermute x0 -> x18, waiting for transfers between devices: none -> 42.2 us  [the longest x6 31.7 us: per_device(): lax.ppermute(mine, 'expert', [(i, (i + k) % n) for i in range(n)])]
    dot_general x2 -> x0, matrix products: 26.3 us -> none  [the longest x1 13.8 us: per_device(): jnp.einsum('escf,escd->fed', hidden, scaled, preferred_element_type=jnp.f...]
    convert_element_type x3 -> x0, local copies, waits for them, and re-layouts: 23.9 us -> none  [the longest x1 21.7 us: per_device(): jnp.einsum('escf,escd->fed', hidden, scaled, preferred_element_type=jnp.f...]
    ppermute x0 -> x18, starting transfers between devices: none -> 20.7 us  [the longest x6 10.5 us: per_device(): lax.ppermute(mine, 'expert', [(i, (i + k) % n) for i in range(n)])]
  transfers between devices with their start and end apart: 5 -> 19, of which waited for: 2 -> 6; matrix products, arithmetic and copies ran while one was open for 24% -> 10% of each run, Pallas kernels for 0% -> 19%
where the time goes in v1:
time: 224 us; the launch traced here: 223 us
  blocking collectives  76.9 us (34%)
  waiting for transfers between devices  46.9 us (21%)
  Pallas kernels  43 us (19%)
  starting transfers between devices  24 us (11%)
  other arithmetic  17.1 us (8%)
  local copies, waits for them, and re-layouts  14 us (6%)
    all_gather x1, blocking collectives, per_device(): tables = lax.all_gather(table, ('dp', 'expert'), axis=0, tiled=False)  76.9 us
    ppermute x6, waiting for transfers between devices, per_device(): lax.ppermute(mine, 'expert', [(i, (i + k) % n) for i in range(n)])  31.7 us
    pallas_call x2, Pallas kernels, backward(): pl.pallas_call(functools.partial(back_kernel, n), out_shape=(jax.ShapeDty...  18 us
    pallas_call x2, Pallas kernels, partial_grad(): pl.pallas_call(functools.partial(part_kernel, bands), out_shape=(out, out...  15.2 us
    ppermute x12, waiting for transfers between devices, swap(): return lax.ppermute(x, 'dp', [(i, i ^ bit) for i in range(n_dp)])  10.5 us
    ppermute x6, starting transfers between devices, per_device(): lax.ppermute(mine, 'expert', [(i, (i + k) % n) for i in range(n)])  10.5 us
    ppermute x12, starting transfers between devices, swap(): return lax.ppermute(x, 'dp', [(i, i ^ bit) for i in range(n_dp)])  10.2 us
    pallas_call x2, Pallas kernels, hidden_to_tokens(): pl.pallas_call(functools.partial(hidden_kernel, n), out_shape=(jax.ShapeD...  9.75 us
  transfers between devices with their start and end apart: 19, of which 6 were waited for; matrix products, arithmetic and copies ran while one was open for 10% of the time, Pallas kernels for 19%

profile of v1, /device:TPU:0, one launch (start us, length us, event | category | flops | bytes accessed | tf_op | source)
XLA Modules:
  0.0 222.8 jit_solution(8706615092789445119)
XLA Ops:
  0.6 1.2 fusion.2
  1.8 3.1 %collective-permute-start = (bf16[128,1024]{1,0:T(8,128)(2,1)S(1)}, bf16[128,1024]{1,0:T(8,128)(2,1)S(1)}, u32[]{:S(2)}, u32[]{:S(2)}) collective-permute-start(bf16[128,1024]{1,0:T(8,128)(2,1)S(1)} %get-tuple-element.32), channel_id=1, source_target_pairs={{0,1},{1,2},{2,3},{3,0},{4,5},{5,6},{6,7},{7,4},{8,9},{9,10},{10,1... | collective-permute-start | bytes 786440 | tf_op jit(solution)/shard_map/ppermute | solution.py:182
  4.9 2.6 %collective-permute-start.1 = (bf16[128,1024]{1,0:T(8,128)(2,1)S(1)}, bf16[128,1024]{1,0:T(8,128)(2,1)S(1)}, u32[]{:S(2)}, u32[]{:S(2)}) collective-permute-start(bf16[128,1024]{1,0:T(8,128)(2,1)S(1)} %get-tuple-element.32), channel_id=1, source_target_pairs={{0,2},{1,3},{2,0},{3,1},{4,6},{5,7},{6,4},{7,5},{8,10},{9,11},{10,... | collective-permute-start | bytes 786440 | tf_op jit(solution)/shard_map/ppermute | solution.py:182
  7.5 1.3 collective-permute-start.2
  8.9 0.7 collective-permute-start.3
  9.5 0.3 collective-permute-start.4
  9.9 4.3 %collective-permute-done = bf16[128,1024]{1,0:T(8,128)(2,1)S(1)} collective-permute-done((bf16[128,1024]{1,0:T(8,128)(2,1)S(1)}, bf16[128,1024]{1,0:T(8,128)(2,1)S(1)}, u32[]{:S(2)}, u32[]{:S(2)}) %collective-permute-start) | collective-permute-done | bytes 262176 | tf_op jit(solution)/shard_map/ppermute | solution.py:182
  14.2 2.5 %collective-permute-start.5 = (bf16[128,1024]{1,0:T(8,128)(2,1)S(1)}, bf16[128,1024]{1,0:T(8,128)(2,1)}, u32[]{:S(2)}, u32[]{:S(2)}) collective-permute-start(bf16[128,1024]{1,0:T(8,128)(2,1)S(1)} %get-tuple-element.31), channel_id=1, source_target_pairs={{0,3},{1,0},{2,1},{3,2},{4,7},{5,4},{6,5},{7,6},{8,11},{9,8},{10,9... | collective-permute-start | bytes 786440 | tf_op jit(solution)/shard_map/ppermute | solution.py:182
  16.7 8.8 %collective-permute-done.1 = bf16[128,1024]{1,0:T(8,128)(2,1)S(1)} collective-permute-done((bf16[128,1024]{1,0:T(8,128)(2,1)S(1)}, bf16[128,1024]{1,0:T(8,128)(2,1)S(1)}, u32[]{:S(2)}, u32[]{:S(2)}) %collective-permute-start.1) | collective-permute-done | bytes 262176 | tf_op jit(solution)/shard_map/ppermute | solution.py:182
  25.6 1.8 collective-permute-start.9
  27.4 1.0 constant_dynamic-slice_fusion
  28.7 2.4 %collective-permute-done.3 = bf16[128,1024]{1,0:T(8,128)(2,1)S(1)} collective-permute-done((bf16[128,1024]{1,0:T(8,128)(2,1)S(1)}, bf16[128,1024]{1,0:T(8,128)(2,1)S(1)}, u32[]{:S(2)}, u32[]{:S(2)}) %collective-permute-start.3) | collective-permute-done | bytes 262176 | tf_op jit(solution)/shard_map/ppermute | solution.py:182
  31.1 16.1 %collective-permute-done.4 = bf16[128,1024]{1,0:T(8,128)(2,1)} collective-permute-done((bf16[128,1024]{1,0:T(8,128)(2,1)S(1)}, bf16[128,1024]{1,0:T(8,128)(2,1)}, u32[]{:S(2)}, u32[]{:S(2)}) %collective-permute-start.4) | collective-permute-done | bytes 262176 | tf_op jit(solution)/shard_map/ppermute | solution.py:182
  47.2 2.1 pad_maximum_fusion.2.tok1_ref.tok_own_ref
  49.3 1.5 collective-permute-start.10
  50.9 1.5 collective-permute-start.6
  52.4 76.9 %all-gather = bf16[512,128]{1,0:T(8,128)(2,1)} all-gather(bf16[16,128]{1,0:T(8,128)(2,1)S(1)} %select_reduce_fusion.1), channel_id=2, replica_groups=mesh['dp'=8,'expert'=4] {'dp','expert'}, dimensions={0}, use_global_device_ids=true | all-gather | bytes 135168 | tf_op jit(solution)/shard_map/all_gather | solution.py:174
  129.4 0.6 pad_add_fusion.sc_ref
  130.0 4.9 %shard_map.76 = (bf16[4,384,512]{2,1,0:T(8,128)(2,1)}, f32[4,4,1,128]{3,2,1,0:T(1,128)}, f32[4,4,1,128]{3,2,1,0:T(1,128)}) custom-call(s32[3]{0:T(128)} %pad_add_fusion.sc_ref, bf16[32,4,4,128]{3,2,1,0:T(4,128)(2,1)} %bitcast.22, bf16[1,4,4,72,768]{4,3,2,1,0:T(8,128)(2,1)} %hid_ref.3), custom_call_target="tpu_custom_call" | custom-call | flops 113246208 | bytes 3145728 | tf_op jit(solution)/shard_map/pallas_call | solution.py:43
  134.8 0.6 pad_add_fusion.1.sc_ref
  135.4 1.0 copy-done.4
  136.4 4.9 %shard_map.78 = (bf16[4,384,512]{2,1,0:T(8,128)(2,1)}, f32[4,4,1,128]{3,2,1,0:T(1,128)}, f32[4,4,1,128]{3,2,1,0:T(1,128)}) custom-call(s32[3]{0:T(128)} %pad_add_fusion.1.sc_ref, bf16[32,4,4,128]{3,2,1,0:T(4,128)(2,1)} %bitcast.23, bf16[1,4,4,72,384]{4,3,2,1,0:T(8,128)(2,1)} %copy-done.4), custom_call_target="tpu_custom_call" | custom-call | flops 113246208 | bytes 3145728 | tf_op jit(solution)/shard_map/pallas_call | solution.py:43
  141.3 7.6 %shard_map.80 = (bf16[2,4,96,1024]{3,2,1,0:T(8,128)(2,1)}, bf16[2,4,96,1024]{3,2,1,0:T(8,128)(2,1)S(1)}) custom-call(s32[1]{0:T(128)} %bitcast.7.sc_ref, bf16[1536,512]{1,0:T(8,128)(2,1)} %bitcast.27, bf16[1536,512]{1,0:T(8,128)(2,1)} %bitcast.29, bf16[512,1024]{1,0:T(8,128)(2,1)S(1)} %pad_maximum_fusion.1.tok0_ref.tok_own_ref, ...), custom_call_target="tpu_custom_call" | custom-call | flops 3221225472 | bytes 8388608 | tf_op jit(solution)/shard_map/pallas_call | solution.py:145
  148.9 7.6 %shard_map.81 = (bf16[2,4,96,1024]{3,2,1,0:T(8,128)(2,1)}, bf16[2,4,96,1024]{3,2,1,0:T(8,128)(2,1)S(1)}) custom-call(s32[1]{0:T(128)} %bitcast.7.sc_ref, bf16[1536,512]{1,0:T(8,128)(2,1)} %bitcast.28, bf16[1536,512]{1,0:T(8,128)(2,1)} %bitcast.30, bf16[512,1024]{1,0:T(8,128)(2,1)} %pad_maximum_fusion.2.tok1_ref.tok_own_ref, ...), custom_call_target="tpu_custom_call" | custom-call | flops 3221225472 | bytes 8388608 | tf_op jit(solution)/shard_map/pallas_call | solution.py:145
  156.5 0.5 collective-permute-start.15
  157.1 0.8 broadcast_in_dim.35
  157.9 1.6 constant_dynamic-update-slice_fusion.3
  159.5 1.6 constant_dynamic-update-slice_fusion.2
  161.1 1.6 constant_dynamic-update-slice_fusion.1
  162.7 2.3 %add_convert_fusion.3 = bf16[1,4,96,1024]{3,2,1,0:T(8,128)(2,1)} fusion(bf16[2,4,96,1024]{3,2,1,0:T(8,128)(2,1)} %collective-permute-done.13, bf16[2,4,96,1024]{3,2,1,0:T(8,128)(2,1)S(1)} %get-tuple-element.25), kind=kLoop, calls=%fused_computation.5 | loop fusion | flops 1572864 | bytes 2359296 | tf_op jit(solution)/shard_map/convert_element_type | solution.py:214
  165.1 2.3 %add_convert_fusion.1 = bf16[1,4,96,1024]{3,2,1,0:T(8,128)(2,1)} fusion(bf16[2,4,96,1024]{3,2,1,0:T(8,128)(2,1)} %collective-permute-done.15, bf16[2,4,96,1024]{3,2,1,0:T(8,128)(2,1)S(1)} %get-tuple-element.27), kind=kLoop, calls=%fused_computation.3 | loop fusion | flops 1572864 | bytes 2359296 | tf_op jit(solution)/shard_map/convert_element_type | solution.py:214
  167.4 2.1 collective-permute-start.16
  169.5 1.6 constant_dynamic-update-slice_fusion.w_ref
  171.1 2.6 %copy-done.15 = bf16[4,384,2048]{2,1,0:T(8,128)(2,1)} copy-done((bf16[4,384,2048]{2,1,0:T(8,128)(2,1)}, bf16[4,384,2048]{2,1,0:T(8,128)(2,1)S(1)}, u32[]{:S(2)}) %copy-start.15) | copy-done | bytes 6291480
  173.8 9.3 %shard_map.79 = (bf16[4,4,72,384]{3,2,1,0:T(8,128)(2,1)S(1)}, f32[4,4,1,128]{3,2,1,0:T(1,128)S(1)}) custom-call(s32[3]{0:T(128)S(1)} %copy-done.8, bf16[512,1024]{1,0:T(8,128)(2,1)} %collective-permute-done.9.tok0_ref.tok_nb_ref, bf16[512,1024]{1,0:T(8,128)(2,1)} %collective-permute-done.10.tok1_ref.tok_nb_ref, bf16[4,384,2048]{2,1,0:T(8,128)(2,1)} %copy-done.15, ...), custom_call_target="tpu_custom_call" | custom-call | flops 3221225472 | bytes 10158080 | tf_op jit(solution)/shard_map/pallas_call | solution.py:94
  183.1 1.6 collective-permute-start.17
  184.7 8.8 %shard_map.77 = (bf16[4,4,72,384]{3,2,1,0:T(8,128)(2,1)S(1)}, f32[4,4,1,128]{3,2,1,0:T(1,128)S(1)}) custom-call(s32[3]{0:T(128)S(1)} %copy-done.9, bf16[512,1024]{1,0:T(8,128)(2,1)S(1)} %copy-done.3, bf16[512,1024]{1,0:T(8,128)(2,1)} %pad_maximum_fusion.2.tok1_ref.tok_own_ref, bf16[4,384,2048]{2,1,0:T(8,128)(2,1)} %copy-done.15, ...), custom_call_target="tpu_custom_call" | custom-call | flops 3221225472 | bytes 10158080 | tf_op jit(solution)/shard_map/pallas_call | solution.py:94
  193.5 0.9 copy-done.6
  194.4 0.6 add.57
  195.0 3.2 %all-to-all-start = ((f32[4,4,128]{2,1,0:T(4,128)}), f32[4,4,128]{2,1,0:T(4,128)S(1)}, u32[]{:S(2)}, u32[]{:S(2)}) async-start(f32[4,4,128]{2,1,0:T(4,128)} %add.57), calls=%async_computation | async-start | bytes 16384 | tf_op jit(solution)/shard_map/all_to_all | solution.py:229
  198.2 0.9 collective-permute-start.12
  199.1 4.7 %all-to-all-done = f32[4,4,128]{2,1,0:T(4,128)S(1)} async-done(((f32[4,4,128]{2,1,0:T(4,128)}), f32[4,4,128]{2,1,0:T(4,128)S(1)}, u32[]{:S(2)}, u32[]{:S(2)}) %all-to-all-start) | async-done | bytes 8224 | tf_op jit(solution)/shard_map/all_to_all | solution.py:229
  203.8 0.6 select_reduce_fusion
  204.4 1.8 fusion
  206.2 1.8 fusion.1
  208.0 1.2 pad_maximum_fusion
  209.3 10.5 %collective-permute-done.12 = bf16[4,4,72,384]{3,2,1,0:T(8,128)(2,1)} collective-permute-done((bf16[4,4,72,384]{3,2,1,0:T(8,128)(2,1)}, bf16[4,4,72,384]{3,2,1,0:T(8,128)(2,1)}, u32[]{:S(2)}, u32[]{:S(2)}) %collective-permute-start.12) | collective-permute-done | bytes 884768 | tf_op jit(solution)/shard_map/ppermute | solution.py:170
  219.8 3.0 %maximum_select_fusion = bf16[1,4,4,72,768]{4,3,2,1,0:T(8,128)(2,1)} fusion(bf16[1,4,4,72,384]{4,3,2,1,0:T(8,128)(2,1)} %bitcast.6, bf16[1,4,4,72,384]{4,3,2,1,0:T(8,128)(2,1)S(1)} %bitcast.19, pred[]{:T(512)S(6)} %eq.16), kind=kLoop, calls=%fused_computation | loop fusion | flops 7962624 | bytes 3538945 | tf_op jit(solution)/shard_map/jit(_where)/select_n | solution.py:223
  (54 shorter events, 0.5 us)
Async XLA Ops:
  0.6 26.8 %copy-start = (bf16[1,4,4,72,768]{4,3,2,1,0:T(8,128)(2,1)S(1)}, bf16[1,4,4,72,768]{4,3,2,1,0:T(8,128)(2,1)}, u32[]{:S(2)}) copy-start(bf16[1,4,4,72,768]{4,3,2,1,0:T(8,128)(2,1)} %hid_ref.3) | copy-start | bytes 5308420
  1.8 12.4 %collective-permute-start = (bf16[128,1024]{1,0:T(8,128)(2,1)S(1)}, bf16[128,1024]{1,0:T(8,128)(2,1)S(1)}, u32[]{:S(2)}, u32[]{:S(2)}) collective-permute-start(bf16[128,1024]{1,0:T(8,128)(2,1)S(1)} %get-tuple-element.32), channel_id=1, source_target_pairs={{0,1},{1,2},{2,3},{3,0},{4,5},{5,6},{6,7},{7,4},{8,9},{9,10},{10,1... | collective-permute-start | bytes 786440 | tf_op jit(solution)/shard_map/ppermute | solution.py:182
  4.9 20.6 %collective-permute-start.1 = (bf16[128,1024]{1,0:T(8,128)(2,1)S(1)}, bf16[128,1024]{1,0:T(8,128)(2,1)S(1)}, u32[]{:S(2)}, u32[]{:S(2)}) collective-permute-start(bf16[128,1024]{1,0:T(8,128)(2,1)S(1)} %get-tuple-element.32), channel_id=1, source_target_pairs={{0,2},{1,3},{2,0},{3,1},{4,6},{5,7},{6,4},{7,5},{8,10},{9,11},{10,... | collective-permute-start | bytes 786440 | tf_op jit(solution)/shard_map/ppermute | solution.py:182
  7.5 18.0 %collective-permute-start.2 = (bf16[128,1024]{1,0:T(8,128)(2,1)S(1)}, bf16[128,1024]{1,0:T(8,128)(2,1)S(1)}, u32[]{:S(2)}, u32[]{:S(2)}) collective-permute-start(bf16[128,1024]{1,0:T(8,128)(2,1)S(1)} %get-tuple-element.32), channel_id=1, source_target_pairs={{0,3},{1,0},{2,1},{3,2},{4,7},{5,4},{6,5},{7,6},{8,11},{9,8},{10,9... | collective-permute-start | bytes 786440 | tf_op jit(solution)/shard_map/ppermute | solution.py:182
  8.9 22.3 %collective-permute-start.3 = (bf16[128,1024]{1,0:T(8,128)(2,1)S(1)}, bf16[128,1024]{1,0:T(8,128)(2,1)S(1)}, u32[]{:S(2)}, u32[]{:S(2)}) collective-permute-start(bf16[128,1024]{1,0:T(8,128)(2,1)S(1)} %get-tuple-element.31), channel_id=1, source_target_pairs={{0,1},{1,2},{2,3},{3,0},{4,5},{5,6},{6,7},{7,4},{8,9},{9,10},{10,1... | collective-permute-start | bytes 786440 | tf_op jit(solution)/shard_map/ppermute | solution.py:182
  9.5 37.7 %collective-permute-start.4 = (bf16[128,1024]{1,0:T(8,128)(2,1)S(1)}, bf16[128,1024]{1,0:T(8,128)(2,1)}, u32[]{:S(2)}, u32[]{:S(2)}) collective-permute-start(bf16[128,1024]{1,0:T(8,128)(2,1)S(1)} %get-tuple-element.31), channel_id=1, source_target_pairs={{0,2},{1,3},{2,0},{3,1},{4,6},{5,7},{6,4},{7,5},{8,10},{9,11},{10,... | collective-permute-start | bytes 786440 | tf_op jit(solution)/shard_map/ppermute | solution.py:182
  14.2 33.0 %collective-permute-start.5 = (bf16[128,1024]{1,0:T(8,128)(2,1)S(1)}, bf16[128,1024]{1,0:T(8,128)(2,1)}, u32[]{:S(2)}, u32[]{:S(2)}) collective-permute-start(bf16[128,1024]{1,0:T(8,128)(2,1)S(1)} %get-tuple-element.31), channel_id=1, source_target_pairs={{0,3},{1,0},{2,1},{3,2},{4,7},{5,4},{6,5},{7,6},{8,11},{9,8},{10,9... | collective-permute-start | bytes 786440 | tf_op jit(solution)/shard_map/ppermute | solution.py:182
  25.6 115.7 %copy-start.2 = (bf16[512,1024]{1,0:T(8,128)(2,1)}, bf16[512,1024]{1,0:T(8,128)(2,1)S(1)}, u32[]{:S(2)}) copy-start(bf16[512,1024]{1,0:T(8,128)(2,1)S(1)} %pad_maximum_fusion.1.tok0_ref.tok_own_ref) | copy-start | bytes 3145732
  25.6 115.7 %collective-permute-start.9 = (bf16[512,1024]{1,0:T(8,128)(2,1)S(1)}, bf16[512,1024]{1,0:T(8,128)(2,1)}, u32[]{:S(2)}, u32[]{:S(2)}) collective-permute-start(bf16[512,1024]{1,0:T(8,128)(2,1)S(1)} %pad_maximum_fusion.1.tok0_ref.tok_own_ref), channel_id=1, source_target_pairs={{0,16},{4,20},{8,24},{12,28},{16,0},{20,4},{24,8},{28,12},{1,17},{... | collective-permute-start | bytes 3145736 | tf_op jit(solution)/shard_map/ppermute | solution.py:170
  27.4 24.9 %copy-start.17 = (bf16[128,8]{0,1:T(8,128)(2,1)S(1)}, bf16[128,8]{0,1:T(8,128)(2,1)}, u32[]{:S(2)}) copy-start(bf16[128,8]{0,1:T(8,128)(2,1)} %param.7) | copy-start | bytes 6148
  27.4 24.9 %copy-start.16 = (s32[128,8]{0,1:T(8,128)S(1)}, s32[128,8]{0,1:T(8,128)}, u32[]{:S(2)}) copy-start(s32[128,8]{0,1:T(8,128)} %param.6) | copy-start | bytes 12292
  28.4 107.0 %collective-permute-start.11 = (bf16[1,4,4,72,384]{4,3,2,1,0:T(8,128)(2,1)}, bf16[1,4,4,72,384]{4,3,2,1,0:T(8,128)(2,1)S(1)}, u32[]{:S(2)}, u32[]{:S(2)}) collective-permute-start(bf16[1,4,4,72,384]{4,3,2,1,0:T(8,128)(2,1)} %constant_dynamic-slice_fusion), channel_id=1, source_target_pairs={{0,16},{4,20},{8,24},{12,28},{16,0},{20,4},{24,8},{28,12},{1,17},{... | collective-permute-start | bytes 2654216 | tf_op jit(solution)/shard_map/ppermute | solution.py:170
  49.3 99.6 %collective-permute-start.10 = (bf16[512,1024]{1,0:T(8,128)(2,1)}, bf16[512,1024]{1,0:T(8,128)(2,1)}, u32[]{:S(2)}, u32[]{:S(2)}) collective-permute-start(bf16[512,1024]{1,0:T(8,128)(2,1)} %pad_maximum_fusion.2.tok1_ref.tok_own_ref), channel_id=1, source_target_pairs={{0,16},{4,20},{8,24},{12,28},{16,0},{20,4},{24,8},{28,12},{1,17},{... | collective-permute-start | bytes 3145736 | tf_op jit(solution)/shard_map/ppermute | solution.py:170
  50.9 106.1 %collective-permute-start.6 = (bf16[4,96,2048]{2,1,0:T(8,128)(2,1)}, bf16[4,96,2048]{2,1,0:T(8,128)(2,1)}, u32[]{:S(2)}, u32[]{:S(2)}) collective-permute-start(bf16[4,96,2048]{2,1,0:T(8,128)(2,1)} %param.9), channel_id=1, source_target_pairs={{0,8},{4,12},{8,0},{12,4},{16,24},{20,28},{24,16},{28,20},{1,9},{5... | collective-permute-start | bytes 4718600 | tf_op jit(solution)/shard_map/ppermute | solution.py:170
  52.4 108.7 %collective-permute-start.7 = (bf16[4,96,2048]{2,1,0:T(8,128)(2,1)}, bf16[4,96,2048]{2,1,0:T(8,128)(2,1)}, u32[]{:S(2)}, u32[]{:S(2)}) collective-permute-start(bf16[4,96,2048]{2,1,0:T(8,128)(2,1)} %param.9), channel_id=1, source_target_pairs={{0,4},{4,0},{8,12},{12,8},{16,20},{20,16},{24,28},{28,24},{1,5},{5... | collective-permute-start | bytes 4718600 | tf_op jit(solution)/shard_map/ppermute | solution.py:170
  135.4 1.0 copy-start.4
  148.9 13.8 %collective-permute-start.13 = (bf16[2,4,96,1024]{3,2,1,0:T(8,128)(2,1)}, bf16[2,4,96,1024]{3,2,1,0:T(8,128)(2,1)}, u32[]{:S(2)}, u32[]{:S(2)}) collective-permute-start(bf16[2,4,96,1024]{3,2,1,0:T(8,128)(2,1)} %get-tuple-element.26), channel_id=1, source_target_pairs={{0,4},{4,0},{8,12},{12,8},{16,20},{20,16},{24,28},{28,24},{1,5},{5... | collective-permute-start | bytes 4718600 | tf_op jit(solution)/shard_map/ppermute | solution.py:170
  156.5 8.5 %collective-permute-start.15 = (bf16[2,4,96,1024]{3,2,1,0:T(8,128)(2,1)}, bf16[2,4,96,1024]{3,2,1,0:T(8,128)(2,1)}, u32[]{:S(2)}, u32[]{:S(2)}) collective-permute-start(bf16[2,4,96,1024]{3,2,1,0:T(8,128)(2,1)} %get-tuple-element.28), channel_id=1, source_target_pairs={{0,4},{4,0},{8,12},{12,8},{16,20},{20,16},{24,28},{28,24},{1,5},{5... | collective-permute-start | bytes 4718600 | tf_op jit(solution)/shard_map/ppermute | solution.py:170
  157.0 12.5 %collective-permute-start.8 = (bf16[4,96,2048]{2,1,0:T(8,128)(2,1)}, bf16[4,96,2048]{2,1,0:T(8,128)(2,1)}, u32[]{:S(2)}, u32[]{:S(2)}) collective-permute-start(bf16[4,96,2048]{2,1,0:T(8,128)(2,1)} %collective-permute-done.6), channel_id=1, source_target_pairs={{0,4},{4,0},{8,12},{12,8},{16,20},{20,16},{24,28},{28,24},{1,5},{5... | collective-permute-start | bytes 4718600 | tf_op jit(solution)/shard_map/ppermute | solution.py:170
  165.0 39.4 %collective-permute-start.14 = (bf16[1,4,96,1024]{3,2,1,0:T(8,128)(2,1)}, bf16[1,4,96,1024]{3,2,1,0:T(8,128)(2,1)}, u32[]{:S(2)}, u32[]{:S(2)}) collective-permute-start(bf16[1,4,96,1024]{3,2,1,0:T(8,128)(2,1)} %add_convert_fusion.3), channel_id=1, source_target_pairs={{0,8},{4,12},{8,0},{12,4},{16,24},{20,28},{24,16},{28,20},{1,9},{5... | collective-permute-start | bytes 2359304 | tf_op jit(solution)/shard_map/ppermute | solution.py:170
  167.4 6.4 %copy-start.5 = (bf16[1,4,4,72,384]{4,3,2,1,0:T(8,128)(2,1)S(1)}, bf16[1,4,4,72,384]{4,3,2,1,0:T(8,128)(2,1)}, u32[]{:S(2)}) copy-start(bf16[1,4,4,72,384]{4,3,2,1,0:T(8,128)(2,1)} %copy-done.4) | copy-start | bytes 2654212
  167.4 6.4 %copy-start.8 = (s32[3]{0:T(128)S(1)}, s32[3]{0:T(128)}, u32[]{:S(2)}) copy-start(s32[3]{0:T(128)} %pad_add_fusion.1.sc_ref) | copy-start | bytes 40
  167.4 6.4 %copy-start.13 = (f32[4,4,1,128]{3,2,1,0:T(1,128)S(1)}, f32[4,4,1,128]{3,2,1,0:T(1,128)}, u32[]{:S(2)}) copy-start(f32[4,4,1,128]{3,2,1,0:T(1,128)} %get-tuple-element.20.wt_ref) | copy-start | bytes 24580
  167.4 6.4 %copy-start.14 = (f32[4,4,1,128]{3,2,1,0:T(1,128)S(1)}, f32[4,4,1,128]{3,2,1,0:T(1,128)}, u32[]{:S(2)}) copy-start(f32[4,4,1,128]{3,2,1,0:T(1,128)} %get-tuple-element.21.rank_ref) | copy-start | bytes 24580
  167.4 38.8 %collective-permute-start.16 = (bf16[1,4,96,1024]{3,2,1,0:T(8,128)(2,1)}, bf16[1,4,96,1024]{3,2,1,0:T(8,128)(2,1)}, u32[]{:S(2)}, u32[]{:S(2)}) collective-permute-start(bf16[1,4,96,1024]{3,2,1,0:T(8,128)(2,1)} %add_convert_fusion.1), channel_id=1, source_target_pairs={{0,8},{4,12},{8,0},{12,4},{16,24},{20,28},{24,16},{28,20},{1,9},{5... | collective-permute-start | bytes 2359304 | tf_op jit(solution)/shard_map/ppermute | solution.py:170
  171.1 2.6 %copy-start.15 = (bf16[4,384,2048]{2,1,0:T(8,128)(2,1)}, bf16[4,384,2048]{2,1,0:T(8,128)(2,1)S(1)}, u32[]{:S(2)}) copy-start(bf16[4,384,2048]{2,1,0:T(8,128)(2,1)S(1)} %constant_dynamic-update-slice_fusion.w_ref) | copy-start | bytes 18874372
  173.7 10.9 %copy-start.1 = (bf16[1,4,4,72,768]{4,3,2,1,0:T(8,128)(2,1)S(1)}, bf16[1,4,4,72,768]{4,3,2,1,0:T(8,128)(2,1)}, u32[]{:S(2)}) copy-start(bf16[1,4,4,72,768]{4,3,2,1,0:T(8,128)(2,1)} %hid_ref.3) | copy-start | bytes 5308420
  173.7 10.9 %copy-start.3 = (bf16[512,1024]{1,0:T(8,128)(2,1)S(1)}, bf16[512,1024]{1,0:T(8,128)(2,1)}, u32[]{:S(2)}) copy-start(bf16[512,1024]{1,0:T(8,128)(2,1)} %copy-done.2) | copy-start | bytes 3145732
  173.8 10.9 %copy-start.9 = (s32[3]{0:T(128)S(1)}, s32[3]{0:T(128)}, u32[]{:S(2)}) copy-start(s32[3]{0:T(128)} %pad_add_fusion.sc_ref) | copy-start | bytes 40
  173.8 10.9 %copy-start.11 = (f32[4,4,1,128]{3,2,1,0:T(1,128)S(1)}, f32[4,4,1,128]{3,2,1,0:T(1,128)}, u32[]{:S(2)}) copy-start(f32[4,4,1,128]{3,2,1,0:T(1,128)} %get-tuple-element.17.wt_ref) | copy-start | bytes 24580
  173.8 10.9 %copy-start.12 = (f32[4,4,1,128]{3,2,1,0:T(1,128)S(1)}, f32[4,4,1,128]{3,2,1,0:T(1,128)}, u32[]{:S(2)}) copy-start(f32[4,4,1,128]{3,2,1,0:T(1,128)} %get-tuple-element.18.rank_ref) | copy-start | bytes 24580
  183.1 1.6 copy-start.10
  183.1 11.3 %collective-permute-start.17 = (f32[4,4,128]{2,1,0:T(4,128)S(1)}, f32[4,4,128]{2,1,0:T(4,128)S(1)}, u32[]{:S(2)}, u32[]{:S(2)}) collective-permute-start(f32[4,4,128]{2,1,0:T(4,128)S(1)} %bitcast.21), channel_id=1, source_target_pairs={{0,16},{4,20},{8,24},{12,28},{16,0},{20,4},{24,8},{28,12},{1,17},{... | collective-permute-start | bytes 24584 | tf_op jit(solution)/shard_map/ppermute | solution.py:170
  193.5 0.9 copy-start.6
  195.0 8.8 %all-to-all-start = ((f32[4,4,128]{2,1,0:T(4,128)}), f32[4,4,128]{2,1,0:T(4,128)S(1)}, u32[]{:S(2)}, u32[]{:S(2)}) async-start(f32[4,4,128]{2,1,0:T(4,128)} %add.57), calls=%async_computation | async-start | bytes 16384 | tf_op jit(solution)/shard_map/all_to_all | solution.py:229
  198.2 21.5 %collective-permute-start.12 = (bf16[4,4,72,384]{3,2,1,0:T(8,128)(2,1)}, bf16[4,4,72,384]{3,2,1,0:T(8,128)(2,1)}, u32[]{:S(2)}, u32[]{:S(2)}) collective-permute-start(bf16[4,4,72,384]{3,2,1,0:T(8,128)(2,1)} %copy-done.10), channel_id=1, source_target_pairs={{0,16},{4,20},{8,24},{12,28},{16,0},{20,4},{24,8},{28,12},{1,17},{... | collective-permute-start | bytes 2654216 | tf_op jit(solution)/shard_map/ppermute | solution.py:170
  208.0 11.8 %copy-start.7 = (bf16[4,4,72,384]{3,2,1,0:T(8,128)(2,1)S(1)}, bf16[4,4,72,384]{3,2,1,0:T(8,128)(2,1)}, u32[]{:S(2)}) copy-start(bf16[4,4,72,384]{3,2,1,0:T(8,128)(2,1)} %copy-done.6) | copy-start | bytes 2654212

commit v2 on v1

--- a/solution.py
+++ b/solution.py
@@ -18,8 +18,8 @@
 
 
 def hidden_kernel(n, sc_ref, tab_ref, hid_ref, hst_ref, wt_ref, rank_ref):
-    experts, toks = tab_ref.shape[2], tab_ref.shape[3]
-    wt = tab_ref[0, 0].astype(F32)
+    experts, toks = tab_ref.shape[1], tab_ref.shape[2]
+    wt = tab_ref[0]
     named = wt > 0
     earlier = (iota((toks, toks), 0) < iota((toks, toks), 1)).astype(BF)
     rank = jnp.dot(named.astype(F32).astype(BF), earlier, preferred_element_type=F32)
@@ -36,7 +36,7 @@
 
 
 def hidden_to_tokens(n, scalars, table, hid, f):
-    experts, toks = table.shape[2], table.shape[3]
+    experts, toks = table.shape[1], table.shape[2]
     src = lambda k, sc: lax.rem(sc[0] + n - k, n)
     row = jax.ShapeDtypeStruct((n, experts, 1, toks), F32)
     row_spec = pl.BlockSpec((1, experts, 1, toks), lambda k, sc: (k, 0, 0, 0))
@@ -47,7 +47,7 @@
             num_scalar_prefetch=1,
             grid=(n,),
             in_specs=[
-                pl.BlockSpec((1, 1, experts, toks), lambda k, sc: (sc[2] * n + src(k, sc), sc[0], 0, 0)),
+                pl.BlockSpec((1, experts, toks), lambda k, sc: (src(k, sc), 0, 0)),
                 pl.BlockSpec((1, experts, 1, CAP, f), lambda k, sc: (0, 0, src(k, sc), 0, sc[1])),
             ],
             out_specs=(
@@ -120,8 +120,9 @@
 
 
 def part_kernel(bands, sc_ref, own_ref, nb_ref, tok_own_ref, tok_nb_ref, send_ref, keep_ref):
-    total = jnp.dot(own_ref[...], tok_own_ref[...], preferred_element_type=F32)
-    total = total + jnp.dot(nb_ref[...], tok_nb_ref[...], preferred_element_type=F32)
+    hidden = jnp.concatenate([own_ref[...], nb_ref[...]], axis=1)
+    toks = jnp.concatenate([tok_own_ref[...], tok_nb_ref[...]], axis=0)
+    total = jnp.dot(hidden, toks, preferred_element_type=F32)
     _, experts, band, cols = send_ref.shape
     total = total.reshape(experts, bands, band, cols).astype(BF)
     for a in range(bands):
@@ -170,9 +171,9 @@
         return lax.ppermute(x, "dp", [(i, i ^ bit) for i in range(n_dp)])
 
     ids = expert_ids[None] == jnp.arange(EXPERTS, dtype=jnp.int32)[:, None, None]
-    table = jnp.sum(jnp.where(ids, route_weights.astype(F32)[None], 0.0), axis=2).astype(BF)
-    tables = lax.all_gather(table, ("dp", "expert"), axis=0, tiled=False)
-    tables = tables.reshape(n_dp * n, n, experts, toks)
+    table = jnp.sum(jnp.where(ids, route_weights.astype(F32)[None], 0.0), axis=2)
+    tab_own = lax.all_to_all(table.reshape(n, experts, toks), "expert", 0, 0, tiled=True)
+    tab_nb = swap(tab_own, bands)
 
     half = d // 2
     tok_own, tok_nb = [], []
@@ -197,10 +198,10 @@
     for r, piece in pieces.items():
         w = lax.dynamic_update_slice(w, piece, (0, (j ^ r) * band, 0))
 
-    sc_own = jnp.stack([z, upper, dp]).astype(jnp.int32)
-    sc_nb = jnp.stack([z, 0 * z, dp ^ bands]).astype(jnp.int32)
-    hs_own, wt_own, rank_own = hidden_to_tokens(n, sc_own, tables, hidden_cache, f)
-    hs_nb, wt_nb, rank_nb = hidden_to_tokens(n, sc_nb, tables, hid_nb, f)
+    sc_own = jnp.stack([z, upper]).astype(jnp.int32)
+    sc_nb = jnp.stack([z, 0 * z]).astype(jnp.int32)
+    hs_own, wt_own, rank_own = hidden_to_tokens(n, sc_own, tab_own, hidden_cache, f)
+    hs_nb, wt_nb, rank_nb = hidden_to_tokens(n, sc_nb, tab_nb, hid_nb, f)
     hs_own, hs_nb = hs_own.reshape(experts * f, -1), hs_nb.reshape(experts * f, -1)
 
     sc_j = jnp.stack([j]).astype(jnp.int32)

time: 224 us -> 195 us (0.87)
  blocking collectives: 76.9 us -> 0 us
  waiting for transfers between devices: 46.9 us -> 70.7 us
  starting transfers between devices: 24 us -> 47.5 us
    all_gather x1 -> x0, blocking collectives: 76.9 us -> none  [per_device(): tables = lax.all_gather(table, ('dp', 'expert'), axis=0, tiled=False)]
    ppermute x12 -> x13, waiting for transfers between devices: 10.5 us -> 29.9 us  [swap(): return lax.ppermute(x, 'dp', [(i, i ^ bit) for i in range(n_dp)])]
    all_to_all x1, starting transfers between devices: 3.24 us -> 17.7 us  [per_device(): lax.all_to_all(sg, 'expert', split_axis=0, concat_axis=0, tiled=True)]
    all_to_all x0 -> x1, starting transfers between devices: none -> 8.37 us  [per_device(): lax.all_to_all(table.reshape(n, experts, toks), 'expert', 0, 0, tiled=True)]
    all_to_all x0 -> x1, waiting for transfers between devices: none -> 4.27 us  [per_device(): lax.all_to_all(table.reshape(n, experts, toks), 'expert', 0, 0, tiled=True)]
    unnamed x36 -> x40, local copies, waits for them, and re-layouts: 4.58 us -> 5.26 us
    ppermute x12 -> x13, starting transfers between devices: 10.2 us -> 10.9 us  [swap(): return lax.ppermute(x, 'dp', [(i, i ^ bit) for i in range(n_dp)])]
  transfers between devices with their start and end apart: 19 -> 21, of which waited for: 6 -> 8; matrix products, arithmetic and copies ran while one was open for 10% -> 12% of each run, Pallas kernels for 19% -> 22%
where the time goes in v2:
time: 195 us; the launch traced here: 194 us
  waiting for transfers between devices  70.7 us (36%)
  starting transfers between devices  47.5 us (24%)
  Pallas kernels  43 us (22%)
  other arithmetic  17.8 us (9%)
  local copies, waits for them, and re-layouts  14.6 us (7%)
    ppermute x6, waiting for transfers between devices, per_device(): lax.ppermute(mine, 'expert', [(i, (i + k) % n) for i in range(n)])  31.7 us
    ppermute x13, waiting for transfers between devices, swap(): return lax.ppermute(x, 'dp', [(i, i ^ bit) for i in range(n_dp)])  29.9 us
    pallas_call x2, Pallas kernels, backward(): pl.pallas_call(functools.partial(back_kernel, n), out_shape=(jax.ShapeDty...  18 us
    all_to_all x1, starting transfers between devices, per_device(): lax.all_to_all(sg, 'expert', split_axis=0, concat_axis=0, tiled=True)  17.7 us
    pallas_call x2, Pallas kernels, partial_grad(): pl.pallas_call(functools.partial(part_kernel, bands), out_shape=(out, out...  15.2 us
    ppermute x13, starting transfers between devices, swap(): return lax.ppermute(x, 'dp', [(i, i ^ bit) for i in range(n_dp)])  10.9 us
    ppermute x6, starting transfers between devices, per_device(): lax.ppermute(mine, 'expert', [(i, (i + k) % n) for i in range(n)])  10.5 us
    pallas_call x2, Pallas kernels, hidden_to_tokens(): pl.pallas_call(functools.partial(hidden_kernel, n), out_shape=(jax.ShapeD...  9.74 us
  transfers between devices with their start and end apart: 21, of which 8 were waited for; matrix products, arithmetic and copies ran while one was open for 12% of the time, Pallas kernels for 22%

profile of v2, /device:TPU:0, one launch (start us, length us, event | category | flops | bytes accessed | tf_op | source)
XLA Modules:
  0.0 194.5 jit_solution(6816717310114699083)
XLA Ops:
  0.6 1.2 fusion.2
  1.8 3.1 %collective-permute-start = (bf16[128,1024]{1,0:T(8,128)(2,1)S(1)}, bf16[128,1024]{1,0:T(8,128)(2,1)S(1)}, u32[]{:S(2)}, u32[]{:S(2)}) collective-permute-start(bf16[128,1024]{1,0:T(8,128)(2,1)S(1)} %get-tuple-element.32), channel_id=1, source_target_pairs={{0,1},{1,2},{2,3},{3,0},{4,5},{5,6},{6,7},{7,4},{8,9},{9,10},{10,1... | collective-permute-start | bytes 786440 | tf_op jit(solution)/shard_map/ppermute | solution.py:183
  4.9 2.6 %collective-permute-start.1 = (bf16[128,1024]{1,0:T(8,128)(2,1)S(1)}, bf16[128,1024]{1,0:T(8,128)(2,1)S(1)}, u32[]{:S(2)}, u32[]{:S(2)}) collective-permute-start(bf16[128,1024]{1,0:T(8,128)(2,1)S(1)} %get-tuple-element.32), channel_id=1, source_target_pairs={{0,2},{1,3},{2,0},{3,1},{4,6},{5,7},{6,4},{7,5},{8,10},{9,11},{10,... | collective-permute-start | bytes 786440 | tf_op jit(solution)/shard_map/ppermute | solution.py:183
  7.5 1.3 collective-permute-start.2
  8.9 0.7 collective-permute-start.3
  9.9 4.3 %collective-permute-done = bf16[128,1024]{1,0:T(8,128)(2,1)S(1)} collective-permute-done((bf16[128,1024]{1,0:T(8,128)(2,1)S(1)}, bf16[128,1024]{1,0:T(8,128)(2,1)S(1)}, u32[]{:S(2)}, u32[]{:S(2)}) %collective-permute-start) | collective-permute-done | bytes 262176 | tf_op jit(solution)/shard_map/ppermute | solution.py:183
  14.2 2.5 %collective-permute-start.5 = (bf16[128,1024]{1,0:T(8,128)(2,1)S(1)}, bf16[128,1024]{1,0:T(8,128)(2,1)}, u32[]{:S(2)}, u32[]{:S(2)}) collective-permute-start(bf16[128,1024]{1,0:T(8,128)(2,1)S(1)} %get-tuple-element.31), channel_id=1, source_target_pairs={{0,3},{1,0},{2,1},{3,2},{4,7},{5,4},{6,5},{7,6},{8,11},{9,8},{10,9... | collective-permute-start | bytes 786440 | tf_op jit(solution)/shard_map/ppermute | solution.py:183
  16.7 8.8 %collective-permute-done.1 = bf16[128,1024]{1,0:T(8,128)(2,1)S(1)} collective-permute-done((bf16[128,1024]{1,0:T(8,128)(2,1)S(1)}, bf16[128,1024]{1,0:T(8,128)(2,1)S(1)}, u32[]{:S(2)}, u32[]{:S(2)}) %collective-permute-start.1) | collective-permute-done | bytes 262176 | tf_op jit(solution)/shard_map/ppermute | solution.py:183
  25.6 1.8 collective-permute-start.9
  27.4 1.0 constant_dynamic-slice_fusion
  28.7 2.4 %collective-permute-done.3 = bf16[128,1024]{1,0:T(8,128)(2,1)S(1)} collective-permute-done((bf16[128,1024]{1,0:T(8,128)(2,1)S(1)}, bf16[128,1024]{1,0:T(8,128)(2,1)S(1)}, u32[]{:S(2)}, u32[]{:S(2)}) %collective-permute-start.3) | collective-permute-done | bytes 262176 | tf_op jit(solution)/shard_map/ppermute | solution.py:183
  31.1 16.1 %collective-permute-done.4 = bf16[128,1024]{1,0:T(8,128)(2,1)} collective-permute-done((bf16[128,1024]{1,0:T(8,128)(2,1)S(1)}, bf16[128,1024]{1,0:T(8,128)(2,1)}, u32[]{:S(2)}, u32[]{:S(2)}) %collective-permute-start.4) | collective-permute-done | bytes 262176 | tf_op jit(solution)/shard_map/ppermute | solution.py:183
  47.2 2.1 %pad_maximum_fusion.2.tok1_ref.tok_own_ref = bf16[512,1024]{1,0:T(8,128)(2,1)} fusion(bf16[128,1024]{1,0:T(8,128)(2,1)} %collective-permute-done.5, bf16[128,1024]{1,0:T(8,128)(2,1)} %collective-permute-done.4, bf16[128,1024]{1,0:T(8,128)(2,1)S(1)} %collective-permute-done.3, bf16[128,1024]{1,0:T(8,128)(2,1)S(1)} %get-tuple-element.31), kind=kLoop, calls=%fused_computation.7 | loop fusion | flops 4194304 | bytes 2097152 | tf_op jit(solution)/shard_map/concatenate | solution.py:185
  49.3 1.5 collective-permute-start.10
  50.9 1.5 collective-permute-start.6
  52.4 0.6 select_reduce_fusion.1
  53.0 8.4 %all-to-all-start = ((f32[4,4,128]{2,1,0:T(4,128)}), f32[4,4,128]{2,1,0:T(4,128)S(1)}, u32[]{:S(2)}, u32[]{:S(2)}) async-start(f32[4,4,128]{2,1,0:T(4,128)} %bitcast.2), calls=%async_computation | async-start | bytes 16384 | tf_op jit(solution)/shard_map/all_to_all | solution.py:175
  61.3 0.6 pad_add_fusion.sc_ref
  62.0 0.7 pad_add_fusion.1.sc_ref
  62.7 4.3 %all-to-all-done.tab_ref = f32[4,4,128]{2,1,0:T(4,128)S(1)} async-done(((f32[4,4,128]{2,1,0:T(4,128)}), f32[4,4,128]{2,1,0:T(4,128)S(1)}, u32[]{:S(2)}, u32[]{:S(2)}) %all-to-all-start) | async-done | bytes 8224 | tf_op jit(solution)/shard_map/all_to_all | solution.py:175
  67.5 4.9 %shard_map.76 = (bf16[4,384,512]{2,1,0:T(8,128)(2,1)}, f32[4,4,1,128]{3,2,1,0:T(1,128)}, f32[4,4,1,128]{3,2,1,0:T(1,128)}) custom-call(s32[2]{0:T(128)} %pad_add_fusion.sc_ref, f32[4,4,128]{2,1,0:T(4,128)} %copy-done.16, bf16[1,4,4,72,768]{4,3,2,1,0:T(8,128)(2,1)} %hid_ref.3), custom_call_target="tpu_custom_call" | custom-call | flops 113246208 | bytes 3145728 | tf_op jit(solution)/shard_map/pallas_call | solution.py:43
  72.4 19.8 %collective-permute-done.12.tab_ref = f32[4,4,128]{2,1,0:T(4,128)S(1)} collective-permute-done((f32[4,4,128]{2,1,0:T(4,128)S(1)}, f32[4,4,128]{2,1,0:T(4,128)S(1)}, u32[]{:S(2)}, u32[]{:S(2)}) %collective-permute-start.12) | collective-permute-done | bytes 8224 | tf_op jit(solution)/shard_map/ppermute | solution.py:171
  92.8 0.9 copy-done.4
  93.7 4.9 %shard_map.78 = (bf16[4,384,512]{2,1,0:T(8,128)(2,1)}, f32[4,4,1,128]{3,2,1,0:T(1,128)}, f32[4,4,1,128]{3,2,1,0:T(1,128)}) custom-call(s32[2]{0:T(128)} %pad_add_fusion.1.sc_ref, f32[4,4,128]{2,1,0:T(4,128)} %copy-done.18, bf16[1,4,4,72,384]{4,3,2,1,0:T(8,128)(2,1)} %copy-done.4), custom_call_target="tpu_custom_call" | custom-call | flops 113246208 | bytes 3145728 | tf_op jit(solution)/shard_map/pallas_call | solution.py:43
  98.6 7.6 %shard_map.80 = (bf16[2,4,96,1024]{3,2,1,0:T(8,128)(2,1)}, bf16[2,4,96,1024]{3,2,1,0:T(8,128)(2,1)S(1)}) custom-call(s32[1]{0:T(128)} %bitcast.5.sc_ref, bf16[1536,512]{1,0:T(8,128)(2,1)} %bitcast.23, bf16[1536,512]{1,0:T(8,128)(2,1)} %bitcast.25, bf16[512,1024]{1,0:T(8,128)(2,1)S(1)} %pad_maximum_fusion.1.tok0_ref.tok_own_ref, ...), custom_call_target="tpu_custom_call" | custom-call | flops 3221225472 | bytes 8388608 | tf_op jit(solution)/shard_map/pallas_call | solution.py:146
  106.2 7.6 %shard_map.81 = (bf16[2,4,96,1024]{3,2,1,0:T(8,128)(2,1)}, bf16[2,4,96,1024]{3,2,1,0:T(8,128)(2,1)S(1)}) custom-call(s32[1]{0:T(128)} %bitcast.5.sc_ref, bf16[1536,512]{1,0:T(8,128)(2,1)} %bitcast.24, bf16[1536,512]{1,0:T(8,128)(2,1)} %bitcast.26, bf16[512,1024]{1,0:T(8,128)(2,1)} %pad_maximum_fusion.2.tok1_ref.tok_own_ref, ...), custom_call_target="tpu_custom_call" | custom-call | flops 3221225472 | bytes 8388608 | tf_op jit(solution)/shard_map/pallas_call | solution.py:146
  114.4 0.8 broadcast_in_dim.35
  115.2 1.6 constant_dynamic-update-slice_fusion.3
  116.8 1.6 constant_dynamic-update-slice_fusion.2
  118.4 1.6 constant_dynamic-update-slice_fusion.1
  120.0 2.3 %add_convert_fusion.3 = bf16[1,4,96,1024]{3,2,1,0:T(8,128)(2,1)} fusion(bf16[2,4,96,1024]{3,2,1,0:T(8,128)(2,1)} %collective-permute-done.14, bf16[2,4,96,1024]{3,2,1,0:T(8,128)(2,1)S(1)} %get-tuple-element.25), kind=kLoop, calls=%fused_computation.5 | loop fusion | flops 1572864 | bytes 2359296 | tf_op jit(solution)/shard_map/convert_element_type | solution.py:215
  122.4 1.7 collective-permute-start.15
  124.1 2.3 %add_convert_fusion.1 = bf16[1,4,96,1024]{3,2,1,0:T(8,128)(2,1)} fusion(bf16[2,4,96,1024]{3,2,1,0:T(8,128)(2,1)} %collective-permute-done.16, bf16[2,4,96,1024]{3,2,1,0:T(8,128)(2,1)S(1)} %get-tuple-element.27), kind=kLoop, calls=%fused_computation.3 | loop fusion | flops 1572864 | bytes 2359296 | tf_op jit(solution)/shard_map/convert_element_type | solution.py:215
  126.8 1.6 constant_dynamic-update-slice_fusion.w_ref
  128.4 2.7 %copy-done.15 = bf16[4,384,2048]{2,1,0:T(8,128)(2,1)} copy-done((bf16[4,384,2048]{2,1,0:T(8,128)(2,1)}, bf16[4,384,2048]{2,1,0:T(8,128)(2,1)S(1)}, u32[]{:S(2)}) %copy-start.15) | copy-done | bytes 6291480
  131.1 9.3 %shard_map.79 = (bf16[4,4,72,384]{3,2,1,0:T(8,128)(2,1)S(1)}, f32[4,4,1,128]{3,2,1,0:T(1,128)S(1)}) custom-call(s32[2]{0:T(128)S(1)} %copy-done.8, bf16[512,1024]{1,0:T(8,128)(2,1)} %collective-permute-done.9.tok0_ref.tok_nb_ref, bf16[512,1024]{1,0:T(8,128)(2,1)} %collective-permute-done.10.tok1_ref.tok_nb_ref, bf16[4,384,2048]{2,1,0:T(8,128)(2,1)} %copy-done.15, ...), custom_call_target="tpu_custom_call" | custom-call | flops 3221225472 | bytes 10158080 | tf_op jit(solution)/shard_map/pallas_call | solution.py:94
  140.4 1.8 collective-permute-start.18
  142.3 8.8 %shard_map.77 = (bf16[4,4,72,384]{3,2,1,0:T(8,128)(2,1)S(1)}, f32[4,4,1,128]{3,2,1,0:T(1,128)S(1)}) custom-call(s32[2]{0:T(128)S(1)} %copy-done.9, bf16[512,1024]{1,0:T(8,128)(2,1)S(1)} %copy-done.3, bf16[512,1024]{1,0:T(8,128)(2,1)} %pad_maximum_fusion.2.tok1_ref.tok_own_ref, bf16[4,384,2048]{2,1,0:T(8,128)(2,1)} %copy-done.15, ...), custom_call_target="tpu_custom_call" | custom-call | flops 3221225472 | bytes 10158080 | tf_op jit(solution)/shard_map/pallas_call | solution.py:94
  151.0 0.9 copy-done.6
  152.6 17.7 %all-to-all-start.1 = ((f32[4,4,128]{2,1,0:T(4,128)}), f32[4,4,128]{2,1,0:T(4,128)S(1)}, u32[]{:S(2)}, u32[]{:S(2)}) async-start(f32[4,4,128]{2,1,0:T(4,128)} %add.57), calls=%async_computation.1 | async-start | bytes 16384 | tf_op jit(solution)/shard_map/all_to_all | solution.py:230
  170.3 0.8 collective-permute-start.13
  171.1 4.8 %all-to-all-done.1 = f32[4,4,128]{2,1,0:T(4,128)S(1)} async-done(((f32[4,4,128]{2,1,0:T(4,128)}), f32[4,4,128]{2,1,0:T(4,128)S(1)}, u32[]{:S(2)}, u32[]{:S(2)}) %all-to-all-start.1) | async-done | bytes 8224 | tf_op jit(solution)/shard_map/all_to_all | solution.py:230
  175.9 0.6 select_reduce_fusion
  176.5 1.8 fusion
  178.3 1.8 fusion.1
  180.1 1.2 pad_maximum_fusion
  181.3 10.1 %collective-permute-done.13 = bf16[4,4,72,384]{3,2,1,0:T(8,128)(2,1)} collective-permute-done((bf16[4,4,72,384]{3,2,1,0:T(8,128)(2,1)}, bf16[4,4,72,384]{3,2,1,0:T(8,128)(2,1)}, u32[]{:S(2)}, u32[]{:S(2)}) %collective-permute-start.13) | collective-permute-done | bytes 884768 | tf_op jit(solution)/shard_map/ppermute | solution.py:171
  191.5 3.0 %maximum_select_fusion = bf16[1,4,4,72,768]{4,3,2,1,0:T(8,128)(2,1)} fusion(bf16[1,4,4,72,384]{4,3,2,1,0:T(8,128)(2,1)} %bitcast.4, bf16[1,4,4,72,384]{4,3,2,1,0:T(8,128)(2,1)S(1)} %bitcast.17, pred[]{:T(512)S(6)} %eq.16), kind=kLoop, calls=%fused_computation | loop fusion | flops 7962624 | bytes 3538945 | tf_op jit(solution)/shard_map/jit(_where)/select_n | solution.py:224
  (61 shorter events, 3.5 us)
Async XLA Ops:
  0.6 26.8 %copy-start = (bf16[1,4,4,72,768]{4,3,2,1,0:T(8,128)(2,1)S(1)}, bf16[1,4,4,72,768]{4,3,2,1,0:T(8,128)(2,1)}, u32[]{:S(2)}) copy-start(bf16[1,4,4,72,768]{4,3,2,1,0:T(8,128)(2,1)} %hid_ref.3) | copy-start | bytes 5308420
  1.8 12.4 %collective-permute-start = (bf16[128,1024]{1,0:T(8,128)(2,1)S(1)}, bf16[128,1024]{1,0:T(8,128)(2,1)S(1)}, u32[]{:S(2)}, u32[]{:S(2)}) collective-permute-start(bf16[128,1024]{1,0:T(8,128)(2,1)S(1)} %get-tuple-element.32), channel_id=1, source_target_pairs={{0,1},{1,2},{2,3},{3,0},{4,5},{5,6},{6,7},{7,4},{8,9},{9,10},{10,1... | collective-permute-start | bytes 786440 | tf_op jit(solution)/shard_map/ppermute | solution.py:183
  4.9 20.6 %collective-permute-start.1 = (bf16[128,1024]{1,0:T(8,128)(2,1)S(1)}, bf16[128,1024]{1,0:T(8,128)(2,1)S(1)}, u32[]{:S(2)}, u32[]{:S(2)}) collective-permute-start(bf16[128,1024]{1,0:T(8,128)(2,1)S(1)} %get-tuple-element.32), channel_id=1, source_target_pairs={{0,2},{1,3},{2,0},{3,1},{4,6},{5,7},{6,4},{7,5},{8,10},{9,11},{10,... | collective-permute-start | bytes 786440 | tf_op jit(solution)/shard_map/ppermute | solution.py:183
  7.5 18.0 %collective-permute-start.2 = (bf16[128,1024]{1,0:T(8,128)(2,1)S(1)}, bf16[128,1024]{1,0:T(8,128)(2,1)S(1)}, u32[]{:S(2)}, u32[]{:S(2)}) collective-permute-start(bf16[128,1024]{1,0:T(8,128)(2,1)S(1)} %get-tuple-element.32), channel_id=1, source_target_pairs={{0,3},{1,0},{2,1},{3,2},{4,7},{5,4},{6,5},{7,6},{8,11},{9,8},{10,9... | collective-permute-start | bytes 786440 | tf_op jit(solution)/shard_map/ppermute | solution.py:183
  8.9 22.3 %collective-permute-start.3 = (bf16[128,1024]{1,0:T(8,128)(2,1)S(1)}, bf16[128,1024]{1,0:T(8,128)(2,1)S(1)}, u32[]{:S(2)}, u32[]{:S(2)}) collective-permute-start(bf16[128,1024]{1,0:T(8,128)(2,1)S(1)} %get-tuple-element.31), channel_id=1, source_target_pairs={{0,1},{1,2},{2,3},{3,0},{4,5},{5,6},{6,7},{7,4},{8,9},{9,10},{10,1... | collective-permute-start | bytes 786440 | tf_op jit(solution)/shard_map/ppermute | solution.py:183
  9.5 37.7 %collective-permute-start.4 = (bf16[128,1024]{1,0:T(8,128)(2,1)S(1)}, bf16[128,1024]{1,0:T(8,128)(2,1)}, u32[]{:S(2)}, u32[]{:S(2)}) collective-permute-start(bf16[128,1024]{1,0:T(8,128)(2,1)S(1)} %get-tuple-element.31), channel_id=1, source_target_pairs={{0,2},{1,3},{2,0},{3,1},{4,6},{5,7},{6,4},{7,5},{8,10},{9,11},{10,... | collective-permute-start | bytes 786440 | tf_op jit(solution)/shard_map/ppermute | solution.py:183
  14.2 33.0 %collective-permute-start.5 = (bf16[128,1024]{1,0:T(8,128)(2,1)S(1)}, bf16[128,1024]{1,0:T(8,128)(2,1)}, u32[]{:S(2)}, u32[]{:S(2)}) collective-permute-start(bf16[128,1024]{1,0:T(8,128)(2,1)S(1)} %get-tuple-element.31), channel_id=1, source_target_pairs={{0,3},{1,0},{2,1},{3,2},{4,7},{5,4},{6,5},{7,6},{8,11},{9,8},{10,9... | collective-permute-start | bytes 786440 | tf_op jit(solution)/shard_map/ppermute | solution.py:183
  25.6 73.0 %copy-start.2 = (bf16[512,1024]{1,0:T(8,128)(2,1)}, bf16[512,1024]{1,0:T(8,128)(2,1)S(1)}, u32[]{:S(2)}) copy-start(bf16[512,1024]{1,0:T(8,128)(2,1)S(1)} %pad_maximum_fusion.1.tok0_ref.tok_own_ref) | copy-start | bytes 3145732
  25.6 73.0 %collective-permute-start.9 = (bf16[512,1024]{1,0:T(8,128)(2,1)S(1)}, bf16[512,1024]{1,0:T(8,128)(2,1)}, u32[]{:S(2)}, u32[]{:S(2)}) collective-permute-start(bf16[512,1024]{1,0:T(8,128)(2,1)S(1)} %pad_maximum_fusion.1.tok0_ref.tok_own_ref), channel_id=1, source_target_pairs={{0,16},{4,20},{8,24},{12,28},{16,0},{20,4},{24,8},{28,12},{1,17},{... | collective-permute-start | bytes 3145736 | tf_op jit(solution)/shard_map/ppermute | solution.py:171
  27.4 24.9 %copy-start.19 = (bf16[128,8]{0,1:T(8,128)(2,1)S(1)}, bf16[128,8]{0,1:T(8,128)(2,1)}, u32[]{:S(2)}) copy-start(bf16[128,8]{0,1:T(8,128)(2,1)} %param.7) | copy-start | bytes 6148
  27.4 24.9 %copy-start.17 = (s32[128,8]{0,1:T(8,128)S(1)}, s32[128,8]{0,1:T(8,128)}, u32[]{:S(2)}) copy-start(s32[128,8]{0,1:T(8,128)} %param.6) | copy-start | bytes 12292
  28.4 63.8 %collective-permute-start.11 = (bf16[1,4,4,72,384]{4,3,2,1,0:T(8,128)(2,1)}, bf16[1,4,4,72,384]{4,3,2,1,0:T(8,128)(2,1)S(1)}, u32[]{:S(2)}, u32[]{:S(2)}) collective-permute-start(bf16[1,4,4,72,384]{4,3,2,1,0:T(8,128)(2,1)} %constant_dynamic-slice_fusion), channel_id=1, source_target_pairs={{0,16},{4,20},{8,24},{12,28},{16,0},{20,4},{24,8},{28,12},{1,17},{... | collective-permute-start | bytes 2654216 | tf_op jit(solution)/shard_map/ppermute | solution.py:171
  49.3 56.9 %collective-permute-start.10 = (bf16[512,1024]{1,0:T(8,128)(2,1)}, bf16[512,1024]{1,0:T(8,128)(2,1)}, u32[]{:S(2)}, u32[]{:S(2)}) collective-permute-start(bf16[512,1024]{1,0:T(8,128)(2,1)} %pad_maximum_fusion.2.tok1_ref.tok_own_ref), channel_id=1, source_target_pairs={{0,16},{4,20},{8,24},{12,28},{16,0},{20,4},{24,8},{28,12},{1,17},{... | collective-permute-start | bytes 3145736 | tf_op jit(solution)/shard_map/ppermute | solution.py:171
  50.9 63.5 %collective-permute-start.6 = (bf16[4,96,2048]{2,1,0:T(8,128)(2,1)}, bf16[4,96,2048]{2,1,0:T(8,128)(2,1)}, u32[]{:S(2)}, u32[]{:S(2)}) collective-permute-start(bf16[4,96,2048]{2,1,0:T(8,128)(2,1)} %param.9), channel_id=1, source_target_pairs={{0,8},{4,12},{8,0},{12,4},{16,24},{20,28},{24,16},{28,20},{1,9},{5... | collective-permute-start | bytes 4718600 | tf_op jit(solution)/shard_map/ppermute | solution.py:171
  53.0 14.0 %all-to-all-start = ((f32[4,4,128]{2,1,0:T(4,128)}), f32[4,4,128]{2,1,0:T(4,128)S(1)}, u32[]{:S(2)}, u32[]{:S(2)}) async-start(f32[4,4,128]{2,1,0:T(4,128)} %bitcast.2), calls=%async_computation | async-start | bytes 16384 | tf_op jit(solution)/shard_map/all_to_all | solution.py:175
  66.9 0.6 copy-start.16
  66.9 25.2 %collective-permute-start.12 = (f32[4,4,128]{2,1,0:T(4,128)S(1)}, f32[4,4,128]{2,1,0:T(4,128)S(1)}, u32[]{:S(2)}, u32[]{:S(2)}) collective-permute-start(f32[4,4,128]{2,1,0:T(4,128)S(1)} %all-to-all-done.tab_ref), channel_id=1, source_target_pairs={{0,16},{4,20},{8,24},{12,28},{16,0},{20,4},{24,8},{28,12},{1,17},{... | collective-permute-start | bytes 24584 | tf_op jit(solution)/shard_map/ppermute | solution.py:171
  92.2 0.6 copy-start.18
  92.2 26.2 %collective-permute-start.7 = (bf16[4,96,2048]{2,1,0:T(8,128)(2,1)}, bf16[4,96,2048]{2,1,0:T(8,128)(2,1)}, u32[]{:S(2)}, u32[]{:S(2)}) collective-permute-start(bf16[4,96,2048]{2,1,0:T(8,128)(2,1)} %param.9), channel_id=1, source_target_pairs={{0,4},{4,0},{8,12},{12,8},{16,20},{20,16},{24,28},{28,24},{1,5},{5... | collective-permute-start | bytes 4718600 | tf_op jit(solution)/shard_map/ppermute | solution.py:171
  92.8 0.9 copy-start.4
  106.2 13.8 %collective-permute-start.14 = (bf16[2,4,96,1024]{3,2,1,0:T(8,128)(2,1)}, bf16[2,4,96,1024]{3,2,1,0:T(8,128)(2,1)}, u32[]{:S(2)}, u32[]{:S(2)}) collective-permute-start(bf16[2,4,96,1024]{3,2,1,0:T(8,128)(2,1)} %get-tuple-element.26), channel_id=1, source_target_pairs={{0,4},{4,0},{8,12},{12,8},{16,20},{20,16},{24,28},{28,24},{1,5},{5... | collective-permute-start | bytes 4718600 | tf_op jit(solution)/shard_map/ppermute | solution.py:171
  113.8 10.2 %collective-permute-start.16 = (bf16[2,4,96,1024]{3,2,1,0:T(8,128)(2,1)}, bf16[2,4,96,1024]{3,2,1,0:T(8,128)(2,1)}, u32[]{:S(2)}, u32[]{:S(2)}) collective-permute-start(bf16[2,4,96,1024]{3,2,1,0:T(8,128)(2,1)} %get-tuple-element.28), channel_id=1, source_target_pairs={{0,4},{4,0},{8,12},{12,8},{16,20},{20,16},{24,28},{28,24},{1,5},{5... | collective-permute-start | bytes 4718600 | tf_op jit(solution)/shard_map/ppermute | solution.py:171
  114.3 12.5 %collective-permute-start.8 = (bf16[4,96,2048]{2,1,0:T(8,128)(2,1)}, bf16[4,96,2048]{2,1,0:T(8,128)(2,1)}, u32[]{:S(2)}, u32[]{:S(2)}) collective-permute-start(bf16[4,96,2048]{2,1,0:T(8,128)(2,1)} %collective-permute-done.6), channel_id=1, source_target_pairs={{0,4},{4,0},{8,12},{12,8},{16,20},{20,16},{24,28},{28,24},{1,5},{5... | collective-permute-start | bytes 4718600 | tf_op jit(solution)/shard_map/ppermute | solution.py:171
  122.4 54.1 %collective-permute-start.15 = (bf16[1,4,96,1024]{3,2,1,0:T(8,128)(2,1)}, bf16[1,4,96,1024]{3,2,1,0:T(8,128)(2,1)}, u32[]{:S(2)}, u32[]{:S(2)}) collective-permute-start(bf16[1,4,96,1024]{3,2,1,0:T(8,128)(2,1)} %add_convert_fusion.3), channel_id=1, source_target_pairs={{0,8},{4,12},{8,0},{12,4},{16,24},{20,28},{24,16},{28,20},{1,9},{5... | collective-permute-start | bytes 2359304 | tf_op jit(solution)/shard_map/ppermute | solution.py:171
  126.4 4.7 %copy-start.5 = (bf16[1,4,4,72,384]{4,3,2,1,0:T(8,128)(2,1)S(1)}, bf16[1,4,4,72,384]{4,3,2,1,0:T(8,128)(2,1)}, u32[]{:S(2)}) copy-start(bf16[1,4,4,72,384]{4,3,2,1,0:T(8,128)(2,1)} %copy-done.4) | copy-start | bytes 2654212
  126.4 4.7 %copy-start.8 = (s32[2]{0:T(128)S(1)}, s32[2]{0:T(128)}, u32[]{:S(2)}) copy-start(s32[2]{0:T(128)} %pad_add_fusion.1.sc_ref) | copy-start | bytes 28
  126.4 4.7 %copy-start.13 = (f32[4,4,1,128]{3,2,1,0:T(1,128)S(1)}, f32[4,4,1,128]{3,2,1,0:T(1,128)}, u32[]{:S(2)}) copy-start(f32[4,4,1,128]{3,2,1,0:T(1,128)} %get-tuple-element.20.wt_ref) | copy-start | bytes 24580
  126.4 4.7 %copy-start.14 = (f32[4,4,1,128]{3,2,1,0:T(1,128)S(1)}, f32[4,4,1,128]{3,2,1,0:T(1,128)}, u32[]{:S(2)}) copy-start(f32[4,4,1,128]{3,2,1,0:T(1,128)} %get-tuple-element.21.rank_ref) | copy-start | bytes 24580
  126.4 51.8 %collective-permute-start.17 = (bf16[1,4,96,1024]{3,2,1,0:T(8,128)(2,1)}, bf16[1,4,96,1024]{3,2,1,0:T(8,128)(2,1)}, u32[]{:S(2)}, u32[]{:S(2)}) collective-permute-start(bf16[1,4,96,1024]{3,2,1,0:T(8,128)(2,1)} %add_convert_fusion.1), channel_id=1, source_target_pairs={{0,8},{4,12},{8,0},{12,4},{16,24},{20,28},{24,16},{28,20},{1,9},{5... | collective-permute-start | bytes 2359304 | tf_op jit(solution)/shard_map/ppermute | solution.py:171
  128.4 2.7 %copy-start.15 = (bf16[4,384,2048]{2,1,0:T(8,128)(2,1)}, bf16[4,384,2048]{2,1,0:T(8,128)(2,1)S(1)}, u32[]{:S(2)}) copy-start(bf16[4,384,2048]{2,1,0:T(8,128)(2,1)S(1)} %constant_dynamic-update-slice_fusion.w_ref) | copy-start | bytes 18874372
  131.1 11.1 %copy-start.1 = (bf16[1,4,4,72,768]{4,3,2,1,0:T(8,128)(2,1)S(1)}, bf16[1,4,4,72,768]{4,3,2,1,0:T(8,128)(2,1)}, u32[]{:S(2)}) copy-start(bf16[1,4,4,72,768]{4,3,2,1,0:T(8,128)(2,1)} %hid_ref.3) | copy-start | bytes 5308420
  131.1 11.1 %copy-start.3 = (bf16[512,1024]{1,0:T(8,128)(2,1)S(1)}, bf16[512,1024]{1,0:T(8,128)(2,1)}, u32[]{:S(2)}) copy-start(bf16[512,1024]{1,0:T(8,128)(2,1)} %copy-done.2) | copy-start | bytes 3145732
  131.1 11.1 %copy-start.9 = (s32[2]{0:T(128)S(1)}, s32[2]{0:T(128)}, u32[]{:S(2)}) copy-start(s32[2]{0:T(128)} %pad_add_fusion.sc_ref) | copy-start | bytes 28
  131.1 11.1 %copy-start.11 = (f32[4,4,1,128]{3,2,1,0:T(1,128)S(1)}, f32[4,4,1,128]{3,2,1,0:T(1,128)}, u32[]{:S(2)}) copy-start(f32[4,4,1,128]{3,2,1,0:T(1,128)} %get-tuple-element.17.wt_ref) | copy-start | bytes 24580
  131.1 11.1 %copy-start.12 = (f32[4,4,1,128]{3,2,1,0:T(1,128)S(1)}, f32[4,4,1,128]{3,2,1,0:T(1,128)}, u32[]{:S(2)}) copy-start(f32[4,4,1,128]{3,2,1,0:T(1,128)} %get-tuple-element.18.rank_ref) | copy-start | bytes 24580
  140.4 1.8 copy-start.10
  140.4 11.5 %collective-permute-start.18 = (f32[4,4,128]{2,1,0:T(4,128)S(1)}, f32[4,4,128]{2,1,0:T(4,128)S(1)}, u32[]{:S(2)}, u32[]{:S(2)}) collective-permute-start(f32[4,4,128]{2,1,0:T(4,128)S(1)} %bitcast.19), channel_id=1, source_target_pairs={{0,16},{4,20},{8,24},{12,28},{16,0},{20,4},{24,8},{28,12},{1,17},{... | collective-permute-start | bytes 24584 | tf_op jit(solution)/shard_map/ppermute | solution.py:171
  151.0 0.9 copy-start.6
  152.6 23.3 %all-to-all-start.1 = ((f32[4,4,128]{2,1,0:T(4,128)}), f32[4,4,128]{2,1,0:T(4,128)S(1)}, u32[]{:S(2)}, u32[]{:S(2)}) async-start(f32[4,4,128]{2,1,0:T(4,128)} %add.57), calls=%async_computation.1 | async-start | bytes 16384 | tf_op jit(solution)/shard_map/all_to_all | solution.py:230
  170.3 21.2 %collective-permute-start.13 = (bf16[4,4,72,384]{3,2,1,0:T(8,128)(2,1)}, bf16[4,4,72,384]{3,2,1,0:T(8,128)(2,1)}, u32[]{:S(2)}, u32[]{:S(2)}) collective-permute-start(bf16[4,4,72,384]{3,2,1,0:T(8,128)(2,1)} %copy-done.10), channel_id=1, source_target_pairs={{0,16},{4,20},{8,24},{12,28},{16,0},{20,4},{24,8},{28,12},{1,17},{... | collective-permute-start | bytes 2654216 | tf_op jit(solution)/shard_map/ppermute | solution.py:171
  180.1 11.4 %copy-start.7 = (bf16[4,4,72,384]{3,2,1,0:T(8,128)(2,1)S(1)}, bf16[4,4,72,384]{3,2,1,0:T(8,128)(2,1)}, u32[]{:S(2)}) copy-start(bf16[4,4,72,384]{3,2,1,0:T(8,128)(2,1)} %copy-done.6) | copy-start | bytes 2654212

commit v3 on v2

v3 whole, which is shorter than its diff:
```python
import functools

import jax
import jax.numpy as jnp
from jax import lax
from jax.experimental import pallas as pl
from jax.experimental.pallas import tpu as pltpu
from jax.sharding import PartitionSpec as P

EXPERTS = 16
CAP = 72
BF = jnp.bfloat16
F32 = jnp.float32
CHUNKS = ((0, 8, False), (8, 12, False), (12, 16, True))
REDUCTIONS = ((0,), (1, 2))


SHORT = pl.CostEstimate(flops=1, bytes_accessed=1, transcendentals=0)


def iota(shape, dim):
    return lax.broadcasted_iota(jnp.int32, shape, dim)


def after(x, *others):
    return lax.optimization_barrier((x, *others))[0]


def hidden_kernel(n, sc_ref, tab_ref, hid_ref, hst_ref, wt_ref, rank_ref):
    experts, toks = tab_ref.shape[1], tab_ref.shape[2]
    earlier = (iota((toks, toks), 0) < iota((toks, toks), 1)).astype(BF)
    slots = iota((CAP, toks), 0).astype(F32)
    for k in range(n):
        s = lax.rem(sc_ref[0] + n - k, n)
        wt = tab_ref[k]
        named = (wt > 0).astype(F32).astype(BF)
        rank = jnp.dot(named, earlier, preferred_element_type=F32)
        for e in range(experts):
            w_row, r_row = wt[e : e + 1], rank[e : e + 1]
            place = jnp.where(slots == r_row, w_row, 0.0).astype(BF)
            moved = lax.dot_general(
                hid_ref[0, e, s], place, (((0,), (0,)), ((), ())), preferred_element_type=F32
            )
            hst_ref[e, :, k * toks : (k + 1) * toks] = moved.astype(BF)
            wt_ref[k, e] = w_row
            rank_ref[k, e] = r_row


def hidden_to_tokens(n, scalars, table, hid, f):
    experts, toks = table.shape[1], table.shape[2]
    row = jax.ShapeDtypeStruct((n, experts, 1, toks), F32)
    row_spec = pl.BlockSpec((n, experts, 1, toks), lambda i, sc: (0, 0, 0, 0))
    return pl.pallas_call(
        functools.partial(hidden_kernel, n),
        out_shape=(jax.ShapeDtypeStruct((experts, f, n * toks), BF), row, row),
        grid_spec=pltpu.PrefetchScalarGridSpec(
            num_scalar_prefetch=1,
            grid=(1,),
            in_specs=[
                pl.BlockSpec((n, experts, toks), lambda i, sc: (0, 0, 0)),
                pl.BlockSpec((1, experts, n, CAP, f), lambda i, sc: (0, 0, 0, 0, sc[1])),
            ],
            out_specs=(
                pl.BlockSpec((experts, f, n * toks), lambda i, sc: (0, 0, 0)),
                row_spec,
                row_spec,
            ),
        ),
        compiler_params=pltpu.CompilerParams(vmem_limit_bytes=16 << 20),
        cost_estimate=SHORT,
    )(scalars, table, hid)


def flat(pieces):
    arrays = [a for chunk in pieces for a, _, _ in chunk]
    specs = [
        pl.BlockSpec((rows, a.shape[1]), functools.partial(lambda g, i, sc: (g, 0), g))
        for chunk in pieces
        for a, rows, g in chunk
    ]
    return arrays, specs, [len(chunk) for chunk in pieces]


def gathered(refs, counts):
    chunks, at = [], 0
    for count in counts:
        refs_here = [refs[at + i][...] for i in range(count)]
        chunks.append(refs_here[0] if count == 1 else jnp.concatenate(refs_here, axis=0))
        at += count
    return chunks, at


def back_kernel(n, counts, group, rels, sc_ref, *refs):
    chunks, at = gathered(refs, counts)
    w_refs, refs = refs[at : at + len(rels)], refs[at + len(rels) :]
    hid_ref, wt_ref, rank_ref, gh_ref, sg_ref, w_all = refs
    toks, (f, d) = wt_ref.shape[3], w_all.shape[1:]
    for rel, ref in zip(rels, w_refs):
        rows = ref.shape[1]
        start = 0 if rel is None else pl.multiple_of((sc_ref[2] ^ rel) * rows, rows)
        for e in range(group):
            w_all[e, pl.ds(start, rows), :] = ref[e]
    tokens = chunks[0] if len(chunks) == 1 else jnp.concatenate(chunks, axis=1)
    z = lax.dot_general(
        tokens, w_all[...].reshape(group * f, d), (((1,), (1,)), ((), ())), preferred_element_type=F32
    )
    eye = iota((toks, toks), 0) == iota((toks, toks), 1)
    slots = iota((CAP, toks), 0).astype(F32)
    for e in range(group):
        for k in range(n):
            s = lax.rem(sc_ref[0] + n - k, n)
            w_row, r_row = wt_ref[k, e], rank_ref[k, e]
            here = (slots == r_row) & (w_row > 0)
            pick = jnp.where(here, 1.0, 0.0).astype(BF)
            weigh = jnp.where(here, w_row, 0.0).astype(BF)
            zk = z[k * toks : (k + 1) * toks, e * f : (e + 1) * f]
            gh_ref[e, s] = jnp.dot(weigh, zk.astype(BF), preferred_element_type=F32).astype(BF)
            hid = lax.dot_general(
                pick, hid_ref[0, e, s], (((0,), (0,)), ((), ())), preferred_element_type=F32
            )
            sg_col = jnp.sum(zk * hid, axis=1, keepdims=True)
            sg_ref[s, e] = jnp.sum(jnp.where(eye, sg_col, 0.0), axis=0, keepdims=True)


def backward(n, scalars, pieces, w_pieces, f, hid, wt, rank, width):
    experts, band, d = w_pieces[0][1].shape
    toks = wt.shape[3]
    rels = [rel for rel, _ in w_pieces]
    group = 2 if experts % 2 == 0 else 1
    arrays, specs, counts = flat(pieces)
    row_spec = pl.BlockSpec((n, group, 1, toks), lambda e, sc: (0, e, 0, 0))
    return pl.pallas_call(
        functools.partial(back_kernel, n, counts, group, rels),
        out_shape=(
            jax.ShapeDtypeStruct((experts, n, CAP, width), BF),
            jax.ShapeDtypeStruct((n, experts, 1, toks), F32),
        ),
        grid_spec=pltpu.PrefetchScalarGridSpec(
            num_scalar_prefetch=1,
            grid=(experts // group,),
            in_specs=specs
            + [pl.BlockSpec((group, band, d), lambda e, sc: (e, 0, 0))] * len(rels)
            + [
                pl.BlockSpec((1, group, n, CAP, f), lambda e, sc: (0, e, 0, 0, sc[1])),
                row_spec,
                row_spec,
            ],
            out_specs=(pl.BlockSpec((group, n, CAP, f), lambda e, sc: (e, 0, 0, sc[1])), row_spec),
            scratch_shapes=[pltpu.VMEM((group, f, d), BF)],
        ),
        compiler_params=pltpu.CompilerParams(vmem_limit_bytes=32 << 20),
        cost_estimate=SHORT,
    )(scalars, *arrays, *[w for _, w in w_pieces], hid, wt, rank)


def insert_kernel(sc_ref, new_ref, old_ref, out_ref):
    out_ref[...] = new_ref[...]


def insert(scalars, new, whole):
    experts, n, cap, f = new.shape
    return pl.pallas_call(
        insert_kernel,
        out_shape=jax.ShapeDtypeStruct(whole.shape, BF),
        grid_spec=pltpu.PrefetchScalarGridSpec(
            num_scalar_prefetch=1,
            grid=(1,),
            in_specs=[
                pl.BlockSpec((experts, n, cap, f), lambda i, sc: (0, 0, 0, 0)),
                pl.BlockSpec(memory_space=pl.ANY),
            ],
            out_specs=pl.BlockSpec((experts, n, cap, f), lambda i, sc: (0, 0, 0, 1 - sc[1])),
        ),
        input_output_aliases={2: 0},
        cost_estimate=SHORT,
    )(scalars, new, whole)


def part_kernel(bands, counts, sc_ref, *refs):
    own, at_own = gathered(refs, counts[0])
    nb, at_nb = gathered(refs[at_own:], counts[1])
    own_ref, nb_ref, send_ref, keep_ref = refs[at_own + at_nb :]
    tokens = jnp.concatenate(
        [jnp.concatenate(c, axis=1) if len(c) > 1 else c[0] for c in (own, nb)], axis=0
    )
    hidden = jnp.concatenate([own_ref[0], nb_ref[0]], axis=1)
    total = jnp.dot(hidden, tokens, preferred_element_type=F32)
    band, cols = send_ref.shape[2:]
    total = total.reshape(bands, band, cols).astype(BF)
    for a in range(bands):
        rel = sc_ref[0] ^ a
        for ref, bit in ((send_ref, 1), (keep_ref, 0)):

            @pl.when(rel % 2 == bit)
            def _():
                ref[rel // 2, 0] = total[a]


def partial_grad(bands, band, scalars, own, nb, pieces_own, pieces_nb):
    experts, f, k = own.shape
    arrays, specs, counts = flat(pieces_own)
    arrays_nb, specs_nb, counts_nb = flat(pieces_nb)
    cols = sum(chunk[0][0].shape[1] for chunk in pieces_own)
    out = jax.ShapeDtypeStruct((bands // 2, experts, band, cols), BF)
    out_spec = pl.BlockSpec((bands // 2, 1, band, cols), lambda e, sc: (0, e, 0, 0))
    hs_spec = pl.BlockSpec((1, f, k), lambda e, sc: (e, 0, 0))
    return pl.pallas_call(
        functools.partial(part_kernel, bands, (counts, counts_nb)),
        out_shape=(out, out),
        grid_spec=pltpu.PrefetchScalarGridSpec(
            num_scalar_prefetch=1,
            grid=(experts,),
            in_specs=specs + specs_nb + [hs_spec, hs_spec],
            out_specs=(out_spec, out_spec),
        ),
        compiler_params=pltpu.CompilerParams(vmem_limit_bytes=32 << 20),
        cost_estimate=SHORT,
    )(scalars, *arrays, *arrays_nb, own, nb)


def per_device(n_dp, n, grad_out, expert_ids, route_weights, hidden_cache, w_down):
    dp, z = lax.axis_index("dp"), lax.axis_index("expert")
    bands = n_dp // 2
    upper, j = dp // bands, dp % bands
    experts, band, d = w_down.shape
    toks = grad_out.shape[0]
    f = bands * band

    def swap(x, bit):
        return lax.ppermute(x, "dp", [(i, i ^ bit) for i in range(n_dp)])

    def spread(x):
        return [x] + [
            lax.ppermute(x, "expert", [(i, (i + k) % n) for i in range(n)]) for k in range(1, n)
        ]

    ids = expert_ids[None] == jnp.arange(EXPERTS, dtype=jnp.int32)[:, None, None]
    table = jnp.sum(jnp.where(ids, route_weights.astype(F32)[None], 0.0), axis=2).astype(BF)

    mine = [grad_out[:, a * d // 16 : b * d // 16] for a, b, _ in CHUNKS]

    def with_table(x, t):
        return jnp.concatenate([x, jnp.pad(t, ((0, 0), (0, x.shape[1] - toks)))], axis=0)

    def tables(blocks):
        rows = [lax.dynamic_slice(b, (toks + z * experts, 0), (experts, toks)) for b in blocks]
        return jnp.stack(rows).astype(F32)

    pieces = {0: w_down}
    bit = bands // 2
    while bit:
        for r in list(pieces):
            pieces[r ^ bit] = swap(pieces[r], bit)
        bit //= 2
    blocks0 = spread(with_table(mine[0], table))
    pair = swap(with_table(mine[2], table), bands)
    outgoing = lax.dynamic_slice_in_dim(hidden_cache, (1 - upper) * f, f, axis=4)
    hid_nb = swap(after(outgoing, pair), bands)
    sc_own = jnp.stack([z, upper, j]).astype(jnp.int32)
    sc_nb = jnp.stack([z, 0 * z, j]).astype(jnp.int32)
    sc_j = jnp.stack([j]).astype(jnp.int32)
    hs_own, wt_own, rank_own = hidden_to_tokens(n, sc_own, tables(blocks0), hidden_cache, f)

    nb0 = swap(jnp.concatenate([b[:toks] for b in blocks0], axis=0), bands)
    blocks1 = spread(after(with_table(mine[1], pair[toks:, :toks]), *blocks0))
    hs_nb, wt_nb, rank_nb = hidden_to_tokens(n, sc_nb, tables(blocks1), hid_nb, f)
    blocks2 = spread(after(jnp.concatenate([mine[2], pair[:toks]], axis=0), *blocks1))
    ready = jnp.concatenate([b[:toks] for b in blocks1], axis=0)
    nb1 = swap(after(ready, hs_own, hs_nb, pieces[bands // 2]), bands)

    own_pieces = [[(b, toks, 0) for b in blocks] for blocks in (blocks0, blocks1, blocks2)]
    nb_pieces = [[(nb0, n * toks, 0)], [(nb1, n * toks, 0)], [(b, toks, 1) for b in blocks2]]

    w_pieces = list(pieces.items())
    if band % 16:
        w = jnp.zeros((experts, f, d), BF)
        for r, piece in w_pieces:
            w = lax.dynamic_update_slice(w, piece, (0, (j ^ r) * band, 0))
        w_pieces = [(None, w)]

    grad_down, partials, at = jnp.zeros((experts, band, d), BF), [], 0
    for members in REDUCTIONS:
        send, keep = partial_grad(
            bands, band, after(sc_j, *partials), hs_own, hs_nb, [own_pieces[i] for i in members], [nb_pieces[i] for i in members]
        )
        if not partials:
            send = after(send, *blocks2[1 : (n + 2) // 2])
        terms = [keep, swap(send, 1)]
        bit = bands // 2
        while bit > 1:
            mid = bit // 2
            going = sum(t[mid:].astype(F32) for t in terms).astype(BF)
            partials.append(going)
            terms = [t[:mid] for t in terms] + [swap(going, bit)]
            bit //= 2
        total = sum(t[0].astype(F32) for t in terms).astype(BF)
        grad_down = lax.dynamic_update_slice(grad_down, total, (0, 0, at))
        at += total.shape[2]

    gh_nb, sg_nb = backward(
        n, after(sc_nb, send), nb_pieces, w_pieces, f, hid_nb, wt_nb, rank_nb, f
    )
    sg_in = swap(sg_nb.reshape(n, experts, toks), bands)
    gh_own, sg_own = backward(
        n, after(sc_own, sg_in), own_pieces, w_pieces, f, hidden_cache, wt_own, rank_own, 2 * f
    )
    grad_hidden = insert(sc_own, swap(after(gh_nb, sg_in), bands), gh_own)
    sg = sg_own.reshape(n, experts, toks) + sg_in
    by_expert = lax.all_to_all(sg, "expert", split_axis=0, concat_axis=0, tiled=True)
    by_expert = by_expert.reshape(EXPERTS, 1, toks)
    chosen = expert_ids.T[None] == jnp.arange(EXPERTS, dtype=jnp.int32)[:, None, None]
    grad_probs = jnp.sum(jnp.where(chosen, by_expert, 0.0), axis=0).T
    return grad_hidden[None], grad_down, grad_probs


def solution(mesh):
    tokens = P(("dp", "expert"), None)
    cache = P("dp", "expert", None, None, None)
    weights = P("expert", "dp", None)
    return jax.shard_map(
        functools.partial(per_device, mesh.shape["dp"], mesh.shape["expert"]),
        mesh=mesh,
        in_specs=(tokens, tokens, tokens, cache, weights),
        out_specs=(cache, weights, tokens),
        check_vma=False,
    )
```

time: 195 us -> 133 us (0.68)
  waiting for transfers between devices: 70.7 us -> 47.6 us
  starting transfers between devices: 47.5 us -> 33.6 us
  Pallas kernels: 43 us -> 29.5 us
  local copies, waits for them, and re-layouts: 14.6 us -> 4.89 us
  other arithmetic: 17.8 us -> 8.11 us
  blocking collectives: 0 us -> 8.58 us
    all_to_all x2 -> x0, starting transfers between devices: 26.1 us -> none  [the longest x1 17.7 us: per_device(): lax.all_to_all(sg, 'expert', split_axis=0, concat_axis=0, tiled=True)]
    ppermute x6 -> x9, waiting for transfers between devices: 31.7 us -> 17.1 us  [spread(): lax.ppermute(x, 'expert', [(i, (i + k) % n) for i in range(n)])]
    ppermute x6 -> x9, starting transfers between devices: 10.5 us -> 23.8 us  [spread(): lax.ppermute(x, 'expert', [(i, (i + k) % n) for i in range(n)])]
    all_to_all x2 -> x0, waiting for transfers between devices: 9.03 us -> none  [the longest x1 4.76 us: per_device(): lax.all_to_all(sg, 'expert', split_axis=0, concat_axis=0, tiled=True)]
    all_to_all x0 -> x1, blocking collectives: none -> 8.58 us  [per_device(): lax.all_to_all(sg, 'expert', split_axis=0, concat_axis=0, tiled=True)]
    pallas_call x4 -> x5, Pallas kernels: 33.2 us -> 26.1 us  [the longest x2 13.7 us: backward(): pl.pallas_call(functools.partial(back_kernel, n, counts, group, rels), ou...]
    pallas_call x2, Pallas kernels: 9.74 us -> 3.33 us  [hidden_to_tokens(): pl.pallas_call(functools.partial(hidden_kernel, n), out_shape=(jax.ShapeD...]
    dynamic_update_slice x4 -> x0, local copies, waits for them, and re-layouts: 6.4 us -> none  [per_device(): w = lax.dynamic_update_slice(w, piece, (0, (j ^ r) * band, 0))]
  transfers between devices with their start and end apart: 21 -> 22, of which waited for: 8 -> 10; matrix products, arithmetic and copies ran while one was open for 12% -> 5% of each run, Pallas kernels for 22% -> 22%
where the time goes in v3:
time: 133 us
  waiting for transfers between devices  47.6 us (36%)
  starting transfers between devices  33.6 us (25%)
  Pallas kernels  29.5 us (22%)
  blocking collectives  8.58 us (6%)
  other arithmetic  8.11 us (6%)
  local copies, waits for them, and re-layouts  4.89 us (4%)
    ppermute x13, waiting for transfers between devices, swap(): return lax.ppermute(x, 'dp', [(i, i ^ bit) for i in range(n_dp)])  30.4 us
    ppermute x9, starting transfers between devices, spread(): lax.ppermute(x, 'expert', [(i, (i + k) % n) for i in range(n)])  23.8 us
    ppermute x9, waiting for transfers between devices, spread(): lax.ppermute(x, 'expert', [(i, (i + k) % n) for i in range(n)])  17.1 us
    pallas_call x2, Pallas kernels, backward(): pl.pallas_call(functools.partial(back_kernel, n, counts, group, rels), ou...  13.7 us
    ppermute x13, starting transfers between devices, swap(): return lax.ppermute(x, 'dp', [(i, i ^ bit) for i in range(n_dp)])  9.78 us
    pallas_call x2, Pallas kernels, partial_grad(): pl.pallas_call(functools.partial(part_kernel, bands, (counts, counts_nb))...  9.52 us
    all_to_all x1, blocking collectives, per_device(): lax.all_to_all(sg, 'expert', split_axis=0, concat_axis=0, tiled=True)  8.58 us
    pallas_call x2, Pallas kernels, hidden_to_tokens(): pl.pallas_call(functools.partial(hidden_kernel, n), out_shape=(jax.ShapeD...  3.33 us
  transfers between devices with their start and end apart: 22, of which 10 were waited for; matrix products, arithmetic and copies ran while one was open for 5% of the time, Pallas kernels for 22%

profile of v3, /device:TPU:0, one launch (start us, length us, event | category | flops | bytes accessed | tf_op | source)
XLA Modules:
  0.0 133.1 jit_solution(16538346105623785993)
XLA Ops:
  0.6 1.1 slice.60
  1.7 0.7 convert_element_type.71
  2.4 0.7 select_reduce_fusion.1
  3.2 3.1 %collective-permute-start = (bf16[144,1024]{1,0:T(8,128)(2,1)S(1)}, bf16[144,1024]{1,0:T(8,128)(2,1)S(1)}, u32[]{:S(2)}, u32[]{:S(2)}) collective-permute-start(bf16[144,1024]{1,0:T(8,128)(2,1)S(1)} %fusion.3.refs_0_), channel_id=1, source_target_pairs={{0,1},{1,2},{2,3},{3,0},{4,5},{5,6},{6,7},{7,4},{8,9},{9,10},{10,1... | collective-permute-start | bytes 884744 | tf_op jit(solution)/shard_map/ppermute | solution.py:234
  6.2 2.6 %collective-permute-start.1 = (bf16[144,1024]{1,0:T(8,128)(2,1)S(1)}, bf16[144,1024]{1,0:T(8,128)(2,1)S(1)}, u32[]{:S(2)}, u32[]{:S(2)}) collective-permute-start(bf16[144,1024]{1,0:T(8,128)(2,1)S(1)} %fusion.3.refs_0_), channel_id=1, source_target_pairs={{0,2},{1,3},{2,0},{3,1},{4,6},{5,7},{6,4},{7,5},{8,10},{9,11},{10,... | collective-permute-start | bytes 884744 | tf_op jit(solution)/shard_map/ppermute | solution.py:234
  8.8 1.3 %collective-permute-start.2 = (bf16[144,1024]{1,0:T(8,128)(2,1)S(1)}, bf16[144,1024]{1,0:T(8,128)(2,1)S(1)}, u32[]{:S(2)}, u32[]{:S(2)}) collective-permute-start(bf16[144,1024]{1,0:T(8,128)(2,1)S(1)} %fusion.3.refs_0_), channel_id=1, source_target_pairs={{0,3},{1,0},{2,1},{3,2},{4,7},{5,4},{6,5},{7,6},{8,11},{9,8},{10,9... | collective-permute-start | bytes 884744 | tf_op jit(solution)/shard_map/ppermute | solution.py:234
  10.2 1.0 fusion.16
  11.2 0.7 fusion.7
  11.8 1.5 %collective-permute-start.4 = (bf16[144,512]{1,0:T(8,128)(2,1)}, bf16[144,512]{1,0:T(8,128)(2,1)}, u32[]{:S(2)}, u32[]{:S(2)}) collective-permute-start(bf16[144,512]{1,0:T(8,128)(2,1)} %fusion.7), channel_id=1, source_target_pairs={{0,16},{4,20},{8,24},{12,28},{16,0},{20,4},{24,8},{28,12},{1,17},{... | collective-permute-start | bytes 442376 | tf_op jit(solution)/shard_map/ppermute | solution.py:230
  13.6 3.7 %collective-permute-done.4 = bf16[144,512]{1,0:T(8,128)(2,1)} collective-permute-done((bf16[144,512]{1,0:T(8,128)(2,1)}, bf16[144,512]{1,0:T(8,128)(2,1)}, u32[]{:S(2)}, u32[]{:S(2)}) %collective-permute-start.4) | collective-permute-done | bytes 147488 | tf_op jit(solution)/shard_map/ppermute | solution.py:230
  17.3 1.5 %collective-permute-start.8 = (bf16[1,4,4,72,384]{4,3,2,1,0:T(8,128)(2,1)S(1)}, bf16[1,4,4,72,384]{4,3,2,1,0:T(8,128)(2,1)S(1)}, u32[]{:S(2)}, u32[]{:S(2)}) collective-permute-start(bf16[1,4,4,72,384]{4,3,2,1,0:T(8,128)(2,1)S(1)} %constant_dynamic-slice_fusion), channel_id=1, source_target_pairs={{0,16},{4,20},{8,24},{12,28},{16,0},{20,4},{24,8},{28,12},{1,17},{... | collective-permute-start | bytes 2654216 | tf_op jit(solution)/shard_map/ppermute | solution.py:230
  18.8 0.7 slice.83
  19.5 0.9 slice.84
  20.4 7.6 %collective-permute-done.1.refs_2_ = bf16[144,1024]{1,0:T(8,128)(2,1)S(1)} collective-permute-done((bf16[144,1024]{1,0:T(8,128)(2,1)S(1)}, bf16[144,1024]{1,0:T(8,128)(2,1)S(1)}, u32[]{:S(2)}, u32[]{:S(2)}) %collective-permute-start.1) | collective-permute-done | bytes 294944 | tf_op jit(solution)/shard_map/ppermute | solution.py:234
  28.1 6.8 %collective-permute-start.5 = (bf16[144,512]{1,0:T(8,128)(2,1)S(1)}, bf16[144,512]{1,0:T(8,128)(2,1)S(1)}, u32[]{:S(2)}, u32[]{:S(2)}) collective-permute-start(bf16[144,512]{1,0:T(8,128)(2,1)S(1)} %fusion.6.refs_0_.refs_4_), channel_id=1, source_target_pairs={{0,1},{1,2},{2,3},{3,0},{4,5},{5,6},{6,7},{7,4},{8,9},{9,10},{10,1... | collective-permute-start | bytes 442376 | tf_op jit(solution)/shard_map/ppermute | solution.py:234
  34.8 1.6 %collective-permute-start.6 = (bf16[144,512]{1,0:T(8,128)(2,1)S(1)}, bf16[144,512]{1,0:T(8,128)(2,1)S(1)}, u32[]{:S(2)}, u32[]{:S(2)}) collective-permute-start(bf16[144,512]{1,0:T(8,128)(2,1)S(1)} %fusion.6.refs_0_.refs_4_), channel_id=1, source_target_pairs={{0,2},{1,3},{2,0},{3,1},{4,6},{5,7},{6,4},{7,5},{8,10},{9,11},{10,... | collective-permute-start | bytes 442376 | tf_op jit(solution)/shard_map/ppermute | solution.py:234
  36.4 0.8 collective-permute-start.7
  37.4 1.6 %collective-permute-start.3 = (bf16[512,1024]{1,0:T(8,128)(2,1)S(1)}, bf16[512,1024]{1,0:T(8,128)(2,1)S(1)}, u32[]{:S(2)}, u32[]{:S(2)}) collective-permute-start(bf16[512,1024]{1,0:T(8,128)(2,1)S(1)} %pad_maximum_fusion.1), channel_id=1, source_target_pairs={{0,16},{4,20},{8,24},{12,28},{16,0},{20,4},{24,8},{28,12},{1,17},{... | collective-permute-start | bytes 3145736 | tf_op jit(solution)/shard_map/ppermute | solution.py:230
  39.0 1.7 %shard_map.76 = (bf16[4,384,512]{2,1,0:T(8,128)(2,1)S(1)}, f32[4,4,1,128]{3,2,1,0:T(1,128)S(1)}, f32[4,4,1,128]{3,2,1,0:T(1,128)S(1)}) custom-call(s32[3]{0:T(128)S(1)} %add_add_fusion.sc_ref, f32[4,4,128]{2,1,0:T(4,128)S(1)} %maximum_convert_fusion.tab_ref, bf16[1,4,4,72,768]{4,3,2,1,0:T(8,128)(2,1)S(1)} %copy-done), custom_call_target="tpu_custom_call" | custom-call | flops 1 | bytes 1 | tf_op jit(solution)/shard_map/pallas_call | solution.py:53
  40.8 1.6 %collective-permute-start.13 = (bf16[4,96,2048]{2,1,0:T(8,128)(2,1)S(1)}, bf16[4,96,2048]{2,1,0:T(8,128)(2,1)S(1)}, u32[]{:S(2)}, u32[]{:S(2)}) collective-permute-start(bf16[4,96,2048]{2,1,0:T(8,128)(2,1)S(1)} %copy-done.1), channel_id=1, source_target_pairs={{0,8},{4,12},{8,0},{12,4},{16,24},{20,28},{24,16},{28,20},{1,9},{5... | collective-permute-start | bytes 4718600 | tf_op jit(solution)/shard_map/ppermute | solution.py:230
  42.3 3.1 %collective-permute-done.6.refs_2_.refs_6_ = bf16[144,512]{1,0:T(8,128)(2,1)S(1)} collective-permute-done((bf16[144,512]{1,0:T(8,128)(2,1)S(1)}, bf16[144,512]{1,0:T(8,128)(2,1)S(1)}, u32[]{:S(2)}, u32[]{:S(2)}) %collective-permute-start.6) | collective-permute-done | bytes 147488 | tf_op jit(solution)/shard_map/ppermute | solution.py:234
  45.4 2.6 %collective-permute-start.10 = (bf16[256,512]{1,0:T(8,128)(2,1)S(1)}, bf16[256,512]{1,0:T(8,128)(2,1)S(1)}, u32[]{:S(2)}, u32[]{:S(2)}) collective-permute-start(bf16[256,512]{1,0:T(8,128)(2,1)S(1)} %pad_maximum_fusion.3.refs_4_.refs_9_.refs_2_.refs_8_), channel_id=1, source_target_pairs={{0,2},{1,3},{2,0},{3,1},{4,6},{5,7},{6,4},{7,5},{8,10},{9,11},{10,... | collective-permute-start | bytes 786440 | tf_op jit(solution)/shard_map/ppermute | solution.py:234
  48.0 3.3 %collective-permute-start.9 = (bf16[256,512]{1,0:T(8,128)(2,1)S(1)}, bf16[256,512]{1,0:T(8,128)(2,1)S(1)}, u32[]{:S(2)}, u32[]{:S(2)}) collective-permute-start(bf16[256,512]{1,0:T(8,128)(2,1)S(1)} %pad_maximum_fusion.3.refs_4_.refs_9_.refs_2_.refs_8_), channel_id=1, source_target_pairs={{0,1},{1,2},{2,3},{3,0},{4,5},{5,6},{6,7},{7,4},{8,9},{9,10},{10,1... | collective-permute-start | bytes 786440 | tf_op jit(solution)/shard_map/ppermute | solution.py:234
  51.4 1.7 %shard_map.77 = (bf16[4,384,512]{2,1,0:T(8,128)(2,1)S(1)}, f32[4,4,1,128]{3,2,1,0:T(1,128)S(1)}, f32[4,4,1,128]{3,2,1,0:T(1,128)S(1)}) custom-call(s32[3]{0:T(128)S(1)} %add_add_fusion.1.sc_ref, f32[4,4,128]{2,1,0:T(4,128)S(1)} %maximum_convert_fusion.1.tab_ref, bf16[1,4,4,72,384]{4,3,2,1,0:T(8,128)(2,1)S(1)} %collective-permute-done.8.hid_ref.refs_10_), custom_call_target="tpu_custom_call" | custom-call | flops 1 | bytes 1 | tf_op jit(solution)/shard_map/pallas_call | solution.py:53
  53.0 9.0 %collective-permute-done.3.refs_4_.refs_0_ = bf16[512,1024]{1,0:T(8,128)(2,1)S(1)} collective-permute-done((bf16[512,1024]{1,0:T(8,128)(2,1)S(1)}, bf16[512,1024]{1,0:T(8,128)(2,1)S(1)}, u32[]{:S(2)}, u32[]{:S(2)}) %collective-permute-start.3) | collective-permute-done | bytes 1048608 | tf_op jit(solution)/shard_map/ppermute | solution.py:230
  62.0 4.8 %shard_map.78 = (bf16[2,4,96,1024]{3,2,1,0:T(8,128)(2,1)S(1)}, bf16[2,4,96,1024]{3,2,1,0:T(8,128)(2,1)S(1)}) custom-call(s32[1]{0:T(128)} %bitcast.2.sc_ref, bf16[144,1024]{1,0:T(8,128)(2,1)S(1)} %fusion.3.refs_0_, bf16[144,1024]{1,0:T(8,128)(2,1)S(1)} %collective-permute-done.refs_1_, bf16[144,1024]{1,0:T(8,128)(2,1)S(1)} %collective-permute-done.1.refs_2_, ...), custom_call_target="tpu_custom_call" | custom-call | flops 1 | bytes 1 | tf_op jit(solution)/shard_map/pallas_call | solution.py:207
  67.0 9.4 %collective-permute-done.13.refs_7_.refs_13_ = bf16[4,96,2048]{2,1,0:T(8,128)(2,1)S(1)} collective-permute-done((bf16[4,96,2048]{2,1,0:T(8,128)(2,1)S(1)}, bf16[4,96,2048]{2,1,0:T(8,128)(2,1)S(1)}, u32[]{:S(2)}, u32[]{:S(2)}) %collective-permute-start.13) | collective-permute-done | bytes 1572896 | tf_op jit(solution)/shard_map/ppermute | solution.py:230
  76.3 0.5 collective-permute-start.14
  76.8 1.7 %collective-permute-start.12 = (bf16[256,512]{1,0:T(8,128)(2,1)S(1)}, bf16[256,512]{1,0:T(8,128)(2,1)S(1)}, u32[]{:S(2)}, u32[]{:S(2)}) collective-permute-start(bf16[256,512]{1,0:T(8,128)(2,1)S(1)} %pad_maximum_fusion.3.refs_4_.refs_9_.refs_2_.refs_8_), channel_id=1, source_target_pairs={{0,3},{1,0},{2,1},{3,2},{4,7},{5,4},{6,5},{7,6},{8,11},{9,8},{10,9... | collective-permute-start | bytes 786440 | tf_op jit(solution)/shard_map/ppermute | solution.py:234
  79.1 6.4 %collective-permute-done.12.refs_7_.refs_12_.refs_5_.refs_11_ = bf16[256,512]{1,0:T(8,128)(2,1)S(1)} collective-permute-done((bf16[256,512]{1,0:T(8,128)(2,1)S(1)}, bf16[256,512]{1,0:T(8,128)(2,1)S(1)}, u32[]{:S(2)}, u32[]{:S(2)}) %collective-permute-start.12) | collective-permute-done | bytes 262176 | tf_op jit(solution)/shard_map/ppermute | solution.py:234
  85.6 2.8 %collective-permute-done.14.refs_8_.refs_1_ = bf16[512,512]{1,0:T(8,128)(2,1)S(1)} collective-permute-done((bf16[512,512]{1,0:T(8,128)(2,1)S(1)}, bf16[512,512]{1,0:T(8,128)(2,1)S(1)}, u32[]{:S(2)}, u32[]{:S(2)}) %collective-permute-start.14) | collective-permute-done | bytes 524320 | tf_op jit(solution)/shard_map/ppermute | solution.py:230
  88.4 4.8 %shard_map.79 = (bf16[2,4,96,1024]{3,2,1,0:T(8,128)(2,1)S(1)}, bf16[2,4,96,1024]{3,2,1,0:T(8,128)(2,1)S(1)}) custom-call(s32[1]{0:T(128)} %bitcast.2.sc_ref, bf16[144,512]{1,0:T(8,128)(2,1)S(1)} %fusion.6.refs_0_.refs_4_, bf16[144,512]{1,0:T(8,128)(2,1)S(1)} %collective-permute-done.5.refs_1_.refs_5_, ...), custom_call_target="tpu_custom_call" | custom-call | flops 1 | bytes 1 | tf_op jit(solution)/shard_map/pallas_call | solution.py:207
  93.3 1.6 %collective-permute-start.19 = (bf16[1,4,96,1024]{3,2,1,0:T(8,128)(2,1)S(1)}, bf16[1,4,96,1024]{3,2,1,0:T(8,128)(2,1)S(1)}, u32[]{:S(2)}, u32[]{:S(2)}) collective-permute-start(bf16[1,4,96,1024]{3,2,1,0:T(8,128)(2,1)S(1)} %add_convert_fusion.3), channel_id=1, source_target_pairs={{0,8},{4,12},{8,0},{12,4},{16,24},{20,28},{24,16},{28,20},{1,9},{5... | collective-permute-start | bytes 2359304 | tf_op jit(solution)/shard_map/ppermute | solution.py:230
  94.8 6.5 %shard_map.80 = (bf16[4,4,72,384]{3,2,1,0:T(8,128)(2,1)S(1)}, f32[4,4,1,128]{3,2,1,0:T(1,128)S(1)}) custom-call(s32[3]{0:T(128)S(1)} %add_add_fusion.1.sc_ref, bf16[512,1024]{1,0:T(8,128)(2,1)S(1)} %collective-permute-done.3.refs_4_.refs_0_, bf16[512,512]{1,0:T(8,128)(2,1)S(1)} %collective-permute-done.14.refs_8_.refs_1_, ...), custom_call_target="tpu_custom_call" | custom-call | flops 1 | bytes 1 | tf_op jit(solution)/shard_map/pallas_call | solution.py:132
  101.3 0.3 collective-permute-start.17
  101.6 3.4 %collective-permute-done.17 = f32[4,4,128]{2,1,0:T(4,128)S(1)} collective-permute-done((f32[4,4,128]{2,1,0:T(4,128)S(1)}, f32[4,4,128]{2,1,0:T(4,128)S(1)}, u32[]{:S(2)}, u32[]{:S(2)}) %collective-permute-start.17) | collective-permute-done | bytes 8224 | tf_op jit(solution)/shard_map/ppermute | solution.py:230
  105.3 1.4 %add_convert_fusion.1 = bf16[1,4,96,1024]{3,2,1,0:T(8,128)(2,1)} fusion(bf16[2,4,96,1024]{3,2,1,0:T(8,128)(2,1)S(1)} %collective-permute-done.20, bf16[2,4,96,1024]{3,2,1,0:T(8,128)(2,1)S(1)} %get-tuple-element.47), kind=kLoop, calls=%fused_computation.2 | loop fusion | flops 1572864 | bytes 2359296 | tf_op jit(solution)/shard_map/convert_element_type | solution.py:292
  106.7 0.5 collective-permute-start.21
  107.2 7.2 %shard_map.81 = (bf16[4,4,72,768]{3,2,1,0:T(8,128)(2,1)}, f32[4,4,1,128]{3,2,1,0:T(1,128)S(1)}) custom-call(s32[3]{0:T(128)S(1)} %add_add_fusion.sc_ref, bf16[144,1024]{1,0:T(8,128)(2,1)S(1)} %fusion.3.refs_0_, bf16[144,1024]{1,0:T(8,128)(2,1)S(1)} %collective-permute-done.refs_1_, bf16[144,1024]{1,0:T(8,128)(2,1)S(1)} %collective-permute-done.1.refs_2_, ...), custom_call_target="tpu_custom_call" | custom-call | flops 1 | bytes 1 | tf_op jit(solution)/shard_map/pallas_call | solution.py:132
  114.5 8.6 %all_to_all.5 = f32[4,4,128]{2,1,0:T(4,128)S(1)} all-to-all(f32[4,4,128]{2,1,0:T(4,128)S(1)} %add.71), channel_id=1, replica_groups=mesh['dp'=8,'expert'=4] {'expert'}, dimensions={0} | all-to-all | bytes 16384 | tf_op jit(solution)/shard_map/all_to_all | solution.py:309
  123.0 0.6 select_reduce_fusion
  123.6 0.4 fusion
  124.1 1.8 %collective-permute-done.18.new_ref = bf16[4,4,72,384]{3,2,1,0:T(8,128)(2,1)S(1)} collective-permute-done((bf16[4,4,72,384]{3,2,1,0:T(8,128)(2,1)S(1)}, bf16[4,4,72,384]{3,2,1,0:T(8,128)(2,1)S(1)}, u32[]{:S(2)}, u32[]{:S(2)}) %collective-permute-start.18) | collective-permute-done | bytes 884768 | tf_op jit(solution)/shard_map/ppermute | solution.py:230
  125.9 0.9 copy-done.6
  126.8 2.9 %shard_map.82 = bf16[4,4,72,768]{3,2,1,0:T(8,128)(2,1)} custom-call(s32[3]{0:T(128)} %copy-done.4, bf16[4,4,72,384]{3,2,1,0:T(8,128)(2,1)} %copy-done.6, bf16[4,4,72,768]{3,2,1,0:T(8,128)(2,1)} %get-tuple-element.46.old_ref), custom_call_target="tpu_custom_call", output_to_operand_aliasing={{}: (2, {})} | custom-call | flops 1 | bytes 1 | tf_op jit(solution)/shard_map/pallas_call | solution.py:162
  129.8 0.4 collective-permute-done.21
  130.2 1.7 %fusion.1 = bf16[4,96,1024]{2,1,0:T(8,128)(2,1)S(1)} fusion(bf16[1,4,96,1024]{3,2,1,0:T(8,128)(2,1)} %collective-permute-done.21, bf16[2,4,96,1024]{3,2,1,0:T(8,128)(2,1)} %copy-done.5, bf16[2,4,96,1024]{3,2,1,0:T(8,128)(2,1)S(1)} %copy-done.3), kind=kLoop, calls=%fused_computation.7 | loop fusion | flops 2359296 | bytes 3145728 | tf_op jit(solution)/shard_map/convert_element_type | solution.py:296
  131.9 1.3 pad_maximum_fusion
  (59 shorter events, 1.7 us)
Async XLA Ops:
  0.6 12.9 %copy-start = (bf16[1,4,4,72,768]{4,3,2,1,0:T(8,128)(2,1)S(1)}, bf16[1,4,4,72,768]{4,3,2,1,0:T(8,128)(2,1)}, u32[]{:S(2)}) copy-start(bf16[1,4,4,72,768]{4,3,2,1,0:T(8,128)(2,1)} %refs_16_.1) | copy-start | bytes 5308420
  3.2 17.3 %collective-permute-start = (bf16[144,1024]{1,0:T(8,128)(2,1)S(1)}, bf16[144,1024]{1,0:T(8,128)(2,1)S(1)}, u32[]{:S(2)}, u32[]{:S(2)}) collective-permute-start(bf16[144,1024]{1,0:T(8,128)(2,1)S(1)} %fusion.3.refs_0_), channel_id=1, source_target_pairs={{0,1},{1,2},{2,3},{3,0},{4,5},{5,6},{6,7},{7,4},{8,9},{9,10},{10,1... | collective-permute-start | bytes 884744 | tf_op jit(solution)/shard_map/ppermute | solution.py:234
  6.2 21.8 %collective-permute-start.1 = (bf16[144,1024]{1,0:T(8,128)(2,1)S(1)}, bf16[144,1024]{1,0:T(8,128)(2,1)S(1)}, u32[]{:S(2)}, u32[]{:S(2)}) collective-permute-start(bf16[144,1024]{1,0:T(8,128)(2,1)S(1)} %fusion.3.refs_0_), channel_id=1, source_target_pairs={{0,2},{1,3},{2,0},{3,1},{4,6},{5,7},{6,4},{7,5},{8,10},{9,11},{10,... | collective-permute-start | bytes 884744 | tf_op jit(solution)/shard_map/ppermute | solution.py:234
  8.8 19.2 %collective-permute-start.2 = (bf16[144,1024]{1,0:T(8,128)(2,1)S(1)}, bf16[144,1024]{1,0:T(8,128)(2,1)S(1)}, u32[]{:S(2)}, u32[]{:S(2)}) collective-permute-start(bf16[144,1024]{1,0:T(8,128)(2,1)S(1)} %fusion.3.refs_0_), channel_id=1, source_target_pairs={{0,3},{1,0},{2,1},{3,2},{4,7},{5,4},{6,5},{7,6},{8,11},{9,8},{10,9... | collective-permute-start | bytes 884744 | tf_op jit(solution)/shard_map/ppermute | solution.py:234
  11.8 5.5 %collective-permute-start.4 = (bf16[144,512]{1,0:T(8,128)(2,1)}, bf16[144,512]{1,0:T(8,128)(2,1)}, u32[]{:S(2)}, u32[]{:S(2)}) collective-permute-start(bf16[144,512]{1,0:T(8,128)(2,1)} %fusion.7), channel_id=1, source_target_pairs={{0,16},{4,20},{8,24},{12,28},{16,0},{20,4},{24,8},{28,12},{1,17},{... | collective-permute-start | bytes 442376 | tf_op jit(solution)/shard_map/ppermute | solution.py:230
  13.5 93.7 %copy-start.4 = (s32[3]{0:T(128)}, s32[3]{0:T(128)S(1)}, u32[]{:S(2)}) copy-start(s32[3]{0:T(128)S(1)} %add_add_fusion.sc_ref) | copy-start | bytes 40
  17.3 34.0 %collective-permute-start.8 = (bf16[1,4,4,72,384]{4,3,2,1,0:T(8,128)(2,1)S(1)}, bf16[1,4,4,72,384]{4,3,2,1,0:T(8,128)(2,1)S(1)}, u32[]{:S(2)}, u32[]{:S(2)}) collective-permute-start(bf16[1,4,4,72,384]{4,3,2,1,0:T(8,128)(2,1)S(1)} %constant_dynamic-slice_fusion), channel_id=1, source_target_pairs={{0,16},{4,20},{8,24},{12,28},{16,0},{20,4},{24,8},{28,12},{1,17},{... | collective-permute-start | bytes 2654216 | tf_op jit(solution)/shard_map/ppermute | solution.py:230
  28.1 12.7 %collective-permute-start.5 = (bf16[144,512]{1,0:T(8,128)(2,1)S(1)}, bf16[144,512]{1,0:T(8,128)(2,1)S(1)}, u32[]{:S(2)}, u32[]{:S(2)}) collective-permute-start(bf16[144,512]{1,0:T(8,128)(2,1)S(1)} %fusion.6.refs_0_.refs_4_), channel_id=1, source_target_pairs={{0,1},{1,2},{2,3},{3,0},{4,5},{5,6},{6,7},{7,4},{8,9},{9,10},{10,1... | collective-permute-start | bytes 442376 | tf_op jit(solution)/shard_map/ppermute | solution.py:234
  34.8 10.6 %collective-permute-start.6 = (bf16[144,512]{1,0:T(8,128)(2,1)S(1)}, bf16[144,512]{1,0:T(8,128)(2,1)S(1)}, u32[]{:S(2)}, u32[]{:S(2)}) collective-permute-start(bf16[144,512]{1,0:T(8,128)(2,1)S(1)} %fusion.6.refs_0_.refs_4_), channel_id=1, source_target_pairs={{0,2},{1,3},{2,0},{3,1},{4,6},{5,7},{6,4},{7,5},{8,10},{9,11},{10,... | collective-permute-start | bytes 442376 | tf_op jit(solution)/shard_map/ppermute | solution.py:234
  36.4 9.0 %collective-permute-start.7 = (bf16[144,512]{1,0:T(8,128)(2,1)S(1)}, bf16[144,512]{1,0:T(8,128)(2,1)S(1)}, u32[]{:S(2)}, u32[]{:S(2)}) collective-permute-start(bf16[144,512]{1,0:T(8,128)(2,1)S(1)} %fusion.6.refs_0_.refs_4_), channel_id=1, source_target_pairs={{0,3},{1,0},{2,1},{3,2},{4,7},{5,4},{6,5},{7,6},{8,11},{9,8},{10,9... | collective-permute-start | bytes 442376 | tf_op jit(solution)/shard_map/ppermute | solution.py:234
  37.4 3.4 %copy-start.1 = (bf16[4,96,2048]{2,1,0:T(8,128)(2,1)S(1)}, bf16[4,96,2048]{2,1,0:T(8,128)(2,1)}, u32[]{:S(2)}) copy-start(bf16[4,96,2048]{2,1,0:T(8,128)(2,1)} %refs_12_.1) | copy-start | bytes 4718596
  37.4 24.6 %collective-permute-start.3 = (bf16[512,1024]{1,0:T(8,128)(2,1)S(1)}, bf16[512,1024]{1,0:T(8,128)(2,1)S(1)}, u32[]{:S(2)}, u32[]{:S(2)}) collective-permute-start(bf16[512,1024]{1,0:T(8,128)(2,1)S(1)} %pad_maximum_fusion.1), channel_id=1, source_target_pairs={{0,16},{4,20},{8,24},{12,28},{16,0},{20,4},{24,8},{28,12},{1,17},{... | collective-permute-start | bytes 3145736 | tf_op jit(solution)/shard_map/ppermute | solution.py:230
  40.8 35.5 %collective-permute-start.13 = (bf16[4,96,2048]{2,1,0:T(8,128)(2,1)S(1)}, bf16[4,96,2048]{2,1,0:T(8,128)(2,1)S(1)}, u32[]{:S(2)}, u32[]{:S(2)}) collective-permute-start(bf16[4,96,2048]{2,1,0:T(8,128)(2,1)S(1)} %copy-done.1), channel_id=1, source_target_pairs={{0,8},{4,12},{8,0},{12,4},{16,24},{20,28},{24,16},{28,20},{1,9},{5... | collective-permute-start | bytes 4718600 | tf_op jit(solution)/shard_map/ppermute | solution.py:230
  45.4 21.3 %collective-permute-start.10 = (bf16[256,512]{1,0:T(8,128)(2,1)S(1)}, bf16[256,512]{1,0:T(8,128)(2,1)S(1)}, u32[]{:S(2)}, u32[]{:S(2)}) collective-permute-start(bf16[256,512]{1,0:T(8,128)(2,1)S(1)} %pad_maximum_fusion.3.refs_4_.refs_9_.refs_2_.refs_8_), channel_id=1, source_target_pairs={{0,2},{1,3},{2,0},{3,1},{4,6},{5,7},{6,4},{7,5},{8,10},{9,11},{10,... | collective-permute-start | bytes 786440 | tf_op jit(solution)/shard_map/ppermute | solution.py:234
  48.0 18.7 %collective-permute-start.9 = (bf16[256,512]{1,0:T(8,128)(2,1)S(1)}, bf16[256,512]{1,0:T(8,128)(2,1)S(1)}, u32[]{:S(2)}, u32[]{:S(2)}) collective-permute-start(bf16[256,512]{1,0:T(8,128)(2,1)S(1)} %pad_maximum_fusion.3.refs_4_.refs_9_.refs_2_.refs_8_), channel_id=1, source_target_pairs={{0,1},{1,2},{2,3},{3,0},{4,5},{5,6},{6,7},{7,4},{8,9},{9,10},{10,1... | collective-permute-start | bytes 786440 | tf_op jit(solution)/shard_map/ppermute | solution.py:234
  66.8 12.1 %collective-permute-start.11 = (bf16[2,4,96,1024]{3,2,1,0:T(8,128)(2,1)S(1)}, bf16[2,4,96,1024]{3,2,1,0:T(8,128)(2,1)S(1)}, u32[]{:S(2)}, u32[]{:S(2)}) collective-permute-start(bf16[2,4,96,1024]{3,2,1,0:T(8,128)(2,1)S(1)} %get-tuple-element.33), channel_id=1, source_target_pairs={{0,4},{4,0},{8,12},{12,8},{16,20},{20,16},{24,28},{28,24},{1,5},{5... | collective-permute-start | bytes 4718600 | tf_op jit(solution)/shard_map/ppermute | solution.py:230
  76.3 12.1 %collective-permute-start.14 = (bf16[512,512]{1,0:T(8,128)(2,1)S(1)}, bf16[512,512]{1,0:T(8,128)(2,1)S(1)}, u32[]{:S(2)}, u32[]{:S(2)}) collective-permute-start(bf16[512,512]{1,0:T(8,128)(2,1)S(1)} %pad_maximum_fusion.2), channel_id=1, source_target_pairs={{0,16},{4,20},{8,24},{12,28},{16,0},{20,4},{24,8},{28,12},{1,17},{... | collective-permute-start | bytes 1572872 | tf_op jit(solution)/shard_map/ppermute | solution.py:230
  76.8 18.0 %collective-permute-start.15 = (bf16[4,96,2048]{2,1,0:T(8,128)(2,1)S(1)}, bf16[4,96,2048]{2,1,0:T(8,128)(2,1)S(1)}, u32[]{:S(2)}, u32[]{:S(2)}) collective-permute-start(bf16[4,96,2048]{2,1,0:T(8,128)(2,1)S(1)} %copy-done.1), channel_id=1, source_target_pairs={{0,4},{4,0},{8,12},{12,8},{16,20},{20,16},{24,28},{28,24},{1,5},{5... | collective-permute-start | bytes 4718600 | tf_op jit(solution)/shard_map/ppermute | solution.py:230
  76.8 8.7 %collective-permute-start.12 = (bf16[256,512]{1,0:T(8,128)(2,1)S(1)}, bf16[256,512]{1,0:T(8,128)(2,1)S(1)}, u32[]{:S(2)}, u32[]{:S(2)}) collective-permute-start(bf16[256,512]{1,0:T(8,128)(2,1)S(1)} %pad_maximum_fusion.3.refs_4_.refs_9_.refs_2_.refs_8_), channel_id=1, source_target_pairs={{0,3},{1,0},{2,1},{3,2},{4,7},{5,4},{6,5},{7,6},{8,11},{9,8},{10,9... | collective-permute-start | bytes 786440 | tf_op jit(solution)/shard_map/ppermute | solution.py:234
  78.6 16.2 %collective-permute-start.16 = (bf16[4,96,2048]{2,1,0:T(8,128)(2,1)S(1)}, bf16[4,96,2048]{2,1,0:T(8,128)(2,1)S(1)}, u32[]{:S(2)}, u32[]{:S(2)}) collective-permute-start(bf16[4,96,2048]{2,1,0:T(8,128)(2,1)S(1)} %collective-permute-done.13.refs_7_.refs_13_), channel_id=1, source_target_pairs={{0,4},{4,0},{8,12},{12,8},{16,20},{20,16},{24,28},{28,24},{1,5},{5... | collective-permute-start | bytes 4718600 | tf_op jit(solution)/shard_map/ppermute | solution.py:230
  93.2 12.1 %copy-start.2 = (bf16[2,4,96,1024]{3,2,1,0:T(8,128)(2,1)}, bf16[2,4,96,1024]{3,2,1,0:T(8,128)(2,1)S(1)}, u32[]{:S(2)}) copy-start(bf16[2,4,96,1024]{3,2,1,0:T(8,128)(2,1)S(1)} %get-tuple-element.47) | copy-start | bytes 4718596
  93.2 12.1 %collective-permute-start.20 = (bf16[2,4,96,1024]{3,2,1,0:T(8,128)(2,1)S(1)}, bf16[2,4,96,1024]{3,2,1,0:T(8,128)(2,1)S(1)}, u32[]{:S(2)}, u32[]{:S(2)}) collective-permute-start(bf16[2,4,96,1024]{3,2,1,0:T(8,128)(2,1)S(1)} %get-tuple-element.36), channel_id=1, source_target_pairs={{0,4},{4,0},{8,12},{12,8},{16,20},{20,16},{24,28},{28,24},{1,5},{5... | collective-permute-start | bytes 4718600 | tf_op jit(solution)/shard_map/ppermute | solution.py:230
  93.3 30.4 %collective-permute-start.19 = (bf16[1,4,96,1024]{3,2,1,0:T(8,128)(2,1)S(1)}, bf16[1,4,96,1024]{3,2,1,0:T(8,128)(2,1)S(1)}, u32[]{:S(2)}, u32[]{:S(2)}) collective-permute-start(bf16[1,4,96,1024]{3,2,1,0:T(8,128)(2,1)S(1)} %add_convert_fusion.3), channel_id=1, source_target_pairs={{0,8},{4,12},{8,0},{12,4},{16,24},{20,28},{24,16},{28,20},{1,9},{5... | collective-permute-start | bytes 2359304 | tf_op jit(solution)/shard_map/ppermute | solution.py:230
  101.3 3.7 %collective-permute-start.17 = (f32[4,4,128]{2,1,0:T(4,128)S(1)}, f32[4,4,128]{2,1,0:T(4,128)S(1)}, u32[]{:S(2)}, u32[]{:S(2)}) collective-permute-start(f32[4,4,128]{2,1,0:T(4,128)S(1)} %bitcast.30), channel_id=1, source_target_pairs={{0,16},{4,20},{8,24},{12,28},{16,0},{20,4},{24,8},{28,12},{1,17},{... | collective-permute-start | bytes 24584 | tf_op jit(solution)/shard_map/ppermute | solution.py:230
  105.0 20.9 %collective-permute-start.18 = (bf16[4,4,72,384]{3,2,1,0:T(8,128)(2,1)S(1)}, bf16[4,4,72,384]{3,2,1,0:T(8,128)(2,1)S(1)}, u32[]{:S(2)}, u32[]{:S(2)}) collective-permute-start(bf16[4,4,72,384]{3,2,1,0:T(8,128)(2,1)S(1)} %get-tuple-element.42), channel_id=1, source_target_pairs={{0,16},{4,20},{8,24},{12,28},{16,0},{20,4},{24,8},{28,12},{1,17},{... | collective-permute-start | bytes 2654216 | tf_op jit(solution)/shard_map/ppermute | solution.py:230
  105.3 9.1 %copy-start.5 = (bf16[2,4,96,1024]{3,2,1,0:T(8,128)(2,1)}, bf16[2,4,96,1024]{3,2,1,0:T(8,128)(2,1)S(1)}, u32[]{:S(2)}) copy-start(bf16[2,4,96,1024]{3,2,1,0:T(8,128)(2,1)S(1)} %collective-permute-done.20) | copy-start | bytes 4718596
  106.7 23.5 %collective-permute-start.21 = (bf16[1,4,96,1024]{3,2,1,0:T(8,128)(2,1)}, bf16[1,4,96,1024]{3,2,1,0:T(8,128)(2,1)}, u32[]{:S(2)}, u32[]{:S(2)}) collective-permute-start(bf16[1,4,96,1024]{3,2,1,0:T(8,128)(2,1)} %add_convert_fusion.1), channel_id=1, source_target_pairs={{0,8},{4,12},{8,0},{12,4},{16,24},{20,28},{24,16},{28,20},{1,9},{5... | collective-permute-start | bytes 2359304 | tf_op jit(solution)/shard_map/ppermute | solution.py:230
  107.2 15.8 %copy-start.7 = (s32[128,8]{0,1:T(8,128)S(1)}, s32[128,8]{0,1:T(8,128)}, u32[]{:S(2)}) copy-start(s32[128,8]{0,1:T(8,128)} %param.6) | copy-start | bytes 12292
  125.9 0.9 copy-start.6
  126.8 3.4 %copy-start.3 = (bf16[2,4,96,1024]{3,2,1,0:T(8,128)(2,1)S(1)}, bf16[2,4,96,1024]{3,2,1,0:T(8,128)(2,1)}, u32[]{:S(2)}) copy-start(bf16[2,4,96,1024]{3,2,1,0:T(8,128)(2,1)} %copy-done.2) | copy-start | bytes 4718596

commit v4 on v3

v4 whole, which is shorter than its diff:
```python
import functools

import jax
import jax.numpy as jnp
from jax import lax
from jax.experimental import pallas as pl
from jax.experimental.pallas import tpu as pltpu
from jax.sharding import PartitionSpec as P

EXPERTS = 16
CAP = 72
BF = jnp.bfloat16
F32 = jnp.float32
SHORT = pl.CostEstimate(flops=1, bytes_accessed=1, transcendentals=0)


def iota(shape, dim):
    return lax.broadcasted_iota(jnp.int32, shape, dim)


def after(x, *others):
    return lax.optimization_barrier((x, *others))[0]


def hidden_kernel(n, experts, sc_ref, tab_ref, hid_ref, hst_ref, wt_ref, rank_ref):
    toks = tab_ref.shape[1]
    earlier = (iota((toks, toks), 0) < iota((toks, toks), 1)).astype(BF)
    slots = iota((CAP, toks), 0).astype(F32)
    table = tab_ref[...].astype(F32)
    rank = jnp.dot((table > 0).astype(F32).astype(BF), earlier, preferred_element_type=F32)
    for k in range(n):
        s = lax.rem(sc_ref[0] + n - k, n)
        for e in range(experts):
            at = k * experts + e
            w_row, r_row = table[at : at + 1], rank[at : at + 1]
            place = jnp.where(slots == r_row, w_row, 0.0).astype(BF)
            moved = lax.dot_general(
                hid_ref[0, e, s], place, (((0,), (0,)), ((), ())), preferred_element_type=F32
            )
            hst_ref[e, :, k * toks : (k + 1) * toks] = moved.astype(BF)
            wt_ref[k, e] = w_row
            rank_ref[k, e] = r_row


def hidden_to_tokens(n, experts, toks, scalars, tokens, hid, f, whole):
    row = jax.ShapeDtypeStruct((n, experts, 1, toks), F32)
    row_spec = pl.BlockSpec((n, experts, 1, toks), lambda i, sc: (0, 0, 0, 0))
    lines = n * experts
    return pl.pallas_call(
        functools.partial(hidden_kernel, n, experts),
        out_shape=(jax.ShapeDtypeStruct((experts, f, n * toks), BF), row, row),
        grid_spec=pltpu.PrefetchScalarGridSpec(
            num_scalar_prefetch=1,
            grid=(1,),
            in_specs=[
                pl.BlockSpec((lines, toks), lambda i, sc: (n * toks // lines, 0)),
                pl.BlockSpec((1, experts, n, CAP, f), lambda i, sc: (0, 0, 0, 0, sc[1] if whole else 0)),
            ],
            out_specs=(
                pl.BlockSpec((experts, f, n * toks), lambda i, sc: (0, 0, 0)),
                row_spec,
                row_spec,
            ),
        ),
        compiler_params=pltpu.CompilerParams(vmem_limit_bytes=16 << 20),
        cost_estimate=SHORT,
    )(scalars, tokens, hid)


def below_kernel(n, experts, sc_ref, *refs):
    *blocks, out_ref = refs
    z = sc_ref[0]
    toks = blocks[0].shape[0] - EXPERTS
    line = iota((EXPERTS, toks), 0)

    def put(k, ref):
        out_ref[k * toks : (k + 1) * toks] = ref[:toks]
        table = ref[toks:, :toks].astype(F32)
        rows = [
            jnp.sum(jnp.where(line == z * experts + e, table, 0.0), axis=0, keepdims=True)
            for e in range(experts)
        ]
        return rows

    tables = [put(k, blocks[k]) for k in range(n)]
    if len(blocks) > n:
        passed = blocks[n]
        rows = [
            jnp.sum(jnp.where(line == z * experts + e, passed[toks:, :toks].astype(F32), 0.0), axis=0, keepdims=True)
            for e in range(experts)
        ]
        for k, place in ((1, 0), (n - 1, n - 1)):
            tables[k] = [jnp.where(z == place, new, old) for new, old in zip(rows, tables[k])]

            @pl.when(z == place)
            def _():
                out_ref[k * toks : (k + 1) * toks] = passed[:toks]

    rows = [row for table in tables for row in table]
    out_ref[n * toks :, :toks] = jnp.concatenate(rows, axis=0).astype(BF)


def below(n, experts, scalars, blocks):
    rows, cols = blocks[0].shape
    toks = rows - EXPERTS
    return pl.pallas_call(
        functools.partial(below_kernel, n, experts),
        out_shape=jax.ShapeDtypeStruct((n * (toks + experts), cols), BF),
        grid_spec=pltpu.PrefetchScalarGridSpec(
            num_scalar_prefetch=1,
            grid=(1,),
            in_specs=[pl.BlockSpec((rows, cols), lambda i, sc: (0, 0))] * len(blocks),
            out_specs=pl.BlockSpec((n * (toks + experts), cols), lambda i, sc: (0, 0)),
        ),
        compiler_params=pltpu.CompilerParams(vmem_limit_bytes=24 << 20),
        cost_estimate=SHORT,
    )(scalars, *blocks)


def flat(pieces):
    arrays = [a for chunk in pieces for a, _, _ in chunk]
    specs = [
        pl.BlockSpec(shape, functools.partial(lambda at, i, sc: at, at))
        for chunk in pieces
        for _, shape, at in chunk
    ]
    return arrays, specs, [len(chunk) for chunk in pieces]


def gathered(refs, counts, n, z, spans=None):
    chunks, at = [], 0
    for i, count in enumerate(counts):
        cols = slice(*spans[i]) if spans else slice(None)
        pieces = [refs[at + k][:, cols] for k in range(count)]
        if count > n:
            passed = pieces.pop()
            for k, place in ((1, 0), (n - 1, n - 1)):
                pieces[k] = jnp.where(z == place, passed, pieces[k])
        chunks.append(pieces[0] if len(pieces) == 1 else jnp.concatenate(pieces, axis=0))
        at += count
    return chunks, at


def back_kernel(n, counts, group, rels, sc_ref, *refs):
    chunks, at = gathered(refs, counts, n, sc_ref[0])
    w_refs, refs = refs[at : at + len(rels)], refs[at + len(rels) :]
    hid_ref, wt_ref, rank_ref, gh_ref, sg_ref, w_all = refs
    toks, (f, d) = wt_ref.shape[3], w_all.shape[1:]
    for rel, ref in zip(rels, w_refs):
        rows = ref.shape[2]
        start = 0 if rel is None else pl.multiple_of((sc_ref[2] ^ rel) * rows, rows)
        for e in range(group):
            w_all[e, pl.ds(start, rows), :] = ref[0, e]
    tokens = chunks[0] if len(chunks) == 1 else jnp.concatenate(chunks, axis=1)
    z = lax.dot_general(
        tokens, w_all[...].reshape(group * f, d), (((1,), (1,)), ((), ())), preferred_element_type=F32
    )
    eye = iota((toks, toks), 0) == iota((toks, toks), 1)
    slots = iota((CAP, toks), 0).astype(F32)
    for e in range(group):
        for k in range(n):
            s = lax.rem(sc_ref[0] + n - k, n)
            w_row, r_row = wt_ref[k, e], rank_ref[k, e]
            here = (slots == r_row) & (w_row > 0)
            pick = jnp.where(here, 1.0, 0.0).astype(BF)
            weigh = jnp.where(here, w_row, 0.0).astype(BF)
            zk = z[k * toks : (k + 1) * toks, e * f : (e + 1) * f]
            gh_ref[e, s] = jnp.dot(weigh, zk.astype(BF), preferred_element_type=F32).astype(BF)
            hid = lax.dot_general(
                pick, hid_ref[0, e, s], (((0,), (0,)), ((), ())), preferred_element_type=F32
            )
            sg_col = jnp.sum(zk * hid, axis=1, keepdims=True)
            sg_ref[s, e] = jnp.sum(jnp.where(eye, sg_col, 0.0), axis=0, keepdims=True)


def backward(n, scalars, pieces, w_pieces, f, hid, wt, rank, whole):
    _, experts, band, d = w_pieces[0][1].shape
    toks = wt.shape[3]
    rels = [rel for rel, _, _ in w_pieces]
    group = 2 if experts % 2 == 0 else 1
    arrays, specs, counts = flat(pieces)
    row_spec = pl.BlockSpec((n, group, 1, toks), lambda e, sc: (0, e, 0, 0))
    return pl.pallas_call(
        functools.partial(back_kernel, n, counts, group, rels),
        out_shape=(
            jax.ShapeDtypeStruct((experts, n, CAP, 2 * f if whole else f), BF),
            jax.ShapeDtypeStruct((n, experts, 1, toks), F32),
        ),
        grid_spec=pltpu.PrefetchScalarGridSpec(
            num_scalar_prefetch=1,
            grid=(experts // group,),
            in_specs=specs
            + [
                pl.BlockSpec((1, group, band, d), functools.partial(lambda i, e, sc: (i, e, 0, 0), i))
                for _, _, i in w_pieces
            ]
            + [
                pl.BlockSpec((1, group, n, CAP, f), lambda e, sc: (0, e, 0, 0, sc[1] if whole else 0)),
                row_spec,
                row_spec,
            ],
            out_specs=(pl.BlockSpec((group, n, CAP, f), lambda e, sc: (e, 0, 0, sc[1] if whole else 0)), row_spec),
            scratch_shapes=[pltpu.VMEM((group, f, d), BF)],
        ),
        compiler_params=pltpu.CompilerParams(vmem_limit_bytes=32 << 20),
        cost_estimate=SHORT,
    )(scalars, *arrays, *[w for _, w, _ in w_pieces], hid, wt, rank)


def insert_kernel(sc_ref, new_ref, old_ref, out_ref, sems):
    experts, n, _, f = new_ref.shape
    at = pl.multiple_of((1 - sc_ref[1]) * f, f)
    copies = [
        pltpu.make_async_copy(new_ref.at[e, s], out_ref.at[e, s, :, pl.ds(at, f)], sems.at[e, s])
        for e in range(experts)
        for s in range(n)
    ]
    for copy in copies:
        copy.start()
    for copy in copies:
        copy.wait()


def insert(scalars, new, whole):
    return pl.pallas_call(
        insert_kernel,
        out_shape=jax.ShapeDtypeStruct(whole.shape, BF),
        in_specs=[
            pl.BlockSpec(memory_space=pltpu.SMEM),
            pl.BlockSpec(memory_space=pltpu.VMEM),
            pl.BlockSpec(memory_space=pl.ANY),
        ],
        out_specs=pl.BlockSpec(memory_space=pl.ANY),
        scratch_shapes=[pltpu.SemaphoreType.DMA(new.shape[:2])],
        input_output_aliases={2: 0},
        cost_estimate=SHORT,
    )(scalars, new, whole)


def part_kernel(n, bands, counts, spans, sc_ref, *refs):
    own, at_own = gathered(refs, counts[0], n, sc_ref[0], spans)
    nb, at_nb = gathered(refs[at_own:], counts[1], n, sc_ref[0], spans)
    own_ref, nb_ref, *send_refs, keep_ref = refs[at_own + at_nb :]
    tokens = jnp.concatenate(
        [jnp.concatenate(c, axis=1) if len(c) > 1 else c[0] for c in (own, nb)], axis=0
    )
    hidden = jnp.concatenate([own_ref[0], nb_ref[0]], axis=1)
    total = jnp.dot(hidden, tokens, preferred_element_type=F32)
    quarter, _, band, cols = keep_ref.shape
    total = total.reshape(bands // 2, band, cols).astype(BF)
    for a in range(bands // 2):
        rel = (sc_ref[2] % (bands // 2)) ^ a
        at = rel // 2

        @pl.when(rel % 2 == 1)
        def _():
            done = 0
            for ref in send_refs:
                width = ref.shape[3]
                ref[at, 0] = total[a, :, done : done + width]
                done += width

        @pl.when(rel % 2 == 0)
        def _():
            keep_ref[at, 0] = total[a]


def partial_grad(n, bands, band, far, parts, scalars, own, nb, pieces_own, pieces_nb, spans):
    experts, f, k = own.shape
    arrays, specs, counts = flat(pieces_own)
    arrays_nb, specs_nb, counts_nb = flat(pieces_nb)
    cols = sum(stop - start for start, stop in spans)
    widths = (*parts, cols)
    half = bands // 2
    hs_spec = pl.BlockSpec((1, f // 2, k), lambda e, sc: (e, (sc[2] // half) ^ int(far), 0))
    return pl.pallas_call(
        functools.partial(part_kernel, n, bands, (counts, counts_nb), spans),
        out_shape=[jax.ShapeDtypeStruct((bands // 4, experts, band, width), BF) for width in widths],
        grid_spec=pltpu.PrefetchScalarGridSpec(
            num_scalar_prefetch=1,
            grid=(experts,),
            in_specs=specs + specs_nb + [hs_spec, hs_spec],
            out_specs=[pl.BlockSpec((bands // 4, 1, band, width), lambda e, sc: (0, e, 0, 0)) for width in widths],
        ),
        compiler_params=pltpu.CompilerParams(vmem_limit_bytes=32 << 20),
        cost_estimate=SHORT,
    )(scalars, *arrays, *arrays_nb, own, nb)


def joined_kernel(widths, *refs):
    out_ref, at = refs[-1], 0
    count = len(widths)
    for i, width in enumerate(widths):
        keep, parts = refs[i], refs[count + 2 * i : count + 2 * i + 2]
        there = jnp.concatenate([x[...] for x in parts], axis=3)
        out_ref[:, :, :, at : at + width] = (keep[...].astype(F32) + there.astype(F32)).astype(BF)
        at += width


def joined(keeps, parts):
    widths = [keep.shape[3] for keep in keeps]
    arrays = [*keeps, *[part for two in parts for part in two]]
    block = lambda x: pl.BlockSpec((x.shape[0], 1, *x.shape[2:]), lambda e: (0, e, 0, 0))
    out = jax.ShapeDtypeStruct((*keeps[0].shape[:3], sum(widths)), BF)
    return pl.pallas_call(
        functools.partial(joined_kernel, widths),
        out_shape=out,
        grid=(out.shape[1],),
        in_specs=[block(x) for x in arrays],
        out_specs=block(out),
        compiler_params=pltpu.CompilerParams(vmem_limit_bytes=16 << 20),
        cost_estimate=SHORT,
    )(*arrays)


def finish_kernel(keep_ref, left_ref, right_ref, there_ref, out_ref):
    near = jnp.concatenate([left_ref[0], right_ref[0]], axis=2).astype(F32)
    out_ref[...] = (keep_ref[0].astype(F32) + near + there_ref[0].astype(F32)).astype(BF)


def finish(keep, near, there):
    _, experts, band, d = keep.shape
    block = lambda x: pl.BlockSpec((1, 1, *x.shape[2:]), lambda e: (0, e, 0, 0))
    return pl.pallas_call(
        finish_kernel,
        out_shape=jax.ShapeDtypeStruct((experts, band, d), BF),
        grid=(experts,),
        in_specs=[block(x) for x in (keep, *near, there)],
        out_specs=pl.BlockSpec((1, band, d), lambda e: (e, 0, 0)),
        compiler_params=pltpu.CompilerParams(vmem_limit_bytes=16 << 20),
        cost_estimate=SHORT,
    )(keep, *near, there)


def per_device(n_dp, n, grad_out, expert_ids, route_weights, hidden_cache, w_down):
    dp, z = lax.axis_index("dp"), lax.axis_index("expert")
    bands = n_dp // 2
    upper, j = dp // bands, dp % bands
    experts, band, d = w_down.shape
    toks = grad_out.shape[0]
    f = bands * band

    def swap(x, bit):
        return lax.ppermute(x, "dp", [(i, i ^ bit) for i in range(n_dp)])

    def spread(x):
        if n != 4:
            return [x] + [
                lax.ppermute(x, "expert", [(i, (i + k) % n) for i in range(n)]) for k in range(1, n)
            ]
        two = lax.ppermute(x, "expert", [(i, (i + 2) % n) for i in range(n)])
        one = lax.ppermute(x, "expert", [(i, i + 1) for i in range(n - 1)])
        three = lax.ppermute(x, "expert", [(i + 1, i) for i in range(n - 1)])
        passed = lax.ppermute(two, "expert", [(2, 3), (1, 0)])
        return [x, one, two, three, passed]

    ids = expert_ids[None] == jnp.arange(EXPERTS, dtype=jnp.int32)[:, None, None]
    table = jnp.sum(jnp.where(ids, route_weights.astype(F32)[None], 0.0), axis=2).astype(BF)

    cut = 10 * d // 16
    table = jnp.pad(table, ((0, 0), (0, cut - toks)))
    blocks = spread(jnp.concatenate([grad_out[:, :cut], table], axis=0))
    w_core = swap(w_down[None], 1)
    outgoing = lax.dynamic_slice_in_dim(hidden_cache, (1 - upper) * f, f, axis=4).reshape(-1, f)
    lefts = [min(left, d - f) for left in range(cut, d, f)]
    outgoing = [outgoing] + [grad_out[:, left : left + f] for left in lefts]
    incoming = swap(after(jnp.concatenate(outgoing, axis=0), w_core), bands)
    count = hidden_cache.size // (2 * f)
    hid_nb = incoming[:count].reshape(1, experts, n, CAP, f)
    pair = [
        incoming[count + i * toks : count + (i + 1) * toks, cut + i * f - left :] for i, left in enumerate(lefts)
    ]
    w_pieces = [(0, w_down[None], 0), (1, w_core, 0)]
    bit = 2
    while bit < bands:
        far = swap(w_down[None] if bit == 2 else jnp.concatenate([a for _, a, _ in w_pieces[::2]]), bit)
        there = swap(far, 1)
        for i in range(far.shape[0]):
            w_pieces += [(w_pieces[2 * i][0] ^ bit, far, i), (w_pieces[2 * i][0] ^ bit ^ 1, there, i)]
        bit *= 2

    scalars = jnp.stack([z, upper, j]).astype(jnp.int32)
    mine = below(n, experts, scalars, blocks)
    hs_own, wt_own, rank_own = hidden_to_tokens(n, experts, toks, scalars, mine, hidden_cache, f, True)
    rest = jnp.concatenate([grad_out[:, cut:], jnp.concatenate(pair, axis=1)], axis=0)
    rests = spread(after(rest, *blocks))
    nb_a = swap(after(mine, incoming), bands)
    hs_nb, wt_nb, rank_nb = hidden_to_tokens(n, experts, toks, scalars, nb_a, hid_nb, f, False)

    own_pieces = [[(mine, (n * toks, cut), (0, 0))], [(b, (toks, d - cut), (0, 0)) for b in rests]]
    nb_pieces = [[(nb_a, (n * toks, cut), (0, 0))], [(b, (toks, d - cut), (1, 0)) for b in rests]]

    if band % 16:
        w = jnp.zeros((experts, f, d), BF)
        for r, array, i in w_pieces:
            w = lax.dynamic_update_slice(w, array[i], (0, (j ^ r) * band, 0))
        w_pieces = [(None, w[None], 0)]

    half = d // 2
    groups = (
        (slice(0, 1), ((0, half),)),
        (slice(0, 2), ((half, cut), (0, d - cut))),
    )
    order, keeps, parts = scalars, [], []
    for chunks, spans in groups:
        tokens = own_pieces[chunks], nb_pieces[chunks], spans
        *far, keep_far = partial_grad(
            n, bands, band, True, (half // 2, half // 2), order, hs_own, hs_nb, *tokens
        )
        order = after(scalars, far[0])
        keeps.append(keep_far)
        parts.append([swap(x, 1) for x in far])
    going = joined(keeps, parts)
    there = swap(going, bands // 2)
    gh_nb, sg_nb = backward(
        n, after(scalars, going), nb_pieces, w_pieces, f, hid_nb, wt_nb, rank_nb, False
    )
    sg_in = swap(sg_nb.reshape(n, experts, toks), bands)
    gh_own, sg_own = backward(
        n, after(scalars, sg_in), own_pieces, w_pieces, f, hidden_cache, wt_own, rank_own, True
    )
    spans = ((0, cut), (0, d - cut))
    *near, keep = partial_grad(
        n, bands, band, False, (half, half), after(scalars, sg_own), hs_own, hs_nb, own_pieces, nb_pieces, spans
    )
    near = [swap(x, 1) for x in near]
    if bands == 4:
        grad_down = finish(keep, near, there)
    else:
        total = keep.astype(F32) + jnp.concatenate(near, axis=3).astype(F32) + there.astype(F32)
        mid = bands // 8
        while mid:
            total, mid = total[:mid] + swap(total[mid:].astype(BF), 4 * mid).astype(F32), mid // 2
        grad_down = total[0].astype(BF)

    grad_hidden = insert(scalars, swap(after(gh_nb, sg_in), bands), gh_own)
    sg = sg_own.reshape(n, experts, toks) + sg_in
    by_expert = lax.all_to_all(sg, "expert", split_axis=0, concat_axis=0, tiled=True)
    by_expert = by_expert.reshape(EXPERTS, 1, toks)
    chosen = expert_ids.T[None] == jnp.arange(EXPERTS, dtype=jnp.int32)[:, None, None]
    grad_probs = jnp.sum(jnp.where(chosen, by_expert, 0.0), axis=0).T
    return grad_hidden[None], grad_down, grad_probs


def solution(mesh):
    tokens = P(("dp", "expert"), None)
    cache = P("dp", "expert", None, None, None)
    weights = P("expert", "dp", None)
    return jax.shard_map(
        functools.partial(per_device, mesh.shape["dp"], mesh.shape["expert"]),
        mesh=mesh,
        in_specs=(tokens, tokens, tokens, cache, weights),
        out_specs=(cache, weights, tokens),
        check_vma=False,
    )
```

time: 133 us -> 131 us (0.985)
  Pallas kernels: 29.5 us -> 40.2 us
  starting transfers between devices: 33.6 us -> 26.3 us
  other arithmetic: 8.11 us -> 2.55 us
    ppermute x9 -> x8, waiting for transfers between devices: 17.1 us -> 36.1 us  [the longest x2 23.6 us: spread(): two = lax.ppermute(x, 'expert', [(i, (i + 2) % n) for i in range(n)])]
    ppermute x13 -> x14, waiting for transfers between devices: 30.4 us -> 12.1 us  [swap(): return lax.ppermute(x, 'dp', [(i, i ^ bit) for i in range(n_dp)])]
    pallas_call x4 -> x8, Pallas kernels: 12.9 us -> 22.2 us  [the longest x3 12 us: partial_grad(): pl.pallas_call(functools.partial(part_kernel, n, bands, (counts, counts_n...]
    ppermute x9 -> x8, starting transfers between devices: 23.8 us -> 15.6 us  [the longest x2 7.7 us: spread(): one = lax.ppermute(x, 'expert', [(i, i + 1) for i in range(n - 1)])]
    convert_element_type x6 -> x0, other arithmetic: 3.84 us -> none  [the longest x2 2.1 us: per_device(): total = sum((t[0].astype(F32) for t in terms)).astype(BF)]
    pallas_call x2, Pallas kernels: 13.7 us -> 15.7 us  [backward(): pl.pallas_call(functools.partial(back_kernel, n, counts, group, rels), ou...]
    slice x11 -> x7, local copies, waits for them, and re-layouts: 3.76 us -> 2.25 us  [the longest x1 1.26 us: per_device(): hid_nb = incoming[:count].reshape(1, experts, n, CAP, f)]
    ppermute x13 -> x14, starting transfers between devices: 9.78 us -> 10.8 us  [swap(): return lax.ppermute(x, 'dp', [(i, i ^ bit) for i in range(n_dp)])]
  transfers between devices with their start and end apart: 22 -> 22, of which waited for: 10 -> 10; matrix products, arithmetic and copies ran while one was open for 5% -> 5% of each run, Pallas kernels for 22% -> 28%
where the time goes in v4:
time: 131 us
  waiting for transfers between devices  48.2 us (37%)
  Pallas kernels  40.2 us (31%)
  starting transfers between devices  26.3 us (20%)
  blocking collectives  7.92 us (6%)
  local copies, waits for them, and re-layouts  4.51 us (3%)
  other arithmetic  2.55 us (2%)
    ppermute x2, waiting for transfers between devices, spread(): two = lax.ppermute(x, 'expert', [(i, (i + 2) % n) for i in range(n)])  23.6 us
    pallas_call x2, Pallas kernels, backward(): pl.pallas_call(functools.partial(back_kernel, n, counts, group, rels), ou...  15.7 us
    ppermute x14, waiting for transfers between devices, swap(): return lax.ppermute(x, 'dp', [(i, i ^ bit) for i in range(n_dp)])  12.1 us
    pallas_call x3, Pallas kernels, partial_grad(): pl.pallas_call(functools.partial(part_kernel, n, bands, (counts, counts_n...  12 us
    ppermute x14, starting transfers between devices, swap(): return lax.ppermute(x, 'dp', [(i, i ^ bit) for i in range(n_dp)])  10.8 us
    all_to_all x1, blocking collectives, per_device(): lax.all_to_all(sg, 'expert', split_axis=0, concat_axis=0, tiled=True)  7.92 us
    ppermute x2, starting transfers between devices, spread(): one = lax.ppermute(x, 'expert', [(i, i + 1) for i in range(n - 1)])  7.7 us
    ppermute x2, waiting for transfers between devices, spread(): passed = lax.ppermute(two, 'expert', [(2, 3), (1, 0)])  6.94 us
  transfers between devices with their start and end apart: 22, of which 10 were waited for; matrix products, arithmetic and copies ran while one was open for 5% of the time, Pallas kernels for 28%

profile of v4, /device:TPU:0, one launch (start us, length us, event | category | flops | bytes accessed | tf_op | source)
XLA Modules:
  0.0 130.6 jit_solution(3043813642469649252)
XLA Ops:
  0.6 0.5 collective-permute-start.4
  1.1 0.7 convert_element_type.8
  1.8 1.3 %constant_dynamic-slice_fusion = bf16[1,4,4,72,384]{4,3,2,1,0:T(8,128)(2,1)S(1)} fusion(bf16[1,4,4,72,768]{4,3,2,1,0:T(8,128)(2,1)} %refs_10_.1, s32[]{:T(128)S(6)} %select_n.25), kind=kLoop, calls=%fused_computation.10 | loop fusion | bytes 1769476 | tf_op jit(solution)/shard_map/dynamic_slice | solution.py:364
  3.2 1.1 pad_maximum_fusion
  4.3 0.1 collective-permute-done.4.refs_7_
  4.4 2.9 %collective-permute-start.5 = (bf16[1408,384]{1,0:T(8,128)(2,1)}, bf16[1408,384]{1,0:T(8,128)(2,1)}, u32[]{:S(2)}, u32[]{:S(2)}) collective-permute-start(bf16[1408,384]{1,0:T(8,128)(2,1)} %pad_maximum_fusion), channel_id=1, source_target_pairs={{0,16},{4,20},{8,24},{12,28},{16,0},{20,4},{24,8},{28,12},{1,17},{... | collective-permute-start | bytes 3244040 | tf_op jit(solution)/shard_map/ppermute | solution.py:344
  7.4 2.7 %collective-permute-start.1 = (bf16[144,1280]{1,0:T(8,128)(2,1)S(1)}, bf16[144,1280]{1,0:T(8,128)(2,1)}, u32[]{:S(2)}, u32[]{:S(2)}) collective-permute-start(bf16[144,1280]{1,0:T(8,128)(2,1)S(1)} %fusion.1.refs_0_), channel_id=1, source_target_pairs={{0,2},{1,3},{2,0},{3,1},{4,6},{5,7},{6,4},{7,5},{8,10},{9,11},{10,... | collective-permute-start | bytes 1105928 | tf_op jit(solution)/shard_map/ppermute | solution.py:351
  10.0 1.5 %collective-permute-start.15 = (bf16[1,4,96,2048]{3,2,1,0:T(8,128)(2,1)S(1)}, bf16[1,4,96,2048]{3,2,1,0:T(8,128)(2,1)}, u32[]{:S(2)}, u32[]{:S(2)}) collective-permute-start(bf16[1,4,96,2048]{3,2,1,0:T(8,128)(2,1)S(1)} %bitcast.15), channel_id=1, source_target_pairs={{0,8},{4,12},{8,0},{12,4},{16,24},{20,28},{24,16},{28,20},{1,9},{5... | collective-permute-start | bytes 4718600 | tf_op jit(solution)/shard_map/ppermute | solution.py:344
  11.5 4.2 %collective-permute-start = (bf16[144,1280]{1,0:T(8,128)(2,1)S(1)}, bf16[144,1280]{1,0:T(8,128)(2,1)}, u32[]{:S(2)}, u32[]{:S(2)}) collective-permute-start(bf16[144,1280]{1,0:T(8,128)(2,1)S(1)} %fusion.1.refs_0_), channel_id=1, source_target_pairs={{0,1},{1,2},{2,3},{4,5},{5,6},{6,7},{8,9},{9,10},{10,11},{12,13},{... | collective-permute-start | bytes 1105928 | tf_op jit(solution)/shard_map/ppermute | solution.py:352
  15.7 1.3 collective-permute-start.2
  17.0 10.8 %collective-permute-done.1.refs_2_ = bf16[144,1280]{1,0:T(8,128)(2,1)} collective-permute-done((bf16[144,1280]{1,0:T(8,128)(2,1)S(1)}, bf16[144,1280]{1,0:T(8,128)(2,1)}, u32[]{:S(2)}, u32[]{:S(2)}) %collective-permute-start.1) | collective-permute-done | bytes 368672 | tf_op jit(solution)/shard_map/ppermute | solution.py:351
  27.8 1.3 collective-permute-start.3
  29.1 0.1 pad_add_fusion.sc_ref
  29.2 5.5 %collective-permute-done.2.refs_3_ = bf16[144,1280]{1,0:T(8,128)(2,1)} collective-permute-done((bf16[144,1280]{1,0:T(8,128)(2,1)S(1)}, bf16[144,1280]{1,0:T(8,128)(2,1)}, u32[]{:S(2)}, u32[]{:S(2)}) %collective-permute-start.2) | collective-permute-done | bytes 368672 | tf_op jit(solution)/shard_map/ppermute | solution.py:353
  34.7 6.9 %collective-permute-done.3.refs_4_ = bf16[144,1280]{1,0:T(8,128)(2,1)} collective-permute-done((bf16[144,1280]{1,0:T(8,128)(2,1)}, bf16[144,1280]{1,0:T(8,128)(2,1)}, u32[]{:S(2)}, u32[]{:S(2)}) %collective-permute-start.3) | collective-permute-done | bytes 368672 | tf_op jit(solution)/shard_map/ppermute | solution.py:354
  41.7 2.0 %shard_map.76.tab_ref.refs_0_ = bf16[528,1280]{1,0:T(8,128)(2,1)S(1)} custom-call(s32[3]{0:T(128)S(1)} %pad_add_fusion.sc_ref, bf16[144,1280]{1,0:T(8,128)(2,1)S(1)} %fusion.1.refs_0_, bf16[144,1280]{1,0:T(8,128)(2,1)} %collective-permute-done.refs_1_, bf16[144,1280]{1,0:T(8,128)(2,1)} %collective-permute-done.1.refs_2_, ...), custom_call_target="tpu_custom_call" | custom-call | flops 1 | bytes 1 | tf_op jit(solution)/shard_map/pallas_call | solution.py:106
  43.7 0.5 collective-permute-start.6
  44.2 1.0 fusion.2
  45.3 0.7 collective-permute-done.15.refs_8_
  46.0 3.5 %collective-permute-start.7 = (bf16[256,768]{1,0:T(8,128)(2,1)S(1)}, bf16[256,768]{1,0:T(8,128)(2,1)S(1)}, u32[]{:S(2)}, u32[]{:S(2)}) collective-permute-start(bf16[256,768]{1,0:T(8,128)(2,1)S(1)} %maximum_maximum_fusion.refs_1_.refs_7_), channel_id=1, source_target_pairs={{0,1},{1,2},{2,3},{4,5},{5,6},{6,7},{8,9},{9,10},{10,11},{12,13},{... | collective-permute-start | bytes 1179656 | tf_op jit(solution)/shard_map/ppermute | solution.py:352
  49.5 1.3 collective-permute-start.9
  50.8 12.8 %collective-permute-done.8.refs_3_.refs_9_ = bf16[256,768]{1,0:T(8,128)(2,1)S(1)} collective-permute-done((bf16[256,768]{1,0:T(8,128)(2,1)S(1)}, bf16[256,768]{1,0:T(8,128)(2,1)S(1)}, u32[]{:S(2)}, u32[]{:S(2)}) %collective-permute-start.8) | collective-permute-done | bytes 393248 | tf_op jit(solution)/shard_map/ppermute | solution.py:351
  63.6 1.3 collective-permute-start.10
  64.9 1.3 %shard_map.77 = (bf16[4,384,512]{2,1,0:T(8,128)(2,1)S(1)}, f32[4,4,1,128]{3,2,1,0:T(1,128)S(1)}, f32[4,4,1,128]{3,2,1,0:T(1,128)S(1)}) custom-call(s32[3]{0:T(128)S(1)} %pad_add_fusion.sc_ref, bf16[528,1280]{1,0:T(8,128)(2,1)S(1)} %shard_map.76.tab_ref.refs_0_, bf16[1,4,4,72,768]{4,3,2,1,0:T(8,128)(2,1)S(1)} %copy-done), custom_call_target="tpu_custom_call" | custom-call | flops 1 | bytes 1 | tf_op jit(solution)/shard_map/pallas_call | solution.py:49
  66.2 1.3 slice.28
  67.5 7.0 %collective-permute-done.6.tab_ref.refs_1_.refs_6_.refs_0_ = bf16[528,1280]{1,0:T(8,128)(2,1)S(1)} collective-permute-done((bf16[528,1280]{1,0:T(8,128)(2,1)S(1)}, bf16[528,1280]{1,0:T(8,128)(2,1)S(1)}, u32[]{:S(2)}, u32[]{:S(2)}) %collective-permute-start.6) | collective-permute-done | bytes 1351712 | tf_op jit(solution)/shard_map/ppermute | solution.py:344
  74.4 1.3 shard_map.78
  75.7 3.1 %shard_map.79 = (bf16[1,4,96,512]{3,2,1,0:T(8,128)(2,1)S(1)}, bf16[1,4,96,512]{3,2,1,0:T(8,128)(2,1)S(1)}, bf16[1,4,96,1024]{3,2,1,0:T(8,128)(2,1)S(1)}) custom-call(s32[3]{0:T(128)S(1)} %pad_add_fusion.sc_ref, bf16[528,1280]{1,0:T(8,128)(2,1)S(1)} %shard_map.76.tab_ref.refs_0_, bf16[528,1280]{1,0:T(8,128)(2,1)S(1)} %collective-permute-done.6.tab_ref.refs_1_.refs_6_.refs_0_, ...), custom_call_target="tpu_custom_call" | custom-call | flops 1 | bytes 1 | tf_op jit(solution)/shard_map/pallas_call | solution.py:276
  78.9 0.5 collective-permute-start.12
  79.4 3.2 %shard_map.80 = (bf16[1,4,96,512]{3,2,1,0:T(8,128)(2,1)S(1)}, bf16[1,4,96,512]{3,2,1,0:T(8,128)(2,1)S(1)}, bf16[1,4,96,1024]{3,2,1,0:T(8,128)(2,1)S(1)}) custom-call(s32[3]{0:T(128)S(1)} %pad_add_fusion.sc_ref, bf16[528,1280]{1,0:T(8,128)(2,1)S(1)} %shard_map.76.tab_ref.refs_0_, bf16[256,768]{1,0:T(8,128)(2,1)S(1)} %maximum_maximum_fusion.refs_1_.refs_7_, ...), custom_call_target="tpu_custom_call" | custom-call | flops 1 | bytes 1 | tf_op jit(solution)/shard_map/pallas_call | solution.py:276
  82.6 0.2 collective-permute-start.13
  82.8 0.4 collective-permute-start.14
  83.2 1.2 collective-permute-done.13.refs_4_
  84.4 0.6 collective-permute-done.14.refs_5_
  85.0 1.8 %shard_map.81 = bf16[1,4,96,2048]{3,2,1,0:T(8,128)(2,1)} custom-call(bf16[1,4,96,1024]{3,2,1,0:T(8,128)(2,1)S(1)} %get-tuple-element.34.refs_0_, bf16[1,4,96,1024]{3,2,1,0:T(8,128)(2,1)S(1)} %get-tuple-element.38.refs_1_, bf16[1,4,96,512]{3,2,1,0:T(8,128)(2,1)S(1)} %collective-permute-done.11.refs_2_, ...), custom_call_target="tpu_custom_call" | custom-call | flops 1 | bytes 1 | tf_op jit(solution)/shard_map/pallas_call | solution.py:305
  86.8 1.4 %collective-permute-start.21 = (bf16[1,4,96,2048]{3,2,1,0:T(8,128)(2,1)}, bf16[1,4,96,2048]{3,2,1,0:T(8,128)(2,1)}, u32[]{:S(2)}, u32[]{:S(2)}) collective-permute-start(bf16[1,4,96,2048]{3,2,1,0:T(8,128)(2,1)} %shard_map.81), channel_id=1, source_target_pairs={{0,8},{4,12},{8,0},{12,4},{16,24},{20,28},{24,16},{28,20},{1,9},{5... | collective-permute-start | bytes 4718600 | tf_op jit(solution)/shard_map/ppermute | solution.py:344
  88.2 7.6 %shard_map.82 = (bf16[4,4,72,384]{3,2,1,0:T(8,128)(2,1)S(1)}, f32[4,4,1,128]{3,2,1,0:T(1,128)S(1)}) custom-call(s32[3]{0:T(128)S(1)} %pad_add_fusion.sc_ref, bf16[528,1280]{1,0:T(8,128)(2,1)S(1)} %collective-permute-done.6.tab_ref.refs_1_.refs_6_.refs_0_, bf16[256,768]{1,0:T(8,128)(2,1)S(1)} %maximum_maximum_fusion.refs_1_.refs_7_, ...), custom_call_target="tpu_custom_call" | custom-call | flops 1 | bytes 1 | tf_op jit(solution)/shard_map/pallas_call | solution.py:183
  95.8 1.2 collective-permute-start.17
  97.0 2.5 %collective-permute-done.17 = f32[4,4,128]{2,1,0:T(4,128)S(1)} collective-permute-done((f32[4,4,128]{2,1,0:T(4,128)S(1)}, f32[4,4,128]{2,1,0:T(4,128)S(1)}, u32[]{:S(2)}, u32[]{:S(2)}) %collective-permute-start.17) | collective-permute-done | bytes 8224 | tf_op jit(solution)/shard_map/ppermute | solution.py:344
  99.5 1.1 collective-permute-start.18
  100.6 8.2 %shard_map.83 = (bf16[4,4,72,768]{3,2,1,0:T(8,128)(2,1)}, f32[4,4,1,128]{3,2,1,0:T(1,128)S(1)}) custom-call(s32[3]{0:T(128)S(1)} %pad_add_fusion.sc_ref, bf16[528,1280]{1,0:T(8,128)(2,1)S(1)} %shard_map.76.tab_ref.refs_0_, bf16[256,768]{1,0:T(8,128)(2,1)S(1)} %maximum_maximum_fusion.refs_1_.refs_7_, ...), custom_call_target="tpu_custom_call" | custom-call | flops 1 | bytes 1 | tf_op jit(solution)/shard_map/pallas_call | solution.py:183
  108.8 5.7 %shard_map.85 = (bf16[1,4,96,1024]{3,2,1,0:T(8,128)(2,1)}, bf16[1,4,96,1024]{3,2,1,0:T(8,128)(2,1)}, bf16[1,4,96,2048]{3,2,1,0:T(8,128)(2,1)S(1)}) custom-call(s32[3]{0:T(128)S(1)} %pad_add_fusion.sc_ref, bf16[528,1280]{1,0:T(8,128)(2,1)S(1)} %shard_map.76.tab_ref.refs_0_, bf16[256,768]{1,0:T(8,128)(2,1)S(1)} %maximum_maximum_fusion.refs_1_.refs_7_, ...), custom_call_target="tpu_custom_call" | custom-call | flops 1 | bytes 1 | tf_op jit(solution)/shard_map/pallas_call | solution.py:276
  114.5 0.5 collective-permute-start.20
  115.0 7.9 %all_to_all.5 = f32[4,4,128]{2,1,0:T(4,128)S(1)} all-to-all(f32[4,4,128]{2,1,0:T(4,128)S(1)} %add.15), channel_id=1, replica_groups=mesh['dp'=8,'expert'=4] {'expert'}, dimensions={0} | all-to-all | bytes 16384 | tf_op jit(solution)/shard_map/all_to_all | solution.py:438
  123.0 0.6 select_reduce_fusion
  123.6 0.9 copy-done.4
  124.5 2.2 %shard_map.84 = bf16[4,4,72,768]{3,2,1,0:T(8,128)(2,1)} custom-call(s32[3]{0:T(128)} %copy-done.2, bf16[4,4,72,384]{3,2,1,0:T(8,128)(2,1)} %copy-done.4, bf16[4,4,72,768]{3,2,1,0:T(8,128)(2,1)} %get-tuple-element.51.old_ref), custom_call_target="tpu_custom_call", output_to_operand_aliasing={{}: (2, {})} | custom-call | flops 1 | bytes 1 | tf_op jit(solution)/shard_map/pallas_call | solution.py:225
  126.8 3.8 %shard_map.86 = bf16[4,96,2048]{2,1,0:T(8,128)(2,1)} custom-call(bf16[1,4,96,2048]{3,2,1,0:T(8,128)(2,1)S(1)} %get-tuple-element.54.keep_ref, bf16[1,4,96,1024]{3,2,1,0:T(8,128)(2,1)S(1)} %collective-permute-done.19.left_ref, bf16[1,4,96,1024]{3,2,1,0:T(8,128)(2,1)S(1)} %collective-permute-done.20.right_ref, ...), custom_call_target="tpu_custom_call" | custom-call | flops 1 | bytes 1 | tf_op jit(solution)/shard_map/pallas_call | solution.py:324
  (36 shorter events, 0.3 us)
Async XLA Ops:
  0.6 3.8 %collective-permute-start.4 = (bf16[1,4,96,2048]{3,2,1,0:T(8,128)(2,1)}, bf16[1,4,96,2048]{3,2,1,0:T(8,128)(2,1)S(1)}, u32[]{:S(2)}, u32[]{:S(2)}) collective-permute-start(bf16[1,4,96,2048]{3,2,1,0:T(8,128)(2,1)} %bitcast.14), channel_id=1, source_target_pairs={{0,4},{4,0},{8,12},{12,8},{16,20},{20,16},{24,28},{28,24},{1,5},{5... | collective-permute-start | bytes 4718600 | tf_op jit(solution)/shard_map/ppermute | solution.py:344
  1.8 1.3 %copy-start.3 = (bf16[128,2048]{1,0:T(8,128)(2,1)S(1)}, bf16[128,2048]{1,0:T(8,128)(2,1)}, u32[]{:S(2)}) copy-start(bf16[128,2048]{1,0:T(8,128)(2,1)} %param.5) | copy-start | bytes 1572868
  3.2 4.1 %copy-start.5 = (s32[128,8]{0,1:T(8,128)S(1)}, s32[128,8]{0,1:T(8,128)}, u32[]{:S(2)}) copy-start(s32[128,8]{0,1:T(8,128)} %param.6) | copy-start | bytes 12292
  3.2 4.1 %slice-start = ((bf16[128,2048]{1,0:T(8,128)(2,1)}), bf16[128,1280]{1,0:T(8,128)(2,1)S(1)}, s32[]{:S(2)}) async-start(bf16[128,2048]{1,0:T(8,128)(2,1)} %param.5), calls=%async_computation.1 | async-start | bytes 655360 | tf_op jit(solution)/shard_map/slice | solution.py:362
  3.2 6.8 %copy-start.1 = (bf16[4,96,2048]{2,1,0:T(8,128)(2,1)S(1)}, bf16[4,96,2048]{2,1,0:T(8,128)(2,1)}, u32[]{:S(2)}) copy-start(bf16[4,96,2048]{2,1,0:T(8,128)(2,1)} %param.9) | copy-start | bytes 4718596
  4.4 39.3 %collective-permute-start.5 = (bf16[1408,384]{1,0:T(8,128)(2,1)}, bf16[1408,384]{1,0:T(8,128)(2,1)}, u32[]{:S(2)}, u32[]{:S(2)}) collective-permute-start(bf16[1408,384]{1,0:T(8,128)(2,1)} %pad_maximum_fusion), channel_id=1, source_target_pairs={{0,16},{4,20},{8,24},{12,28},{16,0},{20,4},{24,8},{28,12},{1,17},{... | collective-permute-start | bytes 3244040 | tf_op jit(solution)/shard_map/ppermute | solution.py:344
  7.4 20.5 %collective-permute-start.1 = (bf16[144,1280]{1,0:T(8,128)(2,1)S(1)}, bf16[144,1280]{1,0:T(8,128)(2,1)}, u32[]{:S(2)}, u32[]{:S(2)}) collective-permute-start(bf16[144,1280]{1,0:T(8,128)(2,1)S(1)} %fusion.1.refs_0_), channel_id=1, source_target_pairs={{0,2},{1,3},{2,0},{3,1},{4,6},{5,7},{6,4},{7,5},{8,10},{9,11},{10,... | collective-permute-start | bytes 1105928 | tf_op jit(solution)/shard_map/ppermute | solution.py:351
  10.0 36.0 %collective-permute-start.15 = (bf16[1,4,96,2048]{3,2,1,0:T(8,128)(2,1)S(1)}, bf16[1,4,96,2048]{3,2,1,0:T(8,128)(2,1)}, u32[]{:S(2)}, u32[]{:S(2)}) collective-permute-start(bf16[1,4,96,2048]{3,2,1,0:T(8,128)(2,1)S(1)} %bitcast.15), channel_id=1, source_target_pairs={{0,8},{4,12},{8,0},{12,4},{16,24},{20,28},{24,16},{28,20},{1,9},{5... | collective-permute-start | bytes 4718600 | tf_op jit(solution)/shard_map/ppermute | solution.py:344
  11.5 17.7 %collective-permute-start = (bf16[144,1280]{1,0:T(8,128)(2,1)S(1)}, bf16[144,1280]{1,0:T(8,128)(2,1)}, u32[]{:S(2)}, u32[]{:S(2)}) collective-permute-start(bf16[144,1280]{1,0:T(8,128)(2,1)S(1)} %fusion.1.refs_0_), channel_id=1, source_target_pairs={{0,1},{1,2},{2,3},{4,5},{5,6},{6,7},{8,9},{9,10},{10,11},{12,13},{... | collective-permute-start | bytes 1105928 | tf_op jit(solution)/shard_map/ppermute | solution.py:352
  15.7 19.0 %collective-permute-start.2 = (bf16[144,1280]{1,0:T(8,128)(2,1)S(1)}, bf16[144,1280]{1,0:T(8,128)(2,1)}, u32[]{:S(2)}, u32[]{:S(2)}) collective-permute-start(bf16[144,1280]{1,0:T(8,128)(2,1)S(1)} %fusion.1.refs_0_), channel_id=1, source_target_pairs={{1,0},{2,1},{3,2},{5,4},{6,5},{7,6},{9,8},{10,9},{11,10},{13,12},{... | collective-permute-start | bytes 1105928 | tf_op jit(solution)/shard_map/ppermute | solution.py:353
  27.8 13.8 %collective-permute-start.3 = (bf16[144,1280]{1,0:T(8,128)(2,1)}, bf16[144,1280]{1,0:T(8,128)(2,1)}, u32[]{:S(2)}, u32[]{:S(2)}) collective-permute-start(bf16[144,1280]{1,0:T(8,128)(2,1)} %collective-permute-done.1.refs_2_), channel_id=1, source_target_pairs={{2,3},{1,0},{6,7},{5,4},{10,11},{9,8},{14,15},{13,12},{18,19},{17,... | collective-permute-start | bytes 1105928 | tf_op jit(solution)/shard_map/ppermute | solution.py:354
  29.2 79.6 %copy-start.2 = (s32[3]{0:T(128)}, s32[3]{0:T(128)S(1)}, u32[]{:S(2)}) copy-start(s32[3]{0:T(128)S(1)} %pad_add_fusion.sc_ref) | copy-start | bytes 40
  29.2 15.9 %slice-start.1 = ((bf16[128,2048]{1,0:T(8,128)(2,1)}), bf16[128,768]{1,0:T(8,128)(2,1)S(1)}, s32[]{:S(2)}) async-start(bf16[128,2048]{1,0:T(8,128)(2,1)} %param.5), calls=%async_computation.2 | async-start | bytes 393216 | tf_op jit(solution)/shard_map/slice | solution.py:385
  41.7 23.2 %copy-start = (bf16[1,4,4,72,768]{4,3,2,1,0:T(8,128)(2,1)S(1)}, bf16[1,4,4,72,768]{4,3,2,1,0:T(8,128)(2,1)}, u32[]{:S(2)}) copy-start(bf16[1,4,4,72,768]{4,3,2,1,0:T(8,128)(2,1)} %refs_10_.1) | copy-start | bytes 5308420
  43.7 30.8 %collective-permute-start.6 = (bf16[528,1280]{1,0:T(8,128)(2,1)S(1)}, bf16[528,1280]{1,0:T(8,128)(2,1)S(1)}, u32[]{:S(2)}, u32[]{:S(2)}) collective-permute-start(bf16[528,1280]{1,0:T(8,128)(2,1)S(1)} %shard_map.76.tab_ref.refs_0_), channel_id=1, source_target_pairs={{0,16},{4,20},{8,24},{12,28},{16,0},{20,4},{24,8},{28,12},{1,17},{... | collective-permute-start | bytes 4055048 | tf_op jit(solution)/shard_map/ppermute | solution.py:344
  45.2 18.4 %collective-permute-start.8 = (bf16[256,768]{1,0:T(8,128)(2,1)S(1)}, bf16[256,768]{1,0:T(8,128)(2,1)S(1)}, u32[]{:S(2)}, u32[]{:S(2)}) collective-permute-start(bf16[256,768]{1,0:T(8,128)(2,1)S(1)} %maximum_maximum_fusion.refs_1_.refs_7_), channel_id=1, source_target_pairs={{0,2},{1,3},{2,0},{3,1},{4,6},{5,7},{6,4},{7,5},{8,10},{9,11},{10,... | collective-permute-start | bytes 1179656 | tf_op jit(solution)/shard_map/ppermute | solution.py:351
  46.0 42.2 %collective-permute-start.16 = (bf16[1,4,96,2048]{3,2,1,0:T(8,128)(2,1)}, bf16[1,4,96,2048]{3,2,1,0:T(8,128)(2,1)S(1)}, u32[]{:S(2)}, u32[]{:S(2)}) collective-permute-start(bf16[1,4,96,2048]{3,2,1,0:T(8,128)(2,1)} %collective-permute-done.15.refs_8_), channel_id=1, source_target_pairs={{0,4},{4,0},{8,12},{12,8},{16,20},{20,16},{24,28},{28,24},{1,5},{5... | collective-permute-start | bytes 4718600 | tf_op jit(solution)/shard_map/ppermute | solution.py:344
  46.0 32.9 %collective-permute-start.7 = (bf16[256,768]{1,0:T(8,128)(2,1)S(1)}, bf16[256,768]{1,0:T(8,128)(2,1)S(1)}, u32[]{:S(2)}, u32[]{:S(2)}) collective-permute-start(bf16[256,768]{1,0:T(8,128)(2,1)S(1)} %maximum_maximum_fusion.refs_1_.refs_7_), channel_id=1, source_target_pairs={{0,1},{1,2},{2,3},{4,5},{5,6},{6,7},{8,9},{9,10},{10,11},{12,13},{... | collective-permute-start | bytes 1179656 | tf_op jit(solution)/shard_map/ppermute | solution.py:352
  49.5 29.9 %collective-permute-start.9 = (bf16[256,768]{1,0:T(8,128)(2,1)S(1)}, bf16[256,768]{1,0:T(8,128)(2,1)S(1)}, u32[]{:S(2)}, u32[]{:S(2)}) collective-permute-start(bf16[256,768]{1,0:T(8,128)(2,1)S(1)} %maximum_maximum_fusion.refs_1_.refs_7_), channel_id=1, source_target_pairs={{1,0},{2,1},{3,2},{5,4},{6,5},{7,6},{9,8},{10,9},{11,10},{13,12},{... | collective-permute-start | bytes 1179656 | tf_op jit(solution)/shard_map/ppermute | solution.py:353
  63.6 15.8 %collective-permute-start.10 = (bf16[256,768]{1,0:T(8,128)(2,1)S(1)}, bf16[256,768]{1,0:T(8,128)(2,1)S(1)}, u32[]{:S(2)}, u32[]{:S(2)}) collective-permute-start(bf16[256,768]{1,0:T(8,128)(2,1)S(1)} %collective-permute-done.8.refs_3_.refs_9_), channel_id=1, source_target_pairs={{2,3},{1,0},{6,7},{5,4},{10,11},{9,8},{14,15},{13,12},{18,19},{17,... | collective-permute-start | bytes 1179656 | tf_op jit(solution)/shard_map/ppermute | solution.py:354
  78.8 4.3 %collective-permute-start.11 = (bf16[1,4,96,512]{3,2,1,0:T(8,128)(2,1)S(1)}, bf16[1,4,96,512]{3,2,1,0:T(8,128)(2,1)S(1)}, u32[]{:S(2)}, u32[]{:S(2)}) collective-permute-start(bf16[1,4,96,512]{3,2,1,0:T(8,128)(2,1)S(1)} %get-tuple-element.35), channel_id=1, source_target_pairs={{0,4},{4,0},{8,12},{12,8},{16,20},{20,16},{24,28},{28,24},{1,5},{5... | collective-permute-start | bytes 1179656 | tf_op jit(solution)/shard_map/ppermute | solution.py:344
  78.9 4.2 %collective-permute-start.12 = (bf16[1,4,96,512]{3,2,1,0:T(8,128)(2,1)S(1)}, bf16[1,4,96,512]{3,2,1,0:T(8,128)(2,1)S(1)}, u32[]{:S(2)}, u32[]{:S(2)}) collective-permute-start(bf16[1,4,96,512]{3,2,1,0:T(8,128)(2,1)S(1)} %get-tuple-element.39), channel_id=1, source_target_pairs={{0,4},{4,0},{8,12},{12,8},{16,20},{20,16},{24,28},{28,24},{1,5},{5... | collective-permute-start | bytes 1179656 | tf_op jit(solution)/shard_map/ppermute | solution.py:344
  82.6 1.8 %collective-permute-start.13 = (bf16[1,4,96,512]{3,2,1,0:T(8,128)(2,1)S(1)}, bf16[1,4,96,512]{3,2,1,0:T(8,128)(2,1)S(1)}, u32[]{:S(2)}, u32[]{:S(2)}) collective-permute-start(bf16[1,4,96,512]{3,2,1,0:T(8,128)(2,1)S(1)} %get-tuple-element.40), channel_id=1, source_target_pairs={{0,4},{4,0},{8,12},{12,8},{16,20},{20,16},{24,28},{28,24},{1,5},{5... | collective-permute-start | bytes 1179656 | tf_op jit(solution)/shard_map/ppermute | solution.py:344
  82.8 2.2 %collective-permute-start.14 = (bf16[1,4,96,512]{3,2,1,0:T(8,128)(2,1)S(1)}, bf16[1,4,96,512]{3,2,1,0:T(8,128)(2,1)S(1)}, u32[]{:S(2)}, u32[]{:S(2)}) collective-permute-start(bf16[1,4,96,512]{3,2,1,0:T(8,128)(2,1)S(1)} %get-tuple-element.41), channel_id=1, source_target_pairs={{0,4},{4,0},{8,12},{12,8},{16,20},{20,16},{24,28},{28,24},{1,5},{5... | collective-permute-start | bytes 1179656 | tf_op jit(solution)/shard_map/ppermute | solution.py:344
  86.8 40.0 %collective-permute-start.21 = (bf16[1,4,96,2048]{3,2,1,0:T(8,128)(2,1)}, bf16[1,4,96,2048]{3,2,1,0:T(8,128)(2,1)}, u32[]{:S(2)}, u32[]{:S(2)}) collective-permute-start(bf16[1,4,96,2048]{3,2,1,0:T(8,128)(2,1)} %shard_map.81), channel_id=1, source_target_pairs={{0,8},{4,12},{8,0},{12,4},{16,24},{20,28},{24,16},{28,20},{1,9},{5... | collective-permute-start | bytes 4718600 | tf_op jit(solution)/shard_map/ppermute | solution.py:344
  95.8 3.7 %collective-permute-start.17 = (f32[4,4,128]{2,1,0:T(4,128)S(1)}, f32[4,4,128]{2,1,0:T(4,128)S(1)}, u32[]{:S(2)}, u32[]{:S(2)}) collective-permute-start(f32[4,4,128]{2,1,0:T(4,128)S(1)} %bitcast.19), channel_id=1, source_target_pairs={{0,16},{4,20},{8,24},{12,28},{16,0},{20,4},{24,8},{28,12},{1,17},{... | collective-permute-start | bytes 24584 | tf_op jit(solution)/shard_map/ppermute | solution.py:344
  99.5 24.1 %collective-permute-start.18 = (bf16[4,4,72,384]{3,2,1,0:T(8,128)(2,1)S(1)}, bf16[4,4,72,384]{3,2,1,0:T(8,128)(2,1)S(1)}, u32[]{:S(2)}, u32[]{:S(2)}) collective-permute-start(bf16[4,4,72,384]{3,2,1,0:T(8,128)(2,1)S(1)} %get-tuple-element.47), channel_id=1, source_target_pairs={{0,16},{4,20},{8,24},{12,28},{16,0},{20,4},{24,8},{28,12},{1,17},{... | collective-permute-start | bytes 2654216 | tf_op jit(solution)/shard_map/ppermute | solution.py:344
  114.5 12.2 %collective-permute-start.19 = (bf16[1,4,96,1024]{3,2,1,0:T(8,128)(2,1)}, bf16[1,4,96,1024]{3,2,1,0:T(8,128)(2,1)S(1)}, u32[]{:S(2)}, u32[]{:S(2)}) collective-permute-start(bf16[1,4,96,1024]{3,2,1,0:T(8,128)(2,1)} %get-tuple-element.55), channel_id=1, source_target_pairs={{0,4},{4,0},{8,12},{12,8},{16,20},{20,16},{24,28},{28,24},{1,5},{5... | collective-permute-start | bytes 2359304 | tf_op jit(solution)/shard_map/ppermute | solution.py:344
  114.5 12.2 %collective-permute-start.20 = (bf16[1,4,96,1024]{3,2,1,0:T(8,128)(2,1)}, bf16[1,4,96,1024]{3,2,1,0:T(8,128)(2,1)S(1)}, u32[]{:S(2)}, u32[]{:S(2)}) collective-permute-start(bf16[1,4,96,1024]{3,2,1,0:T(8,128)(2,1)} %get-tuple-element.56), channel_id=1, source_target_pairs={{0,4},{4,0},{8,12},{12,8},{16,20},{20,16},{24,28},{28,24},{1,5},{5... | collective-permute-start | bytes 2359304 | tf_op jit(solution)/shard_map/ppermute | solution.py:344
  123.6 0.9 copy-start.4

commit v5 on v4

--- a/solution.py
+++ b/solution.py
@@ -62,7 +62,7 @@
                 row_spec,
             ),
         ),
-        compiler_params=pltpu.CompilerParams(vmem_limit_bytes=16 << 20),
+        compiler_params=pltpu.CompilerParams(vmem_limit_bytes=12 << 20),
         cost_estimate=SHORT,
     )(scalars, tokens, hid)
 
@@ -112,7 +112,7 @@
             in_specs=[pl.BlockSpec((rows, cols), lambda i, sc: (0, 0))] * len(blocks),
             out_specs=pl.BlockSpec((n * (toks + experts), cols), lambda i, sc: (0, 0)),
         ),
-        compiler_params=pltpu.CompilerParams(vmem_limit_bytes=24 << 20),
+        compiler_params=pltpu.CompilerParams(vmem_limit_bytes=12 << 20),
         cost_estimate=SHORT,
     )(scalars, *blocks)
 
@@ -202,39 +202,9 @@
             out_specs=(pl.BlockSpec((group, n, CAP, f), lambda e, sc: (e, 0, 0, sc[1] if whole else 0)), row_spec),
             scratch_shapes=[pltpu.VMEM((group, f, d), BF)],
         ),
-        compiler_params=pltpu.CompilerParams(vmem_limit_bytes=32 << 20),
+        compiler_params=pltpu.CompilerParams(vmem_limit_bytes=24 << 20),
         cost_estimate=SHORT,
     )(scalars, *arrays, *[w for _, w, _ in w_pieces], hid, wt, rank)
-
-
-def insert_kernel(sc_ref, new_ref, old_ref, out_ref, sems):
-    experts, n, _, f = new_ref.shape
-    at = pl.multiple_of((1 - sc_ref[1]) * f, f)
-    copies = [
-        pltpu.make_async_copy(new_ref.at[e, s], out_ref.at[e, s, :, pl.ds(at, f)], sems.at[e, s])
-        for e in range(experts)
-        for s in range(n)
-    ]
-    for copy in copies:
-        copy.start()
-    for copy in copies:
-        copy.wait()
-
-
-def insert(scalars, new, whole):
-    return pl.pallas_call(
-        insert_kernel,
-        out_shape=jax.ShapeDtypeStruct(whole.shape, BF),
-        in_specs=[
-            pl.BlockSpec(memory_space=pltpu.SMEM),
-            pl.BlockSpec(memory_space=pltpu.VMEM),
-            pl.BlockSpec(memory_space=pl.ANY),
-        ],
-        out_specs=pl.BlockSpec(memory_space=pl.ANY),
-        scratch_shapes=[pltpu.SemaphoreType.DMA(new.shape[:2])],
-        input_output_aliases={2: 0},
-        cost_estimate=SHORT,
-    )(scalars, new, whole)
 
 
 def part_kernel(n, bands, counts, spans, sc_ref, *refs):
@@ -282,54 +252,68 @@
             in_specs=specs + specs_nb + [hs_spec, hs_spec],
             out_specs=[pl.BlockSpec((bands // 4, 1, band, width), lambda e, sc: (0, e, 0, 0)) for width in widths],
         ),
-        compiler_params=pltpu.CompilerParams(vmem_limit_bytes=32 << 20),
+        compiler_params=pltpu.CompilerParams(vmem_limit_bytes=20 << 20),
         cost_estimate=SHORT,
     )(scalars, *arrays, *arrays_nb, own, nb)
 
 
-def joined_kernel(widths, *refs):
-    out_ref, at = refs[-1], 0
-    count = len(widths)
-    for i, width in enumerate(widths):
-        keep, parts = refs[i], refs[count + 2 * i : count + 2 * i + 2]
-        there = jnp.concatenate([x[...] for x in parts], axis=3)
-        out_ref[:, :, :, at : at + width] = (keep[...].astype(F32) + there.astype(F32)).astype(BF)
-        at += width
-
-
-def joined(keeps, parts):
-    widths = [keep.shape[3] for keep in keeps]
-    arrays = [*keeps, *[part for two in parts for part in two]]
+def joined_kernel(groups, *refs):
+    total, at = None, 0
+    for count in groups:
+        parts = [ref[...].astype(F32) for ref in refs[at : at + count]]
+        term = parts[0] if count == 1 else jnp.concatenate(parts, axis=3)
+        total = term if total is None else total + term
+        at += count
+    refs[-1][...] = total.astype(BF)
+
+
+def joined(terms):
+    arrays = [part for term in terms for part in term]
+    lead, experts, band, _ = arrays[0].shape
+    d = sum(part.shape[3] for part in terms[0])
     block = lambda x: pl.BlockSpec((x.shape[0], 1, *x.shape[2:]), lambda e: (0, e, 0, 0))
-    out = jax.ShapeDtypeStruct((*keeps[0].shape[:3], sum(widths)), BF)
-    return pl.pallas_call(
-        functools.partial(joined_kernel, widths),
-        out_shape=out,
-        grid=(out.shape[1],),
+    out, spec = (lead, experts, band, d), pl.BlockSpec((lead, 1, band, d), lambda e: (0, e, 0, 0))
+    return pl.pallas_call(
+        functools.partial(joined_kernel, [len(term) for term in terms]),
+        out_shape=jax.ShapeDtypeStruct(out, BF),
+        grid=(experts,),
         in_specs=[block(x) for x in arrays],
-        out_specs=block(out),
-        compiler_params=pltpu.CompilerParams(vmem_limit_bytes=16 << 20),
+        out_specs=spec,
+        compiler_params=pltpu.CompilerParams(vmem_limit_bytes=8 << 20),
         cost_estimate=SHORT,
     )(*arrays)
 
 
-def finish_kernel(keep_ref, left_ref, right_ref, there_ref, out_ref):
-    near = jnp.concatenate([left_ref[0], right_ref[0]], axis=2).astype(F32)
-    out_ref[...] = (keep_ref[0].astype(F32) + near + there_ref[0].astype(F32)).astype(BF)
-
-
-def finish(keep, near, there):
-    _, experts, band, d = keep.shape
-    block = lambda x: pl.BlockSpec((1, 1, *x.shape[2:]), lambda e: (0, e, 0, 0))
+def finish_kernel(sc_ref, base_ref, there_ref, new_ref, old_ref, down_ref, hidden_ref):
+    down_ref[0] = (base_ref[0, 0].astype(F32) + there_ref[0, 0].astype(F32)).astype(BF)
+    hidden_ref[...] = new_ref[...]
+
+
+def finish(scalars, base, there, new, whole):
+    _, experts, band, d = base.shape
+    _, n, cap, f = new.shape
+    sums = pl.BlockSpec((1, 1, band, d), lambda e, sc: (0, e, 0, 0))
     return pl.pallas_call(
         finish_kernel,
-        out_shape=jax.ShapeDtypeStruct((experts, band, d), BF),
-        grid=(experts,),
-        in_specs=[block(x) for x in (keep, *near, there)],
-        out_specs=pl.BlockSpec((1, band, d), lambda e: (e, 0, 0)),
-        compiler_params=pltpu.CompilerParams(vmem_limit_bytes=16 << 20),
-        cost_estimate=SHORT,
-    )(keep, *near, there)
+        out_shape=(jax.ShapeDtypeStruct((experts, band, d), BF), jax.ShapeDtypeStruct(whole.shape, BF)),
+        grid_spec=pltpu.PrefetchScalarGridSpec(
+            num_scalar_prefetch=1,
+            grid=(experts,),
+            in_specs=[
+                sums,
+                sums,
+                pl.BlockSpec((1, n, cap, f), lambda e, sc: (e, 0, 0, 0)),
+                pl.BlockSpec(memory_space=pl.ANY),
+            ],
+            out_specs=(
+                pl.BlockSpec((1, band, d), lambda e, sc: (e, 0, 0)),
+                pl.BlockSpec((1, n, cap, f), lambda e, sc: (e, 0, 0, 1 - sc[1])),
+            ),
+        ),
+        input_output_aliases={4: 1},
+        compiler_params=pltpu.CompilerParams(vmem_limit_bytes=12 << 20),
+        cost_estimate=SHORT,
+    )(scalars, base, there, new, whole)
 
 
 def per_device(n_dp, n, grad_out, expert_ids, route_weights, hidden_cache, w_down):
@@ -401,17 +385,15 @@
         (slice(0, 1), ((0, half),)),
         (slice(0, 2), ((half, cut), (0, d - cut))),
     )
-    order, keeps, parts = scalars, [], []
+    order, sums = scalars, []
     for chunks, spans in groups:
         tokens = own_pieces[chunks], nb_pieces[chunks], spans
-        *far, keep_far = partial_grad(
-            n, bands, band, True, (half // 2, half // 2), order, hs_own, hs_nb, *tokens
-        )
+        width = sum(stop - start for start, stop in spans) // 2
+        *far, keep_far = partial_grad(n, bands, band, True, (width, width), order, hs_own, hs_nb, *tokens)
         order = after(scalars, far[0])
-        keeps.append(keep_far)
-        parts.append([swap(x, 1) for x in far])
-    going = joined(keeps, parts)
-    there = swap(going, bands // 2)
+        sums.append([[keep_far], [swap(x, 1) for x in far]])
+    going = joined([[x[i][k] for x in sums for k in ks] for i, ks in ((0, (0,)), (1, (0, 1)))])
+    there = [swap(going, bands // 2)]
     gh_nb, sg_nb = backward(
         n, after(scalars, going), nb_pieces, w_pieces, f, hid_nb, wt_nb, rank_nb, False
     )
@@ -419,23 +401,20 @@
     gh_own, sg_own = backward(
         n, after(scalars, sg_in), own_pieces, w_pieces, f, hidden_cache, wt_own, rank_own, True
     )
+    sg = sg_own.reshape(n, experts, toks) + sg_in
+    by_expert = lax.all_to_all(sg, "expert", split_axis=0, concat_axis=0, tiled=True)
     spans = ((0, cut), (0, d - cut))
     *near, keep = partial_grad(
         n, bands, band, False, (half, half), after(scalars, sg_own), hs_own, hs_nb, own_pieces, nb_pieces, spans
     )
-    near = [swap(x, 1) for x in near]
-    if bands == 4:
-        grad_down = finish(keep, near, there)
-    else:
-        total = keep.astype(F32) + jnp.concatenate(near, axis=3).astype(F32) + there.astype(F32)
-        mid = bands // 8
-        while mid:
-            total, mid = total[:mid] + swap(total[mid:].astype(BF), 4 * mid).astype(F32), mid // 2
-        grad_down = total[0].astype(BF)
-
-    grad_hidden = insert(scalars, swap(after(gh_nb, sg_in), bands), gh_own)
-    sg = sg_own.reshape(n, experts, toks) + sg_in
-    by_expert = lax.all_to_all(sg, "expert", split_axis=0, concat_axis=0, tiled=True)
+    base = joined([[keep], [swap(x, 1) for x in near]])
+    mid = bands // 8
+    there = there[0]
+    while mid:
+        total = base.astype(F32) + there.astype(F32)
+        base, there, mid = total[:mid].astype(BF), swap(total[mid:].astype(BF), 4 * mid), mid // 2
+    gh_in = swap(after(gh_nb, sg_in), bands)
+    grad_down, grad_hidden = finish(scalars, base, there, gh_in, gh_own)
     by_expert = by_expert.reshape(EXPERTS, 1, toks)
     chosen = expert_ids.T[None] == jnp.arange(EXPERTS, dtype=jnp.int32)[:, None, None]
     grad_probs = jnp.sum(jnp.where(chosen, by_expert, 0.0), axis=0).T

time: 131 us -> 126 us (0.962)
  Pallas kernels: 40.2 us -> 35 us
    pallas_call x3, Pallas kernels: 7.86 us -> 3.37 us  [the longest x1 2.55 us: finish(): pl.pallas_call(finish_kernel, out_shape=(jax.ShapeDtypeStruct((experts, b...]
  transfers between devices with their start and end apart: 22 -> 22, of which waited for: 10 -> 12; matrix products, arithmetic and copies ran while one was open for 5% -> 5% of each run, Pallas kernels for 28% -> 26%
where the time goes in v5:
time: 126 us; the launch traced here: 125 us
  waiting for transfers between devices  49.1 us (39%)
  Pallas kernels  35 us (28%)
  starting transfers between devices  26.1 us (21%)
  blocking collectives  7.92 us (6%)
  local copies, waits for them, and re-layouts  3.59 us (3%)
  other arithmetic  2.55 us (2%)
    ppermute x2, waiting for transfers between devices, spread(): two = lax.ppermute(x, 'expert', [(i, (i + 2) % n) for i in range(n)])  23.6 us
    pallas_call x2, Pallas kernels, backward(): pl.pallas_call(functools.partial(back_kernel, n, counts, group, rels), ou...  15.8 us
    ppermute x14, waiting for transfers between devices, swap(): return lax.ppermute(x, 'dp', [(i, i ^ bit) for i in range(n_dp)])  12.6 us
    pallas_call x3, Pallas kernels, partial_grad(): pl.pallas_call(functools.partial(part_kernel, n, bands, (counts, counts_n...  11.2 us
    ppermute x14, starting transfers between devices, swap(): return lax.ppermute(x, 'dp', [(i, i ^ bit) for i in range(n_dp)])  10.5 us
    all_to_all x1, blocking collectives, per_device(): lax.all_to_all(sg, 'expert', split_axis=0, concat_axis=0, tiled=True)  7.92 us
    ppermute x2, starting transfers between devices, spread(): one = lax.ppermute(x, 'expert', [(i, i + 1) for i in range(n - 1)])  7.7 us
    ppermute x2, waiting for transfers between devices, spread(): passed = lax.ppermute(two, 'expert', [(2, 3), (1, 0)])  7.38 us
  transfers between devices with their start and end apart: 22, of which 12 were waited for; matrix products, arithmetic and copies ran while one was open for 5% of the time, Pallas kernels for 26%

profile of v5, /device:TPU:0, one launch (start us, length us, event | category | flops | bytes accessed | tf_op | source)
XLA Modules:
  0.0 125.1 jit_solution(3062494215769444394)
XLA Ops:
  0.6 0.5 collective-permute-start.4
  1.1 0.7 convert_element_type.8
  1.8 1.3 %constant_dynamic-slice_fusion = bf16[1,4,4,72,384]{4,3,2,1,0:T(8,128)(2,1)S(1)} fusion(bf16[1,4,4,72,768]{4,3,2,1,0:T(8,128)(2,1)} %refs_10_.1, s32[]{:T(128)S(6)} %select_n.25), kind=kLoop, calls=%fused_computation.10 | loop fusion | bytes 1769476 | tf_op jit(solution)/shard_map/dynamic_slice | solution.py:348
  3.2 1.1 pad_maximum_fusion
  4.3 0.1 collective-permute-done.4.refs_7_
  4.4 2.9 %collective-permute-start.5 = (bf16[1408,384]{1,0:T(8,128)(2,1)}, bf16[1408,384]{1,0:T(8,128)(2,1)}, u32[]{:S(2)}, u32[]{:S(2)}) collective-permute-start(bf16[1408,384]{1,0:T(8,128)(2,1)} %pad_maximum_fusion), channel_id=1, source_target_pairs={{0,16},{4,20},{8,24},{12,28},{16,0},{20,4},{24,8},{28,12},{1,17},{... | collective-permute-start | bytes 3244040 | tf_op jit(solution)/shard_map/ppermute | solution.py:328
  7.4 2.7 %collective-permute-start.1 = (bf16[144,1280]{1,0:T(8,128)(2,1)S(1)}, bf16[144,1280]{1,0:T(8,128)(2,1)}, u32[]{:S(2)}, u32[]{:S(2)}) collective-permute-start(bf16[144,1280]{1,0:T(8,128)(2,1)S(1)} %fusion.1.refs_0_), channel_id=1, source_target_pairs={{0,2},{1,3},{2,0},{3,1},{4,6},{5,7},{6,4},{7,5},{8,10},{9,11},{10,... | collective-permute-start | bytes 1105928 | tf_op jit(solution)/shard_map/ppermute | solution.py:335
  10.0 1.5 %collective-permute-start.15 = (bf16[1,4,96,2048]{3,2,1,0:T(8,128)(2,1)S(1)}, bf16[1,4,96,2048]{3,2,1,0:T(8,128)(2,1)}, u32[]{:S(2)}, u32[]{:S(2)}) collective-permute-start(bf16[1,4,96,2048]{3,2,1,0:T(8,128)(2,1)S(1)} %bitcast.15), channel_id=1, source_target_pairs={{0,8},{4,12},{8,0},{12,4},{16,24},{20,28},{24,16},{28,20},{1,9},{5... | collective-permute-start | bytes 4718600 | tf_op jit(solution)/shard_map/ppermute | solution.py:328
  11.5 4.2 %collective-permute-start = (bf16[144,1280]{1,0:T(8,128)(2,1)S(1)}, bf16[144,1280]{1,0:T(8,128)(2,1)}, u32[]{:S(2)}, u32[]{:S(2)}) collective-permute-start(bf16[144,1280]{1,0:T(8,128)(2,1)S(1)} %fusion.1.refs_0_), channel_id=1, source_target_pairs={{0,1},{1,2},{2,3},{4,5},{5,6},{6,7},{8,9},{9,10},{10,11},{12,13},{... | collective-permute-start | bytes 1105928 | tf_op jit(solution)/shard_map/ppermute | solution.py:336
  15.7 1.3 %collective-permute-start.2 = (bf16[144,1280]{1,0:T(8,128)(2,1)S(1)}, bf16[144,1280]{1,0:T(8,128)(2,1)}, u32[]{:S(2)}, u32[]{:S(2)}) collective-permute-start(bf16[144,1280]{1,0:T(8,128)(2,1)S(1)} %fusion.1.refs_0_), channel_id=1, source_target_pairs={{1,0},{2,1},{3,2},{5,4},{6,5},{7,6},{9,8},{10,9},{11,10},{13,12},{... | collective-permute-start | bytes 1105928 | tf_op jit(solution)/shard_map/ppermute | solution.py:337
  17.0 10.8 %collective-permute-done.1.refs_2_ = bf16[144,1280]{1,0:T(8,128)(2,1)} collective-permute-done((bf16[144,1280]{1,0:T(8,128)(2,1)S(1)}, bf16[144,1280]{1,0:T(8,128)(2,1)}, u32[]{:S(2)}, u32[]{:S(2)}) %collective-permute-start.1) | collective-permute-done | bytes 368672 | tf_op jit(solution)/shard_map/ppermute | solution.py:335
  27.8 1.3 %collective-permute-start.3 = (bf16[144,1280]{1,0:T(8,128)(2,1)}, bf16[144,1280]{1,0:T(8,128)(2,1)}, u32[]{:S(2)}, u32[]{:S(2)}) collective-permute-start(bf16[144,1280]{1,0:T(8,128)(2,1)} %collective-permute-done.1.refs_2_), channel_id=1, source_target_pairs={{2,3},{1,0},{6,7},{5,4},{10,11},{9,8},{14,15},{13,12},{18,19},{17,... | collective-permute-start | bytes 1105928 | tf_op jit(solution)/shard_map/ppermute | solution.py:338
  29.2 5.5 %collective-permute-done.2.refs_3_ = bf16[144,1280]{1,0:T(8,128)(2,1)} collective-permute-done((bf16[144,1280]{1,0:T(8,128)(2,1)S(1)}, bf16[144,1280]{1,0:T(8,128)(2,1)}, u32[]{:S(2)}, u32[]{:S(2)}) %collective-permute-start.2) | collective-permute-done | bytes 368672 | tf_op jit(solution)/shard_map/ppermute | solution.py:337
  34.7 6.9 %collective-permute-done.3.refs_4_ = bf16[144,1280]{1,0:T(8,128)(2,1)} collective-permute-done((bf16[144,1280]{1,0:T(8,128)(2,1)}, bf16[144,1280]{1,0:T(8,128)(2,1)}, u32[]{:S(2)}, u32[]{:S(2)}) %collective-permute-start.3) | collective-permute-done | bytes 368672 | tf_op jit(solution)/shard_map/ppermute | solution.py:338
  41.7 2.0 %shard_map.76.tab_ref.refs_0_ = bf16[528,1280]{1,0:T(8,128)(2,1)S(1)} custom-call(s32[3]{0:T(128)S(1)} %pad_add_fusion.sc_ref, bf16[144,1280]{1,0:T(8,128)(2,1)S(1)} %fusion.1.refs_0_, bf16[144,1280]{1,0:T(8,128)(2,1)} %collective-permute-done.refs_1_, bf16[144,1280]{1,0:T(8,128)(2,1)} %collective-permute-done.1.refs_2_, ...), custom_call_target="tpu_custom_call" | custom-call | flops 1 | bytes 1 | tf_op jit(solution)/shard_map/pallas_call | solution.py:106
  43.7 0.5 collective-permute-start.6
  44.2 1.0 fusion.2
  45.3 0.7 collective-permute-done.15.refs_8_
  46.0 3.5 %collective-permute-start.7 = (bf16[256,768]{1,0:T(8,128)(2,1)S(1)}, bf16[256,768]{1,0:T(8,128)(2,1)S(1)}, u32[]{:S(2)}, u32[]{:S(2)}) collective-permute-start(bf16[256,768]{1,0:T(8,128)(2,1)S(1)} %maximum_maximum_fusion.refs_1_.refs_7_), channel_id=1, source_target_pairs={{0,1},{1,2},{2,3},{4,5},{5,6},{6,7},{8,9},{9,10},{10,11},{12,13},{... | collective-permute-start | bytes 1179656 | tf_op jit(solution)/shard_map/ppermute | solution.py:336
  49.5 1.3 %collective-permute-start.9 = (bf16[256,768]{1,0:T(8,128)(2,1)S(1)}, bf16[256,768]{1,0:T(8,128)(2,1)S(1)}, u32[]{:S(2)}, u32[]{:S(2)}) collective-permute-start(bf16[256,768]{1,0:T(8,128)(2,1)S(1)} %maximum_maximum_fusion.refs_1_.refs_7_), channel_id=1, source_target_pairs={{1,0},{2,1},{3,2},{5,4},{6,5},{7,6},{9,8},{10,9},{11,10},{13,12},{... | collective-permute-start | bytes 1179656 | tf_op jit(solution)/shard_map/ppermute | solution.py:337
  50.8 12.8 %collective-permute-done.8.refs_3_.refs_9_ = bf16[256,768]{1,0:T(8,128)(2,1)S(1)} collective-permute-done((bf16[256,768]{1,0:T(8,128)(2,1)S(1)}, bf16[256,768]{1,0:T(8,128)(2,1)S(1)}, u32[]{:S(2)}, u32[]{:S(2)}) %collective-permute-start.8) | collective-permute-done | bytes 393248 | tf_op jit(solution)/shard_map/ppermute | solution.py:335
  63.6 1.3 %collective-permute-start.10 = (bf16[256,768]{1,0:T(8,128)(2,1)S(1)}, bf16[256,768]{1,0:T(8,128)(2,1)S(1)}, u32[]{:S(2)}, u32[]{:S(2)}) collective-permute-start(bf16[256,768]{1,0:T(8,128)(2,1)S(1)} %collective-permute-done.8.refs_3_.refs_9_), channel_id=1, source_target_pairs={{2,3},{1,0},{6,7},{5,4},{10,11},{9,8},{14,15},{13,12},{18,19},{17,... | collective-permute-start | bytes 1179656 | tf_op jit(solution)/shard_map/ppermute | solution.py:338
  64.9 1.3 %shard_map.77 = (bf16[4,384,512]{2,1,0:T(8,128)(2,1)S(1)}, f32[4,4,1,128]{3,2,1,0:T(1,128)S(1)}, f32[4,4,1,128]{3,2,1,0:T(1,128)S(1)}) custom-call(s32[3]{0:T(128)S(1)} %pad_add_fusion.sc_ref, bf16[528,1280]{1,0:T(8,128)(2,1)S(1)} %shard_map.76.tab_ref.refs_0_, bf16[1,4,4,72,768]{4,3,2,1,0:T(8,128)(2,1)S(1)} %copy-done), custom_call_target="tpu_custom_call" | custom-call | flops 1 | bytes 1 | tf_op jit(solution)/shard_map/pallas_call | solution.py:49
  66.2 1.3 %slice.28 = bf16[1152,384]{1,0:T(8,128)(2,1)S(1)} slice(bf16[1408,384]{1,0:T(8,128)(2,1)} %collective-permute-done.5), slice={[0:1152], [0:384]} | slice | bytes 1769472 | tf_op jit(solution)/shard_map/slice | solution.py:353
  67.5 7.0 %collective-permute-done.6.tab_ref.refs_1_.refs_6_.refs_0_ = bf16[528,1280]{1,0:T(8,128)(2,1)S(1)} collective-permute-done((bf16[528,1280]{1,0:T(8,128)(2,1)S(1)}, bf16[528,1280]{1,0:T(8,128)(2,1)S(1)}, u32[]{:S(2)}, u32[]{:S(2)}) %collective-permute-start.6) | collective-permute-done | bytes 1351712 | tf_op jit(solution)/shard_map/ppermute | solution.py:328
  74.5 1.3 %shard_map.78 = (bf16[4,384,512]{2,1,0:T(8,128)(2,1)S(1)}, f32[4,4,1,128]{3,2,1,0:T(1,128)S(1)}, f32[4,4,1,128]{3,2,1,0:T(1,128)S(1)}) custom-call(s32[3]{0:T(128)S(1)} %pad_add_fusion.sc_ref, bf16[528,1280]{1,0:T(8,128)(2,1)S(1)} %collective-permute-done.6.tab_ref.refs_1_.refs_6_.refs_0_, bf16[1,4,4,72,384]{4,3,2,1,0:T(8,128)(2,1)S(1)} %bitcast.12), custom_call_target="tpu_custom_call" | custom-call | flops 1 | bytes 1 | tf_op jit(solution)/shard_map/pallas_call | solution.py:49
  75.7 3.1 %shard_map.79 = (bf16[1,4,96,512]{3,2,1,0:T(8,128)(2,1)S(1)}, bf16[1,4,96,512]{3,2,1,0:T(8,128)(2,1)S(1)}, bf16[1,4,96,1024]{3,2,1,0:T(8,128)(2,1)S(1)}) custom-call(s32[3]{0:T(128)S(1)} %pad_add_fusion.sc_ref, bf16[528,1280]{1,0:T(8,128)(2,1)S(1)} %shard_map.76.tab_ref.refs_0_, bf16[528,1280]{1,0:T(8,128)(2,1)S(1)} %collective-permute-done.6.tab_ref.refs_1_.refs_6_.refs_0_, ...), custom_call_target="tpu_custom_call" | custom-call | flops 1 | bytes 1 | tf_op jit(solution)/shard_map/pallas_call | solution.py:246
  79.0 0.4 collective-permute-done.10.refs_5_.refs_11_
  79.4 3.2 %shard_map.80 = (bf16[1,4,96,512]{3,2,1,0:T(8,128)(2,1)S(1)}, bf16[1,4,96,512]{3,2,1,0:T(8,128)(2,1)S(1)}, bf16[1,4,96,1024]{3,2,1,0:T(8,128)(2,1)S(1)}) custom-call(s32[3]{0:T(128)S(1)} %pad_add_fusion.sc_ref, bf16[528,1280]{1,0:T(8,128)(2,1)S(1)} %shard_map.76.tab_ref.refs_0_, bf16[256,768]{1,0:T(8,128)(2,1)S(1)} %maximum_maximum_fusion.refs_1_.refs_7_, ...), custom_call_target="tpu_custom_call" | custom-call | flops 1 | bytes 1 | tf_op jit(solution)/shard_map/pallas_call | solution.py:246
  82.6 0.1 collective-permute-start.13
  82.7 0.4 collective-permute-start.14
  83.1 0.1 collective-permute-start.12
  83.2 1.1 collective-permute-done.13.refs_4_
  84.4 0.6 collective-permute-done.14.refs_5_
  84.9 0.6 collective-permute-done.12.refs_3_
  85.5 0.4 shard_map.81
  85.9 1.5 %collective-permute-start.20 = (bf16[1,4,96,2048]{3,2,1,0:T(8,128)(2,1)S(1)}, bf16[1,4,96,2048]{3,2,1,0:T(8,128)(2,1)S(1)}, u32[]{:S(2)}, u32[]{:S(2)}) collective-permute-start(bf16[1,4,96,2048]{3,2,1,0:T(8,128)(2,1)S(1)} %shard_map.81), channel_id=1, source_target_pairs={{0,8},{4,12},{8,0},{12,4},{16,24},{20,28},{24,16},{28,20},{1,9},{5... | collective-permute-start | bytes 4718600 | tf_op jit(solution)/shard_map/ppermute | solution.py:328
  87.4 7.6 %shard_map.82 = (bf16[4,4,72,384]{3,2,1,0:T(8,128)(2,1)S(1)}, f32[4,4,1,128]{3,2,1,0:T(1,128)S(1)}) custom-call(s32[3]{0:T(128)S(1)} %pad_add_fusion.sc_ref, bf16[528,1280]{1,0:T(8,128)(2,1)S(1)} %collective-permute-done.6.tab_ref.refs_1_.refs_6_.refs_0_, bf16[256,768]{1,0:T(8,128)(2,1)S(1)} %maximum_maximum_fusion.refs_1_.refs_7_, ...), custom_call_target="tpu_custom_call" | custom-call | flops 1 | bytes 1 | tf_op jit(solution)/shard_map/pallas_call | solution.py:183
  95.0 1.2 collective-permute-start.17
  96.2 2.5 %collective-permute-done.17 = f32[4,4,128]{2,1,0:T(4,128)S(1)} collective-permute-done((f32[4,4,128]{2,1,0:T(4,128)S(1)}, f32[4,4,128]{2,1,0:T(4,128)S(1)}, u32[]{:S(2)}, u32[]{:S(2)}) %collective-permute-start.17) | collective-permute-done | bytes 8224 | tf_op jit(solution)/shard_map/ppermute | solution.py:328
  98.7 1.1 collective-permute-start.21
  99.8 8.2 %shard_map.83 = (bf16[4,4,72,768]{3,2,1,0:T(8,128)(2,1)}, f32[4,4,1,128]{3,2,1,0:T(1,128)S(1)}) custom-call(s32[3]{0:T(128)S(1)} %pad_add_fusion.sc_ref, bf16[528,1280]{1,0:T(8,128)(2,1)S(1)} %shard_map.76.tab_ref.refs_0_, bf16[256,768]{1,0:T(8,128)(2,1)S(1)} %maximum_maximum_fusion.refs_1_.refs_7_, ...), custom_call_target="tpu_custom_call" | custom-call | flops 1 | bytes 1 | tf_op jit(solution)/shard_map/pallas_call | solution.py:183
  108.0 5.0 %shard_map.84 = (bf16[1,4,96,1024]{3,2,1,0:T(8,128)(2,1)S(1)}, bf16[1,4,96,1024]{3,2,1,0:T(8,128)(2,1)S(1)}, bf16[1,4,96,2048]{3,2,1,0:T(8,128)(2,1)S(1)}) custom-call(s32[3]{0:T(128)S(1)} %pad_add_fusion.sc_ref, bf16[528,1280]{1,0:T(8,128)(2,1)S(1)} %shard_map.76.tab_ref.refs_0_, bf16[256,768]{1,0:T(8,128)(2,1)S(1)} %maximum_maximum_fusion.refs_1_.refs_7_, ...), custom_call_target="tpu_custom_call" | custom-call | flops 1 | bytes 1 | tf_op jit(solution)/shard_map/pallas_call | solution.py:246
  113.1 0.5 collective-permute-start.19
  113.6 7.9 %all_to_all.5 = f32[4,4,128]{2,1,0:T(4,128)S(1)} all-to-all(f32[4,4,128]{2,1,0:T(4,128)S(1)} %add.15), channel_id=1, replica_groups=mesh['dp'=8,'expert'=4] {'expert'}, dimensions={0} | all-to-all | bytes 16384 | tf_op jit(solution)/shard_map/all_to_all | solution.py:405
  121.5 0.6 select_reduce_fusion
  122.1 0.4 shard_map.85.base_ref
  122.6 2.5 %shard_map.86 = (bf16[4,96,2048]{2,1,0:T(8,128)(2,1)}, bf16[4,4,72,768]{3,2,1,0:T(8,128)(2,1)}) custom-call(s32[3]{0:T(128)S(1)} %pad_add_fusion.sc_ref, bf16[1,4,96,2048]{3,2,1,0:T(8,128)(2,1)S(1)} %shard_map.85.base_ref, bf16[1,4,96,2048]{3,2,1,0:T(8,128)(2,1)S(1)} %collective-permute-done.20.there_ref, ...), custom_call_target="tpu_custom_call", output_to_operand_aliasing={{1}: (4, {})} | custom-call | flops 1 | bytes 1 | tf_op jit(solution)/shard_map/pallas_call | solution.py:296
  (32 shorter events, 0.5 us)
Async XLA Ops:
  0.6 3.8 %collective-permute-start.4 = (bf16[1,4,96,2048]{3,2,1,0:T(8,128)(2,1)}, bf16[1,4,96,2048]{3,2,1,0:T(8,128)(2,1)S(1)}, u32[]{:S(2)}, u32[]{:S(2)}) collective-permute-start(bf16[1,4,96,2048]{3,2,1,0:T(8,128)(2,1)} %bitcast.14), channel_id=1, source_target_pairs={{0,4},{4,0},{8,12},{12,8},{16,20},{20,16},{24,28},{28,24},{1,5},{5... | collective-permute-start | bytes 4718600 | tf_op jit(solution)/shard_map/ppermute | solution.py:328
  1.8 1.3 %copy-start.2 = (bf16[128,2048]{1,0:T(8,128)(2,1)S(1)}, bf16[128,2048]{1,0:T(8,128)(2,1)}, u32[]{:S(2)}) copy-start(bf16[128,2048]{1,0:T(8,128)(2,1)} %param.5) | copy-start | bytes 1572868
  3.2 4.1 %copy-start.3 = (s32[128,8]{0,1:T(8,128)S(1)}, s32[128,8]{0,1:T(8,128)}, u32[]{:S(2)}) copy-start(s32[128,8]{0,1:T(8,128)} %param.6) | copy-start | bytes 12292
  3.2 4.1 %slice-start = ((bf16[128,2048]{1,0:T(8,128)(2,1)}), bf16[128,1280]{1,0:T(8,128)(2,1)S(1)}, s32[]{:S(2)}) async-start(bf16[128,2048]{1,0:T(8,128)(2,1)} %param.5), calls=%async_computation.1 | async-start | bytes 655360 | tf_op jit(solution)/shard_map/slice | solution.py:346
  3.2 6.8 %copy-start.1 = (bf16[4,96,2048]{2,1,0:T(8,128)(2,1)S(1)}, bf16[4,96,2048]{2,1,0:T(8,128)(2,1)}, u32[]{:S(2)}) copy-start(bf16[4,96,2048]{2,1,0:T(8,128)(2,1)} %param.9) | copy-start | bytes 4718596
  4.4 39.3 %collective-permute-start.5 = (bf16[1408,384]{1,0:T(8,128)(2,1)}, bf16[1408,384]{1,0:T(8,128)(2,1)}, u32[]{:S(2)}, u32[]{:S(2)}) collective-permute-start(bf16[1408,384]{1,0:T(8,128)(2,1)} %pad_maximum_fusion), channel_id=1, source_target_pairs={{0,16},{4,20},{8,24},{12,28},{16,0},{20,4},{24,8},{28,12},{1,17},{... | collective-permute-start | bytes 3244040 | tf_op jit(solution)/shard_map/ppermute | solution.py:328
  7.4 20.5 %collective-permute-start.1 = (bf16[144,1280]{1,0:T(8,128)(2,1)S(1)}, bf16[144,1280]{1,0:T(8,128)(2,1)}, u32[]{:S(2)}, u32[]{:S(2)}) collective-permute-start(bf16[144,1280]{1,0:T(8,128)(2,1)S(1)} %fusion.1.refs_0_), channel_id=1, source_target_pairs={{0,2},{1,3},{2,0},{3,1},{4,6},{5,7},{6,4},{7,5},{8,10},{9,11},{10,... | collective-permute-start | bytes 1105928 | tf_op jit(solution)/shard_map/ppermute | solution.py:335
  10.0 36.0 %collective-permute-start.15 = (bf16[1,4,96,2048]{3,2,1,0:T(8,128)(2,1)S(1)}, bf16[1,4,96,2048]{3,2,1,0:T(8,128)(2,1)}, u32[]{:S(2)}, u32[]{:S(2)}) collective-permute-start(bf16[1,4,96,2048]{3,2,1,0:T(8,128)(2,1)S(1)} %bitcast.15), channel_id=1, source_target_pairs={{0,8},{4,12},{8,0},{12,4},{16,24},{20,28},{24,16},{28,20},{1,9},{5... | collective-permute-start | bytes 4718600 | tf_op jit(solution)/shard_map/ppermute | solution.py:328
  11.5 17.7 %collective-permute-start = (bf16[144,1280]{1,0:T(8,128)(2,1)S(1)}, bf16[144,1280]{1,0:T(8,128)(2,1)}, u32[]{:S(2)}, u32[]{:S(2)}) collective-permute-start(bf16[144,1280]{1,0:T(8,128)(2,1)S(1)} %fusion.1.refs_0_), channel_id=1, source_target_pairs={{0,1},{1,2},{2,3},{4,5},{5,6},{6,7},{8,9},{9,10},{10,11},{12,13},{... | collective-permute-start | bytes 1105928 | tf_op jit(solution)/shard_map/ppermute | solution.py:336
  15.7 19.0 %collective-permute-start.2 = (bf16[144,1280]{1,0:T(8,128)(2,1)S(1)}, bf16[144,1280]{1,0:T(8,128)(2,1)}, u32[]{:S(2)}, u32[]{:S(2)}) collective-permute-start(bf16[144,1280]{1,0:T(8,128)(2,1)S(1)} %fusion.1.refs_0_), channel_id=1, source_target_pairs={{1,0},{2,1},{3,2},{5,4},{6,5},{7,6},{9,8},{10,9},{11,10},{13,12},{... | collective-permute-start | bytes 1105928 | tf_op jit(solution)/shard_map/ppermute | solution.py:337
  27.8 13.8 %collective-permute-start.3 = (bf16[144,1280]{1,0:T(8,128)(2,1)}, bf16[144,1280]{1,0:T(8,128)(2,1)}, u32[]{:S(2)}, u32[]{:S(2)}) collective-permute-start(bf16[144,1280]{1,0:T(8,128)(2,1)} %collective-permute-done.1.refs_2_), channel_id=1, source_target_pairs={{2,3},{1,0},{6,7},{5,4},{10,11},{9,8},{14,15},{13,12},{18,19},{17,... | collective-permute-start | bytes 1105928 | tf_op jit(solution)/shard_map/ppermute | solution.py:338
  29.2 16.0 %slice-start.1 = ((bf16[128,2048]{1,0:T(8,128)(2,1)}), bf16[128,768]{1,0:T(8,128)(2,1)S(1)}, s32[]{:S(2)}) async-start(bf16[128,2048]{1,0:T(8,128)(2,1)} %param.5), calls=%async_computation.2 | async-start | bytes 393216 | tf_op jit(solution)/shard_map/slice | solution.py:369
  41.7 23.2 %copy-start = (bf16[1,4,4,72,768]{4,3,2,1,0:T(8,128)(2,1)S(1)}, bf16[1,4,4,72,768]{4,3,2,1,0:T(8,128)(2,1)}, u32[]{:S(2)}) copy-start(bf16[1,4,4,72,768]{4,3,2,1,0:T(8,128)(2,1)} %refs_10_.1) | copy-start | bytes 5308420
  43.7 30.8 %collective-permute-start.6 = (bf16[528,1280]{1,0:T(8,128)(2,1)S(1)}, bf16[528,1280]{1,0:T(8,128)(2,1)S(1)}, u32[]{:S(2)}, u32[]{:S(2)}) collective-permute-start(bf16[528,1280]{1,0:T(8,128)(2,1)S(1)} %shard_map.76.tab_ref.refs_0_), channel_id=1, source_target_pairs={{0,16},{4,20},{8,24},{12,28},{16,0},{20,4},{24,8},{28,12},{1,17},{... | collective-permute-start | bytes 4055048 | tf_op jit(solution)/shard_map/ppermute | solution.py:328
  45.2 18.4 %collective-permute-start.8 = (bf16[256,768]{1,0:T(8,128)(2,1)S(1)}, bf16[256,768]{1,0:T(8,128)(2,1)S(1)}, u32[]{:S(2)}, u32[]{:S(2)}) collective-permute-start(bf16[256,768]{1,0:T(8,128)(2,1)S(1)} %maximum_maximum_fusion.refs_1_.refs_7_), channel_id=1, source_target_pairs={{0,2},{1,3},{2,0},{3,1},{4,6},{5,7},{6,4},{7,5},{8,10},{9,11},{10,... | collective-permute-start | bytes 1179656 | tf_op jit(solution)/shard_map/ppermute | solution.py:335
  46.0 41.4 %collective-permute-start.16 = (bf16[1,4,96,2048]{3,2,1,0:T(8,128)(2,1)}, bf16[1,4,96,2048]{3,2,1,0:T(8,128)(2,1)S(1)}, u32[]{:S(2)}, u32[]{:S(2)}) collective-permute-start(bf16[1,4,96,2048]{3,2,1,0:T(8,128)(2,1)} %collective-permute-done.15.refs_8_), channel_id=1, source_target_pairs={{0,4},{4,0},{8,12},{12,8},{16,20},{20,16},{24,28},{28,24},{1,5},{5... | collective-permute-start | bytes 4718600 | tf_op jit(solution)/shard_map/ppermute | solution.py:328
  46.0 32.9 %collective-permute-start.7 = (bf16[256,768]{1,0:T(8,128)(2,1)S(1)}, bf16[256,768]{1,0:T(8,128)(2,1)S(1)}, u32[]{:S(2)}, u32[]{:S(2)}) collective-permute-start(bf16[256,768]{1,0:T(8,128)(2,1)S(1)} %maximum_maximum_fusion.refs_1_.refs_7_), channel_id=1, source_target_pairs={{0,1},{1,2},{2,3},{4,5},{5,6},{6,7},{8,9},{9,10},{10,11},{12,13},{... | collective-permute-start | bytes 1179656 | tf_op jit(solution)/shard_map/ppermute | solution.py:336
  49.5 29.4 %collective-permute-start.9 = (bf16[256,768]{1,0:T(8,128)(2,1)S(1)}, bf16[256,768]{1,0:T(8,128)(2,1)S(1)}, u32[]{:S(2)}, u32[]{:S(2)}) collective-permute-start(bf16[256,768]{1,0:T(8,128)(2,1)S(1)} %maximum_maximum_fusion.refs_1_.refs_7_), channel_id=1, source_target_pairs={{1,0},{2,1},{3,2},{5,4},{6,5},{7,6},{9,8},{10,9},{11,10},{13,12},{... | collective-permute-start | bytes 1179656 | tf_op jit(solution)/shard_map/ppermute | solution.py:337
  63.6 15.8 %collective-permute-start.10 = (bf16[256,768]{1,0:T(8,128)(2,1)S(1)}, bf16[256,768]{1,0:T(8,128)(2,1)S(1)}, u32[]{:S(2)}, u32[]{:S(2)}) collective-permute-start(bf16[256,768]{1,0:T(8,128)(2,1)S(1)} %collective-permute-done.8.refs_3_.refs_9_), channel_id=1, source_target_pairs={{2,3},{1,0},{6,7},{5,4},{10,11},{9,8},{14,15},{13,12},{18,19},{17,... | collective-permute-start | bytes 1179656 | tf_op jit(solution)/shard_map/ppermute | solution.py:338
  78.9 6.1 %collective-permute-start.11 = (bf16[1,4,96,512]{3,2,1,0:T(8,128)(2,1)S(1)}, bf16[1,4,96,512]{3,2,1,0:T(8,128)(2,1)S(1)}, u32[]{:S(2)}, u32[]{:S(2)}) collective-permute-start(bf16[1,4,96,512]{3,2,1,0:T(8,128)(2,1)S(1)} %get-tuple-element.37), channel_id=1, source_target_pairs={{0,4},{4,0},{8,12},{12,8},{16,20},{20,16},{24,28},{28,24},{1,5},{5... | collective-permute-start | bytes 1179656 | tf_op jit(solution)/shard_map/ppermute | solution.py:328
  82.6 1.8 %collective-permute-start.13 = (bf16[1,4,96,512]{3,2,1,0:T(8,128)(2,1)S(1)}, bf16[1,4,96,512]{3,2,1,0:T(8,128)(2,1)S(1)}, u32[]{:S(2)}, u32[]{:S(2)}) collective-permute-start(bf16[1,4,96,512]{3,2,1,0:T(8,128)(2,1)S(1)} %get-tuple-element.42), channel_id=1, source_target_pairs={{0,4},{4,0},{8,12},{12,8},{16,20},{20,16},{24,28},{28,24},{1,5},{5... | collective-permute-start | bytes 1179656 | tf_op jit(solution)/shard_map/ppermute | solution.py:328
  82.7 2.2 %collective-permute-start.14 = (bf16[1,4,96,512]{3,2,1,0:T(8,128)(2,1)S(1)}, bf16[1,4,96,512]{3,2,1,0:T(8,128)(2,1)S(1)}, u32[]{:S(2)}, u32[]{:S(2)}) collective-permute-start(bf16[1,4,96,512]{3,2,1,0:T(8,128)(2,1)S(1)} %get-tuple-element.43), channel_id=1, source_target_pairs={{0,4},{4,0},{8,12},{12,8},{16,20},{20,16},{24,28},{28,24},{1,5},{5... | collective-permute-start | bytes 1179656 | tf_op jit(solution)/shard_map/ppermute | solution.py:328
  83.1 2.3 %collective-permute-start.12 = (bf16[1,4,96,512]{3,2,1,0:T(8,128)(2,1)S(1)}, bf16[1,4,96,512]{3,2,1,0:T(8,128)(2,1)S(1)}, u32[]{:S(2)}, u32[]{:S(2)}) collective-permute-start(bf16[1,4,96,512]{3,2,1,0:T(8,128)(2,1)S(1)} %get-tuple-element.41), channel_id=1, source_target_pairs={{0,4},{4,0},{8,12},{12,8},{16,20},{20,16},{24,28},{28,24},{1,5},{5... | collective-permute-start | bytes 1179656 | tf_op jit(solution)/shard_map/ppermute | solution.py:328
  85.9 36.7 %collective-permute-start.20 = (bf16[1,4,96,2048]{3,2,1,0:T(8,128)(2,1)S(1)}, bf16[1,4,96,2048]{3,2,1,0:T(8,128)(2,1)S(1)}, u32[]{:S(2)}, u32[]{:S(2)}) collective-permute-start(bf16[1,4,96,2048]{3,2,1,0:T(8,128)(2,1)S(1)} %shard_map.81), channel_id=1, source_target_pairs={{0,8},{4,12},{8,0},{12,4},{16,24},{20,28},{24,16},{28,20},{1,9},{5... | collective-permute-start | bytes 4718600 | tf_op jit(solution)/shard_map/ppermute | solution.py:328
  95.0 3.7 %collective-permute-start.17 = (f32[4,4,128]{2,1,0:T(4,128)S(1)}, f32[4,4,128]{2,1,0:T(4,128)S(1)}, u32[]{:S(2)}, u32[]{:S(2)}) collective-permute-start(f32[4,4,128]{2,1,0:T(4,128)S(1)} %bitcast.19), channel_id=1, source_target_pairs={{0,16},{4,20},{8,24},{12,28},{16,0},{20,4},{24,8},{28,12},{1,17},{... | collective-permute-start | bytes 24584 | tf_op jit(solution)/shard_map/ppermute | solution.py:328
  98.7 23.8 %collective-permute-start.21 = (bf16[4,4,72,384]{3,2,1,0:T(8,128)(2,1)S(1)}, bf16[4,4,72,384]{3,2,1,0:T(8,128)(2,1)S(1)}, u32[]{:S(2)}, u32[]{:S(2)}) collective-permute-start(bf16[4,4,72,384]{3,2,1,0:T(8,128)(2,1)S(1)} %get-tuple-element.57), channel_id=1, source_target_pairs={{0,16},{4,20},{8,24},{12,28},{16,0},{20,4},{24,8},{28,12},{1,17},{... | collective-permute-start | bytes 2654216 | tf_op jit(solution)/shard_map/ppermute | solution.py:328
  113.0 9.1 %collective-permute-start.18 = (bf16[1,4,96,1024]{3,2,1,0:T(8,128)(2,1)S(1)}, bf16[1,4,96,1024]{3,2,1,0:T(8,128)(2,1)S(1)}, u32[]{:S(2)}, u32[]{:S(2)}) collective-permute-start(bf16[1,4,96,1024]{3,2,1,0:T(8,128)(2,1)S(1)} %get-tuple-element.54), channel_id=1, source_target_pairs={{0,4},{4,0},{8,12},{12,8},{16,20},{20,16},{24,28},{28,24},{1,5},{5... | collective-permute-start | bytes 2359304 | tf_op jit(solution)/shard_map/ppermute | solution.py:328
  113.1 9.0 %collective-permute-start.19 = (bf16[1,4,96,1024]{3,2,1,0:T(8,128)(2,1)S(1)}, bf16[1,4,96,1024]{3,2,1,0:T(8,128)(2,1)S(1)}, u32[]{:S(2)}, u32[]{:S(2)}) collective-permute-start(bf16[1,4,96,1024]{3,2,1,0:T(8,128)(2,1)S(1)} %get-tuple-element.55), channel_id=1, source_target_pairs={{0,4},{4,0},{8,12},{12,8},{16,20},{20,16},{24,28},{28,24},{1,5},{5... | collective-permute-start | bytes 2359304 | tf_op jit(solution)/shard_map/ppermute | solution.py:328

commit v6 on v5

--- a/solution.py
+++ b/solution.py
@@ -9,6 +9,7 @@
 
 EXPERTS = 16
 CAP = 72
+PADDED = 80
 BF = jnp.bfloat16
 F32 = jnp.float32
 SHORT = pl.CostEstimate(flops=1, bytes_accessed=1, transcendentals=0)
@@ -35,7 +36,7 @@
             w_row, r_row = table[at : at + 1], rank[at : at + 1]
             place = jnp.where(slots == r_row, w_row, 0.0).astype(BF)
             moved = lax.dot_general(
-                hid_ref[0, e, s], place, (((0,), (0,)), ((), ())), preferred_element_type=F32
+                hid_ref[0, e, s, :CAP], place, (((0,), (0,)), ((), ())), preferred_element_type=F32
             )
             hst_ref[e, :, k * toks : (k + 1) * toks] = moved.astype(BF)
             wt_ref[k, e] = w_row
@@ -53,8 +54,8 @@
             num_scalar_prefetch=1,
             grid=(1,),
             in_specs=[
-                pl.BlockSpec((lines, toks), lambda i, sc: (n * toks // lines, 0)),
-                pl.BlockSpec((1, experts, n, CAP, f), lambda i, sc: (0, 0, 0, 0, sc[1] if whole else 0)),
+                pl.BlockSpec((lines, toks), lambda i, sc: ((n - 1) * toks // lines, 0)),
+                pl.BlockSpec((1, experts, n, hid.shape[3], f), lambda i, sc: (0, 0, 0, 0, sc[1] if whole else 0)),
             ],
             out_specs=(
                 pl.BlockSpec((experts, f, n * toks), lambda i, sc: (0, 0, 0)),
@@ -67,52 +68,84 @@
     )(scalars, tokens, hid)
 
 
+def pack_kernel(lefts, sc_ref, hid_ref, tok_ref, out_ref):
+    _, experts, n, cap, f = hid_ref.shape
+    toks = tok_ref.shape[0]
+    for e in range(experts):
+        for s in range(n):
+            at = (e * n + s) * PADDED
+            out_ref[at : at + cap] = hid_ref[0, e, s]
+            out_ref[at + cap : at + PADDED] = jnp.zeros((PADDED - cap, f), BF)
+    for i, left in enumerate(lefts):
+        at = experts * n * PADDED + i * toks
+        out_ref[at : at + toks] = tok_ref[:, left : left + f]
+
+
+def pack(scalars, hid, tok, lefts, f):
+    _, experts, n, cap, _ = hid.shape
+    rows = experts * n * PADDED + len(lefts) * tok.shape[0]
+    return pl.pallas_call(
+        functools.partial(pack_kernel, lefts),
+        out_shape=jax.ShapeDtypeStruct((rows, f), BF),
+        grid_spec=pltpu.PrefetchScalarGridSpec(
+            num_scalar_prefetch=1,
+            grid=(1,),
+            in_specs=[
+                pl.BlockSpec((1, experts, n, cap, f), lambda i, sc: (0, 0, 0, 0, 1 - sc[1])),
+                pl.BlockSpec(tok.shape, lambda i, sc: (0, 0)),
+            ],
+            out_specs=pl.BlockSpec((rows, f), lambda i, sc: (0, 0)),
+        ),
+        compiler_params=pltpu.CompilerParams(vmem_limit_bytes=12 << 20),
+        cost_estimate=SHORT,
+    )(scalars, hid, tok)
+
+
 def below_kernel(n, experts, sc_ref, *refs):
     *blocks, out_ref = refs
     z = sc_ref[0]
-    toks = blocks[0].shape[0] - EXPERTS
+    toks = blocks[0].shape[0] - EXPERTS // 2
     line = iota((EXPERTS, toks), 0)
 
-    def put(k, ref):
-        out_ref[k * toks : (k + 1) * toks] = ref[:toks]
-        table = ref[toks:, :toks].astype(F32)
-        rows = [
+    def local(ref):
+        table = ref[toks:, : 2 * toks].astype(F32)
+        table = jnp.concatenate([table[:, :toks], table[:, toks:]], axis=0)
+        return [
             jnp.sum(jnp.where(line == z * experts + e, table, 0.0), axis=0, keepdims=True)
             for e in range(experts)
         ]
-        return rows
-
-    tables = [put(k, blocks[k]) for k in range(n)]
+
+    tables = [local(blocks[k]) for k in range(n)]
+    for k in range(1, n):
+        out_ref[(k - 1) * toks : k * toks] = blocks[k][:toks]
     if len(blocks) > n:
         passed = blocks[n]
-        rows = [
-            jnp.sum(jnp.where(line == z * experts + e, passed[toks:, :toks].astype(F32), 0.0), axis=0, keepdims=True)
-            for e in range(experts)
-        ]
+        rows = local(passed)
         for k, place in ((1, 0), (n - 1, n - 1)):
             tables[k] = [jnp.where(z == place, new, old) for new, old in zip(rows, tables[k])]
 
             @pl.when(z == place)
             def _():
-                out_ref[k * toks : (k + 1) * toks] = passed[:toks]
+                out_ref[(k - 1) * toks : k * toks] = passed[:toks]
 
     rows = [row for table in tables for row in table]
-    out_ref[n * toks :, :toks] = jnp.concatenate(rows, axis=0).astype(BF)
+    out_ref[(n - 1) * toks :, :toks] = jnp.concatenate(rows, axis=0).astype(BF)
 
 
 def below(n, experts, scalars, blocks):
     rows, cols = blocks[0].shape
-    toks = rows - EXPERTS
+    toks = rows - EXPERTS // 2
+    height = (n - 1) * toks + n * experts
     return pl.pallas_call(
         functools.partial(below_kernel, n, experts),
-        out_shape=jax.ShapeDtypeStruct((n * (toks + experts), cols), BF),
+        out_shape=jax.ShapeDtypeStruct((height, cols), BF),
         grid_spec=pltpu.PrefetchScalarGridSpec(
             num_scalar_prefetch=1,
             grid=(1,),
             in_specs=[pl.BlockSpec((rows, cols), lambda i, sc: (0, 0))] * len(blocks),
-            out_specs=pl.BlockSpec((n * (toks + experts), cols), lambda i, sc: (0, 0)),
-        ),
-        compiler_params=pltpu.CompilerParams(vmem_limit_bytes=12 << 20),
+            out_specs=pl.BlockSpec((height, cols), lambda i, sc: (0, 0)),
+        ),
+        compiler_params=pltpu.CompilerParams(vmem_limit_bytes=24 << 20),
         cost_estimate=SHORT,
     )(scalars, *blocks)
 
@@ -167,7 +200,7 @@
             zk = z[k * toks : (k + 1) * toks, e * f : (e + 1) * f]
             gh_ref[e, s] = jnp.dot(weigh, zk.astype(BF), preferred_element_type=F32).astype(BF)
             hid = lax.dot_general(
-                pick, hid_ref[0, e, s], (((0,), (0,)), ((), ())), preferred_element_type=F32
+                pick, hid_ref[0, e, s, :CAP], (((0,), (0,)), ((), ())), preferred_element_type=F32
             )
             sg_col = jnp.sum(zk * hid, axis=1, keepdims=True)
             sg_ref[s, e] = jnp.sum(jnp.where(eye, sg_col, 0.0), axis=0, keepdims=True)
@@ -195,7 +228,7 @@
                 for _, _, i in w_pieces
             ]
             + [
-                pl.BlockSpec((1, group, n, CAP, f), lambda e, sc: (0, e, 0, 0, sc[1] if whole else 0)),
+                pl.BlockSpec((1, group, n, hid.shape[3], f), lambda e, sc: (0, e, 0, 0, sc[1] if whole else 0)),
                 row_spec,
                 row_spec,
             ],
@@ -341,19 +374,21 @@
     ids = expert_ids[None] == jnp.arange(EXPERTS, dtype=jnp.int32)[:, None, None]
     table = jnp.sum(jnp.where(ids, route_weights.astype(F32)[None], 0.0), axis=2).astype(BF)
 
-    cut = 10 * d // 16
-    table = jnp.pad(table, ((0, 0), (0, cut - toks)))
+    cut = 11 * d // 16
+    table = jnp.concatenate([table[: EXPERTS // 2], table[EXPERTS // 2 :]], axis=1)
+    table = jnp.pad(table, ((0, 0), (0, cut - 2 * toks)))
     blocks = spread(jnp.concatenate([grad_out[:, :cut], table], axis=0))
     w_core = swap(w_down[None], 1)
-    outgoing = lax.dynamic_slice_in_dim(hidden_cache, (1 - upper) * f, f, axis=4).reshape(-1, f)
-    lefts = [min(left, d - f) for left in range(cut, d, f)]
-    outgoing = [outgoing] + [grad_out[:, left : left + f] for left in lefts]
-    incoming = swap(after(jnp.concatenate(outgoing, axis=0), w_core), bands)
-    count = hidden_cache.size // (2 * f)
-    hid_nb = incoming[:count].reshape(1, experts, n, CAP, f)
-    pair = [
-        incoming[count + i * toks : count + (i + 1) * toks, cut + i * f - left :] for i, left in enumerate(lefts)
-    ]
+    scalars = jnp.stack([z, upper, j]).astype(jnp.int32)
+    lefts = [min(left, d - f) for left in range(0, d, f)]
+    outgoing = pack(scalars, hidden_cache, grad_out, lefts, f)
+    incoming = swap(after(outgoing, w_core), bands)
+    count = experts * n * PADDED
+    hid_nb = incoming[:count].reshape(1, experts, n, PADDED, f)
+    first_nb = jnp.concatenate(
+        [incoming[count + i * toks : count + (i + 1) * toks, i * f - left :] for i, left in enumerate(lefts)], axis=1
+    )
+    first_nb, pair = first_nb[:, :cut], first_nb[:, cut:]
     w_pieces = [(0, w_down[None], 0), (1, w_core, 0)]
     bit = 2
     while bit < bands:
@@ -363,16 +398,15 @@
             w_pieces += [(w_pieces[2 * i][0] ^ bit, far, i), (w_pieces[2 * i][0] ^ bit ^ 1, there, i)]
         bit *= 2
 
-    scalars = jnp.stack([z, upper, j]).astype(jnp.int32)
     mine = below(n, experts, scalars, blocks)
     hs_own, wt_own, rank_own = hidden_to_tokens(n, experts, toks, scalars, mine, hidden_cache, f, True)
-    rest = jnp.concatenate([grad_out[:, cut:], jnp.concatenate(pair, axis=1)], axis=0)
+    rest = jnp.concatenate([grad_out[:, cut:], pair], axis=0)
     rests = spread(after(rest, *blocks))
     nb_a = swap(after(mine, incoming), bands)
     hs_nb, wt_nb, rank_nb = hidden_to_tokens(n, experts, toks, scalars, nb_a, hid_nb, f, False)
 
-    own_pieces = [[(mine, (n * toks, cut), (0, 0))], [(b, (toks, d - cut), (0, 0)) for b in rests]]
-    nb_pieces = [[(nb_a, (n * toks, cut), (0, 0))], [(b, (toks, d - cut), (1, 0)) for b in rests]]
+    own_pieces = [[(blocks[0], (toks, cut), (0, 0)), (mine, ((n - 1) * toks, cut), (0, 0))], [(b, (toks, d - cut), (0, 0)) for b in rests]]
+    nb_pieces = [[(first_nb, (toks, cut), (0, 0)), (nb_a, ((n - 1) * toks, cut), (0, 0))], [(b, (toks, d - cut), (1, 0)) for b in rests]]
 
     if band % 16:
         w = jnp.zeros((experts, f, d), BF)

time: 126 us -> 121 us (0.960)
  waiting for transfers between devices: 49.1 us -> 46.6 us
  Pallas kernels: 35 us -> 32.6 us
  blocking collectives: 7.92 us -> 9.81 us
  other arithmetic: 2.55 us -> 0.83 us
    ppermute x14, waiting for transfers between devices: 12.6 us -> 9.72 us  [swap(): return lax.ppermute(x, 'dp', [(i, i ^ bit) for i in range(n_dp)])]
    ppermute x2, starting transfers between devices: 2.73 us -> 5.31 us  [spread(): two = lax.ppermute(x, 'expert', [(i, (i + 2) % n) for i in range(n)])]
    unnamed x8 -> x12, local copies, waits for them, and re-layouts: 0.02 us -> 2.54 us
    pallas_call x2, Pallas kernels: 15.8 us -> 13.7 us  [backward(): pl.pallas_call(functools.partial(back_kernel, n, counts, group, rels), ou...]
    slice x5 -> x6, local copies, waits for them, and re-layouts: 2.24 us -> 0.17 us  [the longest x1 0.1 us: per_device(): hid_nb = incoming[:count].reshape(1, experts, n, PADDED, f)]
    all_to_all x1, blocking collectives: 7.92 us -> 9.81 us  [per_device(): lax.all_to_all(sg, 'expert', split_axis=0, concat_axis=0, tiled=True)]
    pallas_call x1, Pallas kernels: 1.98 us -> 0.65 us  [below(): pl.pallas_call(functools.partial(below_kernel, n, experts), out_shape=jax...]
    dynamic_slice x1 -> x0, local copies, waits for them, and re-layouts: 1.31 us -> none  [per_device(): lax.dynamic_slice_in_dim(hidden_cache, (1 - upper) * f, f, axis=4)]
  transfers between devices with their start and end apart: 22 -> 22, of which waited for: 12 -> 11; matrix products, arithmetic and copies ran while one was open for 5% -> 1% of each run, Pallas kernels for 26% -> 25%
where the time goes in v6:
time: 121 us
  waiting for transfers between devices  46.6 us (39%)
  Pallas kernels  32.6 us (27%)
  starting transfers between devices  27.1 us (22%)
  blocking collectives  9.81 us (8%)
  local copies, waits for them, and re-layouts  2.71 us (2%)
    ppermute x2, waiting for transfers between devices, spread(): two = lax.ppermute(x, 'expert', [(i, (i + 2) % n) for i in range(n)])  24.1 us
    pallas_call x2, Pallas kernels, backward(): pl.pallas_call(functools.partial(back_kernel, n, counts, group, rels), ou...  13.7 us
    pallas_call x3, Pallas kernels, partial_grad(): pl.pallas_call(functools.partial(part_kernel, n, bands, (counts, counts_n...  11.5 us
    all_to_all x1, blocking collectives, per_device(): lax.all_to_all(sg, 'expert', split_axis=0, concat_axis=0, tiled=True)  9.81 us
    ppermute x14, waiting for transfers between devices, swap(): return lax.ppermute(x, 'dp', [(i, i ^ bit) for i in range(n_dp)])  9.72 us
    ppermute x14, starting transfers between devices, swap(): return lax.ppermute(x, 'dp', [(i, i ^ bit) for i in range(n_dp)])  9.64 us
    ppermute x2, waiting for transfers between devices, spread(): passed = lax.ppermute(two, 'expert', [(2, 3), (1, 0)])  8.05 us
    ppermute x2, starting transfers between devices, spread(): one = lax.ppermute(x, 'expert', [(i, i + 1) for i in range(n - 1)])  6.98 us
  transfers between devices with their start and end apart: 22, of which 11 were waited for; matrix products, arithmetic and copies ran while one was open for 1% of the time, Pallas kernels for 25%

profile of v6, /device:TPU:0, one launch (start us, length us, event | category | flops | bytes accessed | tf_op | source)
XLA Modules:
  0.0 120.5 jit_solution(2747313148095289024)
XLA Ops:
  0.6 0.5 collective-permute-start.4
  1.1 0.1 pad_add_fusion.sc_ref
  1.2 1.5 %copy-done = bf16[1,4,4,72,768]{4,3,2,1,0:T(8,128)(2,1)S(1)} copy-done((bf16[1,4,4,72,768]{4,3,2,1,0:T(8,128)(2,1)S(1)}, bf16[1,4,4,72,768]{4,3,2,1,0:T(8,128)(2,1)}, u32[]{:S(2)}) %copy-start) | copy-done | bytes 1769496
  2.7 1.0 copy-done.3
  3.8 0.8 shard_map.77
  4.5 2.7 %collective-permute-start.5 = (bf16[2048,384]{1,0:T(8,128)(2,1)S(1)}, bf16[2048,384]{1,0:T(8,128)(2,1)S(1)}, u32[]{:S(2)}, u32[]{:S(2)}) collective-permute-start(bf16[2048,384]{1,0:T(8,128)(2,1)S(1)} %shard_map.77), channel_id=1, source_target_pairs={{0,16},{4,20},{8,24},{12,28},{16,0},{20,4},{24,8},{28,12},{1,17},{... | collective-permute-start | bytes 4718600 | tf_op jit(solution)/shard_map/ppermute | solution.py:361
  7.3 1.5 %collective-permute-start.15 = (bf16[1,4,96,2048]{3,2,1,0:T(8,128)(2,1)S(1)}, bf16[1,4,96,2048]{3,2,1,0:T(8,128)(2,1)S(1)}, u32[]{:S(2)}, u32[]{:S(2)}) collective-permute-start(bf16[1,4,96,2048]{3,2,1,0:T(8,128)(2,1)S(1)} %bitcast.14), channel_id=1, source_target_pairs={{0,8},{4,12},{8,0},{12,4},{16,24},{20,28},{24,16},{28,20},{1,9},{5... | collective-permute-start | bytes 4718600 | tf_op jit(solution)/shard_map/ppermute | solution.py:361
  8.9 2.7 %collective-permute-start.1 = (bf16[136,1408]{1,0:T(8,128)(2,1)S(1)}, bf16[136,1408]{1,0:T(8,128)(2,1)S(1)}, u32[]{:S(2)}, u32[]{:S(2)}) collective-permute-start(bf16[136,1408]{1,0:T(8,128)(2,1)S(1)} %pad_maximum_fusion.refs_0_), channel_id=1, source_target_pairs={{0,2},{1,3},{2,0},{3,1},{4,6},{5,7},{6,4},{7,5},{8,10},{9,11},{10,... | collective-permute-start | bytes 1148936 | tf_op jit(solution)/shard_map/ppermute | solution.py:368
  11.6 3.5 %collective-permute-start = (bf16[136,1408]{1,0:T(8,128)(2,1)S(1)}, bf16[136,1408]{1,0:T(8,128)(2,1)S(1)}, u32[]{:S(2)}, u32[]{:S(2)}) collective-permute-start(bf16[136,1408]{1,0:T(8,128)(2,1)S(1)} %pad_maximum_fusion.refs_0_), channel_id=1, source_target_pairs={{0,1},{1,2},{2,3},{4,5},{5,6},{6,7},{8,9},{9,10},{10,11},{12,13},{... | collective-permute-start | bytes 1148936 | tf_op jit(solution)/shard_map/ppermute | solution.py:369
  15.1 1.3 %collective-permute-start.2 = (bf16[136,1408]{1,0:T(8,128)(2,1)S(1)}, bf16[136,1408]{1,0:T(8,128)(2,1)S(1)}, u32[]{:S(2)}, u32[]{:S(2)}) collective-permute-start(bf16[136,1408]{1,0:T(8,128)(2,1)S(1)} %pad_maximum_fusion.refs_0_), channel_id=1, source_target_pairs={{1,0},{2,1},{3,2},{5,4},{6,5},{7,6},{9,8},{10,9},{11,10},{13,12},{... | collective-permute-start | bytes 1148936 | tf_op jit(solution)/shard_map/ppermute | solution.py:370
  16.4 13.5 %collective-permute-done.1.refs_2_ = bf16[136,1408]{1,0:T(8,128)(2,1)S(1)} collective-permute-done((bf16[136,1408]{1,0:T(8,128)(2,1)S(1)}, bf16[136,1408]{1,0:T(8,128)(2,1)S(1)}, u32[]{:S(2)}, u32[]{:S(2)}) %collective-permute-start.1) | collective-permute-done | bytes 383008 | tf_op jit(solution)/shard_map/ppermute | solution.py:368
  29.8 1.3 %collective-permute-start.3 = (bf16[136,1408]{1,0:T(8,128)(2,1)S(1)}, bf16[136,1408]{1,0:T(8,128)(2,1)S(1)}, u32[]{:S(2)}, u32[]{:S(2)}) collective-permute-start(bf16[136,1408]{1,0:T(8,128)(2,1)S(1)} %collective-permute-done.1.refs_2_), channel_id=1, source_target_pairs={{2,3},{1,0},{6,7},{5,4},{10,11},{9,8},{14,15},{13,12},{18,19},{17,... | collective-permute-start | bytes 1148936 | tf_op jit(solution)/shard_map/ppermute | solution.py:371
  31.1 4.7 %collective-permute-done.2.refs_3_ = bf16[136,1408]{1,0:T(8,128)(2,1)S(1)} collective-permute-done((bf16[136,1408]{1,0:T(8,128)(2,1)S(1)}, bf16[136,1408]{1,0:T(8,128)(2,1)S(1)}, u32[]{:S(2)}, u32[]{:S(2)}) %collective-permute-start.2) | collective-permute-done | bytes 383008 | tf_op jit(solution)/shard_map/ppermute | solution.py:370
  35.8 6.4 %collective-permute-done.3.refs_4_ = bf16[136,1408]{1,0:T(8,128)(2,1)S(1)} collective-permute-done((bf16[136,1408]{1,0:T(8,128)(2,1)S(1)}, bf16[136,1408]{1,0:T(8,128)(2,1)S(1)}, u32[]{:S(2)}, u32[]{:S(2)}) %collective-permute-start.3) | collective-permute-done | bytes 383008 | tf_op jit(solution)/shard_map/ppermute | solution.py:371
  42.3 0.7 shard_map.76.tab_ref.refs_1_
  43.0 1.0 collective-permute-start.6
  44.0 2.7 %collective-permute-start.8 = (bf16[256,640]{1,0:T(8,128)(2,1)S(1)}, bf16[256,640]{1,0:T(8,128)(2,1)S(1)}, u32[]{:S(2)}, u32[]{:S(2)}) collective-permute-start(bf16[256,640]{1,0:T(8,128)(2,1)S(1)} %fusion.refs_2_.refs_9_), channel_id=1, source_target_pairs={{0,2},{1,3},{2,0},{3,1},{4,6},{5,7},{6,4},{7,5},{8,10},{9,11},{10,... | collective-permute-start | bytes 983048 | tf_op jit(solution)/shard_map/ppermute | solution.py:368
  46.7 3.5 %collective-permute-start.7 = (bf16[256,640]{1,0:T(8,128)(2,1)S(1)}, bf16[256,640]{1,0:T(8,128)(2,1)S(1)}, u32[]{:S(2)}, u32[]{:S(2)}) collective-permute-start(bf16[256,640]{1,0:T(8,128)(2,1)S(1)} %fusion.refs_2_.refs_9_), channel_id=1, source_target_pairs={{0,1},{1,2},{2,3},{4,5},{5,6},{6,7},{8,9},{9,10},{10,11},{12,13},{... | collective-permute-start | bytes 983048 | tf_op jit(solution)/shard_map/ppermute | solution.py:369
  50.2 1.3 %collective-permute-start.9 = (bf16[256,640]{1,0:T(8,128)(2,1)S(1)}, bf16[256,640]{1,0:T(8,128)(2,1)S(1)}, u32[]{:S(2)}, u32[]{:S(2)}) collective-permute-start(bf16[256,640]{1,0:T(8,128)(2,1)S(1)} %fusion.refs_2_.refs_9_), channel_id=1, source_target_pairs={{1,0},{2,1},{3,2},{5,4},{6,5},{7,6},{9,8},{10,9},{11,10},{13,12},{... | collective-permute-start | bytes 983048 | tf_op jit(solution)/shard_map/ppermute | solution.py:370
  51.5 10.6 %collective-permute-done.8.refs_4_.refs_11_ = bf16[256,640]{1,0:T(8,128)(2,1)S(1)} collective-permute-done((bf16[256,640]{1,0:T(8,128)(2,1)S(1)}, bf16[256,640]{1,0:T(8,128)(2,1)S(1)}, u32[]{:S(2)}, u32[]{:S(2)}) %collective-permute-start.8) | collective-permute-done | bytes 327712 | tf_op jit(solution)/shard_map/ppermute | solution.py:368
  62.1 1.3 %collective-permute-start.10 = (bf16[256,640]{1,0:T(8,128)(2,1)S(1)}, bf16[256,640]{1,0:T(8,128)(2,1)S(1)}, u32[]{:S(2)}, u32[]{:S(2)}) collective-permute-start(bf16[256,640]{1,0:T(8,128)(2,1)S(1)} %collective-permute-done.8.refs_4_.refs_11_), channel_id=1, source_target_pairs={{2,3},{1,0},{6,7},{5,4},{10,11},{9,8},{14,15},{13,12},{18,19},{17,... | collective-permute-start | bytes 983048 | tf_op jit(solution)/shard_map/ppermute | solution.py:371
  63.4 1.3 %shard_map.78 = (bf16[4,384,512]{2,1,0:T(8,128)(2,1)S(1)}, f32[4,4,1,128]{3,2,1,0:T(1,128)S(1)}, f32[4,4,1,128]{3,2,1,0:T(1,128)S(1)}) custom-call(s32[3]{0:T(128)S(1)} %pad_add_fusion.sc_ref, bf16[400,1408]{1,0:T(8,128)(2,1)S(1)} %shard_map.76.tab_ref.refs_1_, bf16[1,4,4,72,768]{4,3,2,1,0:T(8,128)(2,1)S(1)} %copy-done.1), custom_call_target="tpu_custom_call" | custom-call | flops 1 | bytes 1 | tf_op jit(solution)/shard_map/pallas_call | solution.py:50
  64.7 0.1 slice.60
  64.9 3.8 %collective-permute-done.6.tab_ref.refs_3_.refs_8_.refs_1_ = bf16[400,1408]{1,0:T(8,128)(2,1)S(1)} collective-permute-done((bf16[400,1408]{1,0:T(8,128)(2,1)S(1)}, bf16[400,1408]{1,0:T(8,128)(2,1)S(1)}, u32[]{:S(2)}, u32[]{:S(2)}) %collective-permute-start.6) | collective-permute-done | bytes 1126432 | tf_op jit(solution)/shard_map/ppermute | solution.py:361
  68.7 1.3 %shard_map.79 = (bf16[4,384,512]{2,1,0:T(8,128)(2,1)S(1)}, f32[4,4,1,128]{3,2,1,0:T(1,128)S(1)}, f32[4,4,1,128]{3,2,1,0:T(1,128)S(1)}) custom-call(s32[3]{0:T(128)S(1)} %pad_add_fusion.sc_ref, bf16[400,1408]{1,0:T(8,128)(2,1)S(1)} %collective-permute-done.6.tab_ref.refs_3_.refs_8_.refs_1_, bf16[1,4,4,80,384]{4,3,2,1,0:T(8,128)(2,1)S(1)} %bitcast.11), custom_call_target="tpu_custom_call" | custom-call | flops 1 | bytes 1 | tf_op jit(solution)/shard_map/pallas_call | solution.py:50
  70.0 3.1 %shard_map.80 = (bf16[1,4,96,512]{3,2,1,0:T(8,128)(2,1)S(1)}, bf16[1,4,96,512]{3,2,1,0:T(8,128)(2,1)S(1)}, bf16[1,4,96,1024]{3,2,1,0:T(8,128)(2,1)S(1)}) custom-call(s32[3]{0:T(128)S(1)} %pad_add_fusion.sc_ref, bf16[136,1408]{1,0:T(8,128)(2,1)S(1)} %pad_maximum_fusion.refs_0_, bf16[400,1408]{1,0:T(8,128)(2,1)S(1)} %shard_map.76.tab_ref.refs_1_, ...), custom_call_target="tpu_custom_call" | custom-call | flops 1 | bytes 1 | tf_op jit(solution)/shard_map/pallas_call | solution.py:279
  73.1 0.1 collective-permute-start.11
  73.2 1.6 %collective-permute-done.10.refs_6_.refs_13_ = bf16[256,640]{1,0:T(8,128)(2,1)S(1)} collective-permute-done((bf16[256,640]{1,0:T(8,128)(2,1)S(1)}, bf16[256,640]{1,0:T(8,128)(2,1)S(1)}, u32[]{:S(2)}, u32[]{:S(2)}) %collective-permute-start.10) | collective-permute-done | bytes 327712 | tf_op jit(solution)/shard_map/ppermute | solution.py:371
  74.8 3.3 %shard_map.81 = (bf16[1,4,96,512]{3,2,1,0:T(8,128)(2,1)S(1)}, bf16[1,4,96,512]{3,2,1,0:T(8,128)(2,1)S(1)}, bf16[1,4,96,1024]{3,2,1,0:T(8,128)(2,1)S(1)}) custom-call(s32[3]{0:T(128)S(1)} %pad_add_fusion.sc_ref, bf16[136,1408]{1,0:T(8,128)(2,1)S(1)} %pad_maximum_fusion.refs_0_, bf16[400,1408]{1,0:T(8,128)(2,1)S(1)} %shard_map.76.tab_ref.refs_1_, ...), custom_call_target="tpu_custom_call" | custom-call | flops 1 | bytes 1 | tf_op jit(solution)/shard_map/pallas_call | solution.py:279
  78.2 0.5 collective-permute-start.14
  78.7 0.1 collective-permute-start.12
  78.8 1.1 collective-permute-done.13.refs_4_
  79.9 0.6 collective-permute-done.14.refs_5_
  80.5 0.6 collective-permute-done.12.refs_3_
  81.0 0.4 shard_map.82
  81.5 1.6 %collective-permute-start.20 = (bf16[1,4,96,2048]{3,2,1,0:T(8,128)(2,1)S(1)}, bf16[1,4,96,2048]{3,2,1,0:T(8,128)(2,1)S(1)}, u32[]{:S(2)}, u32[]{:S(2)}) collective-permute-start(bf16[1,4,96,2048]{3,2,1,0:T(8,128)(2,1)S(1)} %shard_map.82), channel_id=1, source_target_pairs={{0,8},{4,12},{8,0},{12,4},{16,24},{20,28},{24,16},{28,20},{1,9},{5... | collective-permute-start | bytes 4718600 | tf_op jit(solution)/shard_map/ppermute | solution.py:361
  83.0 6.5 %shard_map.83 = (bf16[4,4,72,384]{3,2,1,0:T(8,128)(2,1)S(1)}, f32[4,4,1,128]{3,2,1,0:T(1,128)S(1)}) custom-call(s32[3]{0:T(128)S(1)} %pad_add_fusion.sc_ref, bf16[128,1408]{1,0:T(8,128)(2,1)S(1)} %pad_maximum_fusion.1.refs_2_.refs_7_.refs_0_, bf16[400,1408]{1,0:T(8,128)(2,1)S(1)} %collective-permute-done.6.tab_ref.refs_3_.refs_8_.refs_1_, ...), custom_call_target="tpu_custom_call" | custom-call | flops 1 | bytes 1 | tf_op jit(solution)/shard_map/pallas_call | solution.py:216
  89.5 0.6 collective-permute-start.17
  90.1 3.1 %collective-permute-done.17 = f32[4,4,128]{2,1,0:T(4,128)S(1)} collective-permute-done((f32[4,4,128]{2,1,0:T(4,128)S(1)}, f32[4,4,128]{2,1,0:T(4,128)S(1)}, u32[]{:S(2)}, u32[]{:S(2)}) %collective-permute-start.17) | collective-permute-done | bytes 8224 | tf_op jit(solution)/shard_map/ppermute | solution.py:361
  93.2 0.5 collective-permute-start.21
  93.7 7.2 %shard_map.84 = (bf16[4,4,72,768]{3,2,1,0:T(8,128)(2,1)}, f32[4,4,1,128]{3,2,1,0:T(1,128)S(1)}) custom-call(s32[3]{0:T(128)S(1)} %pad_add_fusion.sc_ref, bf16[136,1408]{1,0:T(8,128)(2,1)S(1)} %pad_maximum_fusion.refs_0_, bf16[400,1408]{1,0:T(8,128)(2,1)S(1)} %shard_map.76.tab_ref.refs_1_, bf16[256,640]{1,0:T(8,128)(2,1)S(1)} %fusion.refs_2_.refs_9_, ...), custom_call_target="tpu_custom_call" | custom-call | flops 1 | bytes 1 | tf_op jit(solution)/shard_map/pallas_call | solution.py:216
  100.9 5.1 %shard_map.85 = (bf16[1,4,96,1024]{3,2,1,0:T(8,128)(2,1)S(1)}, bf16[1,4,96,1024]{3,2,1,0:T(8,128)(2,1)S(1)}, bf16[1,4,96,2048]{3,2,1,0:T(8,128)(2,1)S(1)}) custom-call(s32[3]{0:T(128)S(1)} %pad_add_fusion.sc_ref, bf16[136,1408]{1,0:T(8,128)(2,1)S(1)} %pad_maximum_fusion.refs_0_, bf16[400,1408]{1,0:T(8,128)(2,1)S(1)} %shard_map.76.tab_ref.refs_1_, ...), custom_call_target="tpu_custom_call" | custom-call | flops 1 | bytes 1 | tf_op jit(solution)/shard_map/pallas_call | solution.py:279
  106.1 0.5 collective-permute-start.19
  106.6 9.8 %all_to_all.5 = f32[4,4,128]{2,1,0:T(4,128)S(1)} all-to-all(f32[4,4,128]{2,1,0:T(4,128)S(1)} %add.11), channel_id=1, replica_groups=mesh['dp'=8,'expert'=4] {'expert'}, dimensions={0} | all-to-all | bytes 16384 | tf_op jit(solution)/shard_map/all_to_all | solution.py:439
  116.4 0.6 select_reduce_fusion
  117.0 0.4 shard_map.86.base_ref
  117.5 0.5 collective-permute-done.20.there_ref
  118.0 2.5 %shard_map.87 = (bf16[4,96,2048]{2,1,0:T(8,128)(2,1)}, bf16[4,4,72,768]{3,2,1,0:T(8,128)(2,1)}) custom-call(s32[3]{0:T(128)S(1)} %pad_add_fusion.sc_ref, bf16[1,4,96,2048]{3,2,1,0:T(8,128)(2,1)S(1)} %shard_map.86.base_ref, bf16[1,4,96,2048]{3,2,1,0:T(8,128)(2,1)S(1)} %collective-permute-done.20.there_ref, ...), custom_call_target="tpu_custom_call", output_to_operand_aliasing={{1}: (4, {})} | custom-call | flops 1 | bytes 1 | tf_op jit(solution)/shard_map/pallas_call | solution.py:329
  (38 shorter events, 0.4 us)
Async XLA Ops:
  0.6 3.9 %collective-permute-start.4 = (bf16[1,4,96,2048]{3,2,1,0:T(8,128)(2,1)}, bf16[1,4,96,2048]{3,2,1,0:T(8,128)(2,1)S(1)}, u32[]{:S(2)}, u32[]{:S(2)}) collective-permute-start(bf16[1,4,96,2048]{3,2,1,0:T(8,128)(2,1)} %bitcast.13), channel_id=1, source_target_pairs={{0,4},{4,0},{8,12},{12,8},{16,20},{20,16},{24,28},{28,24},{1,5},{5... | collective-permute-start | bytes 4718600 | tf_op jit(solution)/shard_map/ppermute | solution.py:361
  1.2 1.5 %copy-start = (bf16[1,4,4,72,768]{4,3,2,1,0:T(8,128)(2,1)S(1)}, bf16[1,4,4,72,768]{4,3,2,1,0:T(8,128)(2,1)}, u32[]{:S(2)}) copy-start(bf16[1,4,4,72,768]{4,3,2,1,0:T(8,128)(2,1)} %refs_11_.1) | copy-start | bytes 5308420
  2.7 1.0 copy-start.3
  3.7 3.5 %copy-start.2 = (bf16[4,96,2048]{2,1,0:T(8,128)(2,1)S(1)}, bf16[4,96,2048]{2,1,0:T(8,128)(2,1)}, u32[]{:S(2)}) copy-start(bf16[4,96,2048]{2,1,0:T(8,128)(2,1)} %param.9) | copy-start | bytes 4718596
  3.7 5.0 %copy-start.5 = (bf16[128,8]{0,1:T(8,128)(2,1)S(1)}, bf16[128,8]{0,1:T(8,128)(2,1)}, u32[]{:S(2)}) copy-start(bf16[128,8]{0,1:T(8,128)(2,1)} %param.7) | copy-start | bytes 6148
  3.7 5.0 %copy-start.4 = (s32[128,8]{0,1:T(8,128)S(1)}, s32[128,8]{0,1:T(8,128)}, u32[]{:S(2)}) copy-start(s32[128,8]{0,1:T(8,128)} %param.6) | copy-start | bytes 12292
  3.8 5.1 %slice-start = ((bf16[128,2048]{1,0:T(8,128)(2,1)}), bf16[128,1408]{1,0:T(8,128)(2,1)S(1)}, s32[]{:S(2)}) async-start(bf16[128,2048]{1,0:T(8,128)(2,1)} %tok_ref.1), calls=%async_computation.1 | async-start | bytes 720896 | tf_op jit(solution)/shard_map/slice | solution.py:380
  4.5 38.4 %collective-permute-start.5 = (bf16[2048,384]{1,0:T(8,128)(2,1)S(1)}, bf16[2048,384]{1,0:T(8,128)(2,1)S(1)}, u32[]{:S(2)}, u32[]{:S(2)}) collective-permute-start(bf16[2048,384]{1,0:T(8,128)(2,1)S(1)} %shard_map.77), channel_id=1, source_target_pairs={{0,16},{4,20},{8,24},{12,28},{16,0},{20,4},{24,8},{28,12},{1,17},{... | collective-permute-start | bytes 4718600 | tf_op jit(solution)/shard_map/ppermute | solution.py:361
  7.3 39.4 %collective-permute-start.15 = (bf16[1,4,96,2048]{3,2,1,0:T(8,128)(2,1)S(1)}, bf16[1,4,96,2048]{3,2,1,0:T(8,128)(2,1)S(1)}, u32[]{:S(2)}, u32[]{:S(2)}) collective-permute-start(bf16[1,4,96,2048]{3,2,1,0:T(8,128)(2,1)S(1)} %bitcast.14), channel_id=1, source_target_pairs={{0,8},{4,12},{8,0},{12,4},{16,24},{20,28},{24,16},{28,20},{1,9},{5... | collective-permute-start | bytes 4718600 | tf_op jit(solution)/shard_map/ppermute | solution.py:361
  8.9 35.1 %slice-start.1 = ((bf16[128,2048]{1,0:T(8,128)(2,1)}), bf16[128,640]{1,0:T(8,128)(2,1)S(1)}, s32[]{:S(2)}) async-start(bf16[128,2048]{1,0:T(8,128)(2,1)} %tok_ref.1), calls=%async_computation.2 | async-start | bytes 327680 | tf_op jit(solution)/shard_map/slice | solution.py:403
  8.9 20.9 %collective-permute-start.1 = (bf16[136,1408]{1,0:T(8,128)(2,1)S(1)}, bf16[136,1408]{1,0:T(8,128)(2,1)S(1)}, u32[]{:S(2)}, u32[]{:S(2)}) collective-permute-start(bf16[136,1408]{1,0:T(8,128)(2,1)S(1)} %pad_maximum_fusion.refs_0_), channel_id=1, source_target_pairs={{0,2},{1,3},{2,0},{3,1},{4,6},{5,7},{6,4},{7,5},{8,10},{9,11},{10,... | collective-permute-start | bytes 1148936 | tf_op jit(solution)/shard_map/ppermute | solution.py:368
  11.6 19.6 %collective-permute-start = (bf16[136,1408]{1,0:T(8,128)(2,1)S(1)}, bf16[136,1408]{1,0:T(8,128)(2,1)S(1)}, u32[]{:S(2)}, u32[]{:S(2)}) collective-permute-start(bf16[136,1408]{1,0:T(8,128)(2,1)S(1)} %pad_maximum_fusion.refs_0_), channel_id=1, source_target_pairs={{0,1},{1,2},{2,3},{4,5},{5,6},{6,7},{8,9},{9,10},{10,11},{12,13},{... | collective-permute-start | bytes 1148936 | tf_op jit(solution)/shard_map/ppermute | solution.py:369
  15.1 20.8 %collective-permute-start.2 = (bf16[136,1408]{1,0:T(8,128)(2,1)S(1)}, bf16[136,1408]{1,0:T(8,128)(2,1)S(1)}, u32[]{:S(2)}, u32[]{:S(2)}) collective-permute-start(bf16[136,1408]{1,0:T(8,128)(2,1)S(1)} %pad_maximum_fusion.refs_0_), channel_id=1, source_target_pairs={{1,0},{2,1},{3,2},{5,4},{6,5},{7,6},{9,8},{10,9},{11,10},{13,12},{... | collective-permute-start | bytes 1148936 | tf_op jit(solution)/shard_map/ppermute | solution.py:370
  29.8 12.4 %collective-permute-start.3 = (bf16[136,1408]{1,0:T(8,128)(2,1)S(1)}, bf16[136,1408]{1,0:T(8,128)(2,1)S(1)}, u32[]{:S(2)}, u32[]{:S(2)}) collective-permute-start(bf16[136,1408]{1,0:T(8,128)(2,1)S(1)} %collective-permute-done.1.refs_2_), channel_id=1, source_target_pairs={{2,3},{1,0},{6,7},{5,4},{10,11},{9,8},{14,15},{13,12},{18,19},{17,... | collective-permute-start | bytes 1148936 | tf_op jit(solution)/shard_map/ppermute | solution.py:371
  42.9 20.5 %copy-start.1 = (bf16[1,4,4,72,768]{4,3,2,1,0:T(8,128)(2,1)S(1)}, bf16[1,4,4,72,768]{4,3,2,1,0:T(8,128)(2,1)}, u32[]{:S(2)}) copy-start(bf16[1,4,4,72,768]{4,3,2,1,0:T(8,128)(2,1)} %refs_11_.1) | copy-start | bytes 5308420
  43.0 25.7 %collective-permute-start.6 = (bf16[400,1408]{1,0:T(8,128)(2,1)S(1)}, bf16[400,1408]{1,0:T(8,128)(2,1)S(1)}, u32[]{:S(2)}, u32[]{:S(2)}) collective-permute-start(bf16[400,1408]{1,0:T(8,128)(2,1)S(1)} %shard_map.76.tab_ref.refs_1_), channel_id=1, source_target_pairs={{0,16},{4,20},{8,24},{12,28},{16,0},{20,4},{24,8},{28,12},{1,17},{... | collective-permute-start | bytes 3379208 | tf_op jit(solution)/shard_map/ppermute | solution.py:361
  44.0 18.1 %collective-permute-start.8 = (bf16[256,640]{1,0:T(8,128)(2,1)S(1)}, bf16[256,640]{1,0:T(8,128)(2,1)S(1)}, u32[]{:S(2)}, u32[]{:S(2)}) collective-permute-start(bf16[256,640]{1,0:T(8,128)(2,1)S(1)} %fusion.refs_2_.refs_9_), channel_id=1, source_target_pairs={{0,2},{1,3},{2,0},{3,1},{4,6},{5,7},{6,4},{7,5},{8,10},{9,11},{10,... | collective-permute-start | bytes 983048 | tf_op jit(solution)/shard_map/ppermute | solution.py:368
  46.7 36.3 %collective-permute-start.16 = (bf16[1,4,96,2048]{3,2,1,0:T(8,128)(2,1)S(1)}, bf16[1,4,96,2048]{3,2,1,0:T(8,128)(2,1)S(1)}, u32[]{:S(2)}, u32[]{:S(2)}) collective-permute-start(bf16[1,4,96,2048]{3,2,1,0:T(8,128)(2,1)S(1)} %collective-permute-done.15.refs_9_), channel_id=1, source_target_pairs={{0,4},{4,0},{8,12},{12,8},{16,20},{20,16},{24,28},{28,24},{1,5},{5... | collective-permute-start | bytes 4718600 | tf_op jit(solution)/shard_map/ppermute | solution.py:361
  46.7 26.5 %collective-permute-start.7 = (bf16[256,640]{1,0:T(8,128)(2,1)S(1)}, bf16[256,640]{1,0:T(8,128)(2,1)S(1)}, u32[]{:S(2)}, u32[]{:S(2)}) collective-permute-start(bf16[256,640]{1,0:T(8,128)(2,1)S(1)} %fusion.refs_2_.refs_9_), channel_id=1, source_target_pairs={{0,1},{1,2},{2,3},{4,5},{5,6},{6,7},{8,9},{9,10},{10,11},{12,13},{... | collective-permute-start | bytes 983048 | tf_op jit(solution)/shard_map/ppermute | solution.py:369
  50.2 23.0 %collective-permute-start.9 = (bf16[256,640]{1,0:T(8,128)(2,1)S(1)}, bf16[256,640]{1,0:T(8,128)(2,1)S(1)}, u32[]{:S(2)}, u32[]{:S(2)}) collective-permute-start(bf16[256,640]{1,0:T(8,128)(2,1)S(1)} %fusion.refs_2_.refs_9_), channel_id=1, source_target_pairs={{1,0},{2,1},{3,2},{5,4},{6,5},{7,6},{9,8},{10,9},{11,10},{13,12},{... | collective-permute-start | bytes 983048 | tf_op jit(solution)/shard_map/ppermute | solution.py:370
  62.1 12.7 %collective-permute-start.10 = (bf16[256,640]{1,0:T(8,128)(2,1)S(1)}, bf16[256,640]{1,0:T(8,128)(2,1)S(1)}, u32[]{:S(2)}, u32[]{:S(2)}) collective-permute-start(bf16[256,640]{1,0:T(8,128)(2,1)S(1)} %collective-permute-done.8.refs_4_.refs_11_), channel_id=1, source_target_pairs={{2,3},{1,0},{6,7},{5,4},{10,11},{9,8},{14,15},{13,12},{18,19},{17,... | collective-permute-start | bytes 983048 | tf_op jit(solution)/shard_map/ppermute | solution.py:371
  73.1 7.4 %collective-permute-start.11 = (bf16[1,4,96,512]{3,2,1,0:T(8,128)(2,1)S(1)}, bf16[1,4,96,512]{3,2,1,0:T(8,128)(2,1)S(1)}, u32[]{:S(2)}, u32[]{:S(2)}) collective-permute-start(bf16[1,4,96,512]{3,2,1,0:T(8,128)(2,1)S(1)} %get-tuple-element.37), channel_id=1, source_target_pairs={{0,4},{4,0},{8,12},{12,8},{16,20},{20,16},{24,28},{28,24},{1,5},{5... | collective-permute-start | bytes 1179656 | tf_op jit(solution)/shard_map/ppermute | solution.py:361
  78.1 1.8 %collective-permute-start.13 = (bf16[1,4,96,512]{3,2,1,0:T(8,128)(2,1)S(1)}, bf16[1,4,96,512]{3,2,1,0:T(8,128)(2,1)S(1)}, u32[]{:S(2)}, u32[]{:S(2)}) collective-permute-start(bf16[1,4,96,512]{3,2,1,0:T(8,128)(2,1)S(1)} %get-tuple-element.42), channel_id=1, source_target_pairs={{0,4},{4,0},{8,12},{12,8},{16,20},{20,16},{24,28},{28,24},{1,5},{5... | collective-permute-start | bytes 1179656 | tf_op jit(solution)/shard_map/ppermute | solution.py:361
  78.2 2.3 %collective-permute-start.14 = (bf16[1,4,96,512]{3,2,1,0:T(8,128)(2,1)S(1)}, bf16[1,4,96,512]{3,2,1,0:T(8,128)(2,1)S(1)}, u32[]{:S(2)}, u32[]{:S(2)}) collective-permute-start(bf16[1,4,96,512]{3,2,1,0:T(8,128)(2,1)S(1)} %get-tuple-element.43), channel_id=1, source_target_pairs={{0,4},{4,0},{8,12},{12,8},{16,20},{20,16},{24,28},{28,24},{1,5},{5... | collective-permute-start | bytes 1179656 | tf_op jit(solution)/shard_map/ppermute | solution.py:361
  78.7 2.3 %collective-permute-start.12 = (bf16[1,4,96,512]{3,2,1,0:T(8,128)(2,1)S(1)}, bf16[1,4,96,512]{3,2,1,0:T(8,128)(2,1)S(1)}, u32[]{:S(2)}, u32[]{:S(2)}) collective-permute-start(bf16[1,4,96,512]{3,2,1,0:T(8,128)(2,1)S(1)} %get-tuple-element.41), channel_id=1, source_target_pairs={{0,4},{4,0},{8,12},{12,8},{16,20},{20,16},{24,28},{28,24},{1,5},{5... | collective-permute-start | bytes 1179656 | tf_op jit(solution)/shard_map/ppermute | solution.py:361
  81.5 36.5 %collective-permute-start.20 = (bf16[1,4,96,2048]{3,2,1,0:T(8,128)(2,1)S(1)}, bf16[1,4,96,2048]{3,2,1,0:T(8,128)(2,1)S(1)}, u32[]{:S(2)}, u32[]{:S(2)}) collective-permute-start(bf16[1,4,96,2048]{3,2,1,0:T(8,128)(2,1)S(1)} %shard_map.82), channel_id=1, source_target_pairs={{0,8},{4,12},{8,0},{12,4},{16,24},{20,28},{24,16},{28,20},{1,9},{5... | collective-permute-start | bytes 4718600 | tf_op jit(solution)/shard_map/ppermute | solution.py:361
  89.5 3.7 %collective-permute-start.17 = (f32[4,4,128]{2,1,0:T(4,128)S(1)}, f32[4,4,128]{2,1,0:T(4,128)S(1)}, u32[]{:S(2)}, u32[]{:S(2)}) collective-permute-start(f32[4,4,128]{2,1,0:T(4,128)S(1)} %bitcast.18), channel_id=1, source_target_pairs={{0,16},{4,20},{8,24},{12,28},{16,0},{20,4},{24,8},{28,12},{1,17},{... | collective-permute-start | bytes 24584 | tf_op jit(solution)/shard_map/ppermute | solution.py:361
  93.2 24.2 %collective-permute-start.21 = (bf16[4,4,72,384]{3,2,1,0:T(8,128)(2,1)S(1)}, bf16[4,4,72,384]{3,2,1,0:T(8,128)(2,1)S(1)}, u32[]{:S(2)}, u32[]{:S(2)}) collective-permute-start(bf16[4,4,72,384]{3,2,1,0:T(8,128)(2,1)S(1)} %get-tuple-element.57), channel_id=1, source_target_pairs={{0,16},{4,20},{8,24},{12,28},{16,0},{20,4},{24,8},{28,12},{1,17},{... | collective-permute-start | bytes 2654216 | tf_op jit(solution)/shard_map/ppermute | solution.py:361
  106.0 11.0 %collective-permute-start.18 = (bf16[1,4,96,1024]{3,2,1,0:T(8,128)(2,1)S(1)}, bf16[1,4,96,1024]{3,2,1,0:T(8,128)(2,1)S(1)}, u32[]{:S(2)}, u32[]{:S(2)}) collective-permute-start(bf16[1,4,96,1024]{3,2,1,0:T(8,128)(2,1)S(1)} %get-tuple-element.54), channel_id=1, source_target_pairs={{0,4},{4,0},{8,12},{12,8},{16,20},{20,16},{24,28},{28,24},{1,5},{5... | collective-permute-start | bytes 2359304 | tf_op jit(solution)/shard_map/ppermute | solution.py:361
  106.1 10.9 %collective-permute-start.19 = (bf16[1,4,96,1024]{3,2,1,0:T(8,128)(2,1)S(1)}, bf16[1,4,96,1024]{3,2,1,0:T(8,128)(2,1)S(1)}, u32[]{:S(2)}, u32[]{:S(2)}) collective-permute-start(bf16[1,4,96,1024]{3,2,1,0:T(8,128)(2,1)S(1)} %get-tuple-element.55), channel_id=1, source_target_pairs={{0,4},{4,0},{8,12},{12,8},{16,20},{20,16},{24,28},{28,24},{1,5},{5... | collective-permute-start | bytes 2359304 | tf_op jit(solution)/shard_map/ppermute | solution.py:361

commit v7 on v6

--- a/solution.py
+++ b/solution.py
@@ -177,7 +177,7 @@
 def back_kernel(n, counts, group, rels, sc_ref, *refs):
     chunks, at = gathered(refs, counts, n, sc_ref[0])
     w_refs, refs = refs[at : at + len(rels)], refs[at + len(rels) :]
-    hid_ref, wt_ref, rank_ref, gh_ref, sg_ref, w_all = refs
+    hid_ref, wt_ref, rank_ref, *added, gh_ref, sg_ref, w_all = refs
     toks, (f, d) = wt_ref.shape[3], w_all.shape[1:]
     for rel, ref in zip(rels, w_refs):
         rows = ref.shape[2]
@@ -203,15 +203,17 @@
                 pick, hid_ref[0, e, s, :CAP], (((0,), (0,)), ((), ())), preferred_element_type=F32
             )
             sg_col = jnp.sum(zk * hid, axis=1, keepdims=True)
-            sg_ref[s, e] = jnp.sum(jnp.where(eye, sg_col, 0.0), axis=0, keepdims=True)
-
-
-def backward(n, scalars, pieces, w_pieces, f, hid, wt, rank, whole):
+            sg_row = jnp.sum(jnp.where(eye, sg_col, 0.0), axis=0, keepdims=True)
+            sg_ref[s, e] = sg_row + added[0][s, e] if added else sg_row
+
+
+def backward(n, scalars, pieces, w_pieces, f, hid, wt, rank, *added):
     _, experts, band, d = w_pieces[0][1].shape
     toks = wt.shape[3]
     rels = [rel for rel, _, _ in w_pieces]
     group = 2 if experts % 2 == 0 else 1
     arrays, specs, counts = flat(pieces)
+    whole = len(added) > 0
     row_spec = pl.BlockSpec((n, group, 1, toks), lambda e, sc: (0, e, 0, 0))
     return pl.pallas_call(
         functools.partial(back_kernel, n, counts, group, rels),
@@ -231,13 +233,14 @@
                 pl.BlockSpec((1, group, n, hid.shape[3], f), lambda e, sc: (0, e, 0, 0, sc[1] if whole else 0)),
                 row_spec,
                 row_spec,
+                *[row_spec] * len(added),
             ],
             out_specs=(pl.BlockSpec((group, n, CAP, f), lambda e, sc: (e, 0, 0, sc[1] if whole else 0)), row_spec),
             scratch_shapes=[pltpu.VMEM((group, f, d), BF)],
         ),
         compiler_params=pltpu.CompilerParams(vmem_limit_bytes=24 << 20),
         cost_estimate=SHORT,
-    )(scalars, *arrays, *[w for _, w, _ in w_pieces], hid, wt, rank)
+    )(scalars, *arrays, *[w for _, w, _ in w_pieces], hid, wt, rank, *added)
 
 
 def part_kernel(n, bands, counts, spans, sc_ref, *refs):
@@ -317,15 +320,18 @@
     )(*arrays)
 
 
-def finish_kernel(sc_ref, base_ref, there_ref, new_ref, old_ref, down_ref, hidden_ref):
-    down_ref[0] = (base_ref[0, 0].astype(F32) + there_ref[0, 0].astype(F32)).astype(BF)
+def finish_kernel(sc_ref, base_ref, *refs):
+    *there, new_ref, _, down_ref, hidden_ref = refs
+    others = [ref[0, 0].astype(F32) for ref in there]
+    others = others[0] if len(others) == 1 else jnp.concatenate(others, axis=1)
+    down_ref[0] = (base_ref[0, 0].astype(F32) + others).astype(BF)
     hidden_ref[...] = new_ref[...]
 
 
 def finish(scalars, base, there, new, whole):
     _, experts, band, d = base.shape
     _, n, cap, f = new.shape
-    sums = pl.BlockSpec((1, 1, band, d), lambda e, sc: (0, e, 0, 0))
+    sums = lambda x: pl.BlockSpec((1, 1, band, x.shape[3]), lambda e, sc: (0, e, 0, 0))
     return pl.pallas_call(
         finish_kernel,
         out_shape=(jax.ShapeDtypeStruct((experts, band, d), BF), jax.ShapeDtypeStruct(whole.shape, BF)),
@@ -333,8 +339,7 @@
             num_scalar_prefetch=1,
             grid=(experts,),
             in_specs=[
-                sums,
-                sums,
+                *[sums(x) for x in (base, *there)],
                 pl.BlockSpec((1, n, cap, f), lambda e, sc: (e, 0, 0, 0)),
                 pl.BlockSpec(memory_space=pl.ANY),
             ],
@@ -343,10 +348,10 @@
                 pl.BlockSpec((1, n, cap, f), lambda e, sc: (e, 0, 0, 1 - sc[1])),
             ),
         ),
-        input_output_aliases={4: 1},
+        input_output_aliases={3 + len(there): 1},
         compiler_params=pltpu.CompilerParams(vmem_limit_bytes=12 << 20),
         cost_estimate=SHORT,
-    )(scalars, base, there, new, whole)
+    )(scalars, base, *there, new, whole)
 
 
 def per_device(n_dp, n, grad_out, expert_ids, route_weights, hidden_cache, w_down):
@@ -414,39 +419,38 @@
             w = lax.dynamic_update_slice(w, array[i], (0, (j ^ r) * band, 0))
         w_pieces = [(None, w[None], 0)]
 
-    half = d // 2
+    half, first = d // 2, 7 * d // 16
     groups = (
-        (slice(0, 1), ((0, half),)),
-        (slice(0, 2), ((half, cut), (0, d - cut))),
+        (slice(0, 1), ((0, first),), 1),
+        (slice(0, 2), ((first, cut), (0, d - cut)), 1),
     )
     order, sums = scalars, []
-    for chunks, spans in groups:
+    for chunks, spans, parts in groups:
         tokens = own_pieces[chunks], nb_pieces[chunks], spans
-        width = sum(stop - start for start, stop in spans) // 2
-        *far, keep_far = partial_grad(n, bands, band, True, (width, width), order, hs_own, hs_nb, *tokens)
+        width = sum(stop - start for start, stop in spans) // parts
+        *far, keep_far = partial_grad(n, bands, band, True, (width,) * parts, order, hs_own, hs_nb, *tokens)
         order = after(scalars, far[0])
-        sums.append([[keep_far], [swap(x, 1) for x in far]])
-    going = joined([[x[i][k] for x in sums for k in ks] for i, ks in ((0, (0,)), (1, (0, 1)))])
-    there = [swap(going, bands // 2)]
+        here = [swap(after(x, *rests) if not sums else x, 1) for x in far]
+        sums.append(joined([[keep_far], here]))
+    there = [swap(x, bands // 2) for x in sums]
     gh_nb, sg_nb = backward(
-        n, after(scalars, going), nb_pieces, w_pieces, f, hid_nb, wt_nb, rank_nb, False
-    )
-    sg_in = swap(sg_nb.reshape(n, experts, toks), bands)
+        n, after(order, sums[0]), nb_pieces, w_pieces, f, hid_nb, wt_nb, rank_nb
+    )
+    sg_in = swap(sg_nb, bands)
     gh_own, sg_own = backward(
-        n, after(scalars, sg_in), own_pieces, w_pieces, f, hidden_cache, wt_own, rank_own, True
-    )
-    sg = sg_own.reshape(n, experts, toks) + sg_in
-    by_expert = lax.all_to_all(sg, "expert", split_axis=0, concat_axis=0, tiled=True)
+        n, after(scalars, sg_in), own_pieces, w_pieces, f, hidden_cache, wt_own, rank_own, sg_in
+    )
+    by_expert = lax.all_to_all(sg_own, "expert", split_axis=0, concat_axis=0, tiled=True)
     spans = ((0, cut), (0, d - cut))
     *near, keep = partial_grad(
         n, bands, band, False, (half, half), after(scalars, sg_own), hs_own, hs_nb, own_pieces, nb_pieces, spans
     )
-    base = joined([[keep], [swap(x, 1) for x in near]])
+    base = joined([[keep], [swap(after(x, there[0]), 1) for x in near]])
     mid = bands // 8
-    there = there[0]
+    there = there if mid == 0 else [jnp.concatenate(there, axis=3)]
     while mid:
-        total = base.astype(F32) + there.astype(F32)
-        base, there, mid = total[:mid].astype(BF), swap(total[mid:].astype(BF), 4 * mid), mid // 2
+        total = base.astype(F32) + there[0].astype(F32)
+        base, there, mid = total[:mid].astype(BF), [swap(total[mid:].astype(BF), 4 * mid)], mid // 2
     gh_in = swap(after(gh_nb, sg_in), bands)
     grad_down, grad_hidden = finish(scalars, base, there, gh_in, gh_own)
     by_expert = by_expert.reshape(EXPERTS, 1, toks)

time: 121 us -> 119 us (0.983)
  waiting for transfers between devices: 46.6 us -> 41.3 us
  starting transfers between devices: 27.1 us -> 29.5 us
    ppermute x14 -> x13, waiting for transfers between devices: 9.72 us -> 5.92 us  [swap(): return lax.ppermute(x, 'dp', [(i, i ^ bit) for i in range(n_dp)])]
    ppermute x14 -> x13, starting transfers between devices: 9.64 us -> 12.1 us  [swap(): return lax.ppermute(x, 'dp', [(i, i ^ bit) for i in range(n_dp)])]
    ppermute x2, waiting for transfers between devices: 24.1 us -> 22.6 us  [spread(): two = lax.ppermute(x, 'expert', [(i, (i + 2) % n) for i in range(n)])]
  transfers between devices with their start and end apart: 22 -> 21, of which waited for: 11 -> 7; matrix products, arithmetic and copies ran while one was open for 1% -> 1% of each run, Pallas kernels for 25% -> 26%
where the time goes in v7:
time: 119 us
  waiting for transfers between devices  41.3 us (35%)
  Pallas kernels  32.9 us (28%)
  starting transfers between devices  29.5 us (25%)
  blocking collectives  10.3 us (9%)
  local copies, waits for them, and re-layouts  2.71 us (2%)
    ppermute x2, waiting for transfers between devices, spread(): two = lax.ppermute(x, 'expert', [(i, (i + 2) % n) for i in range(n)])  22.6 us
    pallas_call x2, Pallas kernels, backward(): pl.pallas_call(functools.partial(back_kernel, n, counts, group, rels), ou...  13.7 us
    ppermute x13, starting transfers between devices, swap(): return lax.ppermute(x, 'dp', [(i, i ^ bit) for i in range(n_dp)])  12.1 us
    pallas_call x3, Pallas kernels, partial_grad(): pl.pallas_call(functools.partial(part_kernel, n, bands, (counts, counts_n...  11.8 us
    all_to_all x1, blocking collectives, per_device(): lax.all_to_all(sg_own, 'expert', split_axis=0, concat_axis=0, tiled=True)  10.3 us
    ppermute x2, waiting for transfers between devices, spread(): passed = lax.ppermute(two, 'expert', [(2, 3), (1, 0)])  7.02 us
    ppermute x2, starting transfers between devices, spread(): one = lax.ppermute(x, 'expert', [(i, i + 1) for i in range(n - 1)])  6.98 us
    ppermute x13, waiting for transfers between devices, swap(): return lax.ppermute(x, 'dp', [(i, i ^ bit) for i in range(n_dp)])  5.92 us
  transfers between devices with their start and end apart: 21, of which 7 were waited for; matrix products, arithmetic and copies ran while one was open for 1% of the time, Pallas kernels for 26%

profile of v7, /device:TPU:0, one launch (start us, length us, event | category | flops | bytes accessed | tf_op | source)
XLA Modules:
  0.0 118.5 jit_solution(7976003848229617635)
XLA Ops:
  0.6 0.5 collective-permute-start.4
  1.1 0.1 pad_add_fusion.sc_ref
  1.2 1.5 %copy-done = bf16[1,4,4,72,768]{4,3,2,1,0:T(8,128)(2,1)S(1)} copy-done((bf16[1,4,4,72,768]{4,3,2,1,0:T(8,128)(2,1)S(1)}, bf16[1,4,4,72,768]{4,3,2,1,0:T(8,128)(2,1)}, u32[]{:S(2)}) %copy-start) | copy-done | bytes 1769496
  2.7 1.0 copy-done.3
  3.8 0.8 shard_map.77
  4.5 2.7 %collective-permute-start.5 = (bf16[2048,384]{1,0:T(8,128)(2,1)S(1)}, bf16[2048,384]{1,0:T(8,128)(2,1)S(1)}, u32[]{:S(2)}, u32[]{:S(2)}) collective-permute-start(bf16[2048,384]{1,0:T(8,128)(2,1)S(1)} %shard_map.77), channel_id=1, source_target_pairs={{0,16},{4,20},{8,24},{12,28},{16,0},{20,4},{24,8},{28,12},{1,17},{... | collective-permute-start | bytes 4718600 | tf_op jit(solution)/shard_map/ppermute | solution.py:366
  7.4 0.0 slice-start.1
  7.4 2.7 %collective-permute-start.1 = (bf16[136,1408]{1,0:T(8,128)(2,1)S(1)}, bf16[136,1408]{1,0:T(8,128)(2,1)S(1)}, u32[]{:S(2)}, u32[]{:S(2)}) collective-permute-start(bf16[136,1408]{1,0:T(8,128)(2,1)S(1)} %pad_maximum_fusion.refs_0_), channel_id=1, source_target_pairs={{0,2},{1,3},{2,0},{3,1},{4,6},{5,7},{6,4},{7,5},{8,10},{9,11},{10,... | collective-permute-start | bytes 1148936 | tf_op jit(solution)/shard_map/ppermute | solution.py:373
  10.1 1.5 %collective-permute-start.12 = (bf16[1,4,96,2048]{3,2,1,0:T(8,128)(2,1)S(1)}, bf16[1,4,96,2048]{3,2,1,0:T(8,128)(2,1)S(1)}, u32[]{:S(2)}, u32[]{:S(2)}) collective-permute-start(bf16[1,4,96,2048]{3,2,1,0:T(8,128)(2,1)S(1)} %bitcast.12), channel_id=1, source_target_pairs={{0,8},{4,12},{8,0},{12,4},{16,24},{20,28},{24,16},{28,20},{1,9},{5... | collective-permute-start | bytes 4718600 | tf_op jit(solution)/shard_map/ppermute | solution.py:366
  11.6 3.5 %collective-permute-start = (bf16[136,1408]{1,0:T(8,128)(2,1)S(1)}, bf16[136,1408]{1,0:T(8,128)(2,1)S(1)}, u32[]{:S(2)}, u32[]{:S(2)}) collective-permute-start(bf16[136,1408]{1,0:T(8,128)(2,1)S(1)} %pad_maximum_fusion.refs_0_), channel_id=1, source_target_pairs={{0,1},{1,2},{2,3},{4,5},{5,6},{6,7},{8,9},{9,10},{10,11},{12,13},{... | collective-permute-start | bytes 1148936 | tf_op jit(solution)/shard_map/ppermute | solution.py:374
  15.1 1.3 %collective-permute-start.2 = (bf16[136,1408]{1,0:T(8,128)(2,1)S(1)}, bf16[136,1408]{1,0:T(8,128)(2,1)S(1)}, u32[]{:S(2)}, u32[]{:S(2)}) collective-permute-start(bf16[136,1408]{1,0:T(8,128)(2,1)S(1)} %pad_maximum_fusion.refs_0_), channel_id=1, source_target_pairs={{1,0},{2,1},{3,2},{5,4},{6,5},{7,6},{9,8},{10,9},{11,10},{13,12},{... | collective-permute-start | bytes 1148936 | tf_op jit(solution)/shard_map/ppermute | solution.py:375
  16.4 12.0 %collective-permute-done.1.refs_2_ = bf16[136,1408]{1,0:T(8,128)(2,1)S(1)} collective-permute-done((bf16[136,1408]{1,0:T(8,128)(2,1)S(1)}, bf16[136,1408]{1,0:T(8,128)(2,1)S(1)}, u32[]{:S(2)}, u32[]{:S(2)}) %collective-permute-start.1) | collective-permute-done | bytes 383008 | tf_op jit(solution)/shard_map/ppermute | solution.py:373
  28.4 1.3 %collective-permute-start.3 = (bf16[136,1408]{1,0:T(8,128)(2,1)S(1)}, bf16[136,1408]{1,0:T(8,128)(2,1)S(1)}, u32[]{:S(2)}, u32[]{:S(2)}) collective-permute-start(bf16[136,1408]{1,0:T(8,128)(2,1)S(1)} %collective-permute-done.1.refs_2_), channel_id=1, source_target_pairs={{2,3},{1,0},{6,7},{5,4},{10,11},{9,8},{14,15},{13,12},{18,19},{17,... | collective-permute-start | bytes 1148936 | tf_op jit(solution)/shard_map/ppermute | solution.py:376
  29.7 5.7 %collective-permute-done.2.refs_3_ = bf16[136,1408]{1,0:T(8,128)(2,1)S(1)} collective-permute-done((bf16[136,1408]{1,0:T(8,128)(2,1)S(1)}, bf16[136,1408]{1,0:T(8,128)(2,1)S(1)}, u32[]{:S(2)}, u32[]{:S(2)}) %collective-permute-start.2) | collective-permute-done | bytes 383008 | tf_op jit(solution)/shard_map/ppermute | solution.py:375
  35.4 6.9 %collective-permute-done.3.refs_4_ = bf16[136,1408]{1,0:T(8,128)(2,1)S(1)} collective-permute-done((bf16[136,1408]{1,0:T(8,128)(2,1)S(1)}, bf16[136,1408]{1,0:T(8,128)(2,1)S(1)}, u32[]{:S(2)}, u32[]{:S(2)}) %collective-permute-start.3) | collective-permute-done | bytes 383008 | tf_op jit(solution)/shard_map/ppermute | solution.py:376
  42.3 0.7 shard_map.76.tab_ref.refs_1_
  43.0 1.0 collective-permute-start.6
  43.9 0.1 fusion.4
  44.0 2.7 %collective-permute-start.8 = (bf16[256,640]{1,0:T(8,128)(2,1)S(1)}, bf16[256,640]{1,0:T(8,128)(2,1)S(1)}, u32[]{:S(2)}, u32[]{:S(2)}) collective-permute-start(bf16[256,640]{1,0:T(8,128)(2,1)S(1)} %fusion.refs_2_.refs_9_), channel_id=1, source_target_pairs={{0,2},{1,3},{2,0},{3,1},{4,6},{5,7},{6,4},{7,5},{8,10},{9,11},{10,... | collective-permute-start | bytes 983048 | tf_op jit(solution)/shard_map/ppermute | solution.py:373
  46.7 3.5 %collective-permute-start.7 = (bf16[256,640]{1,0:T(8,128)(2,1)S(1)}, bf16[256,640]{1,0:T(8,128)(2,1)S(1)}, u32[]{:S(2)}, u32[]{:S(2)}) collective-permute-start(bf16[256,640]{1,0:T(8,128)(2,1)S(1)} %fusion.refs_2_.refs_9_), channel_id=1, source_target_pairs={{0,1},{1,2},{2,3},{4,5},{5,6},{6,7},{8,9},{9,10},{10,11},{12,13},{... | collective-permute-start | bytes 983048 | tf_op jit(solution)/shard_map/ppermute | solution.py:374
  50.2 1.3 %collective-permute-start.9 = (bf16[256,640]{1,0:T(8,128)(2,1)S(1)}, bf16[256,640]{1,0:T(8,128)(2,1)S(1)}, u32[]{:S(2)}, u32[]{:S(2)}) collective-permute-start(bf16[256,640]{1,0:T(8,128)(2,1)S(1)} %fusion.refs_2_.refs_9_), channel_id=1, source_target_pairs={{1,0},{2,1},{3,2},{5,4},{6,5},{7,6},{9,8},{10,9},{11,10},{13,12},{... | collective-permute-start | bytes 983048 | tf_op jit(solution)/shard_map/ppermute | solution.py:375
  51.5 10.6 %collective-permute-done.8.refs_4_.refs_11_ = bf16[256,640]{1,0:T(8,128)(2,1)S(1)} collective-permute-done((bf16[256,640]{1,0:T(8,128)(2,1)S(1)}, bf16[256,640]{1,0:T(8,128)(2,1)S(1)}, u32[]{:S(2)}, u32[]{:S(2)}) %collective-permute-start.8) | collective-permute-done | bytes 327712 | tf_op jit(solution)/shard_map/ppermute | solution.py:373
  62.1 1.3 %collective-permute-start.10 = (bf16[256,640]{1,0:T(8,128)(2,1)S(1)}, bf16[256,640]{1,0:T(8,128)(2,1)S(1)}, u32[]{:S(2)}, u32[]{:S(2)}) collective-permute-start(bf16[256,640]{1,0:T(8,128)(2,1)S(1)} %collective-permute-done.8.refs_4_.refs_11_), channel_id=1, source_target_pairs={{2,3},{1,0},{6,7},{5,4},{10,11},{9,8},{14,15},{13,12},{18,19},{17,... | collective-permute-start | bytes 983048 | tf_op jit(solution)/shard_map/ppermute | solution.py:376
  63.4 0.1 collective-permute-start.13
  63.5 1.3 %shard_map.78 = (bf16[4,384,512]{2,1,0:T(8,128)(2,1)S(1)}, f32[4,4,1,128]{3,2,1,0:T(1,128)S(1)}, f32[4,4,1,128]{3,2,1,0:T(1,128)S(1)}) custom-call(s32[3]{0:T(128)S(1)} %pad_add_fusion.sc_ref, bf16[400,1408]{1,0:T(8,128)(2,1)S(1)} %shard_map.76.tab_ref.refs_1_, bf16[1,4,4,72,768]{4,3,2,1,0:T(8,128)(2,1)S(1)} %copy-done.1), custom_call_target="tpu_custom_call" | custom-call | flops 1 | bytes 1 | tf_op jit(solution)/shard_map/pallas_call | solution.py:50
  64.8 0.1 slice.60
  65.0 3.7 %collective-permute-done.6.tab_ref.refs_3_.refs_8_.refs_1_ = bf16[400,1408]{1,0:T(8,128)(2,1)S(1)} collective-permute-done((bf16[400,1408]{1,0:T(8,128)(2,1)S(1)}, bf16[400,1408]{1,0:T(8,128)(2,1)S(1)}, u32[]{:S(2)}, u32[]{:S(2)}) %collective-permute-start.6) | collective-permute-done | bytes 1126432 | tf_op jit(solution)/shard_map/ppermute | solution.py:366
  68.7 1.3 %shard_map.79 = (bf16[4,384,512]{2,1,0:T(8,128)(2,1)S(1)}, f32[4,4,1,128]{3,2,1,0:T(1,128)S(1)}, f32[4,4,1,128]{3,2,1,0:T(1,128)S(1)}) custom-call(s32[3]{0:T(128)S(1)} %pad_add_fusion.sc_ref, bf16[400,1408]{1,0:T(8,128)(2,1)S(1)} %collective-permute-done.6.tab_ref.refs_3_.refs_8_.refs_1_, bf16[1,4,4,80,384]{4,3,2,1,0:T(8,128)(2,1)S(1)} %bitcast.9), custom_call_target="tpu_custom_call" | custom-call | flops 1 | bytes 1 | tf_op jit(solution)/shard_map/pallas_call | solution.py:50
  70.0 3.2 %shard_map.80 = (bf16[1,4,96,896]{3,2,1,0:T(8,128)(2,1)S(1)}, bf16[1,4,96,896]{3,2,1,0:T(8,128)(2,1)S(1)}) custom-call(s32[3]{0:T(128)S(1)} %pad_add_fusion.sc_ref, bf16[136,1408]{1,0:T(8,128)(2,1)S(1)} %pad_maximum_fusion.refs_0_, bf16[400,1408]{1,0:T(8,128)(2,1)S(1)} %shard_map.76.tab_ref.refs_1_, ...), custom_call_target="tpu_custom_call" | custom-call | flops 1 | bytes 1 | tf_op jit(solution)/shard_map/pallas_call | solution.py:282
  73.2 0.1 collective-permute-done.10.refs_6_.refs_13_
  73.3 3.6 %shard_map.81 = (bf16[1,4,96,1152]{3,2,1,0:T(8,128)(2,1)S(1)}, bf16[1,4,96,1152]{3,2,1,0:T(8,128)(2,1)S(1)}) custom-call(s32[3]{0:T(128)S(1)} %pad_add_fusion.sc_ref, bf16[136,1408]{1,0:T(8,128)(2,1)S(1)} %pad_maximum_fusion.refs_0_, bf16[400,1408]{1,0:T(8,128)(2,1)S(1)} %shard_map.76.tab_ref.refs_1_, bf16[256,640]{1,0:T(8,128)(2,1)S(1)} %fusion.refs_2_.refs_9_, ...), custom_call_target="tpu_custom_call" | custom-call | flops 1 | bytes 1 | tf_op jit(solution)/shard_map/pallas_call | solution.py:282
  76.9 0.6 collective-permute-start.18
  77.5 0.2 shard_map.82
  77.7 1.6 %collective-permute-start.15 = (bf16[1,4,96,896]{3,2,1,0:T(8,128)(2,1)S(1)}, bf16[1,4,96,896]{3,2,1,0:T(8,128)(2,1)S(1)}, u32[]{:S(2)}, u32[]{:S(2)}) collective-permute-start(bf16[1,4,96,896]{3,2,1,0:T(8,128)(2,1)S(1)} %shard_map.82), channel_id=1, source_target_pairs={{0,8},{4,12},{8,0},{12,4},{16,24},{20,28},{24,16},{28,20},{1,9},{5... | collective-permute-start | bytes 2064392 | tf_op jit(solution)/shard_map/ppermute | solution.py:366
  79.3 6.5 %shard_map.83 = (bf16[4,4,72,384]{3,2,1,0:T(8,128)(2,1)S(1)}, f32[4,4,1,128]{3,2,1,0:T(1,128)S(1)}) custom-call(s32[3]{0:T(128)S(1)} %pad_add_fusion.sc_ref, bf16[128,1408]{1,0:T(8,128)(2,1)S(1)} %pad_maximum_fusion.1.refs_2_.refs_7_.refs_0_, bf16[400,1408]{1,0:T(8,128)(2,1)S(1)} %collective-permute-done.6.tab_ref.refs_3_.refs_8_.refs_1_, ...), custom_call_target="tpu_custom_call" | custom-call | flops 1 | bytes 1 | tf_op jit(solution)/shard_map/pallas_call | solution.py:218
  85.8 1.5 %collective-permute-start.14 = (f32[4,4,1,128]{3,2,1,0:T(1,128)S(1)}, f32[4,4,1,128]{3,2,1,0:T(1,128)S(1)}, u32[]{:S(2)}, u32[]{:S(2)}) collective-permute-start(f32[4,4,1,128]{3,2,1,0:T(1,128)S(1)} %get-tuple-element.48), channel_id=1, source_target_pairs={{0,16},{4,20},{8,24},{12,28},{16,0},{20,4},{24,8},{28,12},{1,17},{... | collective-permute-start | bytes 24584 | tf_op jit(solution)/shard_map/ppermute | solution.py:366
  87.3 2.2 %collective-permute-done.14.refs_14_ = f32[4,4,1,128]{3,2,1,0:T(1,128)S(1)} collective-permute-done((f32[4,4,1,128]{3,2,1,0:T(1,128)S(1)}, f32[4,4,1,128]{3,2,1,0:T(1,128)S(1)}, u32[]{:S(2)}, u32[]{:S(2)}) %collective-permute-start.14) | collective-permute-done | bytes 8224 | tf_op jit(solution)/shard_map/ppermute | solution.py:366
  89.5 1.5 %collective-permute-start.20 = (bf16[4,4,72,384]{3,2,1,0:T(8,128)(2,1)S(1)}, bf16[4,4,72,384]{3,2,1,0:T(8,128)(2,1)S(1)}, u32[]{:S(2)}, u32[]{:S(2)}) collective-permute-start(bf16[4,4,72,384]{3,2,1,0:T(8,128)(2,1)S(1)} %get-tuple-element.61), channel_id=1, source_target_pairs={{0,16},{4,20},{8,24},{12,28},{16,0},{20,4},{24,8},{28,12},{1,17},{... | collective-permute-start | bytes 2654216 | tf_op jit(solution)/shard_map/ppermute | solution.py:366
  90.9 0.3 shard_map.87
  91.2 0.6 collective-permute-start.19
  91.8 7.2 %shard_map.84 = (bf16[4,4,72,768]{3,2,1,0:T(8,128)(2,1)}, f32[4,4,1,128]{3,2,1,0:T(1,128)S(1)}) custom-call(s32[3]{0:T(128)S(1)} %pad_add_fusion.sc_ref, bf16[136,1408]{1,0:T(8,128)(2,1)S(1)} %pad_maximum_fusion.refs_0_, bf16[400,1408]{1,0:T(8,128)(2,1)S(1)} %shard_map.76.tab_ref.refs_1_, bf16[256,640]{1,0:T(8,128)(2,1)S(1)} %fusion.refs_2_.refs_9_, ...), custom_call_target="tpu_custom_call" | custom-call | flops 1 | bytes 1 | tf_op jit(solution)/shard_map/pallas_call | solution.py:218
  99.0 5.0 %shard_map.85 = (bf16[1,4,96,1024]{3,2,1,0:T(8,128)(2,1)S(1)}, bf16[1,4,96,1024]{3,2,1,0:T(8,128)(2,1)S(1)}, bf16[1,4,96,2048]{3,2,1,0:T(8,128)(2,1)S(1)}) custom-call(s32[3]{0:T(128)S(1)} %pad_add_fusion.sc_ref, bf16[136,1408]{1,0:T(8,128)(2,1)S(1)} %pad_maximum_fusion.refs_0_, bf16[400,1408]{1,0:T(8,128)(2,1)S(1)} %shard_map.76.tab_ref.refs_1_, ...), custom_call_target="tpu_custom_call" | custom-call | flops 1 | bytes 1 | tf_op jit(solution)/shard_map/pallas_call | solution.py:282
  104.0 0.1 collective-permute-start.17
  104.1 0.5 collective-permute-start.16
  104.6 10.3 %all_to_all.5 = f32[4,4,1,128]{3,2,1,0:T(1,128)S(1)} all-to-all(f32[4,4,1,128]{3,2,1,0:T(1,128)S(1)} %get-tuple-element.52), channel_id=1, replica_groups=mesh['dp'=8,'expert'=4] {'expert'}, dimensions={0} | all-to-all | bytes 16384 | tf_op jit(solution)/shard_map/all_to_all | solution.py:443
  114.9 0.6 select_reduce_fusion
  115.5 0.4 shard_map.86.base_ref
  116.0 2.6 %shard_map.88 = (bf16[4,96,2048]{2,1,0:T(8,128)(2,1)}, bf16[4,4,72,768]{3,2,1,0:T(8,128)(2,1)}) custom-call(s32[3]{0:T(128)S(1)} %pad_add_fusion.sc_ref, bf16[1,4,96,2048]{3,2,1,0:T(8,128)(2,1)S(1)} %shard_map.86.base_ref, bf16[1,4,96,896]{3,2,1,0:T(8,128)(2,1)S(1)} %collective-permute-done.15.refs_0_, ...), custom_call_target="tpu_custom_call", output_to_operand_aliasing={{1}: (5, {})} | custom-call | flops 1 | bytes 1 | tf_op jit(solution)/shard_map/pallas_call | solution.py:335
  (36 shorter events, 0.2 us)
Async XLA Ops:
  0.6 3.9 %collective-permute-start.4 = (bf16[1,4,96,2048]{3,2,1,0:T(8,128)(2,1)}, bf16[1,4,96,2048]{3,2,1,0:T(8,128)(2,1)S(1)}, u32[]{:S(2)}, u32[]{:S(2)}) collective-permute-start(bf16[1,4,96,2048]{3,2,1,0:T(8,128)(2,1)} %bitcast.11), channel_id=1, source_target_pairs={{0,4},{4,0},{8,12},{12,8},{16,20},{20,16},{24,28},{28,24},{1,5},{5... | collective-permute-start | bytes 4718600 | tf_op jit(solution)/shard_map/ppermute | solution.py:366
  1.2 1.5 %copy-start = (bf16[1,4,4,72,768]{4,3,2,1,0:T(8,128)(2,1)S(1)}, bf16[1,4,4,72,768]{4,3,2,1,0:T(8,128)(2,1)}, u32[]{:S(2)}) copy-start(bf16[1,4,4,72,768]{4,3,2,1,0:T(8,128)(2,1)} %refs_11_.1) | copy-start | bytes 5308420
  2.7 1.0 copy-start.3
  3.7 3.5 %copy-start.5 = (bf16[128,8]{0,1:T(8,128)(2,1)S(1)}, bf16[128,8]{0,1:T(8,128)(2,1)}, u32[]{:S(2)}) copy-start(bf16[128,8]{0,1:T(8,128)(2,1)} %param.7) | copy-start | bytes 6148
  3.7 3.5 %copy-start.4 = (s32[128,8]{0,1:T(8,128)S(1)}, s32[128,8]{0,1:T(8,128)}, u32[]{:S(2)}) copy-start(s32[128,8]{0,1:T(8,128)} %param.6) | copy-start | bytes 12292
  3.7 3.6 %slice-start = ((bf16[128,2048]{1,0:T(8,128)(2,1)}), bf16[128,1408]{1,0:T(8,128)(2,1)S(1)}, s32[]{:S(2)}) async-start(bf16[128,2048]{1,0:T(8,128)(2,1)} %tok_ref.1), calls=%async_computation.1 | async-start | bytes 720896 | tf_op jit(solution)/shard_map/slice | solution.py:385
  3.8 6.3 %copy-start.2 = (bf16[4,96,2048]{2,1,0:T(8,128)(2,1)S(1)}, bf16[4,96,2048]{2,1,0:T(8,128)(2,1)}, u32[]{:S(2)}) copy-start(bf16[4,96,2048]{2,1,0:T(8,128)(2,1)} %param.9) | copy-start | bytes 4718596
  4.5 38.4 %collective-permute-start.5 = (bf16[2048,384]{1,0:T(8,128)(2,1)S(1)}, bf16[2048,384]{1,0:T(8,128)(2,1)S(1)}, u32[]{:S(2)}, u32[]{:S(2)}) collective-permute-start(bf16[2048,384]{1,0:T(8,128)(2,1)S(1)} %shard_map.77), channel_id=1, source_target_pairs={{0,16},{4,20},{8,24},{12,28},{16,0},{20,4},{24,8},{28,12},{1,17},{... | collective-permute-start | bytes 4718600 | tf_op jit(solution)/shard_map/ppermute | solution.py:366
  7.4 36.6 %slice-start.1 = ((bf16[128,2048]{1,0:T(8,128)(2,1)}), bf16[128,640]{1,0:T(8,128)(2,1)S(1)}, s32[]{:S(2)}) async-start(bf16[128,2048]{1,0:T(8,128)(2,1)} %tok_ref.1), calls=%async_computation.2 | async-start | bytes 327680 | tf_op jit(solution)/shard_map/slice | solution.py:408
  7.4 21.0 %collective-permute-start.1 = (bf16[136,1408]{1,0:T(8,128)(2,1)S(1)}, bf16[136,1408]{1,0:T(8,128)(2,1)S(1)}, u32[]{:S(2)}, u32[]{:S(2)}) collective-permute-start(bf16[136,1408]{1,0:T(8,128)(2,1)S(1)} %pad_maximum_fusion.refs_0_), channel_id=1, source_target_pairs={{0,2},{1,3},{2,0},{3,1},{4,6},{5,7},{6,4},{7,5},{8,10},{9,11},{10,... | collective-permute-start | bytes 1148936 | tf_op jit(solution)/shard_map/ppermute | solution.py:373
  10.1 53.3 %collective-permute-start.12 = (bf16[1,4,96,2048]{3,2,1,0:T(8,128)(2,1)S(1)}, bf16[1,4,96,2048]{3,2,1,0:T(8,128)(2,1)S(1)}, u32[]{:S(2)}, u32[]{:S(2)}) collective-permute-start(bf16[1,4,96,2048]{3,2,1,0:T(8,128)(2,1)S(1)} %bitcast.12), channel_id=1, source_target_pairs={{0,8},{4,12},{8,0},{12,4},{16,24},{20,28},{24,16},{28,20},{1,9},{5... | collective-permute-start | bytes 4718600 | tf_op jit(solution)/shard_map/ppermute | solution.py:366
  11.6 18.1 %collective-permute-start = (bf16[136,1408]{1,0:T(8,128)(2,1)S(1)}, bf16[136,1408]{1,0:T(8,128)(2,1)S(1)}, u32[]{:S(2)}, u32[]{:S(2)}) collective-permute-start(bf16[136,1408]{1,0:T(8,128)(2,1)S(1)} %pad_maximum_fusion.refs_0_), channel_id=1, source_target_pairs={{0,1},{1,2},{2,3},{4,5},{5,6},{6,7},{8,9},{9,10},{10,11},{12,13},{... | collective-permute-start | bytes 1148936 | tf_op jit(solution)/shard_map/ppermute | solution.py:374
  15.1 20.3 %collective-permute-start.2 = (bf16[136,1408]{1,0:T(8,128)(2,1)S(1)}, bf16[136,1408]{1,0:T(8,128)(2,1)S(1)}, u32[]{:S(2)}, u32[]{:S(2)}) collective-permute-start(bf16[136,1408]{1,0:T(8,128)(2,1)S(1)} %pad_maximum_fusion.refs_0_), channel_id=1, source_target_pairs={{1,0},{2,1},{3,2},{5,4},{6,5},{7,6},{9,8},{10,9},{11,10},{13,12},{... | collective-permute-start | bytes 1148936 | tf_op jit(solution)/shard_map/ppermute | solution.py:375
  28.4 13.9 %collective-permute-start.3 = (bf16[136,1408]{1,0:T(8,128)(2,1)S(1)}, bf16[136,1408]{1,0:T(8,128)(2,1)S(1)}, u32[]{:S(2)}, u32[]{:S(2)}) collective-permute-start(bf16[136,1408]{1,0:T(8,128)(2,1)S(1)} %collective-permute-done.1.refs_2_), channel_id=1, source_target_pairs={{2,3},{1,0},{6,7},{5,4},{10,11},{9,8},{14,15},{13,12},{18,19},{17,... | collective-permute-start | bytes 1148936 | tf_op jit(solution)/shard_map/ppermute | solution.py:376
  42.9 20.6 %copy-start.1 = (bf16[1,4,4,72,768]{4,3,2,1,0:T(8,128)(2,1)S(1)}, bf16[1,4,4,72,768]{4,3,2,1,0:T(8,128)(2,1)}, u32[]{:S(2)}) copy-start(bf16[1,4,4,72,768]{4,3,2,1,0:T(8,128)(2,1)} %refs_11_.1) | copy-start | bytes 5308420
  43.0 25.7 %collective-permute-start.6 = (bf16[400,1408]{1,0:T(8,128)(2,1)S(1)}, bf16[400,1408]{1,0:T(8,128)(2,1)S(1)}, u32[]{:S(2)}, u32[]{:S(2)}) collective-permute-start(bf16[400,1408]{1,0:T(8,128)(2,1)S(1)} %shard_map.76.tab_ref.refs_1_), channel_id=1, source_target_pairs={{0,16},{4,20},{8,24},{12,28},{16,0},{20,4},{24,8},{28,12},{1,17},{... | collective-permute-start | bytes 3379208 | tf_op jit(solution)/shard_map/ppermute | solution.py:366
  44.0 18.1 %collective-permute-start.8 = (bf16[256,640]{1,0:T(8,128)(2,1)S(1)}, bf16[256,640]{1,0:T(8,128)(2,1)S(1)}, u32[]{:S(2)}, u32[]{:S(2)}) collective-permute-start(bf16[256,640]{1,0:T(8,128)(2,1)S(1)} %fusion.refs_2_.refs_9_), channel_id=1, source_target_pairs={{0,2},{1,3},{2,0},{3,1},{4,6},{5,7},{6,4},{7,5},{8,10},{9,11},{10,... | collective-permute-start | bytes 983048 | tf_op jit(solution)/shard_map/ppermute | solution.py:373
  46.7 26.5 %collective-permute-start.7 = (bf16[256,640]{1,0:T(8,128)(2,1)S(1)}, bf16[256,640]{1,0:T(8,128)(2,1)S(1)}, u32[]{:S(2)}, u32[]{:S(2)}) collective-permute-start(bf16[256,640]{1,0:T(8,128)(2,1)S(1)} %fusion.refs_2_.refs_9_), channel_id=1, source_target_pairs={{0,1},{1,2},{2,3},{4,5},{5,6},{6,7},{8,9},{9,10},{10,11},{12,13},{... | collective-permute-start | bytes 983048 | tf_op jit(solution)/shard_map/ppermute | solution.py:374
  50.2 23.0 %collective-permute-start.9 = (bf16[256,640]{1,0:T(8,128)(2,1)S(1)}, bf16[256,640]{1,0:T(8,128)(2,1)S(1)}, u32[]{:S(2)}, u32[]{:S(2)}) collective-permute-start(bf16[256,640]{1,0:T(8,128)(2,1)S(1)} %fusion.refs_2_.refs_9_), channel_id=1, source_target_pairs={{1,0},{2,1},{3,2},{5,4},{6,5},{7,6},{9,8},{10,9},{11,10},{13,12},{... | collective-permute-start | bytes 983048 | tf_op jit(solution)/shard_map/ppermute | solution.py:375
  62.1 11.2 %collective-permute-start.10 = (bf16[256,640]{1,0:T(8,128)(2,1)S(1)}, bf16[256,640]{1,0:T(8,128)(2,1)S(1)}, u32[]{:S(2)}, u32[]{:S(2)}) collective-permute-start(bf16[256,640]{1,0:T(8,128)(2,1)S(1)} %collective-permute-done.8.refs_4_.refs_11_), channel_id=1, source_target_pairs={{2,3},{1,0},{6,7},{5,4},{10,11},{9,8},{14,15},{13,12},{18,19},{17,... | collective-permute-start | bytes 983048 | tf_op jit(solution)/shard_map/ppermute | solution.py:376
  63.4 15.9 %collective-permute-start.13 = (bf16[1,4,96,2048]{3,2,1,0:T(8,128)(2,1)S(1)}, bf16[1,4,96,2048]{3,2,1,0:T(8,128)(2,1)S(1)}, u32[]{:S(2)}, u32[]{:S(2)}) collective-permute-start(bf16[1,4,96,2048]{3,2,1,0:T(8,128)(2,1)S(1)} %collective-permute-done.12.refs_9_), channel_id=1, source_target_pairs={{0,4},{4,0},{8,12},{12,8},{16,20},{20,16},{24,28},{28,24},{1,5},{5... | collective-permute-start | bytes 4718600 | tf_op jit(solution)/shard_map/ppermute | solution.py:366
  73.3 4.2 %collective-permute-start.11 = (bf16[1,4,96,896]{3,2,1,0:T(8,128)(2,1)S(1)}, bf16[1,4,96,896]{3,2,1,0:T(8,128)(2,1)S(1)}, u32[]{:S(2)}, u32[]{:S(2)}) collective-permute-start(bf16[1,4,96,896]{3,2,1,0:T(8,128)(2,1)S(1)} %get-tuple-element.44), channel_id=1, source_target_pairs={{0,4},{4,0},{8,12},{12,8},{16,20},{20,16},{24,28},{28,24},{1,5},{5... | collective-permute-start | bytes 2064392 | tf_op jit(solution)/shard_map/ppermute | solution.py:366
  76.9 14.0 %collective-permute-start.18 = (bf16[1,4,96,1152]{3,2,1,0:T(8,128)(2,1)S(1)}, bf16[1,4,96,1152]{3,2,1,0:T(8,128)(2,1)S(1)}, u32[]{:S(2)}, u32[]{:S(2)}) collective-permute-start(bf16[1,4,96,1152]{3,2,1,0:T(8,128)(2,1)S(1)} %get-tuple-element.41), channel_id=1, source_target_pairs={{0,4},{4,0},{8,12},{12,8},{16,20},{20,16},{24,28},{28,24},{1,5},{5... | collective-permute-start | bytes 2654216 | tf_op jit(solution)/shard_map/ppermute | solution.py:366
  77.7 26.3 %collective-permute-start.15 = (bf16[1,4,96,896]{3,2,1,0:T(8,128)(2,1)S(1)}, bf16[1,4,96,896]{3,2,1,0:T(8,128)(2,1)S(1)}, u32[]{:S(2)}, u32[]{:S(2)}) collective-permute-start(bf16[1,4,96,896]{3,2,1,0:T(8,128)(2,1)S(1)} %shard_map.82), channel_id=1, source_target_pairs={{0,8},{4,12},{8,0},{12,4},{16,24},{20,28},{24,16},{28,20},{1,9},{5... | collective-permute-start | bytes 2064392 | tf_op jit(solution)/shard_map/ppermute | solution.py:366
  85.8 3.7 %collective-permute-start.14 = (f32[4,4,1,128]{3,2,1,0:T(1,128)S(1)}, f32[4,4,1,128]{3,2,1,0:T(1,128)S(1)}, u32[]{:S(2)}, u32[]{:S(2)}) collective-permute-start(f32[4,4,1,128]{3,2,1,0:T(1,128)S(1)} %get-tuple-element.48), channel_id=1, source_target_pairs={{0,16},{4,20},{8,24},{12,28},{16,0},{20,4},{24,8},{28,12},{1,17},{... | collective-permute-start | bytes 24584 | tf_op jit(solution)/shard_map/ppermute | solution.py:366
  89.5 26.5 %collective-permute-start.20 = (bf16[4,4,72,384]{3,2,1,0:T(8,128)(2,1)S(1)}, bf16[4,4,72,384]{3,2,1,0:T(8,128)(2,1)S(1)}, u32[]{:S(2)}, u32[]{:S(2)}) collective-permute-start(bf16[4,4,72,384]{3,2,1,0:T(8,128)(2,1)S(1)} %get-tuple-element.61), channel_id=1, source_target_pairs={{0,16},{4,20},{8,24},{12,28},{16,0},{20,4},{24,8},{28,12},{1,17},{... | collective-permute-start | bytes 2654216 | tf_op jit(solution)/shard_map/ppermute | solution.py:366
  91.2 24.7 %collective-permute-start.19 = (bf16[1,4,96,1152]{3,2,1,0:T(8,128)(2,1)S(1)}, bf16[1,4,96,1152]{3,2,1,0:T(8,128)(2,1)S(1)}, u32[]{:S(2)}, u32[]{:S(2)}) collective-permute-start(bf16[1,4,96,1152]{3,2,1,0:T(8,128)(2,1)S(1)} %shard_map.87), channel_id=1, source_target_pairs={{0,8},{4,12},{8,0},{12,4},{16,24},{20,28},{24,16},{28,20},{1,9},{5... | collective-permute-start | bytes 2654216 | tf_op jit(solution)/shard_map/ppermute | solution.py:366
  104.0 11.5 %collective-permute-start.17 = (bf16[1,4,96,1024]{3,2,1,0:T(8,128)(2,1)S(1)}, bf16[1,4,96,1024]{3,2,1,0:T(8,128)(2,1)S(1)}, u32[]{:S(2)}, u32[]{:S(2)}) collective-permute-start(bf16[1,4,96,1024]{3,2,1,0:T(8,128)(2,1)S(1)} %get-tuple-element.58), channel_id=1, source_target_pairs={{0,4},{4,0},{8,12},{12,8},{16,20},{20,16},{24,28},{28,24},{1,5},{5... | collective-permute-start | bytes 2359304 | tf_op jit(solution)/shard_map/ppermute | solution.py:366
  104.1 11.4 %collective-permute-start.16 = (bf16[1,4,96,1024]{3,2,1,0:T(8,128)(2,1)S(1)}, bf16[1,4,96,1024]{3,2,1,0:T(8,128)(2,1)S(1)}, u32[]{:S(2)}, u32[]{:S(2)}) collective-permute-start(bf16[1,4,96,1024]{3,2,1,0:T(8,128)(2,1)S(1)} %get-tuple-element.56), channel_id=1, source_target_pairs={{0,4},{4,0},{8,12},{12,8},{16,20},{20,16},{24,28},{28,24},{1,5},{5... | collective-permute-start | bytes 2359304 | tf_op jit(solution)/shard_map/ppermute | solution.py:366

commit v8 on v7

--- a/solution.py
+++ b/solution.py
@@ -36,7 +36,7 @@
             w_row, r_row = table[at : at + 1], rank[at : at + 1]
             place = jnp.where(slots == r_row, w_row, 0.0).astype(BF)
             moved = lax.dot_general(
-                hid_ref[0, e, s, :CAP], place, (((0,), (0,)), ((), ())), preferred_element_type=F32
+                hid_ref[0, e, s][:CAP], place, (((0,), (0,)), ((), ())), preferred_element_type=F32
             )
             hst_ref[e, :, k * toks : (k + 1) * toks] = moved.astype(BF)
             wt_ref[k, e] = w_row
@@ -71,11 +71,11 @@
 def pack_kernel(lefts, sc_ref, hid_ref, tok_ref, out_ref):
     _, experts, n, cap, f = hid_ref.shape
     toks = tok_ref.shape[0]
+    blank = jnp.zeros((PADDED - cap, f), BF)
     for e in range(experts):
         for s in range(n):
             at = (e * n + s) * PADDED
-            out_ref[at : at + cap] = hid_ref[0, e, s]
-            out_ref[at + cap : at + PADDED] = jnp.zeros((PADDED - cap, f), BF)
+            out_ref[at : at + PADDED] = jnp.concatenate([hid_ref[0, e, s], blank], axis=0)
     for i, left in enumerate(lefts):
         at = experts * n * PADDED + i * toks
         out_ref[at : at + toks] = tok_ref[:, left : left + f]
@@ -200,7 +200,7 @@
             zk = z[k * toks : (k + 1) * toks, e * f : (e + 1) * f]
             gh_ref[e, s] = jnp.dot(weigh, zk.astype(BF), preferred_element_type=F32).astype(BF)
             hid = lax.dot_general(
-                pick, hid_ref[0, e, s, :CAP], (((0,), (0,)), ((), ())), preferred_element_type=F32
+                pick, hid_ref[0, e, s][:CAP], (((0,), (0,)), ((), ())), preferred_element_type=F32
             )
             sg_col = jnp.sum(zk * hid, axis=1, keepdims=True)
             sg_row = jnp.sum(jnp.where(eye, sg_col, 0.0), axis=0, keepdims=True)
@@ -451,7 +451,7 @@
     while mid:
         total = base.astype(F32) + there[0].astype(F32)
         base, there, mid = total[:mid].astype(BF), [swap(total[mid:].astype(BF), 4 * mid)], mid // 2
-    gh_in = swap(after(gh_nb, sg_in), bands)
+    gh_in = swap(after(gh_nb, sg_in, sums[1]), bands)
     grad_down, grad_hidden = finish(scalars, base, there, gh_in, gh_own)
     by_expert = by_expert.reshape(EXPERTS, 1, toks)
     chosen = expert_ids.T[None] == jnp.arange(EXPERTS, dtype=jnp.int32)[:, None, None]

time: 119 us -> 119 us (level)
  no operation moved by 1% of the time
where the time goes in v8:
time: 119 us; the launch traced here: 118 us
  waiting for transfers between devices  41.1 us (35%)
  Pallas kernels  32.9 us (28%)
  starting transfers between devices  29.4 us (25%)
  blocking collectives  10.3 us (9%)
  local copies, waits for them, and re-layouts  2.71 us (2%)
    ppermute x2, waiting for transfers between devices, spread(): two = lax.ppermute(x, 'expert', [(i, (i + 2) % n) for i in range(n)])  22.7 us
    pallas_call x2, Pallas kernels, backward(): pl.pallas_call(functools.partial(back_kernel, n, counts, group, rels), ou...  13.7 us
    ppermute x13, starting transfers between devices, swap(): return lax.ppermute(x, 'dp', [(i, i ^ bit) for i in range(n_dp)])  12 us
    pallas_call x3, Pallas kernels, partial_grad(): pl.pallas_call(functools.partial(part_kernel, n, bands, (counts, counts_n...  11.8 us
    all_to_all x1, blocking collectives, per_device(): lax.all_to_all(sg_own, 'expert', split_axis=0, concat_axis=0, tiled=True)  10.3 us
    ppermute x2, waiting for transfers between devices, spread(): passed = lax.ppermute(two, 'expert', [(2, 3), (1, 0)])  7.04 us
    ppermute x2, starting transfers between devices, spread(): one = lax.ppermute(x, 'expert', [(i, i + 1) for i in range(n - 1)])  6.98 us
    ppermute x2, waiting for transfers between devices, spread(): three = lax.ppermute(x, 'expert', [(i + 1, i) for i in range(n - 1)])  5.71 us
  transfers between devices with their start and end apart: 21, of which 7 were waited for; matrix products, arithmetic and copies ran while one was open for 1% of the time, Pallas kernels for 26%

profile of v8, /device:TPU:0, one launch (start us, length us, event | category | flops | bytes accessed | tf_op | source)
XLA Modules:
  0.0 118.2 jit_solution(5786836351048303039)
XLA Ops:
  0.6 0.5 collective-permute-start.4
  1.1 0.1 pad_add_fusion.sc_ref
  1.2 1.5 %copy-done = bf16[1,4,4,72,768]{4,3,2,1,0:T(8,128)(2,1)S(1)} copy-done((bf16[1,4,4,72,768]{4,3,2,1,0:T(8,128)(2,1)S(1)}, bf16[1,4,4,72,768]{4,3,2,1,0:T(8,128)(2,1)}, u32[]{:S(2)}) %copy-start) | copy-done | bytes 1769496
  2.7 1.0 copy-done.3
  3.8 0.8 shard_map.77
  4.5 2.7 %collective-permute-start.5 = (bf16[2048,384]{1,0:T(8,128)(2,1)S(1)}, bf16[2048,384]{1,0:T(8,128)(2,1)S(1)}, u32[]{:S(2)}, u32[]{:S(2)}) collective-permute-start(bf16[2048,384]{1,0:T(8,128)(2,1)S(1)} %shard_map.77), channel_id=1, source_target_pairs={{0,16},{4,20},{8,24},{12,28},{16,0},{20,4},{24,8},{28,12},{1,17},{... | collective-permute-start | bytes 4718600 | tf_op jit(solution)/shard_map/ppermute | solution.py:366
  7.4 0.0 slice-start.1
  7.4 2.7 %collective-permute-start.1 = (bf16[136,1408]{1,0:T(8,128)(2,1)S(1)}, bf16[136,1408]{1,0:T(8,128)(2,1)S(1)}, u32[]{:S(2)}, u32[]{:S(2)}) collective-permute-start(bf16[136,1408]{1,0:T(8,128)(2,1)S(1)} %pad_maximum_fusion.refs_0_), channel_id=1, source_target_pairs={{0,2},{1,3},{2,0},{3,1},{4,6},{5,7},{6,4},{7,5},{8,10},{9,11},{10,... | collective-permute-start | bytes 1148936 | tf_op jit(solution)/shard_map/ppermute | solution.py:373
  10.1 1.5 %collective-permute-start.12 = (bf16[1,4,96,2048]{3,2,1,0:T(8,128)(2,1)S(1)}, bf16[1,4,96,2048]{3,2,1,0:T(8,128)(2,1)S(1)}, u32[]{:S(2)}, u32[]{:S(2)}) collective-permute-start(bf16[1,4,96,2048]{3,2,1,0:T(8,128)(2,1)S(1)} %bitcast.12), channel_id=1, source_target_pairs={{0,8},{4,12},{8,0},{12,4},{16,24},{20,28},{24,16},{28,20},{1,9},{5... | collective-permute-start | bytes 4718600 | tf_op jit(solution)/shard_map/ppermute | solution.py:366
  11.6 3.5 %collective-permute-start = (bf16[136,1408]{1,0:T(8,128)(2,1)S(1)}, bf16[136,1408]{1,0:T(8,128)(2,1)S(1)}, u32[]{:S(2)}, u32[]{:S(2)}) collective-permute-start(bf16[136,1408]{1,0:T(8,128)(2,1)S(1)} %pad_maximum_fusion.refs_0_), channel_id=1, source_target_pairs={{0,1},{1,2},{2,3},{4,5},{5,6},{6,7},{8,9},{9,10},{10,11},{12,13},{... | collective-permute-start | bytes 1148936 | tf_op jit(solution)/shard_map/ppermute | solution.py:374
  15.1 1.3 %collective-permute-start.2 = (bf16[136,1408]{1,0:T(8,128)(2,1)S(1)}, bf16[136,1408]{1,0:T(8,128)(2,1)S(1)}, u32[]{:S(2)}, u32[]{:S(2)}) collective-permute-start(bf16[136,1408]{1,0:T(8,128)(2,1)S(1)} %pad_maximum_fusion.refs_0_), channel_id=1, source_target_pairs={{1,0},{2,1},{3,2},{5,4},{6,5},{7,6},{9,8},{10,9},{11,10},{13,12},{... | collective-permute-start | bytes 1148936 | tf_op jit(solution)/shard_map/ppermute | solution.py:375
  16.4 12.0 %collective-permute-done.1.refs_2_ = bf16[136,1408]{1,0:T(8,128)(2,1)S(1)} collective-permute-done((bf16[136,1408]{1,0:T(8,128)(2,1)S(1)}, bf16[136,1408]{1,0:T(8,128)(2,1)S(1)}, u32[]{:S(2)}, u32[]{:S(2)}) %collective-permute-start.1) | collective-permute-done | bytes 383008 | tf_op jit(solution)/shard_map/ppermute | solution.py:373
  28.4 1.3 %collective-permute-start.3 = (bf16[136,1408]{1,0:T(8,128)(2,1)S(1)}, bf16[136,1408]{1,0:T(8,128)(2,1)S(1)}, u32[]{:S(2)}, u32[]{:S(2)}) collective-permute-start(bf16[136,1408]{1,0:T(8,128)(2,1)S(1)} %collective-permute-done.1.refs_2_), channel_id=1, source_target_pairs={{2,3},{1,0},{6,7},{5,4},{10,11},{9,8},{14,15},{13,12},{18,19},{17,... | collective-permute-start | bytes 1148936 | tf_op jit(solution)/shard_map/ppermute | solution.py:376
  29.7 5.7 %collective-permute-done.2.refs_3_ = bf16[136,1408]{1,0:T(8,128)(2,1)S(1)} collective-permute-done((bf16[136,1408]{1,0:T(8,128)(2,1)S(1)}, bf16[136,1408]{1,0:T(8,128)(2,1)S(1)}, u32[]{:S(2)}, u32[]{:S(2)}) %collective-permute-start.2) | collective-permute-done | bytes 383008 | tf_op jit(solution)/shard_map/ppermute | solution.py:375
  35.4 6.9 %collective-permute-done.3.refs_4_ = bf16[136,1408]{1,0:T(8,128)(2,1)S(1)} collective-permute-done((bf16[136,1408]{1,0:T(8,128)(2,1)S(1)}, bf16[136,1408]{1,0:T(8,128)(2,1)S(1)}, u32[]{:S(2)}, u32[]{:S(2)}) %collective-permute-start.3) | collective-permute-done | bytes 383008 | tf_op jit(solution)/shard_map/ppermute | solution.py:376
  42.3 0.7 shard_map.76.tab_ref.refs_1_
  43.0 1.0 collective-permute-start.6
  43.9 0.1 fusion.4
  44.0 2.7 %collective-permute-start.8 = (bf16[256,640]{1,0:T(8,128)(2,1)S(1)}, bf16[256,640]{1,0:T(8,128)(2,1)S(1)}, u32[]{:S(2)}, u32[]{:S(2)}) collective-permute-start(bf16[256,640]{1,0:T(8,128)(2,1)S(1)} %fusion.refs_2_.refs_9_), channel_id=1, source_target_pairs={{0,2},{1,3},{2,0},{3,1},{4,6},{5,7},{6,4},{7,5},{8,10},{9,11},{10,... | collective-permute-start | bytes 983048 | tf_op jit(solution)/shard_map/ppermute | solution.py:373
  46.7 3.5 %collective-permute-start.7 = (bf16[256,640]{1,0:T(8,128)(2,1)S(1)}, bf16[256,640]{1,0:T(8,128)(2,1)S(1)}, u32[]{:S(2)}, u32[]{:S(2)}) collective-permute-start(bf16[256,640]{1,0:T(8,128)(2,1)S(1)} %fusion.refs_2_.refs_9_), channel_id=1, source_target_pairs={{0,1},{1,2},{2,3},{4,5},{5,6},{6,7},{8,9},{9,10},{10,11},{12,13},{... | collective-permute-start | bytes 983048 | tf_op jit(solution)/shard_map/ppermute | solution.py:374
  50.2 1.3 %collective-permute-start.9 = (bf16[256,640]{1,0:T(8,128)(2,1)S(1)}, bf16[256,640]{1,0:T(8,128)(2,1)S(1)}, u32[]{:S(2)}, u32[]{:S(2)}) collective-permute-start(bf16[256,640]{1,0:T(8,128)(2,1)S(1)} %fusion.refs_2_.refs_9_), channel_id=1, source_target_pairs={{1,0},{2,1},{3,2},{5,4},{6,5},{7,6},{9,8},{10,9},{11,10},{13,12},{... | collective-permute-start | bytes 983048 | tf_op jit(solution)/shard_map/ppermute | solution.py:375
  51.5 10.6 %collective-permute-done.8.refs_4_.refs_11_ = bf16[256,640]{1,0:T(8,128)(2,1)S(1)} collective-permute-done((bf16[256,640]{1,0:T(8,128)(2,1)S(1)}, bf16[256,640]{1,0:T(8,128)(2,1)S(1)}, u32[]{:S(2)}, u32[]{:S(2)}) %collective-permute-start.8) | collective-permute-done | bytes 327712 | tf_op jit(solution)/shard_map/ppermute | solution.py:373
  62.1 1.3 %collective-permute-start.10 = (bf16[256,640]{1,0:T(8,128)(2,1)S(1)}, bf16[256,640]{1,0:T(8,128)(2,1)S(1)}, u32[]{:S(2)}, u32[]{:S(2)}) collective-permute-start(bf16[256,640]{1,0:T(8,128)(2,1)S(1)} %collective-permute-done.8.refs_4_.refs_11_), channel_id=1, source_target_pairs={{2,3},{1,0},{6,7},{5,4},{10,11},{9,8},{14,15},{13,12},{18,19},{17,... | collective-permute-start | bytes 983048 | tf_op jit(solution)/shard_map/ppermute | solution.py:376
  63.4 0.1 collective-permute-start.13
  63.5 1.3 %shard_map.78 = (bf16[4,384,512]{2,1,0:T(8,128)(2,1)S(1)}, f32[4,4,1,128]{3,2,1,0:T(1,128)S(1)}, f32[4,4,1,128]{3,2,1,0:T(1,128)S(1)}) custom-call(s32[3]{0:T(128)S(1)} %pad_add_fusion.sc_ref, bf16[400,1408]{1,0:T(8,128)(2,1)S(1)} %shard_map.76.tab_ref.refs_1_, bf16[1,4,4,72,768]{4,3,2,1,0:T(8,128)(2,1)S(1)} %copy-done.1), custom_call_target="tpu_custom_call" | custom-call | flops 1 | bytes 1 | tf_op jit(solution)/shard_map/pallas_call | solution.py:50
  64.9 0.1 slice.60
  65.0 3.7 %collective-permute-done.6.tab_ref.refs_3_.refs_8_.refs_1_ = bf16[400,1408]{1,0:T(8,128)(2,1)S(1)} collective-permute-done((bf16[400,1408]{1,0:T(8,128)(2,1)S(1)}, bf16[400,1408]{1,0:T(8,128)(2,1)S(1)}, u32[]{:S(2)}, u32[]{:S(2)}) %collective-permute-start.6) | collective-permute-done | bytes 1126432 | tf_op jit(solution)/shard_map/ppermute | solution.py:366
  68.7 1.3 %shard_map.79 = (bf16[4,384,512]{2,1,0:T(8,128)(2,1)S(1)}, f32[4,4,1,128]{3,2,1,0:T(1,128)S(1)}, f32[4,4,1,128]{3,2,1,0:T(1,128)S(1)}) custom-call(s32[3]{0:T(128)S(1)} %pad_add_fusion.sc_ref, bf16[400,1408]{1,0:T(8,128)(2,1)S(1)} %collective-permute-done.6.tab_ref.refs_3_.refs_8_.refs_1_, bf16[1,4,4,80,384]{4,3,2,1,0:T(8,128)(2,1)S(1)} %bitcast.9), custom_call_target="tpu_custom_call" | custom-call | flops 1 | bytes 1 | tf_op jit(solution)/shard_map/pallas_call | solution.py:50
  70.0 3.2 %shard_map.80 = (bf16[1,4,96,896]{3,2,1,0:T(8,128)(2,1)S(1)}, bf16[1,4,96,896]{3,2,1,0:T(8,128)(2,1)S(1)}) custom-call(s32[3]{0:T(128)S(1)} %pad_add_fusion.sc_ref, bf16[136,1408]{1,0:T(8,128)(2,1)S(1)} %pad_maximum_fusion.refs_0_, bf16[400,1408]{1,0:T(8,128)(2,1)S(1)} %shard_map.76.tab_ref.refs_1_, ...), custom_call_target="tpu_custom_call" | custom-call | flops 1 | bytes 1 | tf_op jit(solution)/shard_map/pallas_call | solution.py:282
  73.2 0.1 collective-permute-done.10.refs_6_.refs_13_
  73.3 3.6 %shard_map.81 = (bf16[1,4,96,1152]{3,2,1,0:T(8,128)(2,1)S(1)}, bf16[1,4,96,1152]{3,2,1,0:T(8,128)(2,1)S(1)}) custom-call(s32[3]{0:T(128)S(1)} %pad_add_fusion.sc_ref, bf16[136,1408]{1,0:T(8,128)(2,1)S(1)} %pad_maximum_fusion.refs_0_, bf16[400,1408]{1,0:T(8,128)(2,1)S(1)} %shard_map.76.tab_ref.refs_1_, bf16[256,640]{1,0:T(8,128)(2,1)S(1)} %fusion.refs_2_.refs_9_, ...), custom_call_target="tpu_custom_call" | custom-call | flops 1 | bytes 1 | tf_op jit(solution)/shard_map/pallas_call | solution.py:282
  76.9 0.6 collective-permute-start.18
  77.5 0.2 shard_map.82
  77.8 1.6 %collective-permute-start.15 = (bf16[1,4,96,896]{3,2,1,0:T(8,128)(2,1)S(1)}, bf16[1,4,96,896]{3,2,1,0:T(8,128)(2,1)S(1)}, u32[]{:S(2)}, u32[]{:S(2)}) collective-permute-start(bf16[1,4,96,896]{3,2,1,0:T(8,128)(2,1)S(1)} %shard_map.82), channel_id=1, source_target_pairs={{0,8},{4,12},{8,0},{12,4},{16,24},{20,28},{24,16},{28,20},{1,9},{5... | collective-permute-start | bytes 2064392 | tf_op jit(solution)/shard_map/ppermute | solution.py:366
  79.3 6.5 %shard_map.83 = (bf16[4,4,72,384]{3,2,1,0:T(8,128)(2,1)S(1)}, f32[4,4,1,128]{3,2,1,0:T(1,128)S(1)}) custom-call(s32[3]{0:T(128)S(1)} %pad_add_fusion.sc_ref, bf16[128,1408]{1,0:T(8,128)(2,1)S(1)} %pad_maximum_fusion.1.refs_2_.refs_7_.refs_0_, bf16[400,1408]{1,0:T(8,128)(2,1)S(1)} %collective-permute-done.6.tab_ref.refs_3_.refs_8_.refs_1_, ...), custom_call_target="tpu_custom_call" | custom-call | flops 1 | bytes 1 | tf_op jit(solution)/shard_map/pallas_call | solution.py:218
  85.8 1.5 %collective-permute-start.14 = (f32[4,4,1,128]{3,2,1,0:T(1,128)S(1)}, f32[4,4,1,128]{3,2,1,0:T(1,128)S(1)}, u32[]{:S(2)}, u32[]{:S(2)}) collective-permute-start(f32[4,4,1,128]{3,2,1,0:T(1,128)S(1)} %get-tuple-element.48), channel_id=1, source_target_pairs={{0,16},{4,20},{8,24},{12,28},{16,0},{20,4},{24,8},{28,12},{1,17},{... | collective-permute-start | bytes 24584 | tf_op jit(solution)/shard_map/ppermute | solution.py:366
  87.3 0.3 shard_map.87
  87.6 1.9 %collective-permute-done.14.refs_14_ = f32[4,4,1,128]{3,2,1,0:T(1,128)S(1)} collective-permute-done((f32[4,4,1,128]{3,2,1,0:T(1,128)S(1)}, f32[4,4,1,128]{3,2,1,0:T(1,128)S(1)}, u32[]{:S(2)}, u32[]{:S(2)}) %collective-permute-start.14) | collective-permute-done | bytes 8224 | tf_op jit(solution)/shard_map/ppermute | solution.py:366
  89.5 1.5 %collective-permute-start.20 = (bf16[4,4,72,384]{3,2,1,0:T(8,128)(2,1)S(1)}, bf16[4,4,72,384]{3,2,1,0:T(8,128)(2,1)S(1)}, u32[]{:S(2)}, u32[]{:S(2)}) collective-permute-start(bf16[4,4,72,384]{3,2,1,0:T(8,128)(2,1)S(1)} %get-tuple-element.61), channel_id=1, source_target_pairs={{0,16},{4,20},{8,24},{12,28},{16,0},{20,4},{24,8},{28,12},{1,17},{... | collective-permute-start | bytes 2654216 | tf_op jit(solution)/shard_map/ppermute | solution.py:366
  91.0 0.5 collective-permute-start.19
  91.5 7.2 %shard_map.84 = (bf16[4,4,72,768]{3,2,1,0:T(8,128)(2,1)}, f32[4,4,1,128]{3,2,1,0:T(1,128)S(1)}) custom-call(s32[3]{0:T(128)S(1)} %pad_add_fusion.sc_ref, bf16[136,1408]{1,0:T(8,128)(2,1)S(1)} %pad_maximum_fusion.refs_0_, bf16[400,1408]{1,0:T(8,128)(2,1)S(1)} %shard_map.76.tab_ref.refs_1_, bf16[256,640]{1,0:T(8,128)(2,1)S(1)} %fusion.refs_2_.refs_9_, ...), custom_call_target="tpu_custom_call" | custom-call | flops 1 | bytes 1 | tf_op jit(solution)/shard_map/pallas_call | solution.py:218
  98.7 5.0 %shard_map.85 = (bf16[1,4,96,1024]{3,2,1,0:T(8,128)(2,1)S(1)}, bf16[1,4,96,1024]{3,2,1,0:T(8,128)(2,1)S(1)}, bf16[1,4,96,2048]{3,2,1,0:T(8,128)(2,1)S(1)}) custom-call(s32[3]{0:T(128)S(1)} %pad_add_fusion.sc_ref, bf16[136,1408]{1,0:T(8,128)(2,1)S(1)} %pad_maximum_fusion.refs_0_, bf16[400,1408]{1,0:T(8,128)(2,1)S(1)} %shard_map.76.tab_ref.refs_1_, ...), custom_call_target="tpu_custom_call" | custom-call | flops 1 | bytes 1 | tf_op jit(solution)/shard_map/pallas_call | solution.py:282
  103.7 0.1 collective-permute-start.17
  103.8 0.5 collective-permute-start.16
  104.3 10.3 %all_to_all.5 = f32[4,4,1,128]{3,2,1,0:T(1,128)S(1)} all-to-all(f32[4,4,1,128]{3,2,1,0:T(1,128)S(1)} %get-tuple-element.52), channel_id=1, replica_groups=mesh['dp'=8,'expert'=4] {'expert'}, dimensions={0} | all-to-all | bytes 16384 | tf_op jit(solution)/shard_map/all_to_all | solution.py:443
  114.6 0.6 select_reduce_fusion
  115.2 0.4 shard_map.86.base_ref
  115.6 2.6 %shard_map.88 = (bf16[4,96,2048]{2,1,0:T(8,128)(2,1)}, bf16[4,4,72,768]{3,2,1,0:T(8,128)(2,1)}) custom-call(s32[3]{0:T(128)S(1)} %pad_add_fusion.sc_ref, bf16[1,4,96,2048]{3,2,1,0:T(8,128)(2,1)S(1)} %shard_map.86.base_ref, bf16[1,4,96,896]{3,2,1,0:T(8,128)(2,1)S(1)} %collective-permute-done.15.refs_0_, ...), custom_call_target="tpu_custom_call", output_to_operand_aliasing={{1}: (5, {})} | custom-call | flops 1 | bytes 1 | tf_op jit(solution)/shard_map/pallas_call | solution.py:335
  (36 shorter events, 0.2 us)
Async XLA Ops:
  0.6 3.9 %collective-permute-start.4 = (bf16[1,4,96,2048]{3,2,1,0:T(8,128)(2,1)}, bf16[1,4,96,2048]{3,2,1,0:T(8,128)(2,1)S(1)}, u32[]{:S(2)}, u32[]{:S(2)}) collective-permute-start(bf16[1,4,96,2048]{3,2,1,0:T(8,128)(2,1)} %bitcast.11), channel_id=1, source_target_pairs={{0,4},{4,0},{8,12},{12,8},{16,20},{20,16},{24,28},{28,24},{1,5},{5... | collective-permute-start | bytes 4718600 | tf_op jit(solution)/shard_map/ppermute | solution.py:366
  1.2 1.5 %copy-start = (bf16[1,4,4,72,768]{4,3,2,1,0:T(8,128)(2,1)S(1)}, bf16[1,4,4,72,768]{4,3,2,1,0:T(8,128)(2,1)}, u32[]{:S(2)}) copy-start(bf16[1,4,4,72,768]{4,3,2,1,0:T(8,128)(2,1)} %refs_11_.1) | copy-start | bytes 5308420
  2.7 1.0 copy-start.3
  3.7 3.5 %copy-start.5 = (bf16[128,8]{0,1:T(8,128)(2,1)S(1)}, bf16[128,8]{0,1:T(8,128)(2,1)}, u32[]{:S(2)}) copy-start(bf16[128,8]{0,1:T(8,128)(2,1)} %param.7) | copy-start | bytes 6148
  3.7 3.5 %copy-start.4 = (s32[128,8]{0,1:T(8,128)S(1)}, s32[128,8]{0,1:T(8,128)}, u32[]{:S(2)}) copy-start(s32[128,8]{0,1:T(8,128)} %param.6) | copy-start | bytes 12292
  3.7 3.6 %slice-start = ((bf16[128,2048]{1,0:T(8,128)(2,1)}), bf16[128,1408]{1,0:T(8,128)(2,1)S(1)}, s32[]{:S(2)}) async-start(bf16[128,2048]{1,0:T(8,128)(2,1)} %tok_ref.1), calls=%async_computation.1 | async-start | bytes 720896 | tf_op jit(solution)/shard_map/slice | solution.py:385
  3.8 6.3 %copy-start.2 = (bf16[4,96,2048]{2,1,0:T(8,128)(2,1)S(1)}, bf16[4,96,2048]{2,1,0:T(8,128)(2,1)}, u32[]{:S(2)}) copy-start(bf16[4,96,2048]{2,1,0:T(8,128)(2,1)} %param.9) | copy-start | bytes 4718596
  4.5 38.4 %collective-permute-start.5 = (bf16[2048,384]{1,0:T(8,128)(2,1)S(1)}, bf16[2048,384]{1,0:T(8,128)(2,1)S(1)}, u32[]{:S(2)}, u32[]{:S(2)}) collective-permute-start(bf16[2048,384]{1,0:T(8,128)(2,1)S(1)} %shard_map.77), channel_id=1, source_target_pairs={{0,16},{4,20},{8,24},{12,28},{16,0},{20,4},{24,8},{28,12},{1,17},{... | collective-permute-start | bytes 4718600 | tf_op jit(solution)/shard_map/ppermute | solution.py:366
  7.4 36.6 %slice-start.1 = ((bf16[128,2048]{1,0:T(8,128)(2,1)}), bf16[128,640]{1,0:T(8,128)(2,1)S(1)}, s32[]{:S(2)}) async-start(bf16[128,2048]{1,0:T(8,128)(2,1)} %tok_ref.1), calls=%async_computation.2 | async-start | bytes 327680 | tf_op jit(solution)/shard_map/slice | solution.py:408
  7.4 21.0 %collective-permute-start.1 = (bf16[136,1408]{1,0:T(8,128)(2,1)S(1)}, bf16[136,1408]{1,0:T(8,128)(2,1)S(1)}, u32[]{:S(2)}, u32[]{:S(2)}) collective-permute-start(bf16[136,1408]{1,0:T(8,128)(2,1)S(1)} %pad_maximum_fusion.refs_0_), channel_id=1, source_target_pairs={{0,2},{1,3},{2,0},{3,1},{4,6},{5,7},{6,4},{7,5},{8,10},{9,11},{10,... | collective-permute-start | bytes 1148936 | tf_op jit(solution)/shard_map/ppermute | solution.py:373
  10.1 53.4 %collective-permute-start.12 = (bf16[1,4,96,2048]{3,2,1,0:T(8,128)(2,1)S(1)}, bf16[1,4,96,2048]{3,2,1,0:T(8,128)(2,1)S(1)}, u32[]{:S(2)}, u32[]{:S(2)}) collective-permute-start(bf16[1,4,96,2048]{3,2,1,0:T(8,128)(2,1)S(1)} %bitcast.12), channel_id=1, source_target_pairs={{0,8},{4,12},{8,0},{12,4},{16,24},{20,28},{24,16},{28,20},{1,9},{5... | collective-permute-start | bytes 4718600 | tf_op jit(solution)/shard_map/ppermute | solution.py:366
  11.6 18.1 %collective-permute-start = (bf16[136,1408]{1,0:T(8,128)(2,1)S(1)}, bf16[136,1408]{1,0:T(8,128)(2,1)S(1)}, u32[]{:S(2)}, u32[]{:S(2)}) collective-permute-start(bf16[136,1408]{1,0:T(8,128)(2,1)S(1)} %pad_maximum_fusion.refs_0_), channel_id=1, source_target_pairs={{0,1},{1,2},{2,3},{4,5},{5,6},{6,7},{8,9},{9,10},{10,11},{12,13},{... | collective-permute-start | bytes 1148936 | tf_op jit(solution)/shard_map/ppermute | solution.py:374
  15.1 20.3 %collective-permute-start.2 = (bf16[136,1408]{1,0:T(8,128)(2,1)S(1)}, bf16[136,1408]{1,0:T(8,128)(2,1)S(1)}, u32[]{:S(2)}, u32[]{:S(2)}) collective-permute-start(bf16[136,1408]{1,0:T(8,128)(2,1)S(1)} %pad_maximum_fusion.refs_0_), channel_id=1, source_target_pairs={{1,0},{2,1},{3,2},{5,4},{6,5},{7,6},{9,8},{10,9},{11,10},{13,12},{... | collective-permute-start | bytes 1148936 | tf_op jit(solution)/shard_map/ppermute | solution.py:375
  28.4 13.9 %collective-permute-start.3 = (bf16[136,1408]{1,0:T(8,128)(2,1)S(1)}, bf16[136,1408]{1,0:T(8,128)(2,1)S(1)}, u32[]{:S(2)}, u32[]{:S(2)}) collective-permute-start(bf16[136,1408]{1,0:T(8,128)(2,1)S(1)} %collective-permute-done.1.refs_2_), channel_id=1, source_target_pairs={{2,3},{1,0},{6,7},{5,4},{10,11},{9,8},{14,15},{13,12},{18,19},{17,... | collective-permute-start | bytes 1148936 | tf_op jit(solution)/shard_map/ppermute | solution.py:376
  42.9 20.6 %copy-start.1 = (bf16[1,4,4,72,768]{4,3,2,1,0:T(8,128)(2,1)S(1)}, bf16[1,4,4,72,768]{4,3,2,1,0:T(8,128)(2,1)}, u32[]{:S(2)}) copy-start(bf16[1,4,4,72,768]{4,3,2,1,0:T(8,128)(2,1)} %refs_11_.1) | copy-start | bytes 5308420
  43.0 25.7 %collective-permute-start.6 = (bf16[400,1408]{1,0:T(8,128)(2,1)S(1)}, bf16[400,1408]{1,0:T(8,128)(2,1)S(1)}, u32[]{:S(2)}, u32[]{:S(2)}) collective-permute-start(bf16[400,1408]{1,0:T(8,128)(2,1)S(1)} %shard_map.76.tab_ref.refs_1_), channel_id=1, source_target_pairs={{0,16},{4,20},{8,24},{12,28},{16,0},{20,4},{24,8},{28,12},{1,17},{... | collective-permute-start | bytes 3379208 | tf_op jit(solution)/shard_map/ppermute | solution.py:366
  44.0 18.1 %collective-permute-start.8 = (bf16[256,640]{1,0:T(8,128)(2,1)S(1)}, bf16[256,640]{1,0:T(8,128)(2,1)S(1)}, u32[]{:S(2)}, u32[]{:S(2)}) collective-permute-start(bf16[256,640]{1,0:T(8,128)(2,1)S(1)} %fusion.refs_2_.refs_9_), channel_id=1, source_target_pairs={{0,2},{1,3},{2,0},{3,1},{4,6},{5,7},{6,4},{7,5},{8,10},{9,11},{10,... | collective-permute-start | bytes 983048 | tf_op jit(solution)/shard_map/ppermute | solution.py:373
  46.7 26.5 %collective-permute-start.7 = (bf16[256,640]{1,0:T(8,128)(2,1)S(1)}, bf16[256,640]{1,0:T(8,128)(2,1)S(1)}, u32[]{:S(2)}, u32[]{:S(2)}) collective-permute-start(bf16[256,640]{1,0:T(8,128)(2,1)S(1)} %fusion.refs_2_.refs_9_), channel_id=1, source_target_pairs={{0,1},{1,2},{2,3},{4,5},{5,6},{6,7},{8,9},{9,10},{10,11},{12,13},{... | collective-permute-start | bytes 983048 | tf_op jit(solution)/shard_map/ppermute | solution.py:374
  50.2 23.0 %collective-permute-start.9 = (bf16[256,640]{1,0:T(8,128)(2,1)S(1)}, bf16[256,640]{1,0:T(8,128)(2,1)S(1)}, u32[]{:S(2)}, u32[]{:S(2)}) collective-permute-start(bf16[256,640]{1,0:T(8,128)(2,1)S(1)} %fusion.refs_2_.refs_9_), channel_id=1, source_target_pairs={{1,0},{2,1},{3,2},{5,4},{6,5},{7,6},{9,8},{10,9},{11,10},{13,12},{... | collective-permute-start | bytes 983048 | tf_op jit(solution)/shard_map/ppermute | solution.py:375
  62.1 11.2 %collective-permute-start.10 = (bf16[256,640]{1,0:T(8,128)(2,1)S(1)}, bf16[256,640]{1,0:T(8,128)(2,1)S(1)}, u32[]{:S(2)}, u32[]{:S(2)}) collective-permute-start(bf16[256,640]{1,0:T(8,128)(2,1)S(1)} %collective-permute-done.8.refs_4_.refs_11_), channel_id=1, source_target_pairs={{2,3},{1,0},{6,7},{5,4},{10,11},{9,8},{14,15},{13,12},{18,19},{17,... | collective-permute-start | bytes 983048 | tf_op jit(solution)/shard_map/ppermute | solution.py:376
  63.4 15.9 %collective-permute-start.13 = (bf16[1,4,96,2048]{3,2,1,0:T(8,128)(2,1)S(1)}, bf16[1,4,96,2048]{3,2,1,0:T(8,128)(2,1)S(1)}, u32[]{:S(2)}, u32[]{:S(2)}) collective-permute-start(bf16[1,4,96,2048]{3,2,1,0:T(8,128)(2,1)S(1)} %collective-permute-done.12.refs_9_), channel_id=1, source_target_pairs={{0,4},{4,0},{8,12},{12,8},{16,20},{20,16},{24,28},{28,24},{1,5},{5... | collective-permute-start | bytes 4718600 | tf_op jit(solution)/shard_map/ppermute | solution.py:366
  73.3 4.2 %collective-permute-start.11 = (bf16[1,4,96,896]{3,2,1,0:T(8,128)(2,1)S(1)}, bf16[1,4,96,896]{3,2,1,0:T(8,128)(2,1)S(1)}, u32[]{:S(2)}, u32[]{:S(2)}) collective-permute-start(bf16[1,4,96,896]{3,2,1,0:T(8,128)(2,1)S(1)} %get-tuple-element.44), channel_id=1, source_target_pairs={{0,4},{4,0},{8,12},{12,8},{16,20},{20,16},{24,28},{28,24},{1,5},{5... | collective-permute-start | bytes 2064392 | tf_op jit(solution)/shard_map/ppermute | solution.py:366
  76.9 10.4 %collective-permute-start.18 = (bf16[1,4,96,1152]{3,2,1,0:T(8,128)(2,1)S(1)}, bf16[1,4,96,1152]{3,2,1,0:T(8,128)(2,1)S(1)}, u32[]{:S(2)}, u32[]{:S(2)}) collective-permute-start(bf16[1,4,96,1152]{3,2,1,0:T(8,128)(2,1)S(1)} %get-tuple-element.41), channel_id=1, source_target_pairs={{0,4},{4,0},{8,12},{12,8},{16,20},{20,16},{24,28},{28,24},{1,5},{5... | collective-permute-start | bytes 2654216 | tf_op jit(solution)/shard_map/ppermute | solution.py:366
  77.8 25.9 %collective-permute-start.15 = (bf16[1,4,96,896]{3,2,1,0:T(8,128)(2,1)S(1)}, bf16[1,4,96,896]{3,2,1,0:T(8,128)(2,1)S(1)}, u32[]{:S(2)}, u32[]{:S(2)}) collective-permute-start(bf16[1,4,96,896]{3,2,1,0:T(8,128)(2,1)S(1)} %shard_map.82), channel_id=1, source_target_pairs={{0,8},{4,12},{8,0},{12,4},{16,24},{20,28},{24,16},{28,20},{1,9},{5... | collective-permute-start | bytes 2064392 | tf_op jit(solution)/shard_map/ppermute | solution.py:366
  85.8 3.7 %collective-permute-start.14 = (f32[4,4,1,128]{3,2,1,0:T(1,128)S(1)}, f32[4,4,1,128]{3,2,1,0:T(1,128)S(1)}, u32[]{:S(2)}, u32[]{:S(2)}) collective-permute-start(f32[4,4,1,128]{3,2,1,0:T(1,128)S(1)} %get-tuple-element.48), channel_id=1, source_target_pairs={{0,16},{4,20},{8,24},{12,28},{16,0},{20,4},{24,8},{28,12},{1,17},{... | collective-permute-start | bytes 24584 | tf_op jit(solution)/shard_map/ppermute | solution.py:366
  89.5 26.1 %collective-permute-start.20 = (bf16[4,4,72,384]{3,2,1,0:T(8,128)(2,1)S(1)}, bf16[4,4,72,384]{3,2,1,0:T(8,128)(2,1)S(1)}, u32[]{:S(2)}, u32[]{:S(2)}) collective-permute-start(bf16[4,4,72,384]{3,2,1,0:T(8,128)(2,1)S(1)} %get-tuple-element.61), channel_id=1, source_target_pairs={{0,16},{4,20},{8,24},{12,28},{16,0},{20,4},{24,8},{28,12},{1,17},{... | collective-permute-start | bytes 2654216 | tf_op jit(solution)/shard_map/ppermute | solution.py:366
  91.0 24.7 %collective-permute-start.19 = (bf16[1,4,96,1152]{3,2,1,0:T(8,128)(2,1)S(1)}, bf16[1,4,96,1152]{3,2,1,0:T(8,128)(2,1)S(1)}, u32[]{:S(2)}, u32[]{:S(2)}) collective-permute-start(bf16[1,4,96,1152]{3,2,1,0:T(8,128)(2,1)S(1)} %shard_map.87), channel_id=1, source_target_pairs={{0,8},{4,12},{8,0},{12,4},{16,24},{20,28},{24,16},{28,20},{1,9},{5... | collective-permute-start | bytes 2654216 | tf_op jit(solution)/shard_map/ppermute | solution.py:366
  103.7 11.5 %collective-permute-start.17 = (bf16[1,4,96,1024]{3,2,1,0:T(8,128)(2,1)S(1)}, bf16[1,4,96,1024]{3,2,1,0:T(8,128)(2,1)S(1)}, u32[]{:S(2)}, u32[]{:S(2)}) collective-permute-start(bf16[1,4,96,1024]{3,2,1,0:T(8,128)(2,1)S(1)} %get-tuple-element.58), channel_id=1, source_target_pairs={{0,4},{4,0},{8,12},{12,8},{16,20},{20,16},{24,28},{28,24},{1,5},{5... | collective-permute-start | bytes 2359304 | tf_op jit(solution)/shard_map/ppermute | solution.py:366
  103.8 11.4 %collective-permute-start.16 = (bf16[1,4,96,1024]{3,2,1,0:T(8,128)(2,1)S(1)}, bf16[1,4,96,1024]{3,2,1,0:T(8,128)(2,1)S(1)}, u32[]{:S(2)}, u32[]{:S(2)}) collective-permute-start(bf16[1,4,96,1024]{3,2,1,0:T(8,128)(2,1)S(1)} %get-tuple-element.56), channel_id=1, source_target_pairs={{0,4},{4,0},{8,12},{12,8},{16,20},{20,16},{24,28},{28,24},{1,5},{5... | collective-permute-start | bytes 2359304 | tf_op jit(solution)/shard_map/ppermute | solution.py:366

commit v9 on v8

--- a/solution.py
+++ b/solution.py
@@ -443,15 +443,15 @@
     by_expert = lax.all_to_all(sg_own, "expert", split_axis=0, concat_axis=0, tiled=True)
     spans = ((0, cut), (0, d - cut))
     *near, keep = partial_grad(
-        n, bands, band, False, (half, half), after(scalars, sg_own), hs_own, hs_nb, own_pieces, nb_pieces, spans
-    )
-    base = joined([[keep], [swap(after(x, there[0]), 1) for x in near]])
+        n, bands, band, False, (half, half), after(scalars, sg_nb), hs_own, hs_nb, own_pieces, nb_pieces, spans
+    )
+    base = joined([[keep], [swap(after(x, there[0], sg_own), 1) for x in near]])
     mid = bands // 8
     there = there if mid == 0 else [jnp.concatenate(there, axis=3)]
     while mid:
         total = base.astype(F32) + there[0].astype(F32)
         base, there, mid = total[:mid].astype(BF), [swap(total[mid:].astype(BF), 4 * mid)], mid // 2
-    gh_in = swap(after(gh_nb, sg_in, sums[1]), bands)
+    gh_in = swap(after(gh_nb, sg_in, sums[1], keep), bands)
     grad_down, grad_hidden = finish(scalars, base, there, gh_in, gh_own)
     by_expert = by_expert.reshape(EXPERTS, 1, toks)
     chosen = expert_ids.T[None] == jnp.arange(EXPERTS, dtype=jnp.int32)[:, None, None]

time: 119 us -> 117 us (0.983)
  transfers between devices with their start and end apart: 21 -> 21, of which waited for: 7 -> 8; matrix products, arithmetic and copies ran while one was open for 1% -> 1% of each run, Pallas kernels for 26% -> 26%
where the time goes in v9:
time: 117 us
  waiting for transfers between devices  40.4 us (35%)
  Pallas kernels  33.2 us (28%)
  starting transfers between devices  28.5 us (24%)
  blocking collectives  10.2 us (9%)
  local copies, waits for them, and re-layouts  2.71 us (2%)
    ppermute x2, waiting for transfers between devices, spread(): two = lax.ppermute(x, 'expert', [(i, (i + 2) % n) for i in range(n)])  22.7 us
    pallas_call x2, Pallas kernels, backward(): pl.pallas_call(functools.partial(back_kernel, n, counts, group, rels), ou...  13.7 us
    pallas_call x3, Pallas kernels, partial_grad(): pl.pallas_call(functools.partial(part_kernel, n, bands, (counts, counts_n...  12 us
    ppermute x13, starting transfers between devices, swap(): return lax.ppermute(x, 'dp', [(i, i ^ bit) for i in range(n_dp)])  11.1 us
    all_to_all x1, blocking collectives, per_device(): lax.all_to_all(sg_own, 'expert', split_axis=0, concat_axis=0, tiled=True)  10.2 us
    ppermute x2, waiting for transfers between devices, spread(): passed = lax.ppermute(two, 'expert', [(2, 3), (1, 0)])  7.04 us
    ppermute x2, starting transfers between devices, spread(): one = lax.ppermute(x, 'expert', [(i, i + 1) for i in range(n - 1)])  6.98 us
    ppermute x2, waiting for transfers between devices, spread(): three = lax.ppermute(x, 'expert', [(i + 1, i) for i in range(n - 1)])  5.71 us
  transfers between devices with their start and end apart: 21, of which 8 were waited for; matrix products, arithmetic and copies ran while one was open for 1% of the time, Pallas kernels for 26%

profile of v9, /device:TPU:0, one launch (start us, length us, event | category | flops | bytes accessed | tf_op | source)
XLA Modules:
  0.0 116.8 jit_solution(1094274294966430379)
XLA Ops:
  0.6 0.5 collective-permute-start.4
  1.1 0.1 pad_add_fusion.sc_ref
  1.2 1.5 %copy-done = bf16[1,4,4,72,768]{4,3,2,1,0:T(8,128)(2,1)S(1)} copy-done((bf16[1,4,4,72,768]{4,3,2,1,0:T(8,128)(2,1)S(1)}, bf16[1,4,4,72,768]{4,3,2,1,0:T(8,128)(2,1)}, u32[]{:S(2)}) %copy-start) | copy-done | bytes 1769496
  2.7 1.0 copy-done.3
  3.8 0.8 shard_map.77
  4.5 2.7 %collective-permute-start.5 = (bf16[2048,384]{1,0:T(8,128)(2,1)S(1)}, bf16[2048,384]{1,0:T(8,128)(2,1)S(1)}, u32[]{:S(2)}, u32[]{:S(2)}) collective-permute-start(bf16[2048,384]{1,0:T(8,128)(2,1)S(1)} %shard_map.77), channel_id=1, source_target_pairs={{0,16},{4,20},{8,24},{12,28},{16,0},{20,4},{24,8},{28,12},{1,17},{... | collective-permute-start | bytes 4718600 | tf_op jit(solution)/shard_map/ppermute | solution.py:366
  7.4 0.0 slice-start.1
  7.4 2.7 %collective-permute-start.1 = (bf16[136,1408]{1,0:T(8,128)(2,1)S(1)}, bf16[136,1408]{1,0:T(8,128)(2,1)S(1)}, u32[]{:S(2)}, u32[]{:S(2)}) collective-permute-start(bf16[136,1408]{1,0:T(8,128)(2,1)S(1)} %pad_maximum_fusion.refs_0_), channel_id=1, source_target_pairs={{0,2},{1,3},{2,0},{3,1},{4,6},{5,7},{6,4},{7,5},{8,10},{9,11},{10,... | collective-permute-start | bytes 1148936 | tf_op jit(solution)/shard_map/ppermute | solution.py:373
  10.1 1.5 %collective-permute-start.12 = (bf16[1,4,96,2048]{3,2,1,0:T(8,128)(2,1)S(1)}, bf16[1,4,96,2048]{3,2,1,0:T(8,128)(2,1)S(1)}, u32[]{:S(2)}, u32[]{:S(2)}) collective-permute-start(bf16[1,4,96,2048]{3,2,1,0:T(8,128)(2,1)S(1)} %bitcast.12), channel_id=1, source_target_pairs={{0,8},{4,12},{8,0},{12,4},{16,24},{20,28},{24,16},{28,20},{1,9},{5... | collective-permute-start | bytes 4718600 | tf_op jit(solution)/shard_map/ppermute | solution.py:366
  11.6 3.5 %collective-permute-start = (bf16[136,1408]{1,0:T(8,128)(2,1)S(1)}, bf16[136,1408]{1,0:T(8,128)(2,1)S(1)}, u32[]{:S(2)}, u32[]{:S(2)}) collective-permute-start(bf16[136,1408]{1,0:T(8,128)(2,1)S(1)} %pad_maximum_fusion.refs_0_), channel_id=1, source_target_pairs={{0,1},{1,2},{2,3},{4,5},{5,6},{6,7},{8,9},{9,10},{10,11},{12,13},{... | collective-permute-start | bytes 1148936 | tf_op jit(solution)/shard_map/ppermute | solution.py:374
  15.1 1.3 %collective-permute-start.2 = (bf16[136,1408]{1,0:T(8,128)(2,1)S(1)}, bf16[136,1408]{1,0:T(8,128)(2,1)S(1)}, u32[]{:S(2)}, u32[]{:S(2)}) collective-permute-start(bf16[136,1408]{1,0:T(8,128)(2,1)S(1)} %pad_maximum_fusion.refs_0_), channel_id=1, source_target_pairs={{1,0},{2,1},{3,2},{5,4},{6,5},{7,6},{9,8},{10,9},{11,10},{13,12},{... | collective-permute-start | bytes 1148936 | tf_op jit(solution)/shard_map/ppermute | solution.py:375
  16.4 12.0 %collective-permute-done.1.refs_2_ = bf16[136,1408]{1,0:T(8,128)(2,1)S(1)} collective-permute-done((bf16[136,1408]{1,0:T(8,128)(2,1)S(1)}, bf16[136,1408]{1,0:T(8,128)(2,1)S(1)}, u32[]{:S(2)}, u32[]{:S(2)}) %collective-permute-start.1) | collective-permute-done | bytes 383008 | tf_op jit(solution)/shard_map/ppermute | solution.py:373
  28.4 1.3 %collective-permute-start.3 = (bf16[136,1408]{1,0:T(8,128)(2,1)S(1)}, bf16[136,1408]{1,0:T(8,128)(2,1)S(1)}, u32[]{:S(2)}, u32[]{:S(2)}) collective-permute-start(bf16[136,1408]{1,0:T(8,128)(2,1)S(1)} %collective-permute-done.1.refs_2_), channel_id=1, source_target_pairs={{2,3},{1,0},{6,7},{5,4},{10,11},{9,8},{14,15},{13,12},{18,19},{17,... | collective-permute-start | bytes 1148936 | tf_op jit(solution)/shard_map/ppermute | solution.py:376
  29.7 5.7 %collective-permute-done.2.refs_3_ = bf16[136,1408]{1,0:T(8,128)(2,1)S(1)} collective-permute-done((bf16[136,1408]{1,0:T(8,128)(2,1)S(1)}, bf16[136,1408]{1,0:T(8,128)(2,1)S(1)}, u32[]{:S(2)}, u32[]{:S(2)}) %collective-permute-start.2) | collective-permute-done | bytes 383008 | tf_op jit(solution)/shard_map/ppermute | solution.py:375
  35.4 6.9 %collective-permute-done.3.refs_4_ = bf16[136,1408]{1,0:T(8,128)(2,1)S(1)} collective-permute-done((bf16[136,1408]{1,0:T(8,128)(2,1)S(1)}, bf16[136,1408]{1,0:T(8,128)(2,1)S(1)}, u32[]{:S(2)}, u32[]{:S(2)}) %collective-permute-start.3) | collective-permute-done | bytes 383008 | tf_op jit(solution)/shard_map/ppermute | solution.py:376
  42.3 0.7 shard_map.76.tab_ref.refs_1_
  43.0 1.0 collective-permute-start.6
  43.9 0.1 fusion.4
  44.0 2.7 %collective-permute-start.8 = (bf16[256,640]{1,0:T(8,128)(2,1)S(1)}, bf16[256,640]{1,0:T(8,128)(2,1)S(1)}, u32[]{:S(2)}, u32[]{:S(2)}) collective-permute-start(bf16[256,640]{1,0:T(8,128)(2,1)S(1)} %fusion.refs_2_.refs_9_), channel_id=1, source_target_pairs={{0,2},{1,3},{2,0},{3,1},{4,6},{5,7},{6,4},{7,5},{8,10},{9,11},{10,... | collective-permute-start | bytes 983048 | tf_op jit(solution)/shard_map/ppermute | solution.py:373
  46.7 3.5 %collective-permute-start.7 = (bf16[256,640]{1,0:T(8,128)(2,1)S(1)}, bf16[256,640]{1,0:T(8,128)(2,1)S(1)}, u32[]{:S(2)}, u32[]{:S(2)}) collective-permute-start(bf16[256,640]{1,0:T(8,128)(2,1)S(1)} %fusion.refs_2_.refs_9_), channel_id=1, source_target_pairs={{0,1},{1,2},{2,3},{4,5},{5,6},{6,7},{8,9},{9,10},{10,11},{12,13},{... | collective-permute-start | bytes 983048 | tf_op jit(solution)/shard_map/ppermute | solution.py:374
  50.2 1.3 %collective-permute-start.9 = (bf16[256,640]{1,0:T(8,128)(2,1)S(1)}, bf16[256,640]{1,0:T(8,128)(2,1)S(1)}, u32[]{:S(2)}, u32[]{:S(2)}) collective-permute-start(bf16[256,640]{1,0:T(8,128)(2,1)S(1)} %fusion.refs_2_.refs_9_), channel_id=1, source_target_pairs={{1,0},{2,1},{3,2},{5,4},{6,5},{7,6},{9,8},{10,9},{11,10},{13,12},{... | collective-permute-start | bytes 983048 | tf_op jit(solution)/shard_map/ppermute | solution.py:375
  51.5 10.6 %collective-permute-done.8.refs_4_.refs_11_ = bf16[256,640]{1,0:T(8,128)(2,1)S(1)} collective-permute-done((bf16[256,640]{1,0:T(8,128)(2,1)S(1)}, bf16[256,640]{1,0:T(8,128)(2,1)S(1)}, u32[]{:S(2)}, u32[]{:S(2)}) %collective-permute-start.8) | collective-permute-done | bytes 327712 | tf_op jit(solution)/shard_map/ppermute | solution.py:373
  62.1 1.3 %collective-permute-start.10 = (bf16[256,640]{1,0:T(8,128)(2,1)S(1)}, bf16[256,640]{1,0:T(8,128)(2,1)S(1)}, u32[]{:S(2)}, u32[]{:S(2)}) collective-permute-start(bf16[256,640]{1,0:T(8,128)(2,1)S(1)} %collective-permute-done.8.refs_4_.refs_11_), channel_id=1, source_target_pairs={{2,3},{1,0},{6,7},{5,4},{10,11},{9,8},{14,15},{13,12},{18,19},{17,... | collective-permute-start | bytes 983048 | tf_op jit(solution)/shard_map/ppermute | solution.py:376
  63.4 0.1 collective-permute-start.13
  63.5 1.3 %shard_map.78 = (bf16[4,384,512]{2,1,0:T(8,128)(2,1)S(1)}, f32[4,4,1,128]{3,2,1,0:T(1,128)S(1)}, f32[4,4,1,128]{3,2,1,0:T(1,128)S(1)}) custom-call(s32[3]{0:T(128)S(1)} %pad_add_fusion.sc_ref, bf16[400,1408]{1,0:T(8,128)(2,1)S(1)} %shard_map.76.tab_ref.refs_1_, bf16[1,4,4,72,768]{4,3,2,1,0:T(8,128)(2,1)S(1)} %copy-done.1), custom_call_target="tpu_custom_call" | custom-call | flops 1 | bytes 1 | tf_op jit(solution)/shard_map/pallas_call | solution.py:50
  64.9 0.1 slice.60
  65.0 3.7 %collective-permute-done.6.tab_ref.refs_3_.refs_8_.refs_1_ = bf16[400,1408]{1,0:T(8,128)(2,1)S(1)} collective-permute-done((bf16[400,1408]{1,0:T(8,128)(2,1)S(1)}, bf16[400,1408]{1,0:T(8,128)(2,1)S(1)}, u32[]{:S(2)}, u32[]{:S(2)}) %collective-permute-start.6) | collective-permute-done | bytes 1126432 | tf_op jit(solution)/shard_map/ppermute | solution.py:366
  68.7 1.3 %shard_map.79 = (bf16[4,384,512]{2,1,0:T(8,128)(2,1)S(1)}, f32[4,4,1,128]{3,2,1,0:T(1,128)S(1)}, f32[4,4,1,128]{3,2,1,0:T(1,128)S(1)}) custom-call(s32[3]{0:T(128)S(1)} %pad_add_fusion.sc_ref, bf16[400,1408]{1,0:T(8,128)(2,1)S(1)} %collective-permute-done.6.tab_ref.refs_3_.refs_8_.refs_1_, bf16[1,4,4,80,384]{4,3,2,1,0:T(8,128)(2,1)S(1)} %bitcast.9), custom_call_target="tpu_custom_call" | custom-call | flops 1 | bytes 1 | tf_op jit(solution)/shard_map/pallas_call | solution.py:50
  70.0 3.2 %shard_map.80 = (bf16[1,4,96,896]{3,2,1,0:T(8,128)(2,1)S(1)}, bf16[1,4,96,896]{3,2,1,0:T(8,128)(2,1)S(1)}) custom-call(s32[3]{0:T(128)S(1)} %pad_add_fusion.sc_ref, bf16[136,1408]{1,0:T(8,128)(2,1)S(1)} %pad_maximum_fusion.refs_0_, bf16[400,1408]{1,0:T(8,128)(2,1)S(1)} %shard_map.76.tab_ref.refs_1_, ...), custom_call_target="tpu_custom_call" | custom-call | flops 1 | bytes 1 | tf_op jit(solution)/shard_map/pallas_call | solution.py:282
  73.2 0.1 collective-permute-done.10.refs_6_.refs_13_
  73.3 3.7 %shard_map.81 = (bf16[1,4,96,1152]{3,2,1,0:T(8,128)(2,1)S(1)}, bf16[1,4,96,1152]{3,2,1,0:T(8,128)(2,1)S(1)}) custom-call(s32[3]{0:T(128)S(1)} %pad_add_fusion.sc_ref, bf16[136,1408]{1,0:T(8,128)(2,1)S(1)} %pad_maximum_fusion.refs_0_, bf16[400,1408]{1,0:T(8,128)(2,1)S(1)} %shard_map.76.tab_ref.refs_1_, bf16[256,640]{1,0:T(8,128)(2,1)S(1)} %fusion.refs_2_.refs_9_, ...), custom_call_target="tpu_custom_call" | custom-call | flops 1 | bytes 1 | tf_op jit(solution)/shard_map/pallas_call | solution.py:282
  77.0 0.6 collective-permute-start.18
  77.6 0.2 shard_map.82
  77.8 1.6 %collective-permute-start.14 = (bf16[1,4,96,896]{3,2,1,0:T(8,128)(2,1)S(1)}, bf16[1,4,96,896]{3,2,1,0:T(8,128)(2,1)S(1)}, u32[]{:S(2)}, u32[]{:S(2)}) collective-permute-start(bf16[1,4,96,896]{3,2,1,0:T(8,128)(2,1)S(1)} %shard_map.82), channel_id=1, source_target_pairs={{0,8},{4,12},{8,0},{12,4},{16,24},{20,28},{24,16},{28,20},{1,9},{5... | collective-permute-start | bytes 2064392 | tf_op jit(solution)/shard_map/ppermute | solution.py:366
  79.4 6.5 %shard_map.83 = (bf16[4,4,72,384]{3,2,1,0:T(8,128)(2,1)S(1)}, f32[4,4,1,128]{3,2,1,0:T(1,128)S(1)}) custom-call(s32[3]{0:T(128)S(1)} %pad_add_fusion.sc_ref, bf16[128,1408]{1,0:T(8,128)(2,1)S(1)} %pad_maximum_fusion.1.refs_2_.refs_7_.refs_0_, bf16[400,1408]{1,0:T(8,128)(2,1)S(1)} %collective-permute-done.6.tab_ref.refs_3_.refs_8_.refs_1_, ...), custom_call_target="tpu_custom_call" | custom-call | flops 1 | bytes 1 | tf_op jit(solution)/shard_map/pallas_call | solution.py:218
  85.9 1.5 %collective-permute-start.15 = (f32[4,4,1,128]{3,2,1,0:T(1,128)S(1)}, f32[4,4,1,128]{3,2,1,0:T(1,128)S(1)}, u32[]{:S(2)}, u32[]{:S(2)}) collective-permute-start(f32[4,4,1,128]{3,2,1,0:T(1,128)S(1)} %get-tuple-element.48), channel_id=1, source_target_pairs={{0,16},{4,20},{8,24},{12,28},{16,0},{20,4},{24,8},{28,12},{1,17},{... | collective-permute-start | bytes 24584 | tf_op jit(solution)/shard_map/ppermute | solution.py:366
  87.4 5.1 %shard_map.84 = (bf16[1,4,96,1024]{3,2,1,0:T(8,128)(2,1)S(1)}, bf16[1,4,96,1024]{3,2,1,0:T(8,128)(2,1)S(1)}, bf16[1,4,96,2048]{3,2,1,0:T(8,128)(2,1)S(1)}) custom-call(s32[3]{0:T(128)S(1)} %pad_add_fusion.sc_ref, bf16[136,1408]{1,0:T(8,128)(2,1)S(1)} %pad_maximum_fusion.refs_0_, bf16[400,1408]{1,0:T(8,128)(2,1)S(1)} %shard_map.76.tab_ref.refs_1_, ...), custom_call_target="tpu_custom_call" | custom-call | flops 1 | bytes 1 | tf_op jit(solution)/shard_map/pallas_call | solution.py:282
  92.5 0.3 shard_map.87
  92.8 0.6 collective-permute-start.20
  93.5 0.5 collective-permute-start.19
  94.0 7.3 %shard_map.85 = (bf16[4,4,72,768]{3,2,1,0:T(8,128)(2,1)}, f32[4,4,1,128]{3,2,1,0:T(1,128)S(1)}) custom-call(s32[3]{0:T(128)S(1)} %pad_add_fusion.sc_ref, bf16[136,1408]{1,0:T(8,128)(2,1)S(1)} %pad_maximum_fusion.refs_0_, bf16[400,1408]{1,0:T(8,128)(2,1)S(1)} %shard_map.76.tab_ref.refs_1_, bf16[256,640]{1,0:T(8,128)(2,1)S(1)} %fusion.refs_2_.refs_9_, ...), custom_call_target="tpu_custom_call" | custom-call | flops 1 | bytes 1 | tf_op jit(solution)/shard_map/pallas_call | solution.py:218
  101.2 0.5 collective-permute-start.16
  101.8 10.2 %all_to_all.5 = f32[4,4,1,128]{3,2,1,0:T(1,128)S(1)} all-to-all(f32[4,4,1,128]{3,2,1,0:T(1,128)S(1)} %get-tuple-element.55), channel_id=1, replica_groups=mesh['dp'=8,'expert'=4] {'expert'}, dimensions={0} | all-to-all | bytes 16384 | tf_op jit(solution)/shard_map/all_to_all | solution.py:443
  112.0 0.6 select_reduce_fusion
  112.6 0.4 shard_map.86.base_ref
  113.0 0.9 collective-permute-done.20.refs_2_
  113.9 0.3 collective-permute-done.19.refs_1_
  114.2 2.5 %shard_map.88 = (bf16[4,96,2048]{2,1,0:T(8,128)(2,1)}, bf16[4,4,72,768]{3,2,1,0:T(8,128)(2,1)}) custom-call(s32[3]{0:T(128)S(1)} %pad_add_fusion.sc_ref, bf16[1,4,96,2048]{3,2,1,0:T(8,128)(2,1)S(1)} %shard_map.86.base_ref, bf16[1,4,96,896]{3,2,1,0:T(8,128)(2,1)S(1)} %collective-permute-done.14.refs_0_, ...), custom_call_target="tpu_custom_call", output_to_operand_aliasing={{1}: (5, {})} | custom-call | flops 1 | bytes 1 | tf_op jit(solution)/shard_map/pallas_call | solution.py:335
  (36 shorter events, 0.2 us)
Async XLA Ops:
  0.6 3.9 %collective-permute-start.4 = (bf16[1,4,96,2048]{3,2,1,0:T(8,128)(2,1)}, bf16[1,4,96,2048]{3,2,1,0:T(8,128)(2,1)S(1)}, u32[]{:S(2)}, u32[]{:S(2)}) collective-permute-start(bf16[1,4,96,2048]{3,2,1,0:T(8,128)(2,1)} %bitcast.11), channel_id=1, source_target_pairs={{0,4},{4,0},{8,12},{12,8},{16,20},{20,16},{24,28},{28,24},{1,5},{5... | collective-permute-start | bytes 4718600 | tf_op jit(solution)/shard_map/ppermute | solution.py:366
  1.2 1.5 %copy-start = (bf16[1,4,4,72,768]{4,3,2,1,0:T(8,128)(2,1)S(1)}, bf16[1,4,4,72,768]{4,3,2,1,0:T(8,128)(2,1)}, u32[]{:S(2)}) copy-start(bf16[1,4,4,72,768]{4,3,2,1,0:T(8,128)(2,1)} %refs_11_.1) | copy-start | bytes 5308420
  2.7 1.0 copy-start.3
  3.7 3.5 %copy-start.5 = (bf16[128,8]{0,1:T(8,128)(2,1)S(1)}, bf16[128,8]{0,1:T(8,128)(2,1)}, u32[]{:S(2)}) copy-start(bf16[128,8]{0,1:T(8,128)(2,1)} %param.7) | copy-start | bytes 6148
  3.7 3.5 %copy-start.4 = (s32[128,8]{0,1:T(8,128)S(1)}, s32[128,8]{0,1:T(8,128)}, u32[]{:S(2)}) copy-start(s32[128,8]{0,1:T(8,128)} %param.6) | copy-start | bytes 12292
  3.7 3.6 %slice-start = ((bf16[128,2048]{1,0:T(8,128)(2,1)}), bf16[128,1408]{1,0:T(8,128)(2,1)S(1)}, s32[]{:S(2)}) async-start(bf16[128,2048]{1,0:T(8,128)(2,1)} %tok_ref.1), calls=%async_computation.1 | async-start | bytes 720896 | tf_op jit(solution)/shard_map/slice | solution.py:385
  3.8 6.3 %copy-start.2 = (bf16[4,96,2048]{2,1,0:T(8,128)(2,1)S(1)}, bf16[4,96,2048]{2,1,0:T(8,128)(2,1)}, u32[]{:S(2)}) copy-start(bf16[4,96,2048]{2,1,0:T(8,128)(2,1)} %param.9) | copy-start | bytes 4718596
  4.5 38.4 %collective-permute-start.5 = (bf16[2048,384]{1,0:T(8,128)(2,1)S(1)}, bf16[2048,384]{1,0:T(8,128)(2,1)S(1)}, u32[]{:S(2)}, u32[]{:S(2)}) collective-permute-start(bf16[2048,384]{1,0:T(8,128)(2,1)S(1)} %shard_map.77), channel_id=1, source_target_pairs={{0,16},{4,20},{8,24},{12,28},{16,0},{20,4},{24,8},{28,12},{1,17},{... | collective-permute-start | bytes 4718600 | tf_op jit(solution)/shard_map/ppermute | solution.py:366
  7.4 36.6 %slice-start.1 = ((bf16[128,2048]{1,0:T(8,128)(2,1)}), bf16[128,640]{1,0:T(8,128)(2,1)S(1)}, s32[]{:S(2)}) async-start(bf16[128,2048]{1,0:T(8,128)(2,1)} %tok_ref.1), calls=%async_computation.2 | async-start | bytes 327680 | tf_op jit(solution)/shard_map/slice | solution.py:408
  7.4 21.0 %collective-permute-start.1 = (bf16[136,1408]{1,0:T(8,128)(2,1)S(1)}, bf16[136,1408]{1,0:T(8,128)(2,1)S(1)}, u32[]{:S(2)}, u32[]{:S(2)}) collective-permute-start(bf16[136,1408]{1,0:T(8,128)(2,1)S(1)} %pad_maximum_fusion.refs_0_), channel_id=1, source_target_pairs={{0,2},{1,3},{2,0},{3,1},{4,6},{5,7},{6,4},{7,5},{8,10},{9,11},{10,... | collective-permute-start | bytes 1148936 | tf_op jit(solution)/shard_map/ppermute | solution.py:373
  10.1 53.4 %collective-permute-start.12 = (bf16[1,4,96,2048]{3,2,1,0:T(8,128)(2,1)S(1)}, bf16[1,4,96,2048]{3,2,1,0:T(8,128)(2,1)S(1)}, u32[]{:S(2)}, u32[]{:S(2)}) collective-permute-start(bf16[1,4,96,2048]{3,2,1,0:T(8,128)(2,1)S(1)} %bitcast.12), channel_id=1, source_target_pairs={{0,8},{4,12},{8,0},{12,4},{16,24},{20,28},{24,16},{28,20},{1,9},{5... | collective-permute-start | bytes 4718600 | tf_op jit(solution)/shard_map/ppermute | solution.py:366
  11.6 18.1 %collective-permute-start = (bf16[136,1408]{1,0:T(8,128)(2,1)S(1)}, bf16[136,1408]{1,0:T(8,128)(2,1)S(1)}, u32[]{:S(2)}, u32[]{:S(2)}) collective-permute-start(bf16[136,1408]{1,0:T(8,128)(2,1)S(1)} %pad_maximum_fusion.refs_0_), channel_id=1, source_target_pairs={{0,1},{1,2},{2,3},{4,5},{5,6},{6,7},{8,9},{9,10},{10,11},{12,13},{... | collective-permute-start | bytes 1148936 | tf_op jit(solution)/shard_map/ppermute | solution.py:374
  15.1 20.3 %collective-permute-start.2 = (bf16[136,1408]{1,0:T(8,128)(2,1)S(1)}, bf16[136,1408]{1,0:T(8,128)(2,1)S(1)}, u32[]{:S(2)}, u32[]{:S(2)}) collective-permute-start(bf16[136,1408]{1,0:T(8,128)(2,1)S(1)} %pad_maximum_fusion.refs_0_), channel_id=1, source_target_pairs={{1,0},{2,1},{3,2},{5,4},{6,5},{7,6},{9,8},{10,9},{11,10},{13,12},{... | collective-permute-start | bytes 1148936 | tf_op jit(solution)/shard_map/ppermute | solution.py:375
  28.4 13.9 %collective-permute-start.3 = (bf16[136,1408]{1,0:T(8,128)(2,1)S(1)}, bf16[136,1408]{1,0:T(8,128)(2,1)S(1)}, u32[]{:S(2)}, u32[]{:S(2)}) collective-permute-start(bf16[136,1408]{1,0:T(8,128)(2,1)S(1)} %collective-permute-done.1.refs_2_), channel_id=1, source_target_pairs={{2,3},{1,0},{6,7},{5,4},{10,11},{9,8},{14,15},{13,12},{18,19},{17,... | collective-permute-start | bytes 1148936 | tf_op jit(solution)/shard_map/ppermute | solution.py:376
  42.9 20.6 %copy-start.1 = (bf16[1,4,4,72,768]{4,3,2,1,0:T(8,128)(2,1)S(1)}, bf16[1,4,4,72,768]{4,3,2,1,0:T(8,128)(2,1)}, u32[]{:S(2)}) copy-start(bf16[1,4,4,72,768]{4,3,2,1,0:T(8,128)(2,1)} %refs_11_.1) | copy-start | bytes 5308420
  43.0 25.7 %collective-permute-start.6 = (bf16[400,1408]{1,0:T(8,128)(2,1)S(1)}, bf16[400,1408]{1,0:T(8,128)(2,1)S(1)}, u32[]{:S(2)}, u32[]{:S(2)}) collective-permute-start(bf16[400,1408]{1,0:T(8,128)(2,1)S(1)} %shard_map.76.tab_ref.refs_1_), channel_id=1, source_target_pairs={{0,16},{4,20},{8,24},{12,28},{16,0},{20,4},{24,8},{28,12},{1,17},{... | collective-permute-start | bytes 3379208 | tf_op jit(solution)/shard_map/ppermute | solution.py:366
  44.0 18.1 %collective-permute-start.8 = (bf16[256,640]{1,0:T(8,128)(2,1)S(1)}, bf16[256,640]{1,0:T(8,128)(2,1)S(1)}, u32[]{:S(2)}, u32[]{:S(2)}) collective-permute-start(bf16[256,640]{1,0:T(8,128)(2,1)S(1)} %fusion.refs_2_.refs_9_), channel_id=1, source_target_pairs={{0,2},{1,3},{2,0},{3,1},{4,6},{5,7},{6,4},{7,5},{8,10},{9,11},{10,... | collective-permute-start | bytes 983048 | tf_op jit(solution)/shard_map/ppermute | solution.py:373
  46.7 26.5 %collective-permute-start.7 = (bf16[256,640]{1,0:T(8,128)(2,1)S(1)}, bf16[256,640]{1,0:T(8,128)(2,1)S(1)}, u32[]{:S(2)}, u32[]{:S(2)}) collective-permute-start(bf16[256,640]{1,0:T(8,128)(2,1)S(1)} %fusion.refs_2_.refs_9_), channel_id=1, source_target_pairs={{0,1},{1,2},{2,3},{4,5},{5,6},{6,7},{8,9},{9,10},{10,11},{12,13},{... | collective-permute-start | bytes 983048 | tf_op jit(solution)/shard_map/ppermute | solution.py:374
  50.2 23.0 %collective-permute-start.9 = (bf16[256,640]{1,0:T(8,128)(2,1)S(1)}, bf16[256,640]{1,0:T(8,128)(2,1)S(1)}, u32[]{:S(2)}, u32[]{:S(2)}) collective-permute-start(bf16[256,640]{1,0:T(8,128)(2,1)S(1)} %fusion.refs_2_.refs_9_), channel_id=1, source_target_pairs={{1,0},{2,1},{3,2},{5,4},{6,5},{7,6},{9,8},{10,9},{11,10},{13,12},{... | collective-permute-start | bytes 983048 | tf_op jit(solution)/shard_map/ppermute | solution.py:375
  62.1 11.2 %collective-permute-start.10 = (bf16[256,640]{1,0:T(8,128)(2,1)S(1)}, bf16[256,640]{1,0:T(8,128)(2,1)S(1)}, u32[]{:S(2)}, u32[]{:S(2)}) collective-permute-start(bf16[256,640]{1,0:T(8,128)(2,1)S(1)} %collective-permute-done.8.refs_4_.refs_11_), channel_id=1, source_target_pairs={{2,3},{1,0},{6,7},{5,4},{10,11},{9,8},{14,15},{13,12},{18,19},{17,... | collective-permute-start | bytes 983048 | tf_op jit(solution)/shard_map/ppermute | solution.py:376
  63.4 15.9 %collective-permute-start.13 = (bf16[1,4,96,2048]{3,2,1,0:T(8,128)(2,1)S(1)}, bf16[1,4,96,2048]{3,2,1,0:T(8,128)(2,1)S(1)}, u32[]{:S(2)}, u32[]{:S(2)}) collective-permute-start(bf16[1,4,96,2048]{3,2,1,0:T(8,128)(2,1)S(1)} %collective-permute-done.12.refs_9_), channel_id=1, source_target_pairs={{0,4},{4,0},{8,12},{12,8},{16,20},{20,16},{24,28},{28,24},{1,5},{5... | collective-permute-start | bytes 4718600 | tf_op jit(solution)/shard_map/ppermute | solution.py:366
  73.3 4.3 %collective-permute-start.11 = (bf16[1,4,96,896]{3,2,1,0:T(8,128)(2,1)S(1)}, bf16[1,4,96,896]{3,2,1,0:T(8,128)(2,1)S(1)}, u32[]{:S(2)}, u32[]{:S(2)}) collective-permute-start(bf16[1,4,96,896]{3,2,1,0:T(8,128)(2,1)S(1)} %get-tuple-element.44), channel_id=1, source_target_pairs={{0,4},{4,0},{8,12},{12,8},{16,20},{20,16},{24,28},{28,24},{1,5},{5... | collective-permute-start | bytes 2064392 | tf_op jit(solution)/shard_map/ppermute | solution.py:366
  77.0 15.5 %collective-permute-start.18 = (bf16[1,4,96,1152]{3,2,1,0:T(8,128)(2,1)S(1)}, bf16[1,4,96,1152]{3,2,1,0:T(8,128)(2,1)S(1)}, u32[]{:S(2)}, u32[]{:S(2)}) collective-permute-start(bf16[1,4,96,1152]{3,2,1,0:T(8,128)(2,1)S(1)} %get-tuple-element.41), channel_id=1, source_target_pairs={{0,4},{4,0},{8,12},{12,8},{16,20},{20,16},{24,28},{28,24},{1,5},{5... | collective-permute-start | bytes 2654216 | tf_op jit(solution)/shard_map/ppermute | solution.py:366
  77.8 23.4 %collective-permute-start.14 = (bf16[1,4,96,896]{3,2,1,0:T(8,128)(2,1)S(1)}, bf16[1,4,96,896]{3,2,1,0:T(8,128)(2,1)S(1)}, u32[]{:S(2)}, u32[]{:S(2)}) collective-permute-start(bf16[1,4,96,896]{3,2,1,0:T(8,128)(2,1)S(1)} %shard_map.82), channel_id=1, source_target_pairs={{0,8},{4,12},{8,0},{12,4},{16,24},{20,28},{24,16},{28,20},{1,9},{5... | collective-permute-start | bytes 2064392 | tf_op jit(solution)/shard_map/ppermute | solution.py:366
  85.9 7.0 %collective-permute-start.15 = (f32[4,4,1,128]{3,2,1,0:T(1,128)S(1)}, f32[4,4,1,128]{3,2,1,0:T(1,128)S(1)}, u32[]{:S(2)}, u32[]{:S(2)}) collective-permute-start(f32[4,4,1,128]{3,2,1,0:T(1,128)S(1)} %get-tuple-element.48), channel_id=1, source_target_pairs={{0,16},{4,20},{8,24},{12,28},{16,0},{20,4},{24,8},{28,12},{1,17},{... | collective-permute-start | bytes 24584 | tf_op jit(solution)/shard_map/ppermute | solution.py:366
  92.8 21.1 %collective-permute-start.20 = (bf16[4,4,72,384]{3,2,1,0:T(8,128)(2,1)S(1)}, bf16[4,4,72,384]{3,2,1,0:T(8,128)(2,1)S(1)}, u32[]{:S(2)}, u32[]{:S(2)}) collective-permute-start(bf16[4,4,72,384]{3,2,1,0:T(8,128)(2,1)S(1)} %get-tuple-element.61), channel_id=1, source_target_pairs={{0,16},{4,20},{8,24},{12,28},{16,0},{20,4},{24,8},{28,12},{1,17},{... | collective-permute-start | bytes 2654216 | tf_op jit(solution)/shard_map/ppermute | solution.py:366
  93.5 20.8 %collective-permute-start.19 = (bf16[1,4,96,1152]{3,2,1,0:T(8,128)(2,1)S(1)}, bf16[1,4,96,1152]{3,2,1,0:T(8,128)(2,1)S(1)}, u32[]{:S(2)}, u32[]{:S(2)}) collective-permute-start(bf16[1,4,96,1152]{3,2,1,0:T(8,128)(2,1)S(1)} %shard_map.87), channel_id=1, source_target_pairs={{0,8},{4,12},{8,0},{12,4},{16,24},{20,28},{24,16},{28,20},{1,9},{5... | collective-permute-start | bytes 2654216 | tf_op jit(solution)/shard_map/ppermute | solution.py:366
  101.2 11.3 %collective-permute-start.17 = (bf16[1,4,96,1024]{3,2,1,0:T(8,128)(2,1)S(1)}, bf16[1,4,96,1024]{3,2,1,0:T(8,128)(2,1)S(1)}, u32[]{:S(2)}, u32[]{:S(2)}) collective-permute-start(bf16[1,4,96,1024]{3,2,1,0:T(8,128)(2,1)S(1)} %get-tuple-element.58), channel_id=1, source_target_pairs={{0,4},{4,0},{8,12},{12,8},{16,20},{20,16},{24,28},{28,24},{1,5},{5... | collective-permute-start | bytes 2359304 | tf_op jit(solution)/shard_map/ppermute | solution.py:366
  101.2 11.3 %collective-permute-start.16 = (bf16[1,4,96,1024]{3,2,1,0:T(8,128)(2,1)S(1)}, bf16[1,4,96,1024]{3,2,1,0:T(8,128)(2,1)S(1)}, u32[]{:S(2)}, u32[]{:S(2)}) collective-permute-start(bf16[1,4,96,1024]{3,2,1,0:T(8,128)(2,1)S(1)} %get-tuple-element.56), channel_id=1, source_target_pairs={{0,4},{4,0},{8,12},{12,8},{16,20},{20,16},{24,28},{28,24},{1,5},{5... | collective-permute-start | bytes 2359304 | tf_op jit(solution)/shard_map/ppermute | solution.py:366

commit v10 on v9

--- a/solution.py
+++ b/solution.py
@@ -322,30 +322,31 @@
 
 def finish_kernel(sc_ref, base_ref, *refs):
     *there, new_ref, _, down_ref, hidden_ref = refs
-    others = [ref[0, 0].astype(F32) for ref in there]
-    others = others[0] if len(others) == 1 else jnp.concatenate(others, axis=1)
-    down_ref[0] = (base_ref[0, 0].astype(F32) + others).astype(BF)
+    others = [ref[0].astype(F32) for ref in there]
+    others = others[0] if len(others) == 1 else jnp.concatenate(others, axis=2)
+    down_ref[...] = (base_ref[0].astype(F32) + others).astype(BF)
     hidden_ref[...] = new_ref[...]
 
 
 def finish(scalars, base, there, new, whole):
     _, experts, band, d = base.shape
     _, n, cap, f = new.shape
-    sums = lambda x: pl.BlockSpec((1, 1, band, x.shape[3]), lambda e, sc: (0, e, 0, 0))
+    group = 2 if experts % 2 == 0 else 1
+    sums = lambda x: pl.BlockSpec((1, group, band, x.shape[3]), lambda e, sc: (0, e, 0, 0))
     return pl.pallas_call(
         finish_kernel,
         out_shape=(jax.ShapeDtypeStruct((experts, band, d), BF), jax.ShapeDtypeStruct(whole.shape, BF)),
         grid_spec=pltpu.PrefetchScalarGridSpec(
             num_scalar_prefetch=1,
-            grid=(experts,),
+            grid=(experts // group,),
             in_specs=[
                 *[sums(x) for x in (base, *there)],
-                pl.BlockSpec((1, n, cap, f), lambda e, sc: (e, 0, 0, 0)),
+                pl.BlockSpec((group, n, cap, f), lambda e, sc: (e, 0, 0, 0)),
                 pl.BlockSpec(memory_space=pl.ANY),
             ],
             out_specs=(
-                pl.BlockSpec((1, band, d), lambda e, sc: (e, 0, 0)),
-                pl.BlockSpec((1, n, cap, f), lambda e, sc: (e, 0, 0, 1 - sc[1])),
+                pl.BlockSpec((group, band, d), lambda e, sc: (e, 0, 0)),
+                pl.BlockSpec((group, n, cap, f), lambda e, sc: (e, 0, 0, 1 - sc[1])),
             ),
         ),
         input_output_aliases={3 + len(there): 1},

time: 117 us -> 117 us (level)
  no operation moved by 1% of the time
where the time goes in v10:
time: 117 us; the launch traced here: 116 us
  waiting for transfers between devices  40.4 us (35%)
  Pallas kernels  32.8 us (28%)
  starting transfers between devices  28.5 us (24%)
  blocking collectives  10.2 us (9%)
  local copies, waits for them, and re-layouts  2.71 us (2%)
    ppermute x2, waiting for transfers between devices, spread(): two = lax.ppermute(x, 'expert', [(i, (i + 2) % n) for i in range(n)])  22.7 us
    pallas_call x2, Pallas kernels, backward(): pl.pallas_call(functools.partial(back_kernel, n, counts, group, rels), ou...  13.7 us
    pallas_call x3, Pallas kernels, partial_grad(): pl.pallas_call(functools.partial(part_kernel, n, bands, (counts, counts_n...  12 us
    ppermute x13, starting transfers between devices, swap(): return lax.ppermute(x, 'dp', [(i, i ^ bit) for i in range(n_dp)])  11.1 us
    all_to_all x1, blocking collectives, per_device(): lax.all_to_all(sg_own, 'expert', split_axis=0, concat_axis=0, tiled=True)  10.2 us
    ppermute x2, waiting for transfers between devices, spread(): passed = lax.ppermute(two, 'expert', [(2, 3), (1, 0)])  7.04 us
    ppermute x2, starting transfers between devices, spread(): one = lax.ppermute(x, 'expert', [(i, i + 1) for i in range(n - 1)])  6.98 us
    ppermute x2, waiting for transfers between devices, spread(): three = lax.ppermute(x, 'expert', [(i + 1, i) for i in range(n - 1)])  5.71 us
  transfers between devices with their start and end apart: 21, of which 8 were waited for; matrix products, arithmetic and copies ran while one was open for 1% of the time, Pallas kernels for 26%

profile of v10, /device:TPU:0, one launch (start us, length us, event | category | flops | bytes accessed | tf_op | source)
XLA Modules:
  0.0 116.4 jit_solution(9412317041802025089)
XLA Ops:
  0.6 0.5 collective-permute-start.4
  1.1 0.1 pad_add_fusion.sc_ref
  1.2 1.5 %copy-done = bf16[1,4,4,72,768]{4,3,2,1,0:T(8,128)(2,1)S(1)} copy-done((bf16[1,4,4,72,768]{4,3,2,1,0:T(8,128)(2,1)S(1)}, bf16[1,4,4,72,768]{4,3,2,1,0:T(8,128)(2,1)}, u32[]{:S(2)}) %copy-start) | copy-done | bytes 1769496
  2.7 1.0 copy-done.3
  3.8 0.8 shard_map.77
  4.5 2.7 %collective-permute-start.5 = (bf16[2048,384]{1,0:T(8,128)(2,1)S(1)}, bf16[2048,384]{1,0:T(8,128)(2,1)S(1)}, u32[]{:S(2)}, u32[]{:S(2)}) collective-permute-start(bf16[2048,384]{1,0:T(8,128)(2,1)S(1)} %shard_map.77), channel_id=1, source_target_pairs={{0,16},{4,20},{8,24},{12,28},{16,0},{20,4},{24,8},{28,12},{1,17},{... | collective-permute-start | bytes 4718600 | tf_op jit(solution)/shard_map/ppermute | solution.py:367
  7.4 0.0 slice-start.1
  7.4 2.7 %collective-permute-start.1 = (bf16[136,1408]{1,0:T(8,128)(2,1)S(1)}, bf16[136,1408]{1,0:T(8,128)(2,1)S(1)}, u32[]{:S(2)}, u32[]{:S(2)}) collective-permute-start(bf16[136,1408]{1,0:T(8,128)(2,1)S(1)} %pad_maximum_fusion.refs_0_), channel_id=1, source_target_pairs={{0,2},{1,3},{2,0},{3,1},{4,6},{5,7},{6,4},{7,5},{8,10},{9,11},{10,... | collective-permute-start | bytes 1148936 | tf_op jit(solution)/shard_map/ppermute | solution.py:374
  10.1 1.5 %collective-permute-start.12 = (bf16[1,4,96,2048]{3,2,1,0:T(8,128)(2,1)S(1)}, bf16[1,4,96,2048]{3,2,1,0:T(8,128)(2,1)S(1)}, u32[]{:S(2)}, u32[]{:S(2)}) collective-permute-start(bf16[1,4,96,2048]{3,2,1,0:T(8,128)(2,1)S(1)} %bitcast.12), channel_id=1, source_target_pairs={{0,8},{4,12},{8,0},{12,4},{16,24},{20,28},{24,16},{28,20},{1,9},{5... | collective-permute-start | bytes 4718600 | tf_op jit(solution)/shard_map/ppermute | solution.py:367
  11.6 3.5 %collective-permute-start = (bf16[136,1408]{1,0:T(8,128)(2,1)S(1)}, bf16[136,1408]{1,0:T(8,128)(2,1)S(1)}, u32[]{:S(2)}, u32[]{:S(2)}) collective-permute-start(bf16[136,1408]{1,0:T(8,128)(2,1)S(1)} %pad_maximum_fusion.refs_0_), channel_id=1, source_target_pairs={{0,1},{1,2},{2,3},{4,5},{5,6},{6,7},{8,9},{9,10},{10,11},{12,13},{... | collective-permute-start | bytes 1148936 | tf_op jit(solution)/shard_map/ppermute | solution.py:375
  15.1 1.3 %collective-permute-start.2 = (bf16[136,1408]{1,0:T(8,128)(2,1)S(1)}, bf16[136,1408]{1,0:T(8,128)(2,1)S(1)}, u32[]{:S(2)}, u32[]{:S(2)}) collective-permute-start(bf16[136,1408]{1,0:T(8,128)(2,1)S(1)} %pad_maximum_fusion.refs_0_), channel_id=1, source_target_pairs={{1,0},{2,1},{3,2},{5,4},{6,5},{7,6},{9,8},{10,9},{11,10},{13,12},{... | collective-permute-start | bytes 1148936 | tf_op jit(solution)/shard_map/ppermute | solution.py:376
  16.4 12.0 %collective-permute-done.1.refs_2_ = bf16[136,1408]{1,0:T(8,128)(2,1)S(1)} collective-permute-done((bf16[136,1408]{1,0:T(8,128)(2,1)S(1)}, bf16[136,1408]{1,0:T(8,128)(2,1)S(1)}, u32[]{:S(2)}, u32[]{:S(2)}) %collective-permute-start.1) | collective-permute-done | bytes 383008 | tf_op jit(solution)/shard_map/ppermute | solution.py:374
  28.4 1.3 %collective-permute-start.3 = (bf16[136,1408]{1,0:T(8,128)(2,1)S(1)}, bf16[136,1408]{1,0:T(8,128)(2,1)S(1)}, u32[]{:S(2)}, u32[]{:S(2)}) collective-permute-start(bf16[136,1408]{1,0:T(8,128)(2,1)S(1)} %collective-permute-done.1.refs_2_), channel_id=1, source_target_pairs={{2,3},{1,0},{6,7},{5,4},{10,11},{9,8},{14,15},{13,12},{18,19},{17,... | collective-permute-start | bytes 1148936 | tf_op jit(solution)/shard_map/ppermute | solution.py:377
  29.7 5.7 %collective-permute-done.2.refs_3_ = bf16[136,1408]{1,0:T(8,128)(2,1)S(1)} collective-permute-done((bf16[136,1408]{1,0:T(8,128)(2,1)S(1)}, bf16[136,1408]{1,0:T(8,128)(2,1)S(1)}, u32[]{:S(2)}, u32[]{:S(2)}) %collective-permute-start.2) | collective-permute-done | bytes 383008 | tf_op jit(solution)/shard_map/ppermute | solution.py:376
  35.4 6.9 %collective-permute-done.3.refs_4_ = bf16[136,1408]{1,0:T(8,128)(2,1)S(1)} collective-permute-done((bf16[136,1408]{1,0:T(8,128)(2,1)S(1)}, bf16[136,1408]{1,0:T(8,128)(2,1)S(1)}, u32[]{:S(2)}, u32[]{:S(2)}) %collective-permute-start.3) | collective-permute-done | bytes 383008 | tf_op jit(solution)/shard_map/ppermute | solution.py:377
  42.3 0.7 shard_map.76.tab_ref.refs_1_
  43.0 1.0 collective-permute-start.6
  43.9 0.1 fusion.4
  44.0 2.7 %collective-permute-start.8 = (bf16[256,640]{1,0:T(8,128)(2,1)S(1)}, bf16[256,640]{1,0:T(8,128)(2,1)S(1)}, u32[]{:S(2)}, u32[]{:S(2)}) collective-permute-start(bf16[256,640]{1,0:T(8,128)(2,1)S(1)} %fusion.refs_2_.refs_9_), channel_id=1, source_target_pairs={{0,2},{1,3},{2,0},{3,1},{4,6},{5,7},{6,4},{7,5},{8,10},{9,11},{10,... | collective-permute-start | bytes 983048 | tf_op jit(solution)/shard_map/ppermute | solution.py:374
  46.7 3.5 %collective-permute-start.7 = (bf16[256,640]{1,0:T(8,128)(2,1)S(1)}, bf16[256,640]{1,0:T(8,128)(2,1)S(1)}, u32[]{:S(2)}, u32[]{:S(2)}) collective-permute-start(bf16[256,640]{1,0:T(8,128)(2,1)S(1)} %fusion.refs_2_.refs_9_), channel_id=1, source_target_pairs={{0,1},{1,2},{2,3},{4,5},{5,6},{6,7},{8,9},{9,10},{10,11},{12,13},{... | collective-permute-start | bytes 983048 | tf_op jit(solution)/shard_map/ppermute | solution.py:375
  50.2 1.3 %collective-permute-start.9 = (bf16[256,640]{1,0:T(8,128)(2,1)S(1)}, bf16[256,640]{1,0:T(8,128)(2,1)S(1)}, u32[]{:S(2)}, u32[]{:S(2)}) collective-permute-start(bf16[256,640]{1,0:T(8,128)(2,1)S(1)} %fusion.refs_2_.refs_9_), channel_id=1, source_target_pairs={{1,0},{2,1},{3,2},{5,4},{6,5},{7,6},{9,8},{10,9},{11,10},{13,12},{... | collective-permute-start | bytes 983048 | tf_op jit(solution)/shard_map/ppermute | solution.py:376
  51.5 10.6 %collective-permute-done.8.refs_4_.refs_11_ = bf16[256,640]{1,0:T(8,128)(2,1)S(1)} collective-permute-done((bf16[256,640]{1,0:T(8,128)(2,1)S(1)}, bf16[256,640]{1,0:T(8,128)(2,1)S(1)}, u32[]{:S(2)}, u32[]{:S(2)}) %collective-permute-start.8) | collective-permute-done | bytes 327712 | tf_op jit(solution)/shard_map/ppermute | solution.py:374
  62.1 1.3 %collective-permute-start.10 = (bf16[256,640]{1,0:T(8,128)(2,1)S(1)}, bf16[256,640]{1,0:T(8,128)(2,1)S(1)}, u32[]{:S(2)}, u32[]{:S(2)}) collective-permute-start(bf16[256,640]{1,0:T(8,128)(2,1)S(1)} %collective-permute-done.8.refs_4_.refs_11_), channel_id=1, source_target_pairs={{2,3},{1,0},{6,7},{5,4},{10,11},{9,8},{14,15},{13,12},{18,19},{17,... | collective-permute-start | bytes 983048 | tf_op jit(solution)/shard_map/ppermute | solution.py:377
  63.4 0.1 collective-permute-start.13
  63.5 1.3 %shard_map.78 = (bf16[4,384,512]{2,1,0:T(8,128)(2,1)S(1)}, f32[4,4,1,128]{3,2,1,0:T(1,128)S(1)}, f32[4,4,1,128]{3,2,1,0:T(1,128)S(1)}) custom-call(s32[3]{0:T(128)S(1)} %pad_add_fusion.sc_ref, bf16[400,1408]{1,0:T(8,128)(2,1)S(1)} %shard_map.76.tab_ref.refs_1_, bf16[1,4,4,72,768]{4,3,2,1,0:T(8,128)(2,1)S(1)} %copy-done.1), custom_call_target="tpu_custom_call" | custom-call | flops 1 | bytes 1 | tf_op jit(solution)/shard_map/pallas_call | solution.py:50
  64.9 0.1 slice.60
  65.0 3.7 %collective-permute-done.6.tab_ref.refs_3_.refs_8_.refs_1_ = bf16[400,1408]{1,0:T(8,128)(2,1)S(1)} collective-permute-done((bf16[400,1408]{1,0:T(8,128)(2,1)S(1)}, bf16[400,1408]{1,0:T(8,128)(2,1)S(1)}, u32[]{:S(2)}, u32[]{:S(2)}) %collective-permute-start.6) | collective-permute-done | bytes 1126432 | tf_op jit(solution)/shard_map/ppermute | solution.py:367
  68.7 1.3 %shard_map.79 = (bf16[4,384,512]{2,1,0:T(8,128)(2,1)S(1)}, f32[4,4,1,128]{3,2,1,0:T(1,128)S(1)}, f32[4,4,1,128]{3,2,1,0:T(1,128)S(1)}) custom-call(s32[3]{0:T(128)S(1)} %pad_add_fusion.sc_ref, bf16[400,1408]{1,0:T(8,128)(2,1)S(1)} %collective-permute-done.6.tab_ref.refs_3_.refs_8_.refs_1_, bf16[1,4,4,80,384]{4,3,2,1,0:T(8,128)(2,1)S(1)} %bitcast.9), custom_call_target="tpu_custom_call" | custom-call | flops 1 | bytes 1 | tf_op jit(solution)/shard_map/pallas_call | solution.py:50
  70.0 3.2 %shard_map.80 = (bf16[1,4,96,896]{3,2,1,0:T(8,128)(2,1)S(1)}, bf16[1,4,96,896]{3,2,1,0:T(8,128)(2,1)S(1)}) custom-call(s32[3]{0:T(128)S(1)} %pad_add_fusion.sc_ref, bf16[136,1408]{1,0:T(8,128)(2,1)S(1)} %pad_maximum_fusion.refs_0_, bf16[400,1408]{1,0:T(8,128)(2,1)S(1)} %shard_map.76.tab_ref.refs_1_, ...), custom_call_target="tpu_custom_call" | custom-call | flops 1 | bytes 1 | tf_op jit(solution)/shard_map/pallas_call | solution.py:282
  73.2 0.1 collective-permute-done.10.refs_6_.refs_13_
  73.3 3.7 %shard_map.81 = (bf16[1,4,96,1152]{3,2,1,0:T(8,128)(2,1)S(1)}, bf16[1,4,96,1152]{3,2,1,0:T(8,128)(2,1)S(1)}) custom-call(s32[3]{0:T(128)S(1)} %pad_add_fusion.sc_ref, bf16[136,1408]{1,0:T(8,128)(2,1)S(1)} %pad_maximum_fusion.refs_0_, bf16[400,1408]{1,0:T(8,128)(2,1)S(1)} %shard_map.76.tab_ref.refs_1_, bf16[256,640]{1,0:T(8,128)(2,1)S(1)} %fusion.refs_2_.refs_9_, ...), custom_call_target="tpu_custom_call" | custom-call | flops 1 | bytes 1 | tf_op jit(solution)/shard_map/pallas_call | solution.py:282
  77.0 0.6 collective-permute-start.18
  77.6 0.2 shard_map.82
  77.8 1.6 %collective-permute-start.14 = (bf16[1,4,96,896]{3,2,1,0:T(8,128)(2,1)S(1)}, bf16[1,4,96,896]{3,2,1,0:T(8,128)(2,1)S(1)}, u32[]{:S(2)}, u32[]{:S(2)}) collective-permute-start(bf16[1,4,96,896]{3,2,1,0:T(8,128)(2,1)S(1)} %shard_map.82), channel_id=1, source_target_pairs={{0,8},{4,12},{8,0},{12,4},{16,24},{20,28},{24,16},{28,20},{1,9},{5... | collective-permute-start | bytes 2064392 | tf_op jit(solution)/shard_map/ppermute | solution.py:367
  79.4 6.5 %shard_map.83 = (bf16[4,4,72,384]{3,2,1,0:T(8,128)(2,1)S(1)}, f32[4,4,1,128]{3,2,1,0:T(1,128)S(1)}) custom-call(s32[3]{0:T(128)S(1)} %pad_add_fusion.sc_ref, bf16[128,1408]{1,0:T(8,128)(2,1)S(1)} %pad_maximum_fusion.1.refs_2_.refs_7_.refs_0_, bf16[400,1408]{1,0:T(8,128)(2,1)S(1)} %collective-permute-done.6.tab_ref.refs_3_.refs_8_.refs_1_, ...), custom_call_target="tpu_custom_call" | custom-call | flops 1 | bytes 1 | tf_op jit(solution)/shard_map/pallas_call | solution.py:218
  85.9 1.5 %collective-permute-start.15 = (f32[4,4,1,128]{3,2,1,0:T(1,128)S(1)}, f32[4,4,1,128]{3,2,1,0:T(1,128)S(1)}, u32[]{:S(2)}, u32[]{:S(2)}) collective-permute-start(f32[4,4,1,128]{3,2,1,0:T(1,128)S(1)} %get-tuple-element.48), channel_id=1, source_target_pairs={{0,16},{4,20},{8,24},{12,28},{16,0},{20,4},{24,8},{28,12},{1,17},{... | collective-permute-start | bytes 24584 | tf_op jit(solution)/shard_map/ppermute | solution.py:367
  87.4 5.1 %shard_map.84 = (bf16[1,4,96,1024]{3,2,1,0:T(8,128)(2,1)S(1)}, bf16[1,4,96,1024]{3,2,1,0:T(8,128)(2,1)S(1)}, bf16[1,4,96,2048]{3,2,1,0:T(8,128)(2,1)S(1)}) custom-call(s32[3]{0:T(128)S(1)} %pad_add_fusion.sc_ref, bf16[136,1408]{1,0:T(8,128)(2,1)S(1)} %pad_maximum_fusion.refs_0_, bf16[400,1408]{1,0:T(8,128)(2,1)S(1)} %shard_map.76.tab_ref.refs_1_, ...), custom_call_target="tpu_custom_call" | custom-call | flops 1 | bytes 1 | tf_op jit(solution)/shard_map/pallas_call | solution.py:282
  92.5 0.3 shard_map.87
  92.8 0.6 collective-permute-start.20
  93.5 0.5 collective-permute-start.19
  94.0 7.3 %shard_map.85 = (bf16[4,4,72,768]{3,2,1,0:T(8,128)(2,1)}, f32[4,4,1,128]{3,2,1,0:T(1,128)S(1)}) custom-call(s32[3]{0:T(128)S(1)} %pad_add_fusion.sc_ref, bf16[136,1408]{1,0:T(8,128)(2,1)S(1)} %pad_maximum_fusion.refs_0_, bf16[400,1408]{1,0:T(8,128)(2,1)S(1)} %shard_map.76.tab_ref.refs_1_, bf16[256,640]{1,0:T(8,128)(2,1)S(1)} %fusion.refs_2_.refs_9_, ...), custom_call_target="tpu_custom_call" | custom-call | flops 1 | bytes 1 | tf_op jit(solution)/shard_map/pallas_call | solution.py:218
  101.2 0.5 collective-permute-start.16
  101.8 10.2 %all_to_all.5 = f32[4,4,1,128]{3,2,1,0:T(1,128)S(1)} all-to-all(f32[4,4,1,128]{3,2,1,0:T(1,128)S(1)} %get-tuple-element.55), channel_id=1, replica_groups=mesh['dp'=8,'expert'=4] {'expert'}, dimensions={0} | all-to-all | bytes 16384 | tf_op jit(solution)/shard_map/all_to_all | solution.py:444
  112.0 0.6 select_reduce_fusion
  112.6 0.4 shard_map.86.base_ref
  113.0 0.9 collective-permute-done.20.refs_2_
  113.9 0.3 collective-permute-done.19.refs_1_
  114.2 2.2 %shard_map.88 = (bf16[4,96,2048]{2,1,0:T(8,128)(2,1)}, bf16[4,4,72,768]{3,2,1,0:T(8,128)(2,1)}) custom-call(s32[3]{0:T(128)S(1)} %pad_add_fusion.sc_ref, bf16[1,4,96,2048]{3,2,1,0:T(8,128)(2,1)S(1)} %shard_map.86.base_ref, bf16[1,4,96,896]{3,2,1,0:T(8,128)(2,1)S(1)} %collective-permute-done.14.refs_0_, ...), custom_call_target="tpu_custom_call", output_to_operand_aliasing={{1}: (5, {})} | custom-call | flops 1 | bytes 1 | tf_op jit(solution)/shard_map/pallas_call | solution.py:336
  (36 shorter events, 0.2 us)
Async XLA Ops:
  0.6 3.9 %collective-permute-start.4 = (bf16[1,4,96,2048]{3,2,1,0:T(8,128)(2,1)}, bf16[1,4,96,2048]{3,2,1,0:T(8,128)(2,1)S(1)}, u32[]{:S(2)}, u32[]{:S(2)}) collective-permute-start(bf16[1,4,96,2048]{3,2,1,0:T(8,128)(2,1)} %bitcast.11), channel_id=1, source_target_pairs={{0,4},{4,0},{8,12},{12,8},{16,20},{20,16},{24,28},{28,24},{1,5},{5... | collective-permute-start | bytes 4718600 | tf_op jit(solution)/shard_map/ppermute | solution.py:367
  1.2 1.5 %copy-start = (bf16[1,4,4,72,768]{4,3,2,1,0:T(8,128)(2,1)S(1)}, bf16[1,4,4,72,768]{4,3,2,1,0:T(8,128)(2,1)}, u32[]{:S(2)}) copy-start(bf16[1,4,4,72,768]{4,3,2,1,0:T(8,128)(2,1)} %refs_11_.1) | copy-start | bytes 5308420
  2.7 1.0 copy-start.3
  3.7 3.5 %copy-start.5 = (bf16[128,8]{0,1:T(8,128)(2,1)S(1)}, bf16[128,8]{0,1:T(8,128)(2,1)}, u32[]{:S(2)}) copy-start(bf16[128,8]{0,1:T(8,128)(2,1)} %param.7) | copy-start | bytes 6148
  3.7 3.5 %copy-start.4 = (s32[128,8]{0,1:T(8,128)S(1)}, s32[128,8]{0,1:T(8,128)}, u32[]{:S(2)}) copy-start(s32[128,8]{0,1:T(8,128)} %param.6) | copy-start | bytes 12292
  3.7 3.6 %slice-start = ((bf16[128,2048]{1,0:T(8,128)(2,1)}), bf16[128,1408]{1,0:T(8,128)(2,1)S(1)}, s32[]{:S(2)}) async-start(bf16[128,2048]{1,0:T(8,128)(2,1)} %tok_ref.1), calls=%async_computation.1 | async-start | bytes 720896 | tf_op jit(solution)/shard_map/slice | solution.py:386
  3.8 6.3 %copy-start.2 = (bf16[4,96,2048]{2,1,0:T(8,128)(2,1)S(1)}, bf16[4,96,2048]{2,1,0:T(8,128)(2,1)}, u32[]{:S(2)}) copy-start(bf16[4,96,2048]{2,1,0:T(8,128)(2,1)} %param.9) | copy-start | bytes 4718596
  4.5 38.4 %collective-permute-start.5 = (bf16[2048,384]{1,0:T(8,128)(2,1)S(1)}, bf16[2048,384]{1,0:T(8,128)(2,1)S(1)}, u32[]{:S(2)}, u32[]{:S(2)}) collective-permute-start(bf16[2048,384]{1,0:T(8,128)(2,1)S(1)} %shard_map.77), channel_id=1, source_target_pairs={{0,16},{4,20},{8,24},{12,28},{16,0},{20,4},{24,8},{28,12},{1,17},{... | collective-permute-start | bytes 4718600 | tf_op jit(solution)/shard_map/ppermute | solution.py:367
  7.4 36.6 %slice-start.1 = ((bf16[128,2048]{1,0:T(8,128)(2,1)}), bf16[128,640]{1,0:T(8,128)(2,1)S(1)}, s32[]{:S(2)}) async-start(bf16[128,2048]{1,0:T(8,128)(2,1)} %tok_ref.1), calls=%async_computation.2 | async-start | bytes 327680 | tf_op jit(solution)/shard_map/slice | solution.py:409
  7.4 21.0 %collective-permute-start.1 = (bf16[136,1408]{1,0:T(8,128)(2,1)S(1)}, bf16[136,1408]{1,0:T(8,128)(2,1)S(1)}, u32[]{:S(2)}, u32[]{:S(2)}) collective-permute-start(bf16[136,1408]{1,0:T(8,128)(2,1)S(1)} %pad_maximum_fusion.refs_0_), channel_id=1, source_target_pairs={{0,2},{1,3},{2,0},{3,1},{4,6},{5,7},{6,4},{7,5},{8,10},{9,11},{10,... | collective-permute-start | bytes 1148936 | tf_op jit(solution)/shard_map/ppermute | solution.py:374
  10.1 53.4 %collective-permute-start.12 = (bf16[1,4,96,2048]{3,2,1,0:T(8,128)(2,1)S(1)}, bf16[1,4,96,2048]{3,2,1,0:T(8,128)(2,1)S(1)}, u32[]{:S(2)}, u32[]{:S(2)}) collective-permute-start(bf16[1,4,96,2048]{3,2,1,0:T(8,128)(2,1)S(1)} %bitcast.12), channel_id=1, source_target_pairs={{0,8},{4,12},{8,0},{12,4},{16,24},{20,28},{24,16},{28,20},{1,9},{5... | collective-permute-start | bytes 4718600 | tf_op jit(solution)/shard_map/ppermute | solution.py:367
  11.6 18.1 %collective-permute-start = (bf16[136,1408]{1,0:T(8,128)(2,1)S(1)}, bf16[136,1408]{1,0:T(8,128)(2,1)S(1)}, u32[]{:S(2)}, u32[]{:S(2)}) collective-permute-start(bf16[136,1408]{1,0:T(8,128)(2,1)S(1)} %pad_maximum_fusion.refs_0_), channel_id=1, source_target_pairs={{0,1},{1,2},{2,3},{4,5},{5,6},{6,7},{8,9},{9,10},{10,11},{12,13},{... | collective-permute-start | bytes 1148936 | tf_op jit(solution)/shard_map/ppermute | solution.py:375
  15.1 20.3 %collective-permute-start.2 = (bf16[136,1408]{1,0:T(8,128)(2,1)S(1)}, bf16[136,1408]{1,0:T(8,128)(2,1)S(1)}, u32[]{:S(2)}, u32[]{:S(2)}) collective-permute-start(bf16[136,1408]{1,0:T(8,128)(2,1)S(1)} %pad_maximum_fusion.refs_0_), channel_id=1, source_target_pairs={{1,0},{2,1},{3,2},{5,4},{6,5},{7,6},{9,8},{10,9},{11,10},{13,12},{... | collective-permute-start | bytes 1148936 | tf_op jit(solution)/shard_map/ppermute | solution.py:376
  28.4 13.9 %collective-permute-start.3 = (bf16[136,1408]{1,0:T(8,128)(2,1)S(1)}, bf16[136,1408]{1,0:T(8,128)(2,1)S(1)}, u32[]{:S(2)}, u32[]{:S(2)}) collective-permute-start(bf16[136,1408]{1,0:T(8,128)(2,1)S(1)} %collective-permute-done.1.refs_2_), channel_id=1, source_target_pairs={{2,3},{1,0},{6,7},{5,4},{10,11},{9,8},{14,15},{13,12},{18,19},{17,... | collective-permute-start | bytes 1148936 | tf_op jit(solution)/shard_map/ppermute | solution.py:377
  42.9 20.6 %copy-start.1 = (bf16[1,4,4,72,768]{4,3,2,1,0:T(8,128)(2,1)S(1)}, bf16[1,4,4,72,768]{4,3,2,1,0:T(8,128)(2,1)}, u32[]{:S(2)}) copy-start(bf16[1,4,4,72,768]{4,3,2,1,0:T(8,128)(2,1)} %refs_11_.1) | copy-start | bytes 5308420
  43.0 25.7 %collective-permute-start.6 = (bf16[400,1408]{1,0:T(8,128)(2,1)S(1)}, bf16[400,1408]{1,0:T(8,128)(2,1)S(1)}, u32[]{:S(2)}, u32[]{:S(2)}) collective-permute-start(bf16[400,1408]{1,0:T(8,128)(2,1)S(1)} %shard_map.76.tab_ref.refs_1_), channel_id=1, source_target_pairs={{0,16},{4,20},{8,24},{12,28},{16,0},{20,4},{24,8},{28,12},{1,17},{... | collective-permute-start | bytes 3379208 | tf_op jit(solution)/shard_map/ppermute | solution.py:367
  44.0 18.1 %collective-permute-start.8 = (bf16[256,640]{1,0:T(8,128)(2,1)S(1)}, bf16[256,640]{1,0:T(8,128)(2,1)S(1)}, u32[]{:S(2)}, u32[]{:S(2)}) collective-permute-start(bf16[256,640]{1,0:T(8,128)(2,1)S(1)} %fusion.refs_2_.refs_9_), channel_id=1, source_target_pairs={{0,2},{1,3},{2,0},{3,1},{4,6},{5,7},{6,4},{7,5},{8,10},{9,11},{10,... | collective-permute-start | bytes 983048 | tf_op jit(solution)/shard_map/ppermute | solution.py:374
  46.7 26.5 %collective-permute-start.7 = (bf16[256,640]{1,0:T(8,128)(2,1)S(1)}, bf16[256,640]{1,0:T(8,128)(2,1)S(1)}, u32[]{:S(2)}, u32[]{:S(2)}) collective-permute-start(bf16[256,640]{1,0:T(8,128)(2,1)S(1)} %fusion.refs_2_.refs_9_), channel_id=1, source_target_pairs={{0,1},{1,2},{2,3},{4,5},{5,6},{6,7},{8,9},{9,10},{10,11},{12,13},{... | collective-permute-start | bytes 983048 | tf_op jit(solution)/shard_map/ppermute | solution.py:375
  50.2 23.0 %collective-permute-start.9 = (bf16[256,640]{1,0:T(8,128)(2,1)S(1)}, bf16[256,640]{1,0:T(8,128)(2,1)S(1)}, u32[]{:S(2)}, u32[]{:S(2)}) collective-permute-start(bf16[256,640]{1,0:T(8,128)(2,1)S(1)} %fusion.refs_2_.refs_9_), channel_id=1, source_target_pairs={{1,0},{2,1},{3,2},{5,4},{6,5},{7,6},{9,8},{10,9},{11,10},{13,12},{... | collective-permute-start | bytes 983048 | tf_op jit(solution)/shard_map/ppermute | solution.py:376
  62.1 11.2 %collective-permute-start.10 = (bf16[256,640]{1,0:T(8,128)(2,1)S(1)}, bf16[256,640]{1,0:T(8,128)(2,1)S(1)}, u32[]{:S(2)}, u32[]{:S(2)}) collective-permute-start(bf16[256,640]{1,0:T(8,128)(2,1)S(1)} %collective-permute-done.8.refs_4_.refs_11_), channel_id=1, source_target_pairs={{2,3},{1,0},{6,7},{5,4},{10,11},{9,8},{14,15},{13,12},{18,19},{17,... | collective-permute-start | bytes 983048 | tf_op jit(solution)/shard_map/ppermute | solution.py:377
  63.4 15.9 %collective-permute-start.13 = (bf16[1,4,96,2048]{3,2,1,0:T(8,128)(2,1)S(1)}, bf16[1,4,96,2048]{3,2,1,0:T(8,128)(2,1)S(1)}, u32[]{:S(2)}, u32[]{:S(2)}) collective-permute-start(bf16[1,4,96,2048]{3,2,1,0:T(8,128)(2,1)S(1)} %collective-permute-done.12.refs_9_), channel_id=1, source_target_pairs={{0,4},{4,0},{8,12},{12,8},{16,20},{20,16},{24,28},{28,24},{1,5},{5... | collective-permute-start | bytes 4718600 | tf_op jit(solution)/shard_map/ppermute | solution.py:367
  73.3 4.3 %collective-permute-start.11 = (bf16[1,4,96,896]{3,2,1,0:T(8,128)(2,1)S(1)}, bf16[1,4,96,896]{3,2,1,0:T(8,128)(2,1)S(1)}, u32[]{:S(2)}, u32[]{:S(2)}) collective-permute-start(bf16[1,4,96,896]{3,2,1,0:T(8,128)(2,1)S(1)} %get-tuple-element.44), channel_id=1, source_target_pairs={{0,4},{4,0},{8,12},{12,8},{16,20},{20,16},{24,28},{28,24},{1,5},{5... | collective-permute-start | bytes 2064392 | tf_op jit(solution)/shard_map/ppermute | solution.py:367
  77.0 15.5 %collective-permute-start.18 = (bf16[1,4,96,1152]{3,2,1,0:T(8,128)(2,1)S(1)}, bf16[1,4,96,1152]{3,2,1,0:T(8,128)(2,1)S(1)}, u32[]{:S(2)}, u32[]{:S(2)}) collective-permute-start(bf16[1,4,96,1152]{3,2,1,0:T(8,128)(2,1)S(1)} %get-tuple-element.41), channel_id=1, source_target_pairs={{0,4},{4,0},{8,12},{12,8},{16,20},{20,16},{24,28},{28,24},{1,5},{5... | collective-permute-start | bytes 2654216 | tf_op jit(solution)/shard_map/ppermute | solution.py:367
  77.8 23.4 %collective-permute-start.14 = (bf16[1,4,96,896]{3,2,1,0:T(8,128)(2,1)S(1)}, bf16[1,4,96,896]{3,2,1,0:T(8,128)(2,1)S(1)}, u32[]{:S(2)}, u32[]{:S(2)}) collective-permute-start(bf16[1,4,96,896]{3,2,1,0:T(8,128)(2,1)S(1)} %shard_map.82), channel_id=1, source_target_pairs={{0,8},{4,12},{8,0},{12,4},{16,24},{20,28},{24,16},{28,20},{1,9},{5... | collective-permute-start | bytes 2064392 | tf_op jit(solution)/shard_map/ppermute | solution.py:367
  85.9 7.0 %collective-permute-start.15 = (f32[4,4,1,128]{3,2,1,0:T(1,128)S(1)}, f32[4,4,1,128]{3,2,1,0:T(1,128)S(1)}, u32[]{:S(2)}, u32[]{:S(2)}) collective-permute-start(f32[4,4,1,128]{3,2,1,0:T(1,128)S(1)} %get-tuple-element.48), channel_id=1, source_target_pairs={{0,16},{4,20},{8,24},{12,28},{16,0},{20,4},{24,8},{28,12},{1,17},{... | collective-permute-start | bytes 24584 | tf_op jit(solution)/shard_map/ppermute | solution.py:367
  92.8 21.1 %collective-permute-start.20 = (bf16[4,4,72,384]{3,2,1,0:T(8,128)(2,1)S(1)}, bf16[4,4,72,384]{3,2,1,0:T(8,128)(2,1)S(1)}, u32[]{:S(2)}, u32[]{:S(2)}) collective-permute-start(bf16[4,4,72,384]{3,2,1,0:T(8,128)(2,1)S(1)} %get-tuple-element.61), channel_id=1, source_target_pairs={{0,16},{4,20},{8,24},{12,28},{16,0},{20,4},{24,8},{28,12},{1,17},{... | collective-permute-start | bytes 2654216 | tf_op jit(solution)/shard_map/ppermute | solution.py:367
  93.5 20.8 %collective-permute-start.19 = (bf16[1,4,96,1152]{3,2,1,0:T(8,128)(2,1)S(1)}, bf16[1,4,96,1152]{3,2,1,0:T(8,128)(2,1)S(1)}, u32[]{:S(2)}, u32[]{:S(2)}) collective-permute-start(bf16[1,4,96,1152]{3,2,1,0:T(8,128)(2,1)S(1)} %shard_map.87), channel_id=1, source_target_pairs={{0,8},{4,12},{8,0},{12,4},{16,24},{20,28},{24,16},{28,20},{1,9},{5... | collective-permute-start | bytes 2654216 | tf_op jit(solution)/shard_map/ppermute | solution.py:367
  101.2 11.3 %collective-permute-start.17 = (bf16[1,4,96,1024]{3,2,1,0:T(8,128)(2,1)S(1)}, bf16[1,4,96,1024]{3,2,1,0:T(8,128)(2,1)S(1)}, u32[]{:S(2)}, u32[]{:S(2)}) collective-permute-start(bf16[1,4,96,1024]{3,2,1,0:T(8,128)(2,1)S(1)} %get-tuple-element.58), channel_id=1, source_target_pairs={{0,4},{4,0},{8,12},{12,8},{16,20},{20,16},{24,28},{28,24},{1,5},{5... | collective-permute-start | bytes 2359304 | tf_op jit(solution)/shard_map/ppermute | solution.py:367
  101.2 11.3 %collective-permute-start.16 = (bf16[1,4,96,1024]{3,2,1,0:T(8,128)(2,1)S(1)}, bf16[1,4,96,1024]{3,2,1,0:T(8,128)(2,1)S(1)}, u32[]{:S(2)}, u32[]{:S(2)}) collective-permute-start(bf16[1,4,96,1024]{3,2,1,0:T(8,128)(2,1)S(1)} %get-tuple-element.56), channel_id=1, source_target_pairs={{0,4},{4,0},{8,12},{12,8},{16,20},{20,16},{24,28},{28,24},{1,5},{5... | collective-permute-start | bytes 2359304 | tf_op jit(solution)/shard_map/ppermute | solution.py:367
